TPU v7x, 32 devices: a whole 2x2x4 slice. The times are simulated.
32 devices in a mesh: dp: 16 (over z, y, x), tensor: 2 (over core).
Axes of the slice: x: 2, y: 2, z: 4, core: 2. Of those that a mesh axis runs over, the one named last changes fastest.
Arguments:
- embeds: bfloat16 [24576, 640], P('dp'), may hold values from -6 to 6
- domain: int32 [24576, 1], P('dp'), may hold values from 0 to 3; in each aligned block of 768 rows (0 to 767, 768 to 1535, ...) at most 384 rows name the same one
- frozen: int32 [4], replicated, may hold values from 0 to 1, as said below
- labels: int32 [24576], P('dp'), may hold values from 0 to 1
- proj_w: bfloat16 [640, 512], P(None, ('dp', 'tensor')), may hold values from -0.25 to 0.25
- proj_b: bfloat16 [512], P(('dp', 'tensor')), may hold values from -0.625 to 0.625
- w_in: bfloat16 [12, 512, 1024], P(None, 'dp', 'tensor'), may hold values from -0.25 to 0.25
- in_bias: bfloat16 [12, 1024], P(None, ('dp', 'tensor')), may hold values from -0.625 to 0.625
- w_out: bfloat16 [12, 1024, 512], P(None, 'tensor', 'dp'), may hold values from -0.1875 to 0.1875
- out_bias: bfloat16 [12, 512], P(None, ('dp', 'tensor')), may hold values from -0.625 to 0.625
- ln_gain: bfloat16 [12, 512], P(None, ('dp', 'tensor')), may hold values from 0.5 to 1.5
- ln_shift: bfloat16 [12, 512], P(None, ('dp', 'tensor')), may hold values from -0.625 to 0.625
- gate_top: bfloat16 [4, 512, 2], P(None, ('dp', 'tensor')), may hold values from -0.1875 to 0.1875
- gate_shared: bfloat16 [4, 512, 4], P(None, ('dp', 'tensor')), may hold values from -0.1875 to 0.1875
- gate_domain: bfloat16 [4, 512, 2], P(None, ('dp', 'tensor')), may hold values from -0.1875 to 0.1875
- tower_w: bfloat16 [4, 512, 256], P(None, ('dp', 'tensor')), may hold values from -0.25 to 0.25
- tower_b: bfloat16 [4, 256], P(None, ('dp', 'tensor')), may hold values from -0.625 to 0.625
- tower_out: bfloat16 [4, 256], P(None, ('dp', 'tensor')), may hold values from -0.75 to 0.75
- tower_out_b: bfloat16 [4], replicated, may hold values from -3 to 3
Outputs:
- predictions: float32 [24576], P('dp')
- grad_embeds: bfloat16 [24576, 640], P('dp')
- grad_proj_w: float32 [640, 512], P(None, ('dp', 'tensor'))
- grad_proj_b: float32 [512], P(('dp', 'tensor'))
- grad_w_in: float32 [12, 512, 1024], P(None, 'dp', 'tensor')
- grad_in_bias: float32 [12, 1024], P(None, ('dp', 'tensor'))
- grad_w_out: float32 [12, 1024, 512], P(None, 'tensor', 'dp')
- grad_out_bias: float32 [12, 512], P(None, ('dp', 'tensor'))
- grad_ln_gain: float32 [12, 512], P(None, ('dp', 'tensor'))
- grad_ln_shift: float32 [12, 512], P(None, ('dp', 'tensor'))
- grad_gate_top: float32 [4, 512, 2], P(None, ('dp', 'tensor'))
- grad_gate_shared: float32 [4, 512, 4], P(None, ('dp', 'tensor'))
- grad_gate_domain: float32 [4, 512, 2], P(None, ('dp', 'tensor'))
- grad_tower_w: float32 [4, 512, 256], P(None, ('dp', 'tensor'))
- grad_tower_b: float32 [4, 256], P(None, ('dp', 'tensor'))
- grad_tower_out: float32 [4, 256], P(None, ('dp', 'tensor'))
- grad_tower_out_b: float32 [4], replicated
Inputs may be any that keep to these rules, and one draw needn't show every extreme that they name: Among the 768 events of one device's micro-batch (aligned blocks of 768 rows) no domain has more than 384 events; some domain has exactly 384 in some blocks. `frozen`: exactly 2 domains are flagged.
All inputs are finite; a program needn't handle non-finite values.
Results may differ from a plain program's by a relative error of at most 0.017.
Values may be sent and summed in bfloat16 or wider, within the bound.
No kernel may reach another device: no remote copies, remote signals or barrier semaphores. Data moves between devices by JAX's collectives and lax.ppermute only.
A program may use at most 256 MiB of HBM per device.

v0:
```python
import functools
import math

import jax
import jax.numpy as jnp
from jax import lax
from jax.experimental import pallas as pl
from jax.experimental.pallas import tpu as pltpu
from jax.sharding import PartitionSpec as P

D = 512
H = 1024
TW = 256
S = 4
DOM = 4
K = 2
EPS = 1e-05
FROZEN_SHARE = 0.25
TILE = 256
LOCAL = 6
CHUNKS_FORWARD = ((0,), (1, 2), (3, 4), (5,))
CHUNKS_BACKWARD = ((5,), (3, 4), (1, 2), (0,))
VMEM_LIMIT = 56 * 1024 * 1024
PACK = 1792

bf16 = jnp.bfloat16
f32 = jnp.float32


def dims_of(count):
    if count % 4 == 0:
        rest = count // 4
        root = math.isqrt(rest)
        if root * root == rest:
            return (4, root, root)
    return (count, 1, 1)


class Box:
    def __init__(self, count):
        self.count = count
        self.dims = dims_of(count)
        self.strides = (self.dims[1] * self.dims[2], self.dims[2], 1)

    def toward(self, dim, step):
        size, stride = self.dims[dim], self.strides[dim]
        pairs = []
        for chip in range(self.count):
            place = (chip // stride) % size
            pairs.append((chip, chip + ((place + step) % size - place) * stride))
        return pairs

    def send(self, values, dim, step):
        return lax.ppermute(values, "dp", self.toward(dim, step))

    def pieces(self, values, dim):
        size = self.dims[dim]
        return [values] + [self.send(values, dim, size - step) for step in range(1, size)]

    def collect(self, parts, dim):
        size = self.dims[dim]
        total = parts[0].astype(f32)
        for step in range(1, size):
            total = total + self.send(parts[step], dim, step).astype(f32)
        return total

    def others(self):
        me = lax.axis_index("dp")
        ahead, place = 0, 0
        chip = jnp.arange(self.count)
        weights = (1, self.dims[0], self.dims[0] * self.dims[1])
        for size, stride, weight in zip(self.dims, self.strides, weights):
            mine = (me // stride) % size
            ahead = ahead + ((mine + (chip // weight) % size) % size) * stride
            place = place + (((chip // stride) % size - mine) % size) * weight
        return ahead, place


def swap_cores(values):
    return lax.ppermute(values, "tensor", [(0, 1), (1, 0)])


def in_order(core, own, other, axis):
    return jnp.where(
        core == 0,
        jnp.concatenate([own, other], axis),
        jnp.concatenate([other, own], axis),
    )


def gelu_parts(v):
    inner = math.sqrt(2.0 / math.pi)
    square = v * v
    th = jnp.tanh(v * (inner + inner * 0.044715 * square))
    half = 0.5 * (1.0 + th)
    act = v * half
    slope = half + 0.5 * v * (1.0 - th * th) * (inner + 3.0 * inner * 0.044715 * square)
    return act, slope


def nt(a, b):
    return lax.dot_general(a, b, (((1,), (1,)), ((), ())), preferred_element_type=f32)


def tn(a, b):
    return lax.dot_general(a, b, (((0,), (0,)), ((), ())), preferred_element_type=f32)


def nn(a, b):
    return jnp.dot(a, b, preferred_element_type=f32)


def tile_range(expert, bounds, rows):
    if expert < 2:
        return 0, rows // TILE
    low = bounds[expert - 2]
    high = bounds[DOM + expert - 2]
    return low // TILE, jnp.where(high > low, (high + TILE - 1) // TILE, low // TILE)


def forward_kernel(experts, bounds, x_ref, wi_ref, wo_ref, bi_ref, vec_ref, coef_ref, mix_ref, norm_ref, stat_ref):
    rows = x_ref.shape[0]
    mix_ref[...] = jnp.zeros_like(mix_ref)
    for place, expert in enumerate(experts):
        bias_in = bi_ref[expert : expert + 1, :]
        bias_out = vec_ref[expert : expert + 1, :]
        gain = vec_ref[LOCAL + expert : LOCAL + expert + 1, :]
        shift = vec_ref[2 * LOCAL + expert : 2 * LOCAL + expert + 1, :]

        def tile(index, _, place=place, expert=expert, bias_in=bias_in, bias_out=bias_out, gain=gain, shift=shift):
            span = pl.ds(pl.multiple_of(index * TILE, TILE), TILE)
            pre = nn(x_ref[span, :], wi_ref[place]) + bias_in
            act, _ = gelu_parts(pre)
            out = nt(act.astype(bf16), wo_ref[place]) + bias_out
            centre = jnp.mean(out, axis=1, keepdims=True)
            centred = out - centre
            scale = lax.rsqrt(jnp.mean(centred * centred, axis=1, keepdims=True) + EPS)
            norm = centred * scale
            norm_ref[place, span, :] = norm.astype(bf16)
            stat_ref[span, place : place + 1] = scale
            mix_ref[span, :] += coef_ref[span, expert : expert + 1] * (norm * gain + shift)
            return 0

        low, high = tile_range(expert, bounds, rows)
        lax.fori_loop(low, high, tile, 0)


def backward_kernel(
    experts, bounds, x_ref, gb_ref, wi_ref, wo_ref, bi_ref, vec_ref, coef_ref, *refs
):
    count = len(experts)
    norm_refs, stat_refs = refs[:count], refs[count : 2 * count]
    dwi_ref, dwo_ref, dvec_ref, dbi_ref, dcoef_ref, back_ref, wi_sum, wo_sum = refs[2 * count :]
    places = tuple(p for _, p in experts)
    rows = x_ref.shape[0]
    back_ref[...] = jnp.zeros_like(back_ref)
    dvec_ref[...] = jnp.zeros_like(dvec_ref)
    dbi_ref[...] = jnp.zeros_like(dbi_ref)
    for place, (expert, held) in enumerate(experts):
        bias_in = bi_ref[expert : expert + 1, :]
        gain = vec_ref[LOCAL + expert : LOCAL + expert + 1, :]
        shift = vec_ref[2 * LOCAL + expert : 2 * LOCAL + expert + 1, :]
        wi_sum[...] = jnp.zeros_like(wi_sum)
        wo_sum[...] = jnp.zeros_like(wo_sum)

        def tile(index, _, place=place, expert=expert, held=held, bias_in=bias_in, gain=gain, shift=shift):
            span = pl.ds(pl.multiple_of(index * TILE, TILE), TILE)
            x = x_ref[span, :]
            norm = norm_refs[place][0, span, :].astype(f32)
            scale = stat_refs[place][span, held : held + 1]
            grad_block = gb_ref[span, :].astype(f32)
            dcoef_ref[span, place : place + 1] = jnp.sum(
                grad_block * (norm * gain + shift), axis=1, keepdims=True
            )
            grad_exp = coef_ref[span, expert : expert + 1] * grad_block
            scaled = grad_exp * norm
            dvec_ref[place, 1:2, :] += jnp.sum(scaled, axis=0, keepdims=True)
            dvec_ref[place, 2:3, :] += jnp.sum(grad_exp, axis=0, keepdims=True)
            dx = grad_exp * gain
            first = jnp.mean(dx, axis=1, keepdims=True)
            second = jnp.mean(dx * norm, axis=1, keepdims=True)
            grad_sum = scale * (dx - first - norm * second)
            dvec_ref[place, 0:1, :] += jnp.sum(grad_sum, axis=0, keepdims=True)
            grad_low = grad_sum.astype(bf16)
            pre = nn(x, wi_ref[place]) + bias_in
            act, slope = gelu_parts(pre)
            wo_sum[...] += tn(grad_low, act.astype(bf16))
            pre_low = (nn(grad_low, wo_ref[place]) * slope).astype(bf16)
            dbi_ref[place, 0:1, :] += jnp.sum(pre_low.astype(f32), axis=0, keepdims=True)
            wi_sum[...] += tn(x, pre_low)
            back_ref[span, :] += nt(pre_low, wi_ref[place])
            return 0

        low, high = tile_range(expert, bounds, rows)
        lax.fori_loop(low, high, tile, 0)
        dwi_ref[place] = wi_sum[...].astype(bf16)
        dwo_ref[place] = wo_sum[...].astype(bf16)


def tower_kernel(base_ref, mix_ref, row_ref, tw_ref, tv_ref, pred_ref, gb_ref, dw_ref, dv_ref):
    rows = base_ref.shape[0]
    dw_ref[...] = jnp.zeros_like(dw_ref)
    dv_ref[...] = jnp.zeros_like(dv_ref)
    bias = tv_ref[0:1, :]
    head = tv_ref[1:2, :]

    def tile(index, _):
        span = pl.ds(pl.multiple_of(index * TILE, TILE), TILE)
        block = (base_ref[span, :] + mix_ref[span, :].astype(f32)).astype(bf16)
        pre = nn(block, tw_ref[...]) + bias
        act, slope = gelu_parts(pre)
        group = lax.broadcasted_iota(jnp.int32, pre.shape, 1) // TW
        mine = group == row_ref[span, 0:1].astype(jnp.int32)
        act = jnp.where(mine, act, 0.0)
        logit = jnp.sum(act * head, axis=1, keepdims=True) + row_ref[span, 3:4]
        predicted = 1.0 / (1.0 + jnp.exp(-logit))
        grad_logit = row_ref[span, 2:3] * (predicted - row_ref[span, 1:2])
        pred_ref[span, 0:1] = predicted
        pred_ref[span, 1:2] = grad_logit
        dv_ref[1:2, :] += jnp.sum(grad_logit * act, axis=0, keepdims=True)
        grad_pre = jnp.where(mine, grad_logit * head * slope, 0.0)
        dv_ref[0:1, :] += jnp.sum(grad_pre, axis=0, keepdims=True)
        grad_low = grad_pre.astype(bf16)
        dw_ref[...] += tn(block, grad_low)
        gb_ref[span, :] = nt(grad_low, tw_ref[...])
        return 0

    lax.fori_loop(0, rows // TILE, tile, 0)


def params():
    return pltpu.CompilerParams(vmem_limit_bytes=VMEM_LIMIT)


def whole(count):
    return [pl.BlockSpec(memory_space=pltpu.VMEM)] * count


def call_forward(experts, bounds, x, wi, wo, bi, vec, coef):
    rows, count = x.shape[0], len(experts)
    return pl.pallas_call(
        functools.partial(forward_kernel, experts),
        out_shape=(
            jax.ShapeDtypeStruct((rows, D), f32),
            jax.ShapeDtypeStruct((count, rows, D), bf16),
            jax.ShapeDtypeStruct((rows, 128), f32),
        ),
        in_specs=[pl.BlockSpec(memory_space=pltpu.SMEM)] + whole(6),
        out_specs=tuple(whole(3)),
        compiler_params=params(),
        cost_estimate=pl.CostEstimate(
            flops=4 * count * rows * D * H // 2, bytes_accessed=10_000_000, transcendentals=count * rows * H // 2
        ),
        name="experts_forward",
    )(bounds, x, wi, wo, bi, vec, coef)


def call_backward(experts, bounds, x, gb, wi, wo, bi, vec, coef, norms, stats):
    rows, count = x.shape[0], len(experts)
    return pl.pallas_call(
        functools.partial(backward_kernel, experts),
        out_shape=(
            jax.ShapeDtypeStruct((count, D, H), bf16),
            jax.ShapeDtypeStruct((count, D, H), bf16),
            jax.ShapeDtypeStruct((count, 8, D), f32),
            jax.ShapeDtypeStruct((count, 8, H), f32),
            jax.ShapeDtypeStruct((rows, 128), f32),
            jax.ShapeDtypeStruct((rows, D), f32),
        ),
        in_specs=[pl.BlockSpec(memory_space=pltpu.SMEM)] + whole(7 + 2 * count),
        out_specs=tuple(whole(6)),
        scratch_shapes=[pltpu.VMEM((D, H), f32), pltpu.VMEM((D, H), f32)],
        compiler_params=params(),
        cost_estimate=pl.CostEstimate(
            flops=10 * count * rows * D * H // 2, bytes_accessed=20_000_000, transcendentals=count * rows * H // 2
        ),
        name="experts_backward",
    )(bounds, x, gb, wi, wo, bi, vec, coef, *norms, *stats)


def call_tower(base, mix, row_info, tower, tower_vec):
    rows = base.shape[0]
    return pl.pallas_call(
        tower_kernel,
        out_shape=(
            jax.ShapeDtypeStruct((rows, 128), f32),
            jax.ShapeDtypeStruct((rows, D), f32),
            jax.ShapeDtypeStruct((D, DOM * TW), f32),
            jax.ShapeDtypeStruct((8, DOM * TW), f32),
        ),
        in_specs=whole(5),
        out_specs=tuple(whole(4)),
        compiler_params=params(),
        cost_estimate=pl.CostEstimate(
            flops=6 * rows * D * DOM * TW, bytes_accessed=10_000_000, transcendentals=rows * DOM * TW
        ),
        name="towers",
    )(base, mix, row_info, tower, tower_vec)


def own_experts(per_expert, core):
    tail = per_expert.shape[1:]
    shared = per_expert[:S].reshape((2, 2) + tail)
    domain = per_expert[S:].reshape((DOM, K) + tail)

    def of(which):
        return jnp.concatenate(
            [
                lax.dynamic_index_in_dim(shared, which, 0, keepdims=False),
                lax.dynamic_index_in_dim(domain, which, 1, keepdims=False),
            ]
        )

    return of(core), of(1 - core)


def all_experts(own, other, core):
    first = jnp.where(core == 0, own, other)
    second = jnp.where(core == 0, other, own)
    tail = own.shape[1:]
    shared = jnp.concatenate([first[:2], second[:2]])
    domain = jnp.stack([first[2:], second[2:]], axis=1).reshape((DOM * K,) + tail)
    return jnp.concatenate([shared, domain])


def spread_experts(own, core):
    return all_experts(own, jnp.zeros_like(own), core)


def softmax_back(probability, grad_probs):
    return probability * (grad_probs - jnp.sum(probability * grad_probs, axis=0, keepdims=True))


def per_device(
    box,
    embeds,
    domain,
    frozen,
    labels,
    proj_w,
    proj_b,
    w_in,
    in_bias,
    w_out,
    out_bias,
    ln_gain,
    ln_shift,
    gate_top,
    gate_shared,
    gate_domain,
    tower_w,
    tower_b,
    tower_out,
    tower_out_b,
):
    core = lax.axis_index("tensor")
    places = box.count
    rows = embeds.shape[0]
    half_rows = rows // 2
    width = proj_w.shape[1]
    e_in = proj_w.shape[0]
    ahead, place_of = box.others()

    pack = jnp.concatenate(
        [
            proj_w.T,
            jnp.swapaxes(tower_w, 0, 1).reshape(width, DOM * TW),
            jnp.swapaxes(gate_top, 0, 1).reshape(width, 2 * DOM),
            jnp.swapaxes(gate_shared, 0, 1).reshape(width, S * DOM),
            jnp.swapaxes(gate_domain, 0, 1).reshape(width, K * DOM),
            jnp.concatenate([out_bias, ln_gain, ln_shift]).T,
            proj_b[:, None],
            in_bias.reshape(width, 24),
            jnp.concatenate([tower_b, tower_out]).reshape(width, 4),
        ],
        axis=1,
    )
    pack = jnp.pad(pack, ((0, 0), (0, PACK - pack.shape[1])))
    for dim in range(3):
        pack = jnp.concatenate(box.pieces(pack, dim), axis=0)
    pack = pack.reshape(places, 1, width, PACK)
    pack = in_order(core, pack, swap_cores(pack), 1)
    small = pack.reshape(D, PACK)
    proj_t = small[:, :e_in]
    at = e_in
    tower = small[:, at : at + DOM * TW]
    at += DOM * TW
    gates = small[:, at : at + 32]
    at += 32
    vectors = small[:, at : at + 37].astype(f32).T
    at += 37
    bias_blocks = jnp.take(pack[:, :, :, at : at + 28].astype(f32), place_of, axis=0)
    in_bias_all = (
        bias_blocks[..., :24]
        .reshape(places * 2, 12, width * 2)
        .transpose(1, 0, 2)
        .reshape(12, H)
    )
    tower_vec = (
        bias_blocks[..., 24:]
        .reshape(places * 2, 2, DOM, width // 2)
        .transpose(1, 2, 0, 3)
        .reshape(2, DOM * TW)
    )
    tower_vec = jnp.pad(tower_vec, ((0, 6), (0, 0)))
    vec_own = jnp.concatenate([own_experts(vectors[i * 12 : i * 12 + 12], core)[0] for i in range(3)])
    vec_own = jnp.pad(vec_own, ((0, 6), (0, 0)))
    proj_bias = vectors[36]
    bi_own = jnp.pad(own_experts(in_bias_all, core)[0], ((0, 2), (0, 0)))

    wi_own, wi_other = own_experts(w_in, core)
    wo_own, wo_other = own_experts(jnp.swapaxes(w_out, 1, 2), core)
    swapped = swap_cores(jnp.stack([wi_other, wo_other]))
    shards = in_order(core, jnp.stack([wi_own, wo_own]), swapped, 3)

    def gather(experts, after):
        low, high = experts[0], experts[-1] + 1
        shard = shards[:, low:high]
        if after is not None:
            shard = lax.optimization_barrier((shard, after))[0]
        count = high - low
        block = jnp.stack(box.pieces(shard, 0), axis=2)
        wi, wo = block[0], block[1]
        wi_y = jnp.stack(box.pieces(wi, 1), axis=1)
        wo_x = jnp.stack(box.pieces(wo, 2), axis=1)
        wi_full = jnp.stack(box.pieces(wi_y, 2), axis=1)
        wo_full = jnp.stack(box.pieces(wo_x, 1), axis=2)
        return wi_full.reshape(count, D, H), wo_full.reshape(count, D, H), wi_y

    gathered = []
    behind = [None, None]
    for experts in CHUNKS_FORWARD:
        wi, wo, mark = gather(experts, behind[-2])
        behind.append(mark)
        gathered.append((wi, wo))

    ids = domain[:, 0]
    onehot_t = (ids[None, :] == jnp.arange(DOM, dtype=jnp.int32)[:, None]).astype(f32)
    counts = jnp.sum(onehot_t, axis=1).astype(jnp.int32)
    ends = jnp.cumsum(counts)
    starts = ends - counts
    rank = jnp.cumsum(onehot_t, axis=1)
    position = jnp.sum(onehot_t * (rank + starts[:, None].astype(f32)), axis=0).astype(jnp.int32) - 1
    order = (position[None, :] == jnp.arange(rows, dtype=jnp.int32)[:, None])
    order_low = order.astype(bf16)
    bounds = jnp.concatenate([starts, ends])
    slots = jnp.arange(rows, dtype=jnp.int32)
    sorted_t = ((slots[None, :] >= starts[:, None]) & (slots[None, :] < ends[:, None])).astype(f32)
    events = jnp.dot(order_low, embeds, preferred_element_type=f32).astype(bf16)
    targets = jnp.sum(jnp.where(order, labels.astype(f32)[None, :], 0.0), axis=1)

    mixed_in = (
        lax.dot_general(events, proj_t, (((1,), (1,)), ((), ())), preferred_element_type=f32)
        + proj_bias[None, :]
    )
    mixed_low = mixed_in.astype(bf16)

    logits = lax.dot_general(
        gates, mixed_low, (((0,), (1,)), ((), ())), preferred_element_type=f32
    )


    top_prob = jax.nn.softmax(pick_gate(logits, sorted_t, 0, 2), axis=0)
    shared_prob = jax.nn.softmax(pick_gate(logits, sorted_t, 1, 4), axis=0)
    domain_prob = jax.nn.softmax(pick_gate(logits, sorted_t, 2, 2), axis=0)
    shared_coef = lax.dynamic_slice_in_dim(top_prob[0:1] * shared_prob, 2 * core, 2, 0)
    domain_coef = lax.dynamic_slice_in_dim(top_prob[1:2] * domain_prob, core, 1, 0) * sorted_t
    coef = jnp.pad(jnp.concatenate([shared_coef, domain_coef]).T, ((0, 0), (0, 128 - LOCAL)))

    mixes, kept = [], {}
    for experts, (wi, wo) in zip(CHUNKS_FORWARD, gathered):
        mix, norm, stat = call_forward(experts, bounds, mixed_low, wi, wo, bi_own, vec_own, coef)
        mixes.append(mix)
        for place, expert in enumerate(experts):
            kept[expert] = (norm[place : place + 1], stat, place, wi, wo)

    def half(values, which):
        return lax.dynamic_slice_in_dim(values, which * half_rows, half_rows, 0)

    mixture = functools.reduce(jnp.add, mixes)
    arrived = swap_cores(half(mixture, 1 - core).astype(bf16))
    base = half(mixed_in, core) + half(mixture, core)
    frozen_f = frozen.astype(f32)
    weight = 1.0 - (1.0 - FROZEN_SHARE) * jnp.sum(sorted_t * frozen_f[:, None], axis=0)
    row_bias = jnp.sum(sorted_t * tower_out_b.astype(f32)[:, None], axis=0)
    row_domain = jnp.sum(sorted_t * jnp.arange(DOM, dtype=f32)[:, None], axis=0)
    row_info = jnp.pad(jnp.stack([row_domain, targets, weight, row_bias]).T, ((0, 0), (0, 124)))
    row_out, grad_block, d_tower, d_tower_vec = call_tower(
        base, arrived, half(row_info, core), tower, tower_vec
    )
    grad_block_low = grad_block.astype(bf16)
    grad_all = in_order(core, grad_block_low, swap_cores(grad_block_low), 0)

    backs, d_vec, d_bias, d_coef, shard_in, shard_out = [], {}, {}, {}, {}, {}
    for experts in CHUNKS_BACKWARD:
        count = len(experts)
        wi, wo = kept[experts[0]][3:]
        dwi, dwo, dvec, dbi, dcoef, back = call_backward(
            tuple((e, kept[e][2]) for e in experts),
            bounds,
            mixed_low,
            grad_all,
            wi,
            wo,
            bi_own,
            vec_own,
            coef,
            [kept[e][0] for e in experts],
            [kept[e][1] for e in experts],
        )
        backs.append(back)
        box_shape = (count,) + box.dims[::-1] + (2 * width, H)
        dwi, dwo = dwi.reshape(box_shape), dwo.reshape(box_shape)
        nz, ny, nx = box.dims
        part_in = box.collect([dwi[:, s] for s in range(nx)], 2).astype(bf16)
        part_out = box.collect([dwo[:, :, s] for s in range(ny)], 1).astype(bf16)
        part_in = box.collect([part_in[:, s] for s in range(ny)], 1).astype(bf16)
        part_out = box.collect([part_out[:, s] for s in range(nx)], 2).astype(bf16)
        both = jnp.stack([part_in, part_out])
        done = box.collect([both[:, :, s] for s in range(nz)], 0)
        for place, expert in enumerate(experts):
            d_vec[expert], d_bias[expert] = dvec[place], dbi[place, 0]
            d_coef[expert] = dcoef[:, place]
            shard_in[expert], shard_out[expert] = done[0, place], done[1, place]

    back = functools.reduce(jnp.add, backs)
    back_arrived = swap_cores(half(back, 1 - core).astype(bf16))
    coef_own = jnp.stack(
        [d_coef[0], d_coef[1], functools.reduce(jnp.add, [jnp.where(sorted_t[d] > 0.5, d_coef[2 + d], 0.0) for d in range(DOM)])]
    )
    coef_own = jnp.pad(coef_own, ((0, 5), (0, 0)))

    def half_t(values, which):
        return lax.dynamic_slice_in_dim(values, which * half_rows, half_rows, 1)

    mine_coef = half_t(coef_own, core)
    other_coef = swap_cores(half_t(coef_own, 1 - core))
    coef_first = jnp.where(core == 0, mine_coef, other_coef)
    coef_second = jnp.where(core == 0, other_coef, mine_coef)
    d_shared = jnp.concatenate([coef_first[:2], coef_second[:2]])
    d_domain = jnp.concatenate([coef_first[2:3], coef_second[2:3]])
    top_half, shared_half, domain_half = (
        half_t(top_prob, core),
        half_t(shared_prob, core),
        half_t(domain_prob, core),
    )
    sorted_half = half_t(sorted_t, core)
    d_top = jnp.concatenate(
        [
            jnp.sum(d_shared * shared_half, axis=0, keepdims=True),
            jnp.sum(d_domain * domain_half, axis=0, keepdims=True),
        ]
    )
    logit_grads = (
        softmax_back(top_half, d_top),
        softmax_back(shared_half, d_shared * top_half[0:1]),
        softmax_back(domain_half, d_domain * top_half[1:2]),
    )
    spread = jnp.concatenate(
        [sorted_half[d : d + 1] * logit_grads[0] for d in range(DOM)]
        + [sorted_half[d : d + 1] * logit_grads[1] for d in range(DOM)]
        + [sorted_half[d : d + 1] * logit_grads[2] for d in range(DOM)]
    ).astype(bf16)
    mixed_half = half(mixed_low, core)
    d_gates = lax.dot_general(mixed_half, spread, (((0,), (1,)), ((), ())), preferred_element_type=f32)
    gate_back = lax.dot_general(spread, gates, (((0,), (1,)), ((), ())), preferred_element_type=f32)
    grad_mixed = grad_block + half(back, core) + back_arrived.astype(f32) + gate_back
    d_proj_bias = jnp.sum(grad_mixed, axis=0)
    mixed_grad_low = grad_mixed.astype(bf16)
    d_proj_t = lax.dot_general(
        mixed_grad_low, half(events, core), (((0,), (0,)), ((), ())), preferred_element_type=f32
    )
    grad_events = jnp.dot(mixed_grad_low, proj_t, preferred_element_type=f32).astype(bf16)
    grad_events = in_order(core, grad_events, swap_cores(grad_events), 0)
    grad_embeds = lax.dot_general(
        order_low, grad_events, (((0,), (0,)), ((), ())), preferred_element_type=f32
    ).astype(bf16)
    pred_half = jnp.broadcast_to(row_out[None, :, 0], (8, half_rows))
    pred_sorted = in_order(core, pred_half, swap_cores(pred_half), 1)[0]
    predictions = jnp.sum(jnp.where(order, pred_sorted[:, None], 0.0), axis=0)

    d_vectors = jnp.concatenate(
        [
            spread_experts(jnp.stack([d_vec[e][i] for e in range(LOCAL)]), core)
            for i in range(3)
        ]
    )
    d_vectors = jnp.concatenate([d_vectors, d_proj_bias[None]]).T
    d_in_bias = spread_experts(jnp.stack([d_bias[e] for e in range(LOCAL)]), core)
    d_in_blocks = d_in_bias.reshape(12, places, 2, 2 * width).transpose(1, 2, 0, 3)
    d_tower_blocks = (
        d_tower_vec[:2].reshape(2, DOM, places, 2, width // 2).transpose(2, 3, 0, 1, 4)
    )
    d_blocks = jnp.concatenate(
        [
            d_in_blocks.reshape(places, 2, width, 24),
            d_tower_blocks.reshape(places, 2, width, 4),
        ],
        axis=3,
    )
    d_blocks = jnp.take(d_blocks, ahead, axis=0).reshape(D, 28)
    d_small = jnp.concatenate([d_proj_t, d_tower, d_gates, d_vectors, d_blocks], axis=1)
    d_small = jnp.pad(d_small, ((0, 0), (0, PACK - d_small.shape[1])))
    d_small = d_small.reshape(places, 2, width, PACK)
    d_mine = lax.dynamic_index_in_dim(d_small, core, 1, keepdims=False)
    d_other = lax.dynamic_index_in_dim(d_small, 1 - core, 1, keepdims=False).astype(bf16)
    d_mine = (d_mine + swap_cores(d_other).astype(f32)).astype(bf16)
    d_mine = d_mine.reshape(box.dims[::-1] + (width, PACK))
    d_mine = box.collect([d_mine[s] for s in range(box.dims[2])], 2).astype(bf16)
    d_mine = box.collect([d_mine[s] for s in range(box.dims[1])], 1).astype(bf16)
    d_mine = box.collect([d_mine[s] for s in range(box.dims[0])], 0)

    grad_logit = row_out[:, 1]
    d_logit_bias = jnp.sum(sorted_half * grad_logit[None, :], axis=1)
    d_logit_bias = jnp.pad(d_logit_bias[None, :], ((0, 7), (0, 124)))
    d_logit_bias = (d_logit_bias + swap_cores(d_logit_bias))[None]
    for dim in range(3):
        d_logit_bias = jnp.concatenate(box.pieces(d_logit_bias, dim), axis=0)
    d_logit_bias = jnp.sum(jnp.take(d_logit_bias, place_of, axis=0), axis=0)[0, :DOM]

    done = jnp.stack(
        [
            jnp.stack([shard_in[e] for e in range(LOCAL)]),
            jnp.stack([shard_out[e] for e in range(LOCAL)]),
        ]
    )
    keep = lax.dynamic_slice_in_dim(done, core * (H // 2), H // 2, 3)
    give = lax.dynamic_slice_in_dim(done, (1 - core) * (H // 2), H // 2, 3)
    got = swap_cores(give)
    grad_w_in = all_experts(keep[0], got[0], core)
    grad_w_out = jnp.swapaxes(all_experts(keep[1], got[1], core), 1, 2)

    at = e_in
    grad_proj_w = d_mine[:, :at].T
    grad_tower_w = jnp.swapaxes(d_mine[:, at : at + DOM * TW].reshape(width, DOM, TW), 0, 1)
    at += DOM * TW
    d_gate = d_mine[:, at : at + 32]
    grad_gate_top = jnp.swapaxes(d_gate[:, :8].reshape(width, DOM, 2), 0, 1)
    grad_gate_shared = jnp.swapaxes(d_gate[:, 8:24].reshape(width, DOM, S), 0, 1)
    grad_gate_domain = jnp.swapaxes(d_gate[:, 24:].reshape(width, DOM, K), 0, 1)
    at += 32
    d_vecs = d_mine[:, at : at + 37].T
    at += 37
    grad_in_bias = d_mine[:, at : at + 24].reshape(12, 2 * width)
    d_tv = d_mine[:, at + 24 : at + 28].reshape(2, DOM, width // 2)
    return (
        predictions,
        grad_embeds,
        grad_proj_w,
        d_vecs[36],
        grad_w_in,
        grad_in_bias,
        grad_w_out,
        d_vecs[:12],
        d_vecs[12:24],
        d_vecs[24:36],
        grad_gate_top,
        grad_gate_shared,
        grad_gate_domain,
        grad_tower_w,
        d_tv[0],
        d_tv[1],
        d_logit_bias,
    )


def pick_gate(logits, sorted_t, which, size):
    low = (0, 2 * DOM, (2 + S) * DOM)[which]
    return functools.reduce(
        jnp.add,
        [sorted_t[d : d + 1] * logits[low + d * size : low + (d + 1) * size] for d in range(DOM)],
    )


def solution(mesh):
    both = ("dp", "tensor")
    in_specs = (
        P("dp", None),
        P("dp", None),
        P(),
        P("dp"),
        P(None, both),
        P(both),
        P(None, "dp", "tensor"),
        P(None, both),
        P(None, "tensor", "dp"),
        P(None, both),
        P(None, both),
        P(None, both),
        P(None, both, None),
        P(None, both, None),
        P(None, both, None),
        P(None, both, None),
        P(None, both),
        P(None, both),
        P(),
    )
    out_specs = (
        P("dp"),
        P("dp", None),
        P(None, both),
        P(both),
        P(None, "dp", "tensor"),
        P(None, both),
        P(None, "tensor", "dp"),
        P(None, both),
        P(None, both),
        P(None, both),
        P(None, both, None),
        P(None, both, None),
        P(None, both, None),
        P(None, both, None),
        P(None, both),
        P(None, both),
        P(),
    )
    return jax.shard_map(
        functools.partial(per_device, Box(mesh.shape["dp"])),
        mesh=mesh,
        in_specs=in_specs,
        out_specs=out_specs,
        check_vma=False,
    )
```

profile of v0, /device:TPU:0, one launch (start us, length us, event | category | flops | bytes accessed | tf_op | source)
XLA Modules:
  0.0 696.5 jit_solution(2854220275449132400)
XLA Ops:
  62.5 9.6 %collective-permute-done.8 = bf16[2,1,32,1024]{3,2,0,1:T(8,128)(2,1)S(1)} collective-permute-done((bf16[2,1,32,1024]{3,2,0,1:T(8,128)(2,1)S(1)}, bf16[2,1,32,1024]{3,2,0,1:T(8,128)(2,1)S(1)}, u32[]{:S(2)}, u32[]{:S(2)}) %collective-permute-start.8) | collective-permute-done | bytes 131104 | tf_op jit(solution)/shard_map/ppermute | solution.py:54
  74.4 7.7 %collective-permute-done.15 = bf16[2,2,32,1024]{3,2,0,1:T(8,128)(2,1)S(1)} collective-permute-done((bf16[2,2,32,1024]{3,2,0,1:T(8,128)(2,1)S(1)}, bf16[2,2,32,1024]{3,2,0,1:T(8,128)(2,1)S(1)}, u32[]{:S(2)}, u32[]{:S(2)}) %collective-permute-start.15) | collective-permute-done | bytes 262176 | tf_op jit(solution)/shard_map/ppermute | solution.py:54
  98.8 8.5 %collective-permute-done.22 = bf16[2,2,32,1024]{3,2,0,1:T(8,128)(2,1)S(1)} collective-permute-done((bf16[2,2,32,1024]{3,2,0,1:T(8,128)(2,1)S(1)}, bf16[2,2,32,1024]{3,2,0,1:T(8,128)(2,1)S(1)}, u32[]{:S(2)}, u32[]{:S(2)}) %collective-permute-start.22) | collective-permute-done | bytes 262176 | tf_op jit(solution)/shard_map/ppermute | solution.py:54
  109.4 5.6 collective-permute-start.30
  132.5 12.9 %collective-permute-done.31 = bf16[1,4,32,1024]{3,2,1,0:T(8,128)(2,1)S(1)} collective-permute-done((bf16[1,4,32,1024]{3,2,1,0:T(8,128)(2,1)S(1)}, bf16[1,4,32,1024]{3,2,1,0:T(8,128)(2,1)S(1)}, u32[]{:S(2)}, u32[]{:S(2)}) %collective-permute-start.31) | collective-permute-done | bytes 262176 | tf_op jit(solution)/shard_map/ppermute | solution.py:54
  201.0 11.6 %experts_forward.4 = (f32[1536,512]{1,0:T(8,128)}, bf16[1,1536,512]{2,1,0:T(8,128)(2,1)}, f32[1536,128]{1,0:T(8,128)}) custom-call(s32[8]{0:T(128)} %pad_add_fusion.bounds, bf16[1536,512]{1,0:T(8,128)(2,1)} %copy-done.18, bf16[1,512,1024]{2,1,0:T(8,128)(2,1)} %bitcast.620, bf16[1,512,1024]{2,1,0:T(8,128)(2,1)} %bitcast.622, ...), custom_call_target="tpu_custom_call" | custom-call | flops 1610612736 | bytes 10000000 | tf_op jit(solution)/shard_map/experts_forward/pallas_call | solution.py:241
  218.5 6.0 experts_forward.7
  230.3 13.9 %experts_forward.5 = (f32[1536,512]{1,0:T(8,128)}, bf16[2,1536,512]{2,1,0:T(8,128)(2,1)}, f32[1536,128]{1,0:T(8,128)}) custom-call(s32[8]{0:T(128)} %pad_add_fusion.bounds, bf16[1536,512]{1,0:T(8,128)(2,1)} %copy-done.18, bf16[2,512,1024]{2,1,0:T(8,128)(2,1)} %bitcast.595, bf16[2,512,1024]{2,1,0:T(8,128)(2,1)} %bitcast.599, ...), custom_call_target="tpu_custom_call" | custom-call | flops 3221225472 | bytes 10000000 | tf_op jit(solution)/shard_map/experts_forward/pallas_call | solution.py:241
  249.1 13.8 %experts_forward.6 = (f32[1536,512]{1,0:T(8,128)}, bf16[2,1536,512]{2,1,0:T(8,128)(2,1)}, f32[1536,128]{1,0:T(8,128)}) custom-call(s32[8]{0:T(128)} %pad_add_fusion.bounds, bf16[1536,512]{1,0:T(8,128)(2,1)} %copy-done.18, bf16[2,512,1024]{2,1,0:T(8,128)(2,1)} %bitcast.597, bf16[2,512,1024]{2,1,0:T(8,128)(2,1)} %bitcast.601, ...), custom_call_target="tpu_custom_call" | custom-call | flops 3221225472 | bytes 10000000 | tf_op jit(solution)/shard_map/experts_forward/pallas_call | solution.py:241
  279.5 10.4 %towers.1 = (f32[768,128]{1,0:T(8,128)}, f32[768,512]{1,0:T(8,128)}, f32[512,1024]{1,0:T(8,128)}, f32[8,1024]{1,0:T(8,128)}) custom-call(f32[768,512]{1,0:T(8,128)} %dynamic-slice_add_fusion.base_ref, bf16[768,512]{1,0:T(8,128)(2,1)} %collective-permute-done.35.mix_ref, f32[768,128]{1,0:T(8,128)} %pad_dynamic-slice_fusion.4.row_ref, ...), custom_call_target="tpu_custom_call" | custom-call | flops 2415919104 | bytes 10000000 | tf_op jit(solution)/shard_map/towers/pallas_call | solution.py:283
  324.9 19.0 %experts_backward.7 = (bf16[1,512,1024]{2,1,0:T(8,128)(2,1)}, bf16[1,512,1024]{2,1,0:T(8,128)(2,1)}, f32[1,8,512]{2,1,0:T(8,128)}, f32[1,8,1024]{2,1,0:T(8,128)}...) custom-call(s32[8]{0:T(128)} %pad_add_fusion.bounds, bf16[1536,512]{1,0:T(8,128)(2,1)} %copy-done.18, ...), custom_call_target="tpu_custom_call" | custom-call | flops 4026531840 | bytes 20000000 | tf_op jit(solution)/shard_map/experts_backward/pallas_call | solution.py:260
  345.4 23.6 %experts_backward.6 = (bf16[2,512,1024]{2,1,0:T(8,128)(2,1)}, bf16[2,512,1024]{2,1,0:T(8,128)(2,1)}, f32[2,8,512]{2,1,0:T(8,128)}, f32[2,8,1024]{2,1,0:T(8,128)}...) custom-call(s32[8]{0:T(128)} %pad_add_fusion.bounds, bf16[1536,512]{1,0:T(8,128)(2,1)} %copy-done.18, ...), custom_call_target="tpu_custom_call" | custom-call | flops 8053063680 | bytes 20000000 | tf_op jit(solution)/shard_map/experts_backward/pallas_call | solution.py:260
  370.5 24.0 %experts_backward.5 = (bf16[2,512,1024]{2,1,0:T(8,128)(2,1)}, bf16[2,512,1024]{2,1,0:T(8,128)(2,1)}, f32[2,8,512]{2,1,0:T(8,128)}, f32[2,8,1024]{2,1,0:T(8,128)}...) custom-call(s32[8]{0:T(128)} %pad_add_fusion.bounds, bf16[1536,512]{1,0:T(8,128)(2,1)} %copy-done.18, ...), custom_call_target="tpu_custom_call" | custom-call | flops 8053063680 | bytes 20000000 | tf_op jit(solution)/shard_map/experts_backward/pallas_call | solution.py:260
  395.9 8.8 %experts_backward.4 = (bf16[1,512,1024]{2,1,0:T(8,128)(2,1)}, bf16[1,512,1024]{2,1,0:T(8,128)(2,1)}, f32[1,8,512]{2,1,0:T(8,128)}, f32[1,8,1024]{2,1,0:T(8,128)}...) custom-call(s32[8]{0:T(128)} %pad_add_fusion.bounds, bf16[1536,512]{1,0:T(8,128)(2,1)} %copy-done.18, ...), custom_call_target="tpu_custom_call" | custom-call | flops 4026531840 | bytes 20000000 | tf_op jit(solution)/shard_map/experts_backward/pallas_call | solution.py:260
  481.1 8.1 %collective-permute-done.68 = bf16[1,2,4,32,1024]{4,3,2,1,0:T(8,128)(2,1)S(1)} collective-permute-done((bf16[1,2,4,32,1024]{4,3,2,1,0:T(8,128)(2,1)}, bf16[1,2,4,32,1024]{4,3,2,1,0:T(8,128)(2,1)S(1)}, u32[]{:S(2)}, u32[]{:S(2)}) %collective-permute-start.68) | collective-permute-done | bytes 524320 | tf_op jit(solution)/shard_map/ppermute | solution.py:54
  490.7 15.9 %collective-permute-done.70 = bf16[1,2,4,32,1024]{4,3,2,1,0:T(8,128)(2,1)S(1)} collective-permute-done((bf16[1,2,4,32,1024]{4,3,2,1,0:T(8,128)(2,1)S(1)}, bf16[1,2,4,32,1024]{4,3,2,1,0:T(8,128)(2,1)S(1)}, u32[]{:S(2)}, u32[]{:S(2)}) %collective-permute-start.70) | collective-permute-done | bytes 524320 | tf_op jit(solution)/shard_map/ppermute | solution.py:54
  546.8 11.8 %collective-permute-done.61 = bf16[2,2,4,32,1024]{4,3,0,2,1:T(8,128)(2,1)S(1)} collective-permute-done((bf16[2,2,4,32,1024]{4,3,0,2,1:T(8,128)(2,1)S(1)}, bf16[2,2,4,32,1024]{4,3,0,2,1:T(8,128)(2,1)S(1)}, u32[]{:S(2)}, u32[]{:S(2)}) %collective-permute-start.61) | collective-permute-done | bytes 1048608 | tf_op jit(solution)/shard_map/ppermute | solution.py:54
  559.7 6.2 collective-permute-done.63
  567.1 10.0 %collective-permute-done.55 = bf16[2,4,32,1024]{3,2,0,1:T(8,128)(2,1)S(1)} collective-permute-done((bf16[2,4,32,1024]{3,2,0,1:T(8,128)(2,1)S(1)}, bf16[2,4,32,1024]{3,2,0,1:T(8,128)(2,1)S(1)}, u32[]{:S(2)}, u32[]{:S(2)}) %collective-permute-start.55) | collective-permute-done | bytes 524320 | tf_op jit(solution)/shard_map/ppermute | solution.py:54
  596.9 7.7 %fusion.6 = bf16[1536,640]{1,0:T(8,128)(2,1)} fusion(s32[1536]{0:T(1024)S(1)} %copy-done.97, bf16[768,640]{1,0:T(8,128)(2,1)} %collective-permute-done.40, bf16[768,640]{1,0:T(8,128)(2,1)} %convolution_convert_fusion, pred[]{:T(512)S(6)} %eq.87), kind=kOutput, calls=%fused_computation.15 | convolution fusion | flops 3032088576 | bytes 3938305 | tf_op jit(solution)/shard_map/dot_general | solution.py:575
  610.9 9.7 %collective-permute-done.66 = bf16[2,2,32,1024]{3,2,1,0:T(8,128)(2,1)S(1)} collective-permute-done((bf16[2,2,32,1024]{3,2,1,0:T(8,128)(2,1)}, bf16[2,2,32,1024]{3,2,1,0:T(8,128)(2,1)S(1)}, u32[]{:S(2)}, u32[]{:S(2)}) %collective-permute-start.66) | collective-permute-done | bytes 262176 | tf_op jit(solution)/shard_map/ppermute | solution.py:54
  627.8 5.9 add_convert_fusion
  653.2 6.6 collective-permute-done.46
  659.8 26.1 %collective-permute-done.45 = bf16[16,1792]{0,1:T(8,128)(2,1)S(1)} collective-permute-done((bf16[16,1792]{0,1:T(8,128)(2,1)S(1)}, bf16[16,1792]{0,1:T(8,128)(2,1)S(1)}, u32[]{:S(2)}, u32[]{:S(2)}) %collective-permute-start.45) | collective-permute-done | bytes 57376 | tf_op jit(solution)/shard_map/ppermute | solution.py:54
  (730 shorter events, 409.8 us)
Async XLA Ops:
  10.1 27.3 %collective-permute-start = (bf16[16,1792]{1,0:T(8,128)(2,1)}, bf16[16,1792]{1,0:T(8,128)(2,1)}, u32[]{:S(2)}, u32[]{:S(2)}) collective-permute-start(bf16[16,1792]{1,0:T(8,128)(2,1)} %get-tuple-element.370), channel_id=1, source_target_pairs={{0,24},{2,26},{4,28},{6,30},{8,0},{10,2},{12,4},{14,6},{16,8},{18,... | collective-permute-start | bytes 172040 | tf_op jit(solution)/shard_map/ppermute | solution.py:54
  22.4 26.2 %collective-permute-start.6 = (bf16[2,6,32,512]{3,2,0,1:T(8,128)(2,1)}, bf16[2,6,32,512]{3,2,0,1:T(8,128)(2,1)}, u32[]{:S(2)}, u32[]{:S(2)}) collective-permute-start(bf16[2,6,32,512]{3,2,0,1:T(8,128)(2,1)} %pad_maximum_fusion.23), channel_id=1, source_target_pairs={{0,1},{1,0},{2,3},{3,2},{4,5},{5,4},{6,7},{7,6},{8,9},{9,8},{10,11... | collective-permute-start | bytes 1179656 | tf_op jit(solution)/shard_map/ppermute | solution.py:80
  47.1 44.4 %collective-permute-start.4 = (bf16[128,1792]{1,0:T(8,128)(2,1)}, bf16[128,1792]{1,0:T(8,128)(2,1)S(1)}, u32[]{:S(2)}, u32[]{:S(2)}) collective-permute-start(bf16[128,1792]{1,0:T(8,128)(2,1)} %get-tuple-element.350), channel_id=1, source_target_pairs={{0,2},{2,0},{4,6},{6,4},{8,10},{10,8},{12,14},{14,12},{16,18},{18,... | collective-permute-start | bytes 1376264 | tf_op jit(solution)/shard_map/ppermute | solution.py:54
  98.3 30.0 %collective-permute-start.11 = (bf16[1,2,4,32,1024]{4,3,2,1,0:T(8,128)(2,1)S(1)}, bf16[1,2,4,32,1024]{4,3,2,1,0:T(8,128)(2,1)S(1)}, u32[]{:S(2)}, u32[]{:S(2)}) collective-permute-start(bf16[1,2,4,32,1024]{4,3,2,1,0:T(8,128)(2,1)S(1)} %get-tuple-element.325), channel_id=1, source_target_pairs={{0,2},{2,0},{4,6},{6,4},{8,10},{10,8},{12,14},{14,12},{16,18},{18,... | collective-permute-start | bytes 1572872 | tf_op jit(solution)/shard_map/ppermute | solution.py:54
  122.3 32.0 %collective-permute-start.5 = (bf16[16,1,16,1792]{3,2,1,0:T(8,128)(2,1)S(1)}, bf16[16,1,16,1792]{3,2,1,0:T(8,128)(2,1)S(1)}, u32[]{:S(2)}, u32[]{:S(2)}) collective-permute-start(bf16[16,1,16,1792]{3,2,1,0:T(8,128)(2,1)S(1)} %bitcast.635), channel_id=1, source_target_pairs={{0,1},{1,0},{2,3},{3,2},{4,5},{5,4},{6,7},{7,6},{8,9},{9,8},{10,11... | collective-permute-start | bytes 2752520 | tf_op jit(solution)/shard_map/ppermute | solution.py:80
  145.4 79.1 %collective-permute-start.18 = (bf16[2,2,4,32,1024]{4,3,0,2,1:T(8,128)(2,1)}, bf16[2,2,4,32,1024]{4,3,0,2,1:T(8,128)(2,1)}, u32[]{:S(2)}, u32[]{:S(2)}) collective-permute-start(bf16[2,2,4,32,1024]{4,3,0,2,1:T(8,128)(2,1)} %get-tuple-element.283), channel_id=1, source_target_pairs={{0,2},{2,0},{4,6},{6,4},{8,10},{10,8},{12,14},{14,12},{16,18},{18,... | collective-permute-start | bytes 3145736 | tf_op jit(solution)/shard_map/ppermute | solution.py:54
  146.8 80.6 %collective-permute-start.20 = (bf16[2,2,4,32,1024]{4,3,0,2,1:T(8,128)(2,1)}, bf16[2,2,4,32,1024]{4,3,0,2,1:T(8,128)(2,1)}, u32[]{:S(2)}, u32[]{:S(2)}) collective-permute-start(bf16[2,2,4,32,1024]{4,3,0,2,1:T(8,128)(2,1)} %get-tuple-element.277), channel_id=1, source_target_pairs={{0,4},{2,6},{4,0},{6,2},{8,12},{10,14},{12,8},{14,10},{16,20},{18,... | collective-permute-start | bytes 3145736 | tf_op jit(solution)/shard_map/ppermute | solution.py:54
  149.2 67.1 %collective-permute-start.32 = (bf16[1,2,4,32,1024]{4,3,0,2,1:T(8,128)(2,1)}, bf16[1,2,4,32,1024]{4,3,0,2,1:T(8,128)(2,1)}, u32[]{:S(2)}, u32[]{:S(2)}) collective-permute-start(bf16[1,2,4,32,1024]{4,3,0,2,1:T(8,128)(2,1)} %get-tuple-element.333), channel_id=1, source_target_pairs={{0,2},{2,0},{4,6},{6,4},{8,10},{10,8},{12,14},{14,12},{16,18},{18,... | collective-permute-start | bytes 1572872 | tf_op jit(solution)/shard_map/ppermute | solution.py:54
  152.3 60.2 %collective-permute-start.34 = (bf16[1,2,4,32,1024]{4,3,0,2,1:T(8,128)(2,1)}, bf16[1,2,4,32,1024]{4,3,0,2,1:T(8,128)(2,1)}, u32[]{:S(2)}, u32[]{:S(2)}) collective-permute-start(bf16[1,2,4,32,1024]{4,3,0,2,1:T(8,128)(2,1)} %get-tuple-element.327), channel_id=1, source_target_pairs={{0,4},{2,6},{4,0},{6,2},{8,12},{10,14},{12,8},{14,10},{16,20},{18,... | collective-permute-start | bytes 1572872 | tf_op jit(solution)/shard_map/ppermute | solution.py:54
  154.3 89.9 %collective-permute-start.25 = (bf16[2,2,4,32,1024]{4,3,0,2,1:T(8,128)(2,1)}, bf16[2,2,4,32,1024]{4,3,0,2,1:T(8,128)(2,1)}, u32[]{:S(2)}, u32[]{:S(2)}) collective-permute-start(bf16[2,2,4,32,1024]{4,3,0,2,1:T(8,128)(2,1)} %get-tuple-element.291), channel_id=1, source_target_pairs={{0,2},{2,0},{4,6},{6,4},{8,10},{10,8},{12,14},{14,12},{16,18},{18,... | collective-permute-start | bytes 3145736 | tf_op jit(solution)/shard_map/ppermute | solution.py:54
  212.6 34.7 %collective-permute-start.27 = (bf16[2,2,4,32,1024]{4,3,0,2,1:T(8,128)(2,1)S(1)}, bf16[2,2,4,32,1024]{4,3,0,2,1:T(8,128)(2,1)S(1)}, u32[]{:S(2)}, u32[]{:S(2)}) collective-permute-start(bf16[2,2,4,32,1024]{4,3,0,2,1:T(8,128)(2,1)S(1)} %copy-done.35), channel_id=1, source_target_pairs={{0,4},{2,6},{4,0},{6,2},{8,12},{10,14},{12,8},{14,10},{16,20},{18,... | collective-permute-start | bytes 3145736 | tf_op jit(solution)/shard_map/ppermute | solution.py:54
  418.6 50.5 %collective-permute-start.39 = (f32[8,768]{1,0:T(8,128)}, f32[8,768]{1,0:T(8,128)}, u32[]{:S(2)}, u32[]{:S(2)}) collective-permute-start(f32[8,768]{1,0:T(8,128)} %constant_dynamic-slice_fusion.4), channel_id=1, source_target_pairs={{0,1},{1,0},{2,3},{3,2},{4,5},{5,4},{6,7},{7,6},{8,9},{9,8},{10,11... | collective-permute-start | bytes 73736 | tf_op jit(solution)/shard_map/ppermute | solution.py:80
  426.7 82.8 %collective-permute-start.38 = (bf16[768,512]{1,0:T(8,128)(2,1)}, bf16[768,512]{1,0:T(8,128)(2,1)}, u32[]{:S(2)}, u32[]{:S(2)}) collective-permute-start(bf16[768,512]{1,0:T(8,128)(2,1)} %dynamic-slice_convert_fusion.1), channel_id=1, source_target_pairs={{0,1},{1,0},{2,3},{3,2},{4,5},{5,4},{6,7},{7,6},{8,9},{9,8},{10,11... | collective-permute-start | bytes 2359304 | tf_op jit(solution)/shard_map/ppermute | solution.py:80
  440.4 36.0 %collective-permute-start.47 = (bf16[1,2,4,32,1024]{4,3,2,1,0:T(8,128)(2,1)}, bf16[1,2,4,32,1024]{4,3,2,1,0:T(8,128)(2,1)}, u32[]{:S(2)}, u32[]{:S(2)}) collective-permute-start(bf16[1,2,4,32,1024]{4,3,2,1,0:T(8,128)(2,1)} %slice_bitcast_fusion.16), channel_id=1, source_target_pairs={{0,2},{2,0},{4,6},{6,4},{8,10},{10,8},{12,14},{14,12},{16,18},{18,... | collective-permute-start | bytes 1572872 | tf_op jit(solution)/shard_map/ppermute | solution.py:54
  442.9 35.8 %collective-permute-start.49 = (bf16[1,2,4,32,1024]{4,3,2,1,0:T(8,128)(2,1)}, bf16[1,2,4,32,1024]{4,3,2,1,0:T(8,128)(2,1)}, u32[]{:S(2)}, u32[]{:S(2)}) collective-permute-start(bf16[1,2,4,32,1024]{4,3,2,1,0:T(8,128)(2,1)} %slice_bitcast_fusion.14), channel_id=1, source_target_pairs={{0,4},{2,6},{4,0},{6,2},{8,12},{10,14},{12,8},{14,10},{16,20},{18,... | collective-permute-start | bytes 1572872 | tf_op jit(solution)/shard_map/ppermute | solution.py:54
  446.6 94.8 %collective-permute-start.54 = (bf16[2,2,4,32,1024]{4,3,0,2,1:T(8,128)(2,1)}, bf16[2,2,4,32,1024]{4,3,0,2,1:T(8,128)(2,1)}, u32[]{:S(2)}, u32[]{:S(2)}) collective-permute-start(bf16[2,2,4,32,1024]{4,3,0,2,1:T(8,128)(2,1)} %bitcast.574), channel_id=1, source_target_pairs={{0,2},{2,0},{4,6},{6,4},{8,10},{10,8},{12,14},{14,12},{16,18},{18,... | collective-permute-start | bytes 3145736 | tf_op jit(solution)/shard_map/ppermute | solution.py:54
  469.1 74.5 %collective-permute-start.56 = (bf16[2,2,4,32,1024]{4,3,0,2,1:T(8,128)(2,1)}, bf16[2,2,4,32,1024]{4,3,0,2,1:T(8,128)(2,1)}, u32[]{:S(2)}, u32[]{:S(2)}) collective-permute-start(bf16[2,2,4,32,1024]{4,3,0,2,1:T(8,128)(2,1)} %bitcast.573), channel_id=1, source_target_pairs={{0,4},{2,6},{4,0},{6,2},{8,12},{10,14},{12,8},{14,10},{16,20},{18,... | collective-permute-start | bytes 3145736 | tf_op jit(solution)/shard_map/ppermute | solution.py:54
  478.7 27.9 %collective-permute-start.70 = (bf16[1,2,4,32,1024]{4,3,2,1,0:T(8,128)(2,1)S(1)}, bf16[1,2,4,32,1024]{4,3,2,1,0:T(8,128)(2,1)S(1)}, u32[]{:S(2)}, u32[]{:S(2)}) collective-permute-start(bf16[1,2,4,32,1024]{4,3,2,1,0:T(8,128)(2,1)S(1)} %copy-done.53), channel_id=1, source_target_pairs={{0,4},{2,6},{4,0},{6,2},{8,12},{10,14},{12,8},{14,10},{16,20},{18,... | collective-permute-start | bytes 1572872 | tf_op jit(solution)/shard_map/ppermute | solution.py:54
  540.6 56.2 %collective-permute-start.40 = (bf16[768,640]{1,0:T(8,128)(2,1)}, bf16[768,640]{1,0:T(8,128)(2,1)}, u32[]{:S(2)}, u32[]{:S(2)}) collective-permute-start(bf16[768,640]{1,0:T(8,128)(2,1)} %convolution_convert_fusion), channel_id=1, source_target_pairs={{0,1},{1,0},{2,3},{3,2},{4,5},{5,4},{6,7},{7,6},{8,9},{9,8},{10,11... | collective-permute-start | bytes 2949128 | tf_op jit(solution)/shard_map/ppermute | solution.py:80
  541.4 46.1 %collective-permute-start.41 = (bf16[16,16,1792]{2,1,0:T(8,128)(2,1)S(1)}, bf16[16,16,1792]{2,1,0:T(8,128)(2,1)S(1)}, u32[]{:S(2)}, u32[]{:S(2)}) collective-permute-start(bf16[16,16,1792]{2,1,0:T(8,128)(2,1)S(1)} %fusion.28), channel_id=1, source_target_pairs={{0,1},{1,0},{2,3},{3,2},{4,5},{5,4},{6,7},{7,6},{8,9},{9,8},{10,11... | collective-permute-start | bytes 2752520 | tf_op jit(solution)/shard_map/ppermute | solution.py:80
  543.7 33.5 %collective-permute-start.55 = (bf16[2,4,32,1024]{3,2,0,1:T(8,128)(2,1)S(1)}, bf16[2,4,32,1024]{3,2,0,1:T(8,128)(2,1)S(1)}, u32[]{:S(2)}, u32[]{:S(2)}) collective-permute-start(bf16[2,4,32,1024]{3,2,0,1:T(8,128)(2,1)S(1)} %slice_bitcast_fusion.12), channel_id=1, source_target_pairs={{0,4},{2,6},{4,0},{6,2},{8,12},{10,14},{12,8},{14,10},{16,20},{18,... | collective-permute-start | bytes 1572872 | tf_op jit(solution)/shard_map/ppermute | solution.py:54
  648.0 37.9 %collective-permute-start.45 = (bf16[16,1792]{0,1:T(8,128)(2,1)S(1)}, bf16[16,1792]{0,1:T(8,128)(2,1)S(1)}, u32[]{:S(2)}, u32[]{:S(2)}) collective-permute-start(bf16[16,1792]{0,1:T(8,128)(2,1)S(1)} %get-tuple-element.263), channel_id=1, source_target_pairs={{0,16},{2,18},{4,20},{6,22},{8,24},{10,26},{12,28},{14,30},{16,0},... | collective-permute-start | bytes 172040 | tf_op jit(solution)/shard_map/ppermute | solution.py:54
  650.0 35.9 %collective-permute-start.44 = (bf16[16,1792]{0,1:T(8,128)(2,1)S(1)}, bf16[16,1792]{0,1:T(8,128)(2,1)S(1)}, u32[]{:S(2)}, u32[]{:S(2)}) collective-permute-start(bf16[16,1792]{0,1:T(8,128)(2,1)S(1)} %get-tuple-element.261), channel_id=1, source_target_pairs={{0,8},{2,10},{4,12},{6,14},{8,16},{10,18},{12,20},{14,22},{16,24},... | collective-permute-start | bytes 172040 | tf_op jit(solution)/shard_map/ppermute | solution.py:54
  653.2 39.2 %collective-permute-start.75 = (f32[2,6,32,512]{3,2,1,0:T(8,128)}, f32[2,6,32,512]{3,2,1,0:T(8,128)}, u32[]{:S(2)}, u32[]{:S(2)}) collective-permute-start(f32[2,6,32,512]{3,2,1,0:T(8,128)} %get-tuple-element.269), channel_id=1, source_target_pairs={{0,1},{1,0},{2,3},{3,2},{4,5},{5,4},{6,7},{7,6},{8,9},{9,8},{10,11... | collective-permute-start | bytes 2359304 | tf_op jit(solution)/shard_map/ppermute | solution.py:80
  (166 other events, 1647.3 us)
where the time goes:
time: 707 us; the launch traced here: 697 us
  waiting for transfers between devices  180 us (25%)
  local copies, waits for them, and re-layouts  169 us (24%)
  Pallas kernels  131 us (19%)
  other arithmetic  99.8 us (14%)
  starting transfers between devices  90.4 us (13%)
  matrix products  23.3 us (3%)
    ppermute x71, waiting for transfers between devices, send(): return lax.ppermute(values, 'dp', self.toward(dim, step))  180 us
    ppermute x71, starting transfers between devices, send(): return lax.ppermute(values, 'dp', self.toward(dim, step))  88.8 us
    pallas_call x4, Pallas kernels, call_backward(): pl.pallas_call(functools.partial(backward_kernel, experts), out_shape=(ja...  75.4 us
    pallas_call x4, Pallas kernels, call_forward(): pl.pallas_call(functools.partial(forward_kernel, experts), out_shape=(jax...  45.3 us
    unnamed x237, local copies, waits for them, and re-layouts  29.9 us
  transfers between devices with their start and end apart: 82, of which 28 were waited for; matrix products, arithmetic and copies ran while one was open for 32% of the time, Pallas kernels for 5%

commit v1 on v0

v1 whole, which is shorter than its diff:
```python
import functools
import math

import jax
import jax.numpy as jnp
from jax import lax
from jax.experimental import pallas as pl
from jax.experimental.pallas import tpu as pltpu
from jax.sharding import PartitionSpec as P

D = 512
H = 1024
HALF = H // 2
TW = 256
S = 4
DOM = 4
K = 2
EPS = 1e-05
FROZEN_SHARE = 0.25
TILE = 256
LOCAL = 6
CHUNKS = ((5, 0), (4, 1), (3, 2))
VMEM_LIMIT = 48 * 1024 * 1024
PACK = 1792
SETS = (
    tuple(range(2)) + tuple(S + K * d for d in reversed(range(DOM))),
    tuple(range(2, 4)) + tuple(S + K * d + 1 for d in range(DOM)),
)
COEF, SCALE, DCOEF, DOMAIN, LABEL, WEIGHT, BIAS = 0, 6, 12, 18, 19, 20, 21
LOW, HIGH, ROLE, DOMAIN_OF, START, END, CORE = 0, 4, 8, 9, 13, 17, 21

bf16 = jnp.bfloat16
f32 = jnp.float32


def dims_of(count):
    if count % 4 == 0:
        rest = count // 4
        root = math.isqrt(rest)
        if root * root == rest:
            return (4, root, root)
    return (count, 1, 1)


class Box:
    def __init__(self, count):
        first, second, third = dims_of(count)
        self.count = count
        self.dims = (2, first // 2, second, third)
        self.strides = (second * third, 2 * second * third, third, 1)

    def role(self, chip):
        return (chip // self.strides[0]) % 2

    def partner(self, chip):
        return chip + (1 - 2 * self.role(chip)) * self.strides[0]

    def send(self, values, flip=0, z=0, y=0, x=0):
        pairs = []
        for chip in range(self.count):
            to = chip
            for step, size, stride in zip((flip, z, y, x), self.dims, self.strides):
                place = (chip // stride) % size
                to += ((place + step) % size - place) * stride
            pairs.append((chip, to))
        return lax.ppermute(values, "dp", pairs)

    def to_partner(self, values, home):
        pairs = []
        for chip in range(self.count):
            for core in range(2):
                if (core == self.role(chip)) == home:
                    pairs.append((2 * chip + core, 2 * self.partner(chip) + core))
        return lax.ppermute(values, ("dp", "tensor"), pairs)

    def pieces(self, values, dim):
        size = self.dims[("flip", "z", "y", "x").index(dim)]
        return [self.send(values, **{dim: -k}) for k in range(1, size)]

    def hand_out(self, parts, dim):
        return [self.send(part, **{dim: k}) for k, part in enumerate(parts) if k]

    def plane(self):
        _, _, ny, nx = self.dims
        return [(x, y) for x in range(nx) for y in range(ny)][1:]

    def gather_plane(self, values):
        return [values] + [self.send(values, y=-y, x=-x) for x, y in self.plane()]

    def hand_out_plane(self, parts):
        return [self.send(part, y=y, x=x) for part, (x, y) in zip(parts[1:], self.plane())]

    def same_sum(self, values, dim):
        number = ("flip", "z", "y", "x").index(dim)
        size, stride = self.dims[number], self.strides[number]
        found = jnp.stack([values] + self.pieces(values, dim))
        if size > 2:
            mine = (lax.axis_index("dp") // stride) % size
            found = jnp.take(found, (jnp.arange(size) - mine) % size, axis=0)
        return functools.reduce(jnp.add, [found[k] for k in range(size)])

    def others(self):
        me = lax.axis_index("dp")
        chip = jnp.arange(self.count)
        ahead, place, weight = 0, 0, 1
        for dim, (size, stride) in enumerate(zip(self.dims, self.strides)):
            mine = (me // stride) % size if dim else 0
            ahead = ahead + ((mine + (chip // weight) % size) % size) * stride
            place = place + (((chip // stride) % size - mine) % size) * weight
            weight *= size
        return ahead, place


def swap_cores(values):
    return lax.ppermute(values, "tensor", [(0, 1), (1, 0)])


def in_order(which, own, other, axis):
    return jnp.where(
        which == 0,
        jnp.concatenate([own, other], axis),
        jnp.concatenate([other, own], axis),
    )


def step(*values):
    return lax.optimization_barrier(values)


def total(first, arrived):
    return functools.reduce(jnp.add, [a.astype(f32) for a in arrived], first.astype(f32))


def gelu_parts(v):
    inner = math.sqrt(2.0 / math.pi)
    square = v * v
    th = jnp.tanh(v * (inner + inner * 0.044715 * square))
    half = 0.5 * (1.0 + th)
    act = v * half
    slope = half + 0.5 * v * (1.0 - th * th) * (inner + 3.0 * inner * 0.044715 * square)
    return act, slope


def nt(a, b):
    return lax.dot_general(a, b, (((1,), (1,)), ((), ())), preferred_element_type=f32)


def tn(a, b):
    return lax.dot_general(a, b, (((0,), (0,)), ((), ())), preferred_element_type=f32)


def nn(a, b):
    return jnp.dot(a, b, preferred_element_type=f32)


def softmax_rows(v):
    e = jnp.exp(v - jnp.max(v, axis=0, keepdims=True))
    return e / jnp.sum(e, axis=0, keepdims=True)


def prepare_kernel(ints, floats, rows_ref, embeds_ref, proj_ref, gates_ref, vec_ref, ev_ref, x_ref, mix_ref, cols_ref, prob_ref):
    tiles_of_half = pl.num_programs(0) // 2
    index = pl.program_id(0)
    role = ints[ROLE]
    count = rows_ref.shape[1]
    slot = index * TILE + lax.broadcasted_iota(jnp.int32, (TILE, count), 0)
    order = jnp.where(rows_ref[0:1, :].astype(jnp.int32) == slot, 1.0, 0.0).astype(bf16)
    events = nn(order, embeds_ref[...]).astype(bf16)
    ev_ref[...] = events
    mixed = nt(events, proj_ref[...]) + vec_ref[3 * LOCAL : 3 * LOCAL + 1, :]
    low = mixed.astype(bf16)
    x_ref[...] = low
    mix_ref[...] = mixed * jnp.where(index // tiles_of_half == role, 1.0, 0.0)
    logits = jnp.transpose(nn(low, gates_ref[...]))
    place = index * TILE + lax.broadcasted_iota(jnp.int32, (1, TILE), 1)
    picks = [
        jnp.where((place >= ints[START + d]) & (place < ints[END + d]), 1.0, 0.0) for d in range(DOM)
    ]

    def pick(low_row, size):
        return softmax_rows(
            functools.reduce(
                jnp.add,
                [picks[d] * logits[low_row + d * size : low_row + (d + 1) * size] for d in range(DOM)],
            )
        )

    top, shared, domain = pick(0, 2), pick(2 * DOM, S), pick((2 + S) * DOM, K)
    prob_ref[...] = jnp.concatenate([top, shared, domain], axis=0)
    first = role == 0
    own_shared = top[0:1] * jnp.where(first, shared[:2], shared[2:])
    own_domain = top[1:2] * jnp.where(first, domain[0:1], domain[1:2])
    labels = nt(rows_ref[...].astype(bf16), order)
    coef = [own_domain * jnp.where(first, picks[DOM - 1 - d], picks[d]) for d in range(DOM)]
    table = [
        own_shared,
        *coef,
        jnp.zeros((DOMAIN - SCALE, TILE), f32),
        sum(float(d) * picks[d] for d in range(DOM)),
        labels[1:2],
        sum(floats[d] * picks[d] for d in range(DOM)),
        sum(floats[DOM + d] * picks[d] for d in range(DOM)),
        jnp.zeros((128 - BIAS - 1, TILE), f32),
    ]
    cols_ref[...] = jnp.transpose(jnp.concatenate(table, axis=0))


def tile_of(expert, step, ints):
    if expert < 2:
        return step, True
    low, high = ints[LOW + expert - 2], ints[HIGH + expert - 2]
    return jnp.minimum(low + step, jnp.maximum(high - 1, 0)), low + step < high


def with_column(table, column, values):
    lane = lax.broadcasted_iota(jnp.int32, table.shape, 1)
    return jnp.where(lane == column, values, table)


def forward_kernel(
    expert, ints, x_ref, wi_a, wi_b, wo_a, wo_b, bi_ref, vec_ref, cols_in, mix_in, cols_ref, mix_ref, norm_ref
):
    step = pl.program_id(0)
    _, busy = tile_of(expert, step, ints)

    def work():
        x = x_ref[...]
        pre_a = nn(x, wi_a[0]) + bi_ref[expert : expert + 1, :HALF]
        act_a = gelu_parts(pre_a)[0].astype(bf16)
        pre_b = nn(x, wi_b[0]) + bi_ref[expert : expert + 1, HALF:]
        act_b = gelu_parts(pre_b)[0].astype(bf16)
        out = nt(act_a, wo_a[0]) + nt(act_b, wo_b[0]) + vec_ref[expert : expert + 1, :]
        centre = jnp.mean(out, axis=1, keepdims=True)
        centred = out - centre
        scale = lax.rsqrt(jnp.mean(centred * centred, axis=1, keepdims=True) + EPS)
        norm = centred * scale
        norm_ref[...] = norm.astype(bf16)
        cols = cols_in[...]
        cols_ref[...] = with_column(cols, SCALE + expert, scale)
        gain = vec_ref[LOCAL + expert : LOCAL + expert + 1, :]
        shift = vec_ref[2 * LOCAL + expert : 2 * LOCAL + expert + 1, :]
        mix_ref[...] = mix_in[...] + cols[:, COEF + expert : COEF + expert + 1] * (norm * gain + shift)

    if expert < 2:
        work()
    else:
        pl.when(busy)(work)

        @pl.when(jnp.logical_not(busy) & (step == 0))
        def _():
            cols_ref[...] = cols_in[...]
            mix_ref[...] = mix_in[...]


def backward_kernel(
    expert,
    ints,
    x_ref,
    gb_ref,
    norm_ref,
    wi_a,
    wi_b,
    wo_a,
    wo_b,
    bi_ref,
    vec_ref,
    cols_in,
    back_in,
    cols_ref,
    back_ref,
    keep_ref,
    give_ref,
    dvec_ref,
    dbi_ref,
    in_a,
    in_b,
    out_a,
    out_b,
):
    step = pl.program_id(0)
    _, busy = tile_of(expert, step, ints)

    @pl.when(step == 0)
    def _():
        for ref in (in_a, in_b, out_a, out_b, dvec_ref, dbi_ref):
            ref[...] = jnp.zeros_like(ref)
        if expert >= 2:
            cols_ref[...] = cols_in[...]
            back_ref[...] = back_in[...]

    def work():
        x = x_ref[...]
        norm = norm_ref[...].astype(f32)
        cols = cols_in[...]
        grad_block = gb_ref[...].astype(f32)
        gain = vec_ref[LOCAL + expert : LOCAL + expert + 1, :]
        shift = vec_ref[2 * LOCAL + expert : 2 * LOCAL + expert + 1, :]
        scale = cols[:, SCALE + expert : SCALE + expert + 1]
        grad_exp = cols[:, COEF + expert : COEF + expert + 1] * grad_block
        scaled = grad_exp * norm
        dx = grad_exp * gain
        first = jnp.mean(dx, axis=1, keepdims=True)
        second = jnp.mean(dx * norm, axis=1, keepdims=True)
        grad_sum = scale * (dx - first - norm * second)
        grad_low = grad_sum.astype(bf16)
        pre_a = nn(x, wi_a[0]) + bi_ref[expert : expert + 1, :HALF]
        act_a, slope_a = gelu_parts(pre_a)
        low_a = (nn(grad_low, wo_a[0]) * slope_a).astype(bf16)
        pre_b = nn(x, wi_b[0]) + bi_ref[expert : expert + 1, HALF:]
        act_b, slope_b = gelu_parts(pre_b)
        low_b = (nn(grad_low, wo_b[0]) * slope_b).astype(bf16)
        out_a[...] += tn(grad_low, act_a.astype(bf16))
        in_a[...] += tn(x, low_a)
        out_b[...] += tn(grad_low, act_b.astype(bf16))
        in_b[...] += tn(x, low_b)
        back_ref[...] = back_in[...] + (nt(low_a, wi_a[0]) + nt(low_b, wi_b[0]))
        dcoef = jnp.sum(grad_block * (norm * gain + shift), axis=1, keepdims=True)
        if expert < 2:
            cols_ref[...] = with_column(cols, DCOEF + expert, dcoef)
        else:
            mine = cols[:, DOMAIN : DOMAIN + 1] == ints[DOMAIN_OF + expert - 2].astype(f32)
            column = cols[:, DCOEF + 2 : DCOEF + 3] + jnp.where(mine, dcoef, 0.0)
            cols_ref[...] = with_column(cols, DCOEF + 2, column)
        dvec_ref[0:1, :] += jnp.sum(grad_sum, axis=0, keepdims=True)
        dvec_ref[1:2, :] += jnp.sum(scaled, axis=0, keepdims=True)
        dvec_ref[2:3, :] += jnp.sum(grad_exp, axis=0, keepdims=True)
        dbi_ref[0:1, :HALF] += jnp.sum(low_a.astype(f32), axis=0, keepdims=True)
        dbi_ref[0:1, HALF:] += jnp.sum(low_b.astype(f32), axis=0, keepdims=True)

    if expert < 2:
        work()
    else:
        pl.when(busy)(work)

    @pl.when(step == pl.num_programs(0) - 1)
    def _():
        keep_ref[0] = in_a[...].astype(bf16)
        keep_ref[1] = out_a[...].astype(bf16)
        give_ref[0] = in_b[...].astype(bf16)
        give_ref[1] = out_b[...].astype(bf16)


def tower_kernel(ints, mix_ref, other_ref, cols_ref, tw_ref, tv_ref, out_ref, gb_ref, low_ref, dw_ref, dv_ref):
    @pl.when(pl.program_id(0) == 0)
    def _():
        dw_ref[...] = jnp.zeros_like(dw_ref)
        dv_ref[...] = jnp.zeros_like(dv_ref)

    bias = tv_ref[0:1, :]
    head = tv_ref[1:2, :]
    cols = cols_ref[...]
    block = (mix_ref[...] + other_ref[...].astype(f32)).astype(bf16)
    pre = nn(block, tw_ref[...]) + bias
    act, slope = gelu_parts(pre)
    group = lax.broadcasted_iota(jnp.int32, pre.shape, 1) // TW
    mine = group == cols[:, DOMAIN : DOMAIN + 1].astype(jnp.int32)
    act = jnp.where(mine, act, 0.0)
    logit = jnp.sum(act * head, axis=1, keepdims=True) + cols[:, BIAS : BIAS + 1]
    predicted = 1.0 / (1.0 + jnp.exp(-logit))
    grad_logit = cols[:, WEIGHT : WEIGHT + 1] * (predicted - cols[:, LABEL : LABEL + 1])
    lane = lax.broadcasted_iota(jnp.int32, cols.shape, 1)
    out_ref[...] = jnp.transpose(jnp.where(lane == 0, predicted, jnp.where(lane == 1, grad_logit, 0.0)))[:8]
    dv_ref[1:2, :] += jnp.sum(grad_logit * act, axis=0, keepdims=True)
    grad_pre = jnp.where(mine, grad_logit * head * slope, 0.0)
    dv_ref[0:1, :] += jnp.sum(grad_pre, axis=0, keepdims=True)
    grad_low = grad_pre.astype(bf16)
    grad_block = nt(grad_low, tw_ref[...])
    gb_ref[...] = grad_block
    low_ref[...] = grad_block.astype(bf16)
    dw_ref[...] += tn(block, grad_low)


def lines_kernel(ints, row_ref, dv_ref, *refs):
    out_ref = refs[LOCAL]
    first_set, first_core = ints[ROLE] == 0, ints[CORE] == 0
    mine = [r[0:1, :] for r in refs[:LOCAL]]
    mine = jnp.concatenate(
        [jnp.where(first_core, m[:, :HALF], m[:, HALF:]) for m in mine]
        + [jnp.where(first_core, m[:, HALF:], m[:, :HALF]) for m in mine]
    )
    slot = lax.broadcasted_iota(jnp.int32, (1, row_ref.shape[1]), 1) + ints[ROLE] * row_ref.shape[1]
    lane = lax.broadcasted_iota(jnp.int32, (1, HALF), 1)
    bias = jnp.zeros((1, HALF), f32)
    for d in range(DOM):
        inside = (slot >= ints[START + d]) & (slot < ints[END + d])
        bias = jnp.where(
            lane == d, jnp.sum(jnp.where(inside, row_ref[1:2, :], 0.0), axis=1, keepdims=True), bias
        )
    out_ref[...] = jnp.concatenate(
        [
            jnp.where(first_set, mine, 0.0),
            jnp.where(first_set, 0.0, mine),
            dv_ref[0:2, :HALF],
            dv_ref[0:2, HALF:],
            bias,
            jnp.zeros((3, HALF), f32),
        ]
    )


def call_lines(ints, row_out, dv, bias_grads):
    return pl.pallas_call(
        lines_kernel,
        grid_spec=pltpu.PrefetchScalarGridSpec(
            num_scalar_prefetch=1,
            grid=(1,),
            in_specs=[fixed(row_out.shape), fixed(dv.shape)] + [fixed((8, H))] * LOCAL,
            out_specs=fixed((32, HALF)),
        ),
        out_shape=jax.ShapeDtypeStruct((32, HALF), f32),
        compiler_params=params(),
        name="lines",
    )(ints, row_out, dv, *bias_grads)


def softmax_back(probability, grad_probs):
    return probability * (grad_probs - jnp.sum(probability * grad_probs, axis=0, keepdims=True))


def finish_kernel(
    ints, gb_ref, back_ref, other_ref, cols_ref, coef_ref, prob_ref, x_ref, ev_ref, gates_ref, proj_ref, tower_ref, *refs
):
    vec_refs, (ge_ref, small_ref, proj_sum, gate_sum, bias_sum) = refs[:LOCAL], refs[LOCAL:]
    index = pl.program_id(0)
    last = pl.num_programs(0) - 1
    first = ints[ROLE] == 0

    @pl.when(index == 0)
    def _():
        for ref in (proj_sum, gate_sum, bias_sum):
            ref[...] = jnp.zeros_like(ref)

    mine = jnp.transpose(cols_ref[...])[DCOEF : DCOEF + 3]
    other = coef_ref[0:3, :]
    one, two = jnp.where(first, mine, other), jnp.where(first, other, mine)
    d_shared = jnp.concatenate([one[0:2], two[0:2]], axis=0)
    d_domain = jnp.concatenate([one[2:3], two[2:3]], axis=0)
    top, shared, domain = prob_ref[0:2, :], prob_ref[2:6, :], prob_ref[6:8, :]
    d_top = jnp.concatenate(
        [
            jnp.sum(d_shared * shared, axis=0, keepdims=True),
            jnp.sum(d_domain * domain, axis=0, keepdims=True),
        ],
        axis=0,
    )
    grads = (
        softmax_back(top, d_top),
        softmax_back(shared, d_shared * top[0:1]),
        softmax_back(domain, d_domain * top[1:2]),
    )
    place = (ints[ROLE] * pl.num_programs(0) + index) * TILE + lax.broadcasted_iota(
        jnp.int32, (1, TILE), 1
    )
    picks = [
        jnp.where((place >= ints[START + d]) & (place < ints[END + d]), 1.0, 0.0) for d in range(DOM)
    ]
    spread = jnp.concatenate(
        [picks[d] * grad for grad in grads for d in range(DOM)] + [jnp.zeros((96, TILE), f32)],
        axis=0,
    )
    spread = jnp.transpose(spread).astype(bf16)
    gate_sum[...] += tn(x_ref[...], spread)
    grad_mixed = (
        gb_ref[...] + back_ref[...] + other_ref[...].astype(f32) + nt(spread, gates_ref[...])
    )
    bias_sum[0:1, :] += jnp.sum(grad_mixed, axis=0, keepdims=True)
    low = grad_mixed.astype(bf16)
    proj_sum[...] += tn(low, ev_ref[...])
    ge_ref[...] = nn(low, proj_ref[...]).astype(bf16)

    @pl.when(index == last)
    def _():
        e_in = proj_sum.shape[1]
        vectors = jnp.concatenate([r[0:3, :] for r in vec_refs], axis=0)
        rows = jnp.concatenate(
            [
                jnp.zeros((32, D), f32),
                jnp.where(first, vectors, 0.0),
                jnp.where(first, 0.0, vectors),
                bias_sum[0:1, :],
                jnp.zeros((59, D), f32),
            ],
            axis=0,
        )
        small_ref[:, :e_in] = proj_sum[...].astype(bf16)
        small_ref[:, e_in : e_in + DOM * TW] = tower_ref[...].astype(bf16)
        small_ref[:, e_in + DOM * TW :] = (gate_sum[...] + jnp.transpose(rows)).astype(bf16)


def call_finish(ints, gb, back, other, cols, coef, probs, x, events, gates, proj_t, tower, vecs):
    rows, e_in = gb.shape[0], events.shape[1]
    tiles = rows // TILE

    def kept(width):
        return pl.BlockSpec((TILE, width), lambda i, ints: (ints[ROLE] * tiles + i, 0))

    def tile(width):
        return pl.BlockSpec((TILE, width), lambda i, *_: (i, 0))

    return pl.pallas_call(
        finish_kernel,
        grid_spec=pltpu.PrefetchScalarGridSpec(
            num_scalar_prefetch=1,
            grid=(tiles,),
            in_specs=[
                tile(D),
                kept(D),
                tile(D),
                kept(128),
                pl.BlockSpec((8, TILE), lambda i, *_: (0, i)),
                pl.BlockSpec((8, TILE), lambda i, ints: (0, ints[ROLE] * tiles + i)),
                kept(D),
                kept(e_in),
                fixed(gates.shape),
                fixed(proj_t.shape),
                fixed(tower.shape),
            ]
            + [fixed((8, D))] * LOCAL,
            out_specs=(tile(e_in), fixed((D, PACK))),
            scratch_shapes=[pltpu.VMEM((D, e_in), f32), pltpu.VMEM((D, 128), f32), pltpu.VMEM((8, D), f32)],
        ),
        out_shape=(jax.ShapeDtypeStruct((rows, e_in), bf16), jax.ShapeDtypeStruct((D, PACK), bf16)),
        compiler_params=params(),
        cost_estimate=pl.CostEstimate(
            flops=4 * rows * D * (e_in + 128), bytes_accessed=10_000_000, transcendentals=0
        ),
        name="finish",
    )(ints, gb, back, other, cols, coef, probs, x, events, gates, proj_t, tower, *vecs)


def small_kernel(*refs):
    *parts, proj_ref, tower_ref, lines_ref = refs
    added = functools.reduce(jnp.add, [p[...].astype(f32) for p in parts])
    e_in = proj_ref.shape[1]
    proj_ref[...] = added[:, :e_in]
    for d in range(DOM):
        tower_ref[d] = added[:, e_in + d * TW : e_in + (d + 1) * TW]
    lines_ref[...] = added[:, e_in + DOM * TW :]


def call_small(parts):
    width = parts[0].shape[0]
    e_in = PACK - DOM * TW - 128
    return pl.pallas_call(
        small_kernel,
        grid=(1,),
        in_specs=[fixed(p.shape) for p in parts],
        out_specs=(fixed((width, e_in)), fixed((DOM, width, TW)), fixed((width, 128))),
        out_shape=(
            jax.ShapeDtypeStruct((width, e_in), f32),
            jax.ShapeDtypeStruct((DOM, width, TW), f32),
            jax.ShapeDtypeStruct((width, 128), f32),
        ),
        compiler_params=params(),
        name="small",
    )(*parts)


def place_kernel(ints, *refs):
    *parts, in_ref, out_ref = refs
    half = len(parts) // 2
    first = ints[ROLE] == 0
    for chunk, (own, other) in enumerate(zip(parts[:half], parts[half:])):
        for place, expert in enumerate(CHUNKS[chunk]):
            for which, ref in enumerate((in_ref, out_ref)):
                a, b = own[which, place].astype(f32), other[which, place].astype(f32)
                ref[SETS[0][expert]] = jnp.where(first, a, b)
                ref[SETS[1][expert]] = jnp.where(first, b, a)


def call_place(ints, own, other):
    rows, width = own[0].shape[2:]
    shape = (2 * LOCAL, rows, width)
    return pl.pallas_call(
        place_kernel,
        grid_spec=pltpu.PrefetchScalarGridSpec(
            num_scalar_prefetch=1,
            grid=(1,),
            in_specs=[fixed(a.shape) for a in (*own, *other)],
            out_specs=(fixed(shape), fixed(shape)),
        ),
        out_shape=(jax.ShapeDtypeStruct(shape, f32),) * 2,
        compiler_params=params(),
        name="place",
    )(ints, *own, *other)


def params():
    return pltpu.CompilerParams(vmem_limit_bytes=VMEM_LIMIT)


def fixed(shape):
    return pl.BlockSpec(shape, lambda i, *_: (0,) * len(shape))


def choose_kernel(own_ids, other_ids, in_own, out_own, in_other, out_other, own_ref, other_ref):
    own_ref[0], own_ref[1] = in_own[...], out_own[...]
    other_ref[0], other_ref[1] = in_other[...], out_other[...]


def call_choose(own_ids, other_ids, w_in, w_out_t):
    block = (1,) + w_in.shape[1:]
    shape = jax.ShapeDtypeStruct((2, LOCAL) + w_in.shape[1:], bf16)
    own = pl.BlockSpec(block, lambda i, a, b: (a[i], 0, 0))
    other = pl.BlockSpec(block, lambda i, a, b: (b[i], 0, 0))
    out = pl.BlockSpec((2,) + block, lambda i, a, b: (0, i, 0, 0))
    return pl.pallas_call(
        choose_kernel,
        grid_spec=pltpu.PrefetchScalarGridSpec(
            num_scalar_prefetch=2, grid=(LOCAL,), in_specs=[own, own, other, other], out_specs=(out, out)
        ),
        out_shape=(shape, shape),
        compiler_params=params(),
        cost_estimate=pl.CostEstimate(flops=0, bytes_accessed=2_000_000, transcendentals=0),
        name="choose",
    )(own_ids, other_ids, w_in, w_out_t, w_in, w_out_t)


def call_prepare(ints, floats, table, embeds, proj_t, gates, vec):
    rows = embeds.shape[0]
    tiles = rows // TILE
    e_in = embeds.shape[1]

    def tile(width):
        return pl.BlockSpec((TILE, width), lambda i, *_: (i, 0))

    return pl.pallas_call(
        prepare_kernel,
        grid_spec=pltpu.PrefetchScalarGridSpec(
            num_scalar_prefetch=2,
            grid=(tiles,),
            in_specs=[fixed(table.shape), fixed(embeds.shape), fixed(proj_t.shape), fixed(gates.shape), fixed(vec.shape)],
            out_specs=(
                tile(e_in),
                tile(D),
                tile(D),
                tile(128),
                pl.BlockSpec((8, TILE), lambda i, *_: (0, i)),
            ),
        ),
        out_shape=(
            jax.ShapeDtypeStruct((rows, e_in), bf16),
            jax.ShapeDtypeStruct((rows, D), bf16),
            jax.ShapeDtypeStruct((rows, D), f32),
            jax.ShapeDtypeStruct((rows, 128), f32),
            jax.ShapeDtypeStruct((8, rows), f32),
        ),
        compiler_params=params(),
        cost_estimate=pl.CostEstimate(
            flops=2 * rows * e_in * (rows + D), bytes_accessed=12_000_000, transcendentals=rows * 8
        ),
        name="prepare",
    )(ints, floats, table, embeds, proj_t, gates, vec)


def expert_specs(expert, place, rows):
    steps = rows // TILE if expert < 2 else rows // TILE // 2 + 1

    def tile(width):
        return pl.BlockSpec((TILE, width), lambda i, ints: (tile_of(expert, i, ints)[0], 0))

    weights = [pl.BlockSpec((1, D, HALF), lambda i, *_: (place, 0, 0))] * 4
    return steps, tile, weights


def call_forward(expert, place, ints, x, weights, bi, vec, cols, mix):
    rows = x.shape[0]
    steps, tile, weight_specs = expert_specs(expert, place, rows)
    return pl.pallas_call(
        functools.partial(forward_kernel, expert),
        grid_spec=pltpu.PrefetchScalarGridSpec(
            num_scalar_prefetch=1,
            grid=(steps,),
            in_specs=[tile(D)] + weight_specs + [fixed(bi.shape), fixed(vec.shape), tile(128), tile(D)],
            out_specs=(tile(128), tile(D), tile(D)),
        ),
        out_shape=(
            jax.ShapeDtypeStruct((rows, 128), f32),
            jax.ShapeDtypeStruct((rows, D), f32),
            jax.ShapeDtypeStruct((rows, D), bf16),
        ),
        input_output_aliases={8: 0, 9: 1},
        compiler_params=params(),
        cost_estimate=pl.CostEstimate(
            flops=4 * steps * TILE * D * H, bytes_accessed=12_000_000, transcendentals=steps * TILE * H
        ),
        name="expert_forward",
    )(ints, x, *weights, bi, vec, cols, mix)


def call_backward(expert, place, ints, x, gb, norm, weights, bi, vec, cols, back):
    rows = x.shape[0]
    steps, tile, weight_specs = expert_specs(expert, place, rows)
    if gb.shape[0] == rows:
        gb_spec = tile(D)
    else:
        half_tiles = rows // TILE // 2
        gb_spec = pl.BlockSpec(
            (TILE, D),
            lambda i, ints: (
                jnp.clip(tile_of(expert, i, ints)[0] - ints[ROLE] * half_tiles, 0, half_tiles - 1),
                0,
            ),
        )
    return pl.pallas_call(
        functools.partial(backward_kernel, expert),
        grid_spec=pltpu.PrefetchScalarGridSpec(
            num_scalar_prefetch=1,
            grid=(steps,),
            in_specs=[tile(D), gb_spec, tile(D)]
            + weight_specs
            + [fixed(bi.shape), fixed(vec.shape), tile(128), tile(D)],
            out_specs=(
                tile(128),
                tile(D),
                fixed((2, D, HALF)),
                fixed((2, D, HALF)),
                fixed((8, D)),
                fixed((8, H)),
            ),
            scratch_shapes=[pltpu.VMEM((D, HALF), f32)] * 4,
        ),
        out_shape=(
            jax.ShapeDtypeStruct((rows, 128), f32),
            jax.ShapeDtypeStruct((rows, D), f32),
            jax.ShapeDtypeStruct((2, D, HALF), bf16),
            jax.ShapeDtypeStruct((2, D, HALF), bf16),
            jax.ShapeDtypeStruct((8, D), f32),
            jax.ShapeDtypeStruct((8, H), f32),
        ),
        input_output_aliases={10: 0, 11: 1},
        compiler_params=params(),
        cost_estimate=pl.CostEstimate(
            flops=10 * steps * TILE * D * H, bytes_accessed=20_000_000, transcendentals=steps * TILE * H
        ),
        name="expert_backward",
    )(ints, x, gb, norm, *weights, bi, vec, cols, back)


def call_tower(ints, mix, other, cols, tower, tower_vec):
    rows = other.shape[0]
    tiles = rows // TILE

    def kept(width):
        return pl.BlockSpec((TILE, width), lambda i, ints: (ints[ROLE] * tiles + i, 0))

    def tile(width):
        return pl.BlockSpec((TILE, width), lambda i, *_: (i, 0))

    return pl.pallas_call(
        tower_kernel,
        grid_spec=pltpu.PrefetchScalarGridSpec(
            num_scalar_prefetch=1,
            grid=(tiles,),
            in_specs=[kept(D), tile(D), kept(128), fixed(tower.shape), fixed(tower_vec.shape)],
            out_specs=(
                pl.BlockSpec((8, TILE), lambda i, *_: (0, i)),
                tile(D),
                tile(D),
                fixed((D, DOM * TW)),
                fixed((8, DOM * TW)),
            ),
        ),
        out_shape=(
            jax.ShapeDtypeStruct((8, rows), f32),
            jax.ShapeDtypeStruct((rows, D), f32),
            jax.ShapeDtypeStruct((rows, D), bf16),
            jax.ShapeDtypeStruct((D, DOM * TW), f32),
            jax.ShapeDtypeStruct((8, DOM * TW), f32),
        ),
        compiler_params=params(),
        cost_estimate=pl.CostEstimate(
            flops=6 * rows * D * DOM * TW, bytes_accessed=10_000_000, transcendentals=rows * DOM * TW
        ),
        name="towers",
    )(ints, mix, other, cols, tower, tower_vec)


def per_device(
    box,
    embeds,
    domain,
    frozen,
    labels,
    proj_w,
    proj_b,
    w_in,
    in_bias,
    w_out,
    out_bias,
    ln_gain,
    ln_shift,
    gate_top,
    gate_shared,
    gate_domain,
    tower_w,
    tower_b,
    tower_out,
    tower_out_b,
):
    core = lax.axis_index("tensor")
    role = box.role(lax.axis_index("dp"))
    at_home = core == role
    places = box.count
    rows = embeds.shape[0]
    half_rows = rows // 2
    width = proj_w.shape[1]
    e_in = proj_w.shape[0]
    ahead, place_of = box.others()
    nz, ny, nx = box.dims[1:]
    sets = jnp.array(SETS, jnp.int32)
    set_own, set_other = sets[role], sets[1 - role]

    def half(values, which, axis=0):
        return lax.dynamic_slice_in_dim(values, which * half_rows, half_rows, axis)

    own, other = call_choose(set_own, set_other, w_in, jnp.swapaxes(w_out, 1, 2))

    lines = jnp.concatenate(
        [
            jnp.swapaxes(gate_top, 1, 2).reshape(2 * DOM, width),
            jnp.swapaxes(gate_shared, 1, 2).reshape(S * DOM, width),
            jnp.swapaxes(gate_domain, 1, 2).reshape(K * DOM, width),
            out_bias,
            ln_gain,
            ln_shift,
            proj_b[None],
            in_bias[:, :width],
            in_bias[:, width:],
            jnp.concatenate([tower_b, tower_out], axis=1),
            jnp.zeros((31, width), bf16),
        ]
    )
    lines, _ = step(lines, other)
    pack = jnp.concatenate(
        [proj_w.T, jnp.swapaxes(tower_w, 0, 1).reshape(width, DOM * TW), lines.T], axis=1
    )
    event_rows = jnp.concatenate(
        [domain.astype(f32).T, labels.astype(f32)[None], jnp.zeros((6, rows), f32)]
    )

    other_in = box.send(other, flip=1)
    rows_in = box.to_partner(event_rows, True)
    pack = in_order(role, pack, box.send(pack, flip=1), 0)
    own, other_in, rows_in, pack, embeds = step(own, other_in, rows_in, pack, embeds)

    first = in_order(role, own[:, :3], other_in[:, :3], 2)
    first_z = box.pieces(first, "z")
    pack = jnp.concatenate([pack] + box.pieces(pack, "z"))
    embeds_in = [box.to_partner(embeds[:half_rows], True)]
    event_rows = jnp.where(at_home, event_rows, rows_in)
    ids = event_rows[0]
    onehot = (ids[None, :] == jnp.arange(DOM, dtype=f32)[:, None]).astype(f32)
    rank = jnp.cumsum(onehot, axis=1)
    counts = rank[:, -1]
    ends = jnp.cumsum(counts)
    starts = ends - counts
    position = jnp.sum(onehot * (rank + starts[:, None]), axis=0) - 1.0
    second = in_order(role, own[:, 3:], other_in[:, 3:], 2)
    first, first_z, pack, second, position, starts, ends, embeds_in, embeds = step(
        first, first_z, pack, second, position, starts, ends, embeds_in, embeds
    )

    def along_z(block, found):
        found = [block] + found
        return jnp.stack([b[0] for b in found], axis=1), jnp.stack([b[1] for b in found], axis=1)

    first_i, first_o = along_z(first, first_z)
    first_iy, first_ox = box.pieces(first_i, "y"), box.pieces(first_o, "x")
    second_z = box.pieces(second, "z")
    pack = jnp.concatenate(box.gather_plane(pack), axis=0).reshape(places, 1, width, PACK)
    embeds_in.append(box.to_partner(embeds[half_rows:], True))
    embeds = jnp.where(at_home, embeds, jnp.concatenate(embeds_in))
    first_i, first_o, first_iy, first_ox, second, second_z, pack, embeds = step(
        first_i, first_o, first_iy, first_ox, second, second_z, pack, embeds
    )

    small = in_order(core, pack, swap_cores(pack), 1).reshape(D, PACK)
    first_i = jnp.stack([first_i] + first_iy, axis=1)
    first_o = jnp.stack([first_o] + first_ox, axis=1)
    first_ix, first_oy = box.pieces(first_i, "x"), box.pieces(first_o, "y")
    second_i, second_o = along_z(second, second_z)
    second_iy, second_ox = box.pieces(second_i, "y"), box.pieces(second_o, "x")

    proj_t = small[:, :e_in]
    tower = small[:, e_in : e_in + DOM * TW]
    gates = small[:, e_in + DOM * TW :]
    picked = jnp.concatenate(
        [
            32 + set_own,
            44 + set_own,
            56 + set_own,
            jnp.array([68] + [128] * 5),
            69 + set_own,
            81 + set_own,
            93 + jnp.arange(4),
        ]
    )
    choose = (picked[:, None] == jnp.arange(128)[None, :]).astype(bf16)
    vec = nt(choose, gates)
    blocks = jnp.take(vec[24:].reshape(16, places, 2 * width), place_of, axis=1)
    bi = (
        blocks[:12]
        .reshape(2, LOCAL, places, 2, width)
        .transpose(1, 2, 3, 0, 4)
        .reshape(LOCAL, H)
    )
    bi = jnp.pad(bi, ((0, 2), (0, 0)))
    bi = jnp.where(core == 0, bi, jnp.concatenate([bi[:, HALF:], bi[:, :HALF]], axis=1))
    tower_vec = (
        blocks[12:]
        .reshape(DOM, places, 2, 2, width // 2)
        .transpose(3, 0, 1, 2, 4)
        .reshape(2, DOM * TW)
    )
    tower_vec = jnp.pad(tower_vec, ((0, 6), (0, 0)))

    table = jnp.concatenate([position[None], event_rows[1:]])
    start_i, end_i = starts.astype(jnp.int32), ends.astype(jnp.int32)
    empty = end_i == start_i
    low = jnp.where(empty, 0, start_i // TILE)
    high = jnp.where(empty, 0, (end_i + TILE - 1) // TILE)
    domains = jnp.arange(DOM, dtype=jnp.int32)
    ints = jnp.concatenate(
        [
            jnp.where(role == 0, low[::-1], low),
            jnp.where(role == 0, high[::-1], high),
            role[None],
            jnp.where(role == 0, DOM - 1 - domains, domains),
            start_i,
            end_i,
            core[None],
            jnp.zeros((2,), jnp.int32),
        ]
    )
    loss_weight = 1.0 - (1.0 - FROZEN_SHARE) * frozen.astype(f32)
    floats = jnp.concatenate([loss_weight, tower_out_b.astype(f32)])
    events, x, mix, cols, probs = call_prepare(ints, floats, table, embeds, proj_t, gates, vec)
    (
        first_i, first_o, first_ix, first_oy, second_i, second_o, second_iy, second_ox,
        events, x, mix, cols, probs, vec, bi, tower, tower_vec,
    ) = step(
        first_i, first_o, first_ix, first_oy, second_i, second_o, second_iy, second_ox,
        events, x, mix, cols, probs, vec, bi, tower, tower_vec,
    )

    def full(i, ix, o, oy):
        count = i.shape[0]
        wi = jnp.stack([i] + ix, axis=1).reshape(count, D, HALF)
        wo = jnp.stack([o] + oy, axis=2).reshape(count, D, HALF)
        return (wi, swap_cores(wi), wo, swap_cores(wo))

    norms = {}
    first_w = full(first_i, first_ix, first_o, first_oy)
    second_i = jnp.stack([second_i] + second_iy, axis=1)
    second_o = jnp.stack([second_o] + second_ox, axis=1)
    second_ix, second_oy = box.pieces(second_i, "x"), box.pieces(second_o, "y")
    for expert in range(3):
        cols, mix, norms[expert] = call_forward(expert, expert, ints, x, first_w, bi, vec, cols, mix)
    second_i, second_o, second_ix, second_oy, cols, mix = step(
        second_i, second_o, second_ix, second_oy, cols, mix
    )
    second_w = full(second_i, second_ix, second_o, second_oy)
    for expert in (3, 4):
        cols, mix, norms[expert] = call_forward(
            expert, expert - 3, ints, x, second_w, bi, vec, cols, mix
        )
    give_mix = half(mix, 1 - role).astype(bf16)
    give_mix, mix = step(give_mix, mix)
    other_mix = box.send(give_mix, flip=1)
    cols, mix, norms[5] = call_forward(5, 2, ints, x, second_w, bi, vec, cols, mix)
    row_out, grad_block, grad_low, d_tower, d_tower_vec = call_tower(
        ints, mix, other_mix, cols, tower, tower_vec
    )

    d_vec, d_bias, keep, give = {}, {}, {}, {}
    box_shape = (nx, ny, nz, 2, 2 * width, HALF)

    def backward(expert, grad, cols, back):
        pair, place = (first_w, expert) if expert < 3 else (second_w, expert - 3)
        cols, back, keep[expert], give[expert], d_vec[expert], d_bias[expert] = call_backward(
            expert, place, ints, x, grad, norms[expert], pair, bi, vec, cols, back
        )
        return cols, back

    def both_cores(experts):
        def one(which):
            return jnp.stack(
                [
                    total(keep[e][which], [give[e][which]]).astype(bf16).reshape(box_shape)
                    for e in experts
                ]
            )

        return one(0), one(1)

    class Scatter:
        def __init__(self, experts):
            self.experts = experts
            self.i, self.o = both_cores(experts)
            self.i = [self.i[:, k] for k in range(nx)]
            self.o = [self.o[:, :, k] for k in range(ny)]
            self.state = (
                self.i[0], self.o[0], box.hand_out(self.i, "x"), box.hand_out(self.o, "y")
            )

        def second(self):
            i, o, i_in, o_in = self.state
            i, o = total(i, i_in).astype(bf16), total(o, o_in).astype(bf16)
            i, o = [i[:, k] for k in range(ny)], [o[:, k] for k in range(nx)]
            self.state = (i[0], o[0], box.hand_out(i, "y"), box.hand_out(o, "x"))

        def third(self):
            i, o, i_in, o_in = self.state
            both = jnp.stack([total(i, i_in).astype(bf16), total(o, o_in).astype(bf16)])
            both = [both[:, :, k] for k in range(nz)]
            self.state = (both[0], box.hand_out(both, "z"))

        def fourth(self):
            both = total(*self.state)
            mine = lax.dynamic_index_in_dim(both, role, 2, keepdims=False)
            other = lax.dynamic_index_in_dim(both, 1 - role, 2, keepdims=False).astype(bf16)
            self.state = (mine, box.send(other, flip=1))

    def sync(scatters, *values):
        states, values = step([c.state for c in scatters], values)
        for c, state in zip(scatters, states):
            c.state = state
        return values

    back = jnp.zeros((rows, D), f32)
    grad_in = box.send(grad_low, flip=1)
    cols, back = backward(5, grad_low, cols, back)
    grad_in, cols, back, keep[5], give[5] = step(grad_in, cols, back, keep[5], give[5])
    grad_all = in_order(role, grad_low, grad_in, 0)
    give[5] = swap_cores(give[5])
    cols, back = backward(0, grad_all, cols, back)
    cols, back, keep[5], give[5], keep[0], give[0] = step(
        cols, back, keep[5], give[5], keep[0], give[0]
    )
    give[0] = swap_cores(give[0])
    cols, back = backward(4, grad_all, cols, back)
    cols, back, keep[0], give[0], keep[4], give[4] = step(
        cols, back, keep[0], give[0], keep[4], give[4]
    )
    c0 = Scatter(CHUNKS[0])
    give[4] = swap_cores(give[4])
    cols, back = backward(1, grad_all, cols, back)
    cols, back, keep[4], give[4], keep[1], give[1] = sync(
        [c0], cols, back, keep[4], give[4], keep[1], give[1]
    )
    c0.second()
    give[1] = swap_cores(give[1])
    cols, back = backward(3, grad_all, cols, back)
    cols, back, keep[1], give[1], keep[3], give[3] = sync(
        [c0], cols, back, keep[1], give[1], keep[3], give[3]
    )
    c0.third()
    c1 = Scatter(CHUNKS[1])
    give[3] = swap_cores(give[3])
    cols, back = backward(2, grad_all, cols, back)
    cols, back, keep[3], give[3], keep[2], give[2], d_vec, d_bias, row_out = sync(
        [c0, c1], cols, back, keep[3], give[3], keep[2], give[2], d_vec, d_bias, row_out
    )
    back_in = box.send(half(back, 1 - role).astype(bf16), flip=1)
    coef_t = half(cols, 1 - role)[:, DCOEF : DCOEF + 8].T
    coef_in = box.send(coef_t, flip=1)
    c0.fourth()
    c1.second()
    give[2] = swap_cores(give[2])
    d_lines = call_lines(ints, row_out, d_tower_vec, [d_bias[e] for e in range(LOCAL)])
    d_lines = d_lines + swap_cores(d_lines)
    back, back_in, coef_in, keep[2], give[2], d_lines = sync(
        [c0, c1], back, back_in, coef_in, keep[2], give[2], d_lines
    )
    c1.third()
    c2 = Scatter(CHUNKS[2])
    d_lines = box.same_sum(d_lines, "flip")
    grad_events, d_small = call_finish(
        ints, grad_block, back, back_in, cols, coef_in, probs, x, events, gates, proj_t, d_tower,
        [d_vec[e] for e in range(LOCAL)],
    )
    grad_events, d_small, d_lines = sync([c1, c2], grad_events, d_small, d_lines)
    c1.fourth()
    c2.second()
    d_small = d_small.reshape(places, 2, width, PACK)
    d_other = swap_cores(lax.dynamic_index_in_dim(d_small, 1 - core, 1, keepdims=False))
    events_in = box.to_partner(grad_events, False)
    rows_in = box.to_partner(row_out, False)
    d_lines = box.same_sum(d_lines, "z")
    d_small, d_other, grad_events, events_in, row_out, rows_in, d_lines = sync(
        [c1, c2], d_small, d_other, grad_events, events_in, row_out, rows_in, d_lines
    )
    c2.third()
    d_mine = total(lax.dynamic_index_in_dim(d_small, core, 1, keepdims=False), [d_other])
    d_mine = d_mine.astype(bf16).reshape(nx * ny, nz, 2, width, PACK)
    d_parts = [d_mine[k] for k in range(nx * ny)]
    d_in = box.hand_out_plane(d_parts)
    d_lines = box.same_sum(d_lines, "y")
    grad_events = in_order(role, grad_events, events_in, 0)
    order = position[None, :] == jnp.arange(rows, dtype=f32)[:, None]
    grad_embeds = lax.dot_general(
        order.astype(bf16), grad_events, (((0,), (0,)), ((), ())), preferred_element_type=f32
    ).astype(bf16)
    predicted = in_order(role, row_out, rows_in, 1)
    predictions = jnp.sum(jnp.where(order, predicted[0][:, None], 0.0), axis=0)
    predictions = jnp.broadcast_to(predictions[None], (8, rows))
    d_mine, d_in, grad_embeds, predictions, d_lines = sync(
        [c2], d_parts[0], d_in, grad_embeds, predictions, d_lines
    )
    c2.fourth()
    d_mine = total(d_mine, d_in).astype(bf16)
    same = [lax.dynamic_index_in_dim(d_mine[k], role, 0, keepdims=False) for k in range(nz)]
    flip = [lax.dynamic_index_in_dim(d_mine[k], 1 - role, 0, keepdims=False) for k in range(nz)]
    d_in = box.hand_out(same, "z") + [box.send(f, flip=1, z=k) for k, f in enumerate(flip)]
    d_lines = box.same_sum(d_lines, "x")
    grad_embeds = jnp.where(at_home, grad_embeds, swap_cores(grad_embeds))
    predictions = jnp.where(at_home, predictions, swap_cores(predictions))[0]

    scatters = (c0, c1, c2)
    grad_w_in, grad_w_out = call_place(
        ints, [c.state[0] for c in scatters], [c.state[1] for c in scatters]
    )
    proj_grad, grad_tower_w, columns = call_small([same[0]] + d_in)
    columns = columns.T
    grad_gates = [
        jnp.swapaxes(columns[low : low + DOM * size].reshape(DOM, size, width), 1, 2)
        for low, size in ((0, 2), (2 * DOM, S), ((2 + S) * DOM, K))
    ]
    found = {j: 18 * r + 3 * i for r, row in enumerate(SETS) for i, j in enumerate(row)}
    experts = range(2 * LOCAL)

    def vectors(which):
        return jnp.stack([columns[32 + found[j] + which] for j in experts])

    device = 2 * lax.axis_index("dp") + core
    d_bias_rows = {j: 12 * r + i for r, row in enumerate(SETS) for i, j in enumerate(row)}
    in_bias_grad = jnp.stack(
        [jnp.concatenate([d_lines[d_bias_rows[j]], d_lines[d_bias_rows[j] + 6]]) for j in experts]
    )
    in_bias_grad = lax.dynamic_slice_in_dim(in_bias_grad, device * 2 * width, 2 * width, 1)
    d_tv = jnp.concatenate([d_lines[24:26], d_lines[26:28]], axis=1).reshape(2, DOM, TW)
    d_tv = lax.dynamic_slice_in_dim(d_tv, device * (width // 2), width // 2, 2)
    return (
        predictions,
        grad_embeds,
        proj_grad.T,
        columns[68],
        grad_w_in,
        in_bias_grad,
        jnp.swapaxes(grad_w_out, 1, 2),
        vectors(0),
        vectors(1),
        vectors(2),
        *grad_gates,
        grad_tower_w,
        d_tv[0],
        d_tv[1],
        d_lines[28, :DOM],
    )


def solution(mesh):
    both = ("dp", "tensor")
    in_specs = (
        P("dp", None),
        P("dp", None),
        P(),
        P("dp"),
        P(None, both),
        P(both),
        P(None, "dp", "tensor"),
        P(None, both),
        P(None, "tensor", "dp"),
        P(None, both),
        P(None, both),
        P(None, both),
        P(None, both, None),
        P(None, both, None),
        P(None, both, None),
        P(None, both, None),
        P(None, both),
        P(None, both),
        P(),
    )
    out_specs = (
        P("dp"),
        P("dp", None),
        P(None, both),
        P(both),
        P(None, "dp", "tensor"),
        P(None, both),
        P(None, "tensor", "dp"),
        P(None, both),
        P(None, both),
        P(None, both),
        P(None, both, None),
        P(None, both, None),
        P(None, both, None),
        P(None, both, None),
        P(None, both),
        P(None, both),
        P(),
    )
    return jax.shard_map(
        functools.partial(per_device, Box(mesh.shape["dp"])),
        mesh=mesh,
        in_specs=in_specs,
        out_specs=out_specs,
        check_vma=False,
    )
```

time: 707 us -> 453 us (0.64)
  local copies, waits for them, and re-layouts: 169 us -> 67.7 us
  waiting for transfers between devices: 180 us -> 82 us
  other arithmetic: 99.8 us -> 48.5 us
  Pallas kernels: 131 us -> 148 us
  matrix products: 23.3 us -> 6.72 us
    ppermute x71 -> x53, waiting for transfers between devices: 180 us -> 75.9 us  [the longest x48 73 us: send(): return lax.ppermute(values, 'dp', pairs)]
    slice x67 -> x29, local copies, waits for them, and re-layouts: 50 us -> 8.29 us  [the longest x5 2.14 us: per_device(): columns[low:low + DOM * size].reshape(DOM, size, width)]
    dot_general x8 -> x2, matrix products: 23.3 us -> 6.72 us  [the longest x1 6.54 us: per_device(): lax.dot_general(order.astype(bf16), grad_events, (((0,), (0,)), ((), ()))...]
    pallas_call x9 -> x19, Pallas kernels: 131 us -> 148 us  [the longest x6 71.1 us: call_backward(): pl.pallas_call(functools.partial(backward_kernel, expert), grid_spec=pltp...]
    concatenate x14 -> x5, local copies, waits for them, and re-layouts: 14.9 us -> 0.95 us  [the longest x1 0.6 us: per_device(): jnp.concatenate([32 + set_own, 44 + set_own, 56 + set_own, jnp.array([68]...]
    add x9 -> x10, other arithmetic: 15.6 us -> 1.86 us  [the longest x3 1.16 us: total(): functools.reduce(jnp.add, [a.astype(f32) for a in arrived], first.astype(...]
    another operation x37 -> x12, local copies, waits for them, and re-layouts: 16.1 us -> 5.09 us  [the longest x2 1.64 us: full(): wi = jnp.stack([i] + ix, axis=1).reshape(count, D, HALF)]
    squeeze x26 -> x14, local copies, waits for them, and re-layouts: 13.8 us -> 4.09 us  [the longest x6 1.74 us: second(): i, o = ([i[:, k] for k in range(ny)], [o[:, k] for k in range(nx)])]
  transfers between devices with their start and end apart: 82 -> 68, of which waited for: 28 -> 21; matrix products, arithmetic and copies ran while one was open for 32% -> 18% of each run, Pallas kernels for 5% -> 28%
where the time goes in v1:
time: 453 us; the launch traced here: 448 us
  Pallas kernels  148 us (33%)
  starting transfers between devices  92.8 us (20%)
  waiting for transfers between devices  82 us (18%)
  local copies, waits for them, and re-layouts  67.7 us (15%)
  other arithmetic  48.5 us (11%)
  matrix products  6.72 us (1%)
    ppermute x48, waiting for transfers between devices, send(): return lax.ppermute(values, 'dp', pairs)  73 us
    ppermute x48, starting transfers between devices, send(): return lax.ppermute(values, 'dp', pairs)  72.9 us
    pallas_call x6, Pallas kernels, call_backward(): pl.pallas_call(functools.partial(backward_kernel, expert), grid_spec=pltp...  71.1 us
    pallas_call x6, Pallas kernels, call_forward(): pl.pallas_call(functools.partial(forward_kernel, expert), grid_spec=pltpu...  43.4 us
    unnamed x165, local copies, waits for them, and re-layouts  32.2 us
    ppermute x5, starting transfers between devices, to_partner(): return lax.ppermute(values, ('dp', 'tensor'), pairs)  17.7 us
    pallas_call x1, Pallas kernels, call_prepare(): pl.pallas_call(prepare_kernel, grid_spec=pltpu.PrefetchScalarGridSpec(num...  12.5 us
    pallas_call x1, Pallas kernels, call_tower(): pl.pallas_call(tower_kernel, grid_spec=pltpu.PrefetchScalarGridSpec(num_s...  9.19 us
  transfers between devices with their start and end apart: 68, of which 21 were waited for; matrix products, arithmetic and copies ran while one was open for 18% of the time, Pallas kernels for 28%

profile of v1, /device:TPU:0, one launch (start us, length us, event | category | flops | bytes accessed | tf_op | source)
XLA Modules:
  0.0 447.9 jit_solution(3639029402527903147)
XLA Ops:
  2.3 4.9 %collective-permute-start.1 = (f32[8,1536]{1,0:T(8,128)S(1)}, f32[8,1536]{1,0:T(8,128)S(1)}, u32[]{:S(2)}, u32[]{:S(2)}) collective-permute-start(f32[8,1536]{1,0:T(8,128)S(1)} %maximum_maximum_fusion), channel_id=1, source_target_pairs={{0,8},{2,10},{4,12},{6,14},{9,1},{11,3},{13,5},{15,7},{16,24},{18,... | collective-permute-start | bytes 147464 | tf_op jit(solution)/shard_map/ppermute | solution.py:74
  27.5 5.4 %collective-permute-start.5 = (bf16[768,640]{1,0:T(8,128)(2,1)}, bf16[768,640]{1,0:T(8,128)(2,1)}, u32[]{:S(2)}, u32[]{:S(2)}) collective-permute-start(bf16[768,640]{1,0:T(8,128)(2,1)} %slice.499), channel_id=1, source_target_pairs={{0,8},{2,10},{4,12},{6,14},{9,1},{11,3},{13,5},{15,7},{16,24},{18,... | collective-permute-start | bytes 2949128 | tf_op jit(solution)/shard_map/ppermute | solution.py:74
  36.8 15.8 %collective-permute-done.4 = bf16[32,1792]{1,0:T(8,128)(2,1)S(1)} collective-permute-done((bf16[32,1792]{1,0:T(8,128)(2,1)}, bf16[32,1792]{1,0:T(8,128)(2,1)S(1)}, u32[]{:S(2)}, u32[]{:S(2)}) %collective-permute-start.4) | collective-permute-done | bytes 114720 | tf_op jit(solution)/shard_map/ppermute | solution.py:66
  97.5 12.5 %prepare.1 = (bf16[1536,640]{1,0:T(8,128)(2,1)S(1)}, bf16[1536,512]{1,0:T(8,128)(2,1)S(1)}, f32[1536,512]{1,0:T(8,128)}, f32[1536,128]{1,0:T(8,128)S(1)}, f32[8,1536]{1,0:T(8,128)S(1)}) custom-call(s32[24]{0:T(128)S(1)} %concatenate.128.ints, f32[8]{0:T(128)S(1)} %pad_maximum_fusion.41.floats, f32[8,1536]{1,0:T(8,128)S(1)} %pad_maximum_fusion.24.rows_ref, ...), custom_call_target="tpu_custom_call" | custom-call | flops 4026531840 | bytes 12000000 | tf_op jit(solution)/shard_map/prepare/pallas_call | solution.py:627
  128.0 10.1 %expert_forward.6 = (f32[1536,128]{1,0:T(8,128)S(1)}, f32[1536,512]{1,0:T(8,128)}, bf16[1536,512]{1,0:T(8,128)(2,1)S(1)}) custom-call(s32[24]{0:T(128)S(1)} %concatenate.128.ints, bf16[1536,512]{1,0:T(8,128)(2,1)S(1)} %get-tuple-element.273.x_ref, bf16[3,512,512]{2,1,0:T(8,128)(2,1)S(1)} %bitcast.274, ...), custom_call_target="tpu_custom_call", output_to_operand_aliasing={{0}: (8, {}), {1}: (9, {})} | custom-call | flops 3221225472 | bytes 12000000 | tf_op jit(solution)/shard_map/expert_forward/pallas_call | solution.py:669
  139.3 10.1 %expert_forward.7 = (f32[1536,128]{1,0:T(8,128)S(1)}, f32[1536,512]{1,0:T(8,128)}, bf16[1536,512]{1,0:T(8,128)(2,1)S(1)}) custom-call(s32[24]{0:T(128)S(1)} %concatenate.128.ints, bf16[1536,512]{1,0:T(8,128)(2,1)S(1)} %get-tuple-element.273.x_ref, bf16[3,512,512]{2,1,0:T(8,128)(2,1)S(1)} %bitcast.275, ...), custom_call_target="tpu_custom_call", output_to_operand_aliasing={{0}: (8, {}), {1}: (9, {})} | custom-call | flops 3221225472 | bytes 12000000 | tf_op jit(solution)/shard_map/expert_forward/pallas_call | solution.py:669
  164.3 5.6 %expert_forward.9 = (f32[1536,128]{1,0:T(8,128)S(1)}, f32[1536,512]{1,0:T(8,128)}, bf16[1536,512]{1,0:T(8,128)(2,1)S(1)}) custom-call(s32[24]{0:T(128)S(1)} %concatenate.128.ints, bf16[1536,512]{1,0:T(8,128)(2,1)S(1)} %get-tuple-element.273.x_ref, bf16[3,512,512]{2,1,0:T(8,128)(2,1)} %bitcast.51.wi_a, ...), custom_call_target="tpu_custom_call", output_to_operand_aliasing={{0}: (8, {}), {1}: (9, {})} | custom-call | flops 2147483648 | bytes 12000000 | tf_op jit(solution)/shard_map/expert_forward/pallas_call | solution.py:669
  171.0 7.9 %expert_forward.10 = (f32[1536,128]{1,0:T(8,128)S(1)}, f32[1536,512]{1,0:T(8,128)}, bf16[1536,512]{1,0:T(8,128)(2,1)S(1)}) custom-call(s32[24]{0:T(128)S(1)} %concatenate.128.ints, bf16[1536,512]{1,0:T(8,128)(2,1)S(1)} %get-tuple-element.273.x_ref, bf16[3,512,512]{2,1,0:T(8,128)(2,1)} %bitcast.51.wi_a, ...), custom_call_target="tpu_custom_call", output_to_operand_aliasing={{0}: (8, {}), {1}: (9, {})} | custom-call | flops 2147483648 | bytes 12000000 | tf_op jit(solution)/shard_map/expert_forward/pallas_call | solution.py:669
  181.8 5.6 %expert_forward.11 = (f32[1536,128]{1,0:T(8,128)S(1)}, f32[1536,512]{1,0:T(8,128)}, bf16[1536,512]{1,0:T(8,128)(2,1)S(1)}) custom-call(s32[24]{0:T(128)S(1)} %concatenate.128.ints, bf16[1536,512]{1,0:T(8,128)(2,1)S(1)} %get-tuple-element.273.x_ref, bf16[3,512,512]{2,1,0:T(8,128)(2,1)} %bitcast.51.wi_a, ...), custom_call_target="tpu_custom_call", output_to_operand_aliasing={{0}: (8, {}), {1}: (9, {})} | custom-call | flops 2147483648 | bytes 12000000 | tf_op jit(solution)/shard_map/expert_forward/pallas_call | solution.py:669
  188.5 11.2 %collective-permute-done.24.other_ref = bf16[768,512]{1,0:T(8,128)(2,1)S(1)} collective-permute-done((bf16[768,512]{1,0:T(8,128)(2,1)S(1)}, bf16[768,512]{1,0:T(8,128)(2,1)S(1)}, u32[]{:S(2)}, u32[]{:S(2)}) %collective-permute-start.24) | collective-permute-done | bytes 786464 | tf_op jit(solution)/shard_map/ppermute | solution.py:66
  199.8 9.2 %towers.1 = (f32[8,768]{1,0:T(8,128)S(1)}, f32[768,512]{1,0:T(8,128)S(1)}, bf16[768,512]{1,0:T(8,128)(2,1)S(1)}, f32[512,1024]{1,0:T(8,128)}, f32[8,1024]{1,0:T(8,128)S(1)}) custom-call(s32[24]{0:T(128)S(1)} %concatenate.128.ints, f32[1536,512]{1,0:T(8,128)} %get-tuple-element.303.mix_ref, bf16[768,512]{1,0:T(8,128)(2,1)S(1)} %collective-permute-done.24.other_ref, ...), custom_call_target="tpu_custom_call" | custom-call | flops 2415919104 | bytes 10000000 | tf_op jit(solution)/shard_map/towers/pallas_call | solution.py:750
  212.7 8.5 %expert_backward.6 = (f32[1536,128]{1,0:T(8,128)S(1)}, f32[1536,512]{1,0:T(8,128)}, bf16[2,512,512]{2,1,0:T(8,128)(2,1)S(1)}, bf16[2,512,512]{2,1,0:T(8,128)(2,1...) custom-call(s32[24]{0:T(128)S(1)} %concatenate.128.ints, ...), custom_call_target="tpu_custom_call", output_to_operand_aliasing={{0}: (10, {}), {1}: (11, {})} | custom-call | flops 5368709120 | bytes 20000000 | tf_op jit(solution)/shard_map/expert_backward/pallas_call | solution.py:705
  222.2 5.7 %collective-permute-done.25 = bf16[768,512]{1,0:T(8,128)(2,1)S(1)} collective-permute-done((bf16[768,512]{1,0:T(8,128)(2,1)S(1)}, bf16[768,512]{1,0:T(8,128)(2,1)S(1)}, u32[]{:S(2)}, u32[]{:S(2)}) %collective-permute-start.25) | collective-permute-done | bytes 786464 | tf_op jit(solution)/shard_map/ppermute | solution.py:66
  228.5 17.6 %expert_backward.7 = (f32[1536,128]{1,0:T(8,128)S(1)}, f32[1536,512]{1,0:T(8,128)}, bf16[2,512,512]{2,1,0:T(8,128)(2,1)S(1)}, bf16[2,512,512]{2,1,0:T(8,128)(2,1...) custom-call(s32[24]{0:T(128)S(1)} %concatenate.128.ints, ...), custom_call_target="tpu_custom_call", output_to_operand_aliasing={{0}: (10, {}), {1}: (11, {})} | custom-call | flops 8053063680 | bytes 20000000 | tf_op jit(solution)/shard_map/expert_backward/pallas_call | solution.py:705
  250.7 12.8 %expert_backward.8 = (f32[1536,128]{1,0:T(8,128)S(1)}, f32[1536,512]{1,0:T(8,128)}, bf16[2,512,512]{2,1,0:T(8,128)(2,1)S(1)}, bf16[2,512,512]{2,1,0:T(8,128)(2,1...) custom-call(s32[24]{0:T(128)S(1)} %concatenate.128.ints, ...), custom_call_target="tpu_custom_call", output_to_operand_aliasing={{0}: (10, {}), {1}: (11, {})} | custom-call | flops 5368709120 | bytes 20000000 | tf_op jit(solution)/shard_map/expert_backward/pallas_call | solution.py:705
  269.7 17.4 %expert_backward.9 = (f32[1536,128]{1,0:T(8,128)S(1)}, f32[1536,512]{1,0:T(8,128)}, bf16[2,512,512]{2,1,0:T(8,128)(2,1)S(1)}, bf16[2,512,512]{2,1,0:T(8,128)(2,1...) custom-call(s32[24]{0:T(128)S(1)} %concatenate.128.ints, ...), custom_call_target="tpu_custom_call", output_to_operand_aliasing={{0}: (10, {}), {1}: (11, {})} | custom-call | flops 8053063680 | bytes 20000000 | tf_op jit(solution)/shard_map/expert_backward/pallas_call | solution.py:705
  289.9 8.4 %expert_backward.10 = (f32[1536,128]{1,0:T(8,128)S(1)}, f32[1536,512]{1,0:T(8,128)}, bf16[2,512,512]{2,1,0:T(8,128)(2,1)S(1)}, bf16[2,512,512]{2,1,0:T(8,128)(2,...) custom-call(s32[24]{0:T(128)S(1)} %concatenate.128.ints, ...), custom_call_target="tpu_custom_call", output_to_operand_aliasing={{0}: (10, {}), {1}: (11, {})} | custom-call | flops 5368709120 | bytes 20000000 | tf_op jit(solution)/shard_map/expert_backward/pallas_call | solution.py:705
  302.6 7.6 %collective-permute-start.34 = (bf16[2,2,2,32,512]{4,3,1,0,2:T(8,128)(2,1)S(1)}, bf16[2,2,2,32,512]{4,3,1,0,2:T(8,128)(2,1)S(1)}, u32[]{:S(2)}, u32[]{:S(2)}) collective-permute-start(bf16[2,2,2,32,512]{4,3,1,0,2:T(8,128)(2,1)S(1)} %get-tuple-element.597), channel_id=1, source_target_pairs={{0,16},{2,18},{4,20},{6,22},{8,24},{10,26},{12,28},{14,30},{16,0},... | collective-permute-start | bytes 786440 | tf_op jit(solution)/shard_map/ppermute | solution.py:66
  311.0 6.4 %expert_backward.11 = (f32[1536,128]{1,0:T(8,128)S(1)}, f32[1536,512]{1,0:T(8,128)}, bf16[2,512,512]{2,1,0:T(8,128)(2,1)S(1)}, bf16[2,512,512]{2,1,0:T(8,128)(2,...) custom-call(s32[24]{0:T(128)S(1)} %concatenate.128.ints, ...), custom_call_target="tpu_custom_call", output_to_operand_aliasing={{0}: (10, {}), {1}: (11, {})} | custom-call | flops 5368709120 | bytes 20000000 | tf_op jit(solution)/shard_map/expert_backward/pallas_call | solution.py:705
  336.7 5.6 %collective-permute-done.39 = bf16[2,2,2,32,512]{4,3,0,2,1:T(8,128)(2,1)S(1)} collective-permute-done((bf16[2,2,2,32,512]{4,3,0,2,1:T(8,128)(2,1)S(1)}, bf16[2,2,2,32,512]{4,3,0,2,1:T(8,128)(2,1)S(1)}, u32[]{:S(2)}, u32[]{:S(2)}) %collective-permute-start.39) | collective-permute-done | bytes 262176 | tf_op jit(solution)/shard_map/ppermute | solution.py:66
  343.8 6.3 %collective-permute-done.41.other_ref = bf16[768,512]{1,0:T(8,128)(2,1)S(1)} collective-permute-done((bf16[768,512]{1,0:T(8,128)(2,1)}, bf16[768,512]{1,0:T(8,128)(2,1)S(1)}, u32[]{:S(2)}, u32[]{:S(2)}) %collective-permute-start.41) | collective-permute-done | bytes 786464 | tf_op jit(solution)/shard_map/ppermute | solution.py:66
  371.1 7.5 %finish.1 = (bf16[768,640]{1,0:T(8,128)(2,1)}, bf16[512,1792]{1,0:T(8,128)(2,1)}) custom-call(s32[24]{0:T(128)S(1)} %concatenate.128.ints, f32[768,512]{1,0:T(8,128)S(1)} %copy-done.8, f32[1536,512]{1,0:T(8,128)} %get-tuple-element.416.back_ref, bf16[768,512]{1,0:T(8,128)(2,1)S(1)} %copy-done.18, f32[1536,128]{1,0:T(8,128)S(1)} %get-tuple-element.396.cols_ref, ...), custom_call_target="tpu_custom_call" | custom-call | flops 1207959552 | bytes 10000000 | tf_op jit(solution)/shard_map/finish/pallas_call | solution.py:500
  393.9 6.6 %collective-permute-start.49 = (bf16[2,2,32,512]{3,2,1,0:T(8,128)(2,1)}, bf16[2,2,32,512]{3,2,1,0:T(8,128)(2,1)S(1)}, u32[]{:S(2)}, u32[]{:S(2)}) collective-permute-start(bf16[2,2,32,512]{3,2,1,0:T(8,128)(2,1)} %fusion.38), channel_id=1, source_target_pairs={{0,8},{2,10},{4,12},{6,14},{8,0},{10,2},{12,4},{14,6},{16,24},{18,... | collective-permute-start | bytes 393224 | tf_op jit(solution)/shard_map/ppermute | solution.py:66
  412.6 6.5 %fusion.2 = bf16[1536,640]{1,0:T(8,128)(2,1)S(1)} fusion(f32[1536]{0:T(1024)S(1)} %add_bitcast_fusion.1, bf16[768,640]{1,0:T(8,128)(2,1)} %collective-permute-done.53, bf16[768,640]{1,0:T(8,128)(2,1)} %get-tuple-element.446, pred[]{:T(512)S(6)} %eq.79), kind=kOutput, calls=%fused_computation.5 | convolution fusion | flops 3032088576 | bytes 3938305 | tf_op jit(solution)/shard_map/dot_general | solution.py:1102
  (495 shorter events, 230.1 us)
Async XLA Ops:
  2.3 21.9 %collective-permute-start.1 = (f32[8,1536]{1,0:T(8,128)S(1)}, f32[8,1536]{1,0:T(8,128)S(1)}, u32[]{:S(2)}, u32[]{:S(2)}) collective-permute-start(f32[8,1536]{1,0:T(8,128)S(1)} %maximum_maximum_fusion), channel_id=1, source_target_pairs={{0,8},{2,10},{4,12},{6,14},{9,1},{11,3},{13,5},{15,7},{16,24},{18,... | collective-permute-start | bytes 147464 | tf_op jit(solution)/shard_map/ppermute | solution.py:74
  27.5 26.0 %collective-permute-start.5 = (bf16[768,640]{1,0:T(8,128)(2,1)}, bf16[768,640]{1,0:T(8,128)(2,1)}, u32[]{:S(2)}, u32[]{:S(2)}) collective-permute-start(bf16[768,640]{1,0:T(8,128)(2,1)} %slice.499), channel_id=1, source_target_pairs={{0,8},{2,10},{4,12},{6,14},{9,1},{11,3},{13,5},{15,7},{16,24},{18,... | collective-permute-start | bytes 2949128 | tf_op jit(solution)/shard_map/ppermute | solution.py:74
  33.3 20.2 %collective-permute-start.3 = (bf16[2,3,64,512]{3,2,1,0:T(8,128)(2,1)S(1)}, bf16[2,3,64,512]{3,2,1,0:T(8,128)(2,1)S(1)}, u32[]{:S(2)}, u32[]{:S(2)}) collective-permute-start(bf16[2,3,64,512]{3,2,1,0:T(8,128)(2,1)S(1)} %maximum_select_fusion.5), channel_id=1, source_target_pairs={{0,16},{2,18},{4,20},{6,22},{8,24},{10,26},{12,28},{14,30},{16,0},... | collective-permute-start | bytes 1179656 | tf_op jit(solution)/shard_map/ppermute | solution.py:66
  58.1 20.0 %collective-permute-start.12 = (bf16[768,640]{1,0:T(8,128)(2,1)}, bf16[768,640]{1,0:T(8,128)(2,1)}, u32[]{:S(2)}, u32[]{:S(2)}) collective-permute-start(bf16[768,640]{1,0:T(8,128)(2,1)} %slice.504), channel_id=1, source_target_pairs={{0,8},{2,10},{4,12},{6,14},{9,1},{11,3},{13,5},{15,7},{16,24},{18,... | collective-permute-start | bytes 2949128 | tf_op jit(solution)/shard_map/ppermute | solution.py:74
  86.0 25.3 %collective-permute-start.15 = (bf16[3,2,64,512]{3,2,0,1:T(8,128)(2,1)}, bf16[3,2,64,512]{3,2,0,1:T(8,128)(2,1)}, u32[]{:S(2)}, u32[]{:S(2)}) collective-permute-start(bf16[3,2,64,512]{3,2,0,1:T(8,128)(2,1)} %pad_maximum_fusion.17), channel_id=1, source_target_pairs={{0,4},{2,6},{4,0},{6,2},{8,12},{10,14},{12,8},{14,10},{16,20},{18,... | collective-permute-start | bytes 1179656 | tf_op jit(solution)/shard_map/ppermute | solution.py:66
  88.1 23.2 %collective-permute-start.16 = (bf16[3,2,64,512]{3,2,0,1:T(8,128)(2,1)}, bf16[3,2,64,512]{3,2,0,1:T(8,128)(2,1)}, u32[]{:S(2)}, u32[]{:S(2)}) collective-permute-start(bf16[3,2,64,512]{3,2,0,1:T(8,128)(2,1)} %pad_maximum_fusion.18), channel_id=1, source_target_pairs={{0,2},{2,0},{4,6},{6,4},{8,10},{10,8},{12,14},{14,12},{16,18},{18,... | collective-permute-start | bytes 1179656 | tf_op jit(solution)/shard_map/ppermute | solution.py:66
  90.5 24.2 %collective-permute-start.14 = (bf16[3,2,2,64,512]{4,3,0,2,1:T(8,128)(2,1)}, bf16[3,2,2,64,512]{4,3,0,2,1:T(8,128)(2,1)}, u32[]{:S(2)}, u32[]{:S(2)}) collective-permute-start(bf16[3,2,2,64,512]{4,3,0,2,1:T(8,128)(2,1)} %pad_maximum_fusion.6), channel_id=1, source_target_pairs={{0,4},{2,6},{4,0},{6,2},{8,12},{10,14},{12,8},{14,10},{16,20},{18,... | collective-permute-start | bytes 2359304 | tf_op jit(solution)/shard_map/ppermute | solution.py:66
  93.2 23.3 %collective-permute-start.13 = (bf16[3,2,2,64,512]{4,3,0,2,1:T(8,128)(2,1)}, bf16[3,2,2,64,512]{4,3,0,2,1:T(8,128)(2,1)}, u32[]{:S(2)}, u32[]{:S(2)}) collective-permute-start(bf16[3,2,2,64,512]{4,3,0,2,1:T(8,128)(2,1)} %pad_maximum_fusion.5), channel_id=1, source_target_pairs={{0,2},{2,0},{4,6},{6,4},{8,10},{10,8},{12,14},{14,12},{16,18},{18,... | collective-permute-start | bytes 2359304 | tf_op jit(solution)/shard_map/ppermute | solution.py:66
  122.2 32.7 %collective-permute-start.19 = (bf16[3,2,2,64,512]{4,3,0,2,1:T(8,128)(2,1)S(1)}, bf16[3,2,2,64,512]{4,3,0,2,1:T(8,128)(2,1)S(1)}, u32[]{:S(2)}, u32[]{:S(2)}) collective-permute-start(bf16[3,2,2,64,512]{4,3,0,2,1:T(8,128)(2,1)S(1)} %pad_maximum_fusion.8), channel_id=1, source_target_pairs={{0,4},{2,6},{4,0},{6,2},{8,12},{10,14},{12,8},{14,10},{16,20},{18,... | collective-permute-start | bytes 2359304 | tf_op jit(solution)/shard_map/ppermute | solution.py:66
  124.2 30.7 %collective-permute-start.18 = (bf16[3,2,2,64,512]{4,3,0,2,1:T(8,128)(2,1)S(1)}, bf16[3,2,2,64,512]{4,3,0,2,1:T(8,128)(2,1)S(1)}, u32[]{:S(2)}, u32[]{:S(2)}) collective-permute-start(bf16[3,2,2,64,512]{4,3,0,2,1:T(8,128)(2,1)S(1)} %pad_maximum_fusion.7), channel_id=1, source_target_pairs={{0,2},{2,0},{4,6},{6,4},{8,10},{10,8},{12,14},{14,12},{16,18},{18,... | collective-permute-start | bytes 2359304 | tf_op jit(solution)/shard_map/ppermute | solution.py:66
  263.5 23.7 %collective-permute-start.30 = (bf16[2,512,512]{2,1,0:T(8,128)(2,1)S(1)}, bf16[2,512,512]{2,1,0:T(8,128)(2,1)S(1)}, u32[]{:S(2)}, u32[]{:S(2)}) collective-permute-start(bf16[2,512,512]{2,1,0:T(8,128)(2,1)S(1)} %get-tuple-element.343), channel_id=1, source_target_pairs={{0,1},{1,0},{2,3},{3,2},{4,5},{5,4},{6,7},{7,6},{8,9},{9,8},{10,11... | collective-permute-start | bytes 3145736 | tf_op jit(solution)/shard_map/ppermute | solution.py:115
  265.3 21.9 %collective-permute-start.29 = (bf16[2,2,2,2,32,512]{5,4,0,3,2,1:T(8,128)(2,1)S(1)}, bf16[2,2,2,2,32,512]{5,4,0,3,2,1:T(8,128)(2,1)S(1)}, u32[]{:S(2)}, u32[]{:S(2)}) collective-permute-start(bf16[2,2,2,2,32,512]{5,4,0,3,2,1:T(8,128)(2,1)S(1)} %bitcast.322), channel_id=1, source_target_pairs={{0,4},{2,6},{4,0},{6,2},{8,12},{10,14},{12,8},{14,10},{16,20},{18,... | collective-permute-start | bytes 1572872 | tf_op jit(solution)/shard_map/ppermute | solution.py:66
  299.5 22.8 %collective-permute-start.36 = (bf16[2,2,2,2,32,512]{5,4,0,3,2,1:T(8,128)(2,1)S(1)}, bf16[2,2,2,2,32,512]{5,4,0,3,2,1:T(8,128)(2,1)S(1)}, u32[]{:S(2)}, u32[]{:S(2)}) collective-permute-start(bf16[2,2,2,2,32,512]{5,4,0,3,2,1:T(8,128)(2,1)S(1)} %bitcast.321), channel_id=1, source_target_pairs={{0,4},{2,6},{4,0},{6,2},{8,12},{10,14},{12,8},{14,10},{16,20},{18,... | collective-permute-start | bytes 1572872 | tf_op jit(solution)/shard_map/ppermute | solution.py:66
  300.4 21.8 %collective-permute-start.35 = (bf16[2,2,2,2,32,512]{5,4,0,3,2,1:T(8,128)(2,1)S(1)}, bf16[2,2,2,2,32,512]{5,4,0,3,2,1:T(8,128)(2,1)S(1)}, u32[]{:S(2)}, u32[]{:S(2)}) collective-permute-start(bf16[2,2,2,2,32,512]{5,4,0,3,2,1:T(8,128)(2,1)S(1)} %get-tuple-element.575), channel_id=1, source_target_pairs={{0,2},{2,0},{4,6},{6,4},{8,10},{10,8},{12,14},{14,12},{16,18},{18,... | collective-permute-start | bytes 1572872 | tf_op jit(solution)/shard_map/ppermute | solution.py:66
  302.3 19.9 %collective-permute-start.37 = (bf16[2,512,512]{2,1,0:T(8,128)(2,1)S(1)}, bf16[2,512,512]{2,1,0:T(8,128)(2,1)S(1)}, u32[]{:S(2)}, u32[]{:S(2)}) collective-permute-start(bf16[2,512,512]{2,1,0:T(8,128)(2,1)S(1)} %get-tuple-element.373), channel_id=1, source_target_pairs={{0,1},{1,0},{2,3},{3,2},{4,5},{5,4},{6,7},{7,6},{8,9},{9,8},{10,11... | collective-permute-start | bytes 3145736 | tf_op jit(solution)/shard_map/ppermute | solution.py:115
  302.6 19.7 %collective-permute-start.34 = (bf16[2,2,2,32,512]{4,3,1,0,2:T(8,128)(2,1)S(1)}, bf16[2,2,2,32,512]{4,3,1,0,2:T(8,128)(2,1)S(1)}, u32[]{:S(2)}, u32[]{:S(2)}) collective-permute-start(bf16[2,2,2,32,512]{4,3,1,0,2:T(8,128)(2,1)S(1)} %get-tuple-element.597), channel_id=1, source_target_pairs={{0,16},{2,18},{4,20},{6,22},{8,24},{10,26},{12,28},{14,30},{16,0},... | collective-permute-start | bytes 786440 | tf_op jit(solution)/shard_map/ppermute | solution.py:66
  330.5 19.6 %collective-permute-start.41 = (bf16[768,512]{1,0:T(8,128)(2,1)}, bf16[768,512]{1,0:T(8,128)(2,1)S(1)}, u32[]{:S(2)}, u32[]{:S(2)}) collective-permute-start(bf16[768,512]{1,0:T(8,128)(2,1)} %dynamic-slice_convert_fusion), channel_id=1, source_target_pairs={{0,8},{2,10},{4,12},{6,14},{8,0},{10,2},{12,4},{14,6},{16,24},{18,... | collective-permute-start | bytes 2359304 | tf_op jit(solution)/shard_map/ppermute | solution.py:66
  352.2 26.5 %collective-permute-start.47 = (bf16[2,2,2,2,32,512]{5,4,0,3,2,1:T(8,128)(2,1)}, bf16[2,2,2,2,32,512]{5,4,0,3,2,1:T(8,128)(2,1)}, u32[]{:S(2)}, u32[]{:S(2)}) collective-permute-start(bf16[2,2,2,2,32,512]{5,4,0,3,2,1:T(8,128)(2,1)} %bitcast.260), channel_id=1, source_target_pairs={{0,4},{2,6},{4,0},{6,2},{8,12},{10,14},{12,8},{14,10},{16,20},{18,... | collective-permute-start | bytes 1572872 | tf_op jit(solution)/shard_map/ppermute | solution.py:66
  355.0 23.7 %collective-permute-start.46 = (bf16[2,2,2,2,32,512]{5,4,0,3,2,1:T(8,128)(2,1)}, bf16[2,2,2,2,32,512]{5,4,0,3,2,1:T(8,128)(2,1)}, u32[]{:S(2)}, u32[]{:S(2)}) collective-permute-start(bf16[2,2,2,2,32,512]{5,4,0,3,2,1:T(8,128)(2,1)} %get-tuple-element.571), channel_id=1, source_target_pairs={{0,2},{2,0},{4,6},{6,4},{8,10},{10,8},{12,14},{14,12},{16,18},{18,... | collective-permute-start | bytes 1572872 | tf_op jit(solution)/shard_map/ppermute | solution.py:66
  356.3 22.4 %collective-permute-start.45 = (bf16[2,2,2,32,512]{4,3,1,0,2:T(8,128)(2,1)}, bf16[2,2,2,32,512]{4,3,1,0,2:T(8,128)(2,1)}, u32[]{:S(2)}, u32[]{:S(2)}) collective-permute-start(bf16[2,2,2,32,512]{4,3,1,0,2:T(8,128)(2,1)} %get-tuple-element.591), channel_id=1, source_target_pairs={{0,16},{2,18},{4,20},{6,22},{8,24},{10,26},{12,28},{14,30},{16,0},... | collective-permute-start | bytes 786440 | tf_op jit(solution)/shard_map/ppermute | solution.py:66
  359.0 29.1 %collective-permute-start.54 = (f32[8,768]{1,0:T(8,128)}, f32[8,768]{1,0:T(8,128)S(1)}, u32[]{:S(2)}, u32[]{:S(2)}) collective-permute-start(f32[8,768]{1,0:T(8,128)} %copy-done.19), channel_id=1, source_target_pairs={{1,9},{3,11},{5,13},{7,15},{8,0},{10,2},{12,4},{14,6},{17,25},{19,... | collective-permute-start | bytes 73736 | tf_op jit(solution)/shard_map/ppermute | solution.py:74
  380.7 22.9 %collective-permute-start.50 = (bf16[2,2,2,32,512]{4,3,0,2,1:T(8,128)(2,1)}, bf16[2,2,2,32,512]{4,3,0,2,1:T(8,128)(2,1)}, u32[]{:S(2)}, u32[]{:S(2)}) collective-permute-start(bf16[2,2,2,32,512]{4,3,0,2,1:T(8,128)(2,1)} %get-tuple-element.589), channel_id=1, source_target_pairs={{0,4},{2,6},{4,0},{6,2},{8,12},{10,14},{12,8},{14,10},{16,20},{18,... | collective-permute-start | bytes 786440 | tf_op jit(solution)/shard_map/ppermute | solution.py:66
  382.6 21.0 %collective-permute-start.52 = (bf16[16,16,1792]{2,1,0:T(8,128)(2,1)}, bf16[16,16,1792]{2,1,0:T(8,128)(2,1)}, u32[]{:S(2)}, u32[]{:S(2)}) collective-permute-start(bf16[16,16,1792]{2,1,0:T(8,128)(2,1)} %dynamic-slice_bitcast_fusion), channel_id=1, source_target_pairs={{0,1},{1,0},{2,3},{3,2},{4,5},{5,4},{6,7},{7,6},{8,9},{9,8},{10,11... | collective-permute-start | bytes 2752520 | tf_op jit(solution)/shard_map/ppermute | solution.py:115
  382.6 21.0 %collective-permute-start.53 = (bf16[768,640]{1,0:T(8,128)(2,1)}, bf16[768,640]{1,0:T(8,128)(2,1)}, u32[]{:S(2)}, u32[]{:S(2)}) collective-permute-start(bf16[768,640]{1,0:T(8,128)(2,1)} %get-tuple-element.446), channel_id=1, source_target_pairs={{1,9},{3,11},{5,13},{7,15},{8,0},{10,2},{12,4},{14,6},{17,25},{19,... | collective-permute-start | bytes 2949128 | tf_op jit(solution)/shard_map/ppermute | solution.py:74
  (119 other events, 1313.5 us)

commit v2 on v1

v2 whole, which is shorter than its diff:
```python
import functools
import math

import jax
import jax.numpy as jnp
from jax import lax
from jax.experimental import pallas as pl
from jax.experimental.pallas import tpu as pltpu
from jax.sharding import PartitionSpec as P

D = 512
H = 1024
HALF = H // 2
TW = 256
S = 4
DOM = 4
K = 2
EPS = 1e-05
FROZEN_SHARE = 0.25
TILE = 256
LOCAL = 6
CHUNKS = ((0, 1, 2), (3, 4, 5))
VMEM_LIMIT = 48 * 1024 * 1024
PACK = 1792
SETS = (
    tuple(range(2)) + tuple(S + K * d for d in reversed(range(DOM))),
    tuple(range(2, 4)) + tuple(S + K * d + 1 for d in range(DOM)),
)
COEF, SCALE, DCOEF, DOMAIN, LABEL, WEIGHT, BIAS = 0, 6, 12, 18, 19, 20, 21
LOW, HIGH, ROLE, DOMAIN_OF, START, END, CORE = 0, 4, 8, 9, 13, 17, 21

bf16 = jnp.bfloat16
f32 = jnp.float32


def dims_of(count):
    if count % 4 == 0:
        rest = count // 4
        root = math.isqrt(rest)
        if root * root == rest:
            return (4, root, root)
    return (count, 1, 1)


class Box:
    def __init__(self, count):
        first, second, third = dims_of(count)
        self.count = count
        self.dims = (2, first // 2, second, third)
        self.strides = (second * third, 2 * second * third, third, 1)

    def role(self, chip):
        return (chip // self.strides[0]) % 2

    def partner(self, chip):
        return chip + (1 - 2 * self.role(chip)) * self.strides[0]

    def send(self, values, flip=0, z=0, y=0, x=0):
        pairs = []
        for chip in range(self.count):
            to = chip
            for step, size, stride in zip((flip, z, y, x), self.dims, self.strides):
                place = (chip // stride) % size
                to += ((place + step) % size - place) * stride
            pairs.append((chip, to))
        return lax.ppermute(values, "dp", pairs)

    def to_partner(self, values, home):
        pairs = []
        for chip in range(self.count):
            for core in range(2):
                if (core == self.role(chip)) == home:
                    pairs.append((2 * chip + core, 2 * self.partner(chip) + core))
        return lax.ppermute(values, ("dp", "tensor"), pairs)

    def pieces(self, values, dim):
        size = self.dims[("flip", "z", "y", "x").index(dim)]
        return [self.send(values, **{dim: -k}) for k in range(1, size)]

    def hand_out(self, parts, dim):
        return [self.send(part, **{dim: k}) for k, part in enumerate(parts) if k]

    def line(self, shards):
        same, other = shards
        steps = range(self.dims[1])
        return [self.send(same, z=-z) for z in steps if z], [
            self.send(other, flip=1, z=-z) for z in steps
        ]

    def in_line(self, own, found, role, axis):
        same, other = found
        return [in_order(role, s, o, axis) for s, o in zip([own] + same, other)]

    def hand_out_flip(self, parts):
        return [self.send(part, flip=1, z=k) for k, part in enumerate(parts)]

    def plane(self):
        _, _, ny, nx = self.dims
        return [(x, y) for x in range(nx) for y in range(ny)][1:]

    def gather_plane(self, values):
        return [values] + [self.send(values, y=-y, x=-x) for x, y in self.plane()]

    def hand_out_plane(self, parts):
        return [self.send(part, y=y, x=x) for part, (x, y) in zip(parts[1:], self.plane())]

    def same_sum(self, values, dim):
        number = ("flip", "z", "y", "x").index(dim)
        size, stride = self.dims[number], self.strides[number]
        found = jnp.stack([values] + self.pieces(values, dim))
        if size > 2:
            mine = (lax.axis_index("dp") // stride) % size
            found = jnp.take(found, (jnp.arange(size) - mine) % size, axis=0)
        return functools.reduce(jnp.add, [found[k] for k in range(size)])

    def places(self):
        me = lax.axis_index("dp")
        chip = jnp.arange(self.count)
        place, weight = 0, 1
        for dim, (size, stride) in enumerate(zip(self.dims, self.strides)):
            mine = (me // stride) % size if dim else 0
            place = place + (((chip // stride) % size - mine) % size) * weight
            weight *= size
        return place

    def ahead(self):
        me = lax.axis_index("dp")
        place = jnp.arange(self.count)
        chip, weight = 0, 1
        for dim, (size, stride) in enumerate(zip(self.dims, self.strides)):
            mine = (me // stride) % size if dim else 0
            chip = chip + ((mine + (place // weight) % size) % size) * stride
            weight *= size
        return chip


def swap_cores(values):
    return lax.ppermute(values, "tensor", [(0, 1), (1, 0)])


def in_order(which, own, other, axis):
    return jnp.where(
        which == 0,
        jnp.concatenate([own, other], axis),
        jnp.concatenate([other, own], axis),
    )


def step(*values):
    return lax.optimization_barrier(values)


def total(first, arrived):
    return functools.reduce(jnp.add, [a.astype(f32) for a in arrived], first.astype(f32))


def gelu_parts(v):
    inner = math.sqrt(2.0 / math.pi)
    square = v * v
    th = jnp.tanh(v * (inner + inner * 0.044715 * square))
    half = 0.5 * (1.0 + th)
    act = v * half
    slope = half + 0.5 * v * (1.0 - th * th) * (inner + 3.0 * inner * 0.044715 * square)
    return act, slope


def nt(a, b):
    return lax.dot_general(a, b, (((1,), (1,)), ((), ())), preferred_element_type=f32)


def tn(a, b):
    return lax.dot_general(a, b, (((0,), (0,)), ((), ())), preferred_element_type=f32)


def nn(a, b):
    return jnp.dot(a, b, preferred_element_type=f32)


def softmax_rows(v):
    e = jnp.exp(v - jnp.max(v, axis=0, keepdims=True))
    return e / jnp.sum(e, axis=0, keepdims=True)


def prepare_kernel(ints, floats, rows_ref, embeds_ref, proj_ref, gates_ref, vec_ref, ev_ref, x_ref, mix_ref, cols_ref, prob_ref):
    tiles_of_half = pl.num_programs(0) // 2
    index = pl.program_id(0)
    role = ints[ROLE]
    count = rows_ref.shape[1]
    slot = index * TILE + lax.broadcasted_iota(jnp.int32, (TILE, count), 0)
    here = rows_ref[0:1, :].astype(jnp.int32) == slot
    order = jnp.where(here, 1.0, 0.0).astype(bf16)
    label = jnp.sum(jnp.where(here, rows_ref[1:2, :], 0.0), axis=1, keepdims=True)
    events = nn(order, embeds_ref[...]).astype(bf16)
    ev_ref[...] = events
    mixed = nt(events, proj_ref[...]) + vec_ref[3 * LOCAL : 3 * LOCAL + 1, :]
    low = mixed.astype(bf16)
    x_ref[...] = low
    mix_ref[...] = mixed * jnp.where(index // tiles_of_half == role, 1.0, 0.0)
    logits = jnp.transpose(nn(low, gates_ref[...]))
    place = index * TILE + lax.broadcasted_iota(jnp.int32, (1, TILE), 1)
    picks = [
        jnp.where((place >= ints[START + d]) & (place < ints[END + d]), 1.0, 0.0) for d in range(DOM)
    ]

    def pick(low_row, size):
        return softmax_rows(
            functools.reduce(
                jnp.add,
                [picks[d] * logits[low_row + d * size : low_row + (d + 1) * size] for d in range(DOM)],
            )
        )

    top, shared, domain = pick(0, 2), pick(2 * DOM, S), pick((2 + S) * DOM, K)
    prob_ref[...] = jnp.concatenate([top, shared, domain], axis=0)
    first = role == 0
    own_shared = top[0:1] * jnp.where(first, shared[:2], shared[2:])
    own_domain = top[1:2] * jnp.where(first, domain[0:1], domain[1:2])
    coef = [own_domain * jnp.where(first, picks[DOM - 1 - d], picks[d]) for d in range(DOM)]
    table = [
        own_shared,
        *coef,
        jnp.zeros((DOMAIN - SCALE, TILE), f32),
        sum(float(d) * picks[d] for d in range(DOM)),
        jnp.zeros((1, TILE), f32),
        sum(floats[d] * picks[d] for d in range(DOM)),
        sum(floats[DOM + d] * picks[d] for d in range(DOM)),
        jnp.zeros((128 - BIAS - 1, TILE), f32),
    ]
    cols_ref[...] = with_column(jnp.transpose(jnp.concatenate(table, axis=0)), LABEL, label)


def with_column(table, column, values):
    lane = lax.broadcasted_iota(jnp.int32, table.shape, 1)
    return jnp.where(lane == column, values, table)


def tiles_of(expert, ints, first, count):
    low = jnp.maximum(ints[LOW + expert - 2], first)
    high = jnp.minimum(ints[HIGH + expert - 2], first + count)
    return low - first, jnp.maximum(high, low) - first


def each_span(expert, ints, first, rows, work):
    if expert < 2:
        work(slice(0, rows))
    else:
        low, high = tiles_of(expert, ints, first, rows // TILE)

        def one(index, _):
            work(pl.ds(pl.multiple_of(index * TILE, TILE), TILE))
            return 0

        lax.fori_loop(low, high, one, 0)


def join(pieces, held):
    count = len(pieces) // 2
    for core in range(2):
        mine = pieces[core * count : core * count + count]
        by_x, by_y = split_pieces(mine)
        nx, ny = len(by_x), len(by_y)
        rows = by_x[0].shape[3]
        nz = by_x[0].shape[1]

        def at(x, y, z):
            return pl.ds(((x * ny + y) * nz + z) * rows, rows)

        for x in range(nx):
            for y in range(ny):
                for z in range(nz):
                    held[core][at(x, y, z), :] = by_x[x][y, z, 0]
                    held[2 + core][at(x, y, z), :] = by_y[y][x, z, 0]


def split_pieces(pieces):
    nx = pieces[-1].shape[0]
    return pieces[:nx], pieces[nx:]


def forward_kernel(experts, own, aliased, number, ints, x_ref, *refs):
    arrays = sorted({e // 3 for e in experts})
    weights = {a: refs[number * k : number * (k + 1)] for k, a in enumerate(arrays)}
    refs = refs[number * len(arrays) :]
    refs, held = refs[:-4], refs[-4:]
    wi_a, wi_b, wo_a, wo_b = held
    bi_ref, vec_ref, cols_in, mix_in = refs[:4]
    cols_ref, mix_ref, *norm_refs = refs[4 + aliased :]
    norm_refs = dict(zip(arrays, norm_refs))
    rows = x_ref.shape[0]
    half = ints[ROLE] if own else 1 - ints[ROLE]
    step = pl.program_id(0)

    @pl.when(step == 0)
    def _():
        cols_ref[...] = cols_in[...]
        mix_ref[...] = mix_in[...]

    def work(expert, span):
        x = x_ref[span, :]
        pre_a = nn(x, wi_a[...]) + bi_ref[expert : expert + 1, :HALF]
        act_a = gelu_parts(pre_a)[0].astype(bf16)
        pre_b = nn(x, wi_b[...]) + bi_ref[expert : expert + 1, HALF:]
        act_b = gelu_parts(pre_b)[0].astype(bf16)
        out = nt(act_a, wo_a[...]) + nt(act_b, wo_b[...]) + vec_ref[expert : expert + 1, :]
        centre = jnp.mean(out, axis=1, keepdims=True)
        centred = out - centre
        scale = lax.rsqrt(jnp.mean(centred * centred, axis=1, keepdims=True) + EPS)
        norm = centred * scale
        norm_refs[expert // 3][0, span, :] = norm.astype(bf16)
        cols = cols_ref[span, :]
        cols_ref[span, :] = with_column(cols, SCALE + expert, scale)
        gain = vec_ref[LOCAL + expert : LOCAL + expert + 1, :]
        shift = vec_ref[2 * LOCAL + expert : 2 * LOCAL + expert + 1, :]
        mix_ref[span, :] += cols[:, COEF + expert : COEF + expert + 1] * (norm * gain + shift)

    for place, expert in enumerate(experts):

        @pl.when(step == place)
        def _(expert=expert):
            join(weights[expert // 3], held)
            each_span(expert, ints, half * (rows // TILE), rows, functools.partial(work, expert))


def backward_kernel(experts, halves, keeps_back, adds, number, ints, x_ref, *refs):
    gb_refs, refs = refs[: len(halves)], refs[len(halves) :]
    norm_ref, pieces, refs = refs[0], refs[1 : 1 + number], refs[1 + number :]
    bi_ref, vec_ref, cols_in = refs[:3]
    refs, held = refs[3:-4], refs[-4:]
    wi_a, wi_b, wo_a, wo_b = held
    join(pieces, held)
    back_in, refs = refs[0], refs[1:]
    if adds:
        dvec_in, dbi_in = refs[:2]
        refs = refs[2:]
    cols_ref, back_ref, keep_ref, give_ref, dvec_ref, dbi_ref, in_a, in_b, out_a, out_b = refs
    rows = x_ref.shape[0]
    half_tiles = rows // TILE // len(halves)
    first = 0 if len(halves) == 2 else (ints[ROLE] if halves[0] == "own" else 1 - ints[ROLE]) * half_tiles
    step = pl.program_id(0)

    @pl.when(step == 0)
    def _():
        cols_ref[...] = cols_in[...]
        back_ref[...] = back_in[...] if keeps_back else jnp.zeros_like(back_ref)

    dvec_ref[...] = dvec_in[...] if adds else jnp.zeros_like(dvec_ref)
    dbi_ref[...] = dbi_in[...] if adds else jnp.zeros_like(dbi_ref)

    def work(expert, span):
        whole = isinstance(span, slice)

        def add(ref, values):
            ref[...] = values if whole else ref[...] + values

        x = x_ref[span, :]
        norm = norm_ref[0, span, :].astype(f32)
        cols = cols_ref[span, :]
        if len(halves) == 1:
            grad_block = gb_refs[0][span, :].astype(f32)
        else:
            half = span.start // (half_tiles * TILE)
            inner = pl.ds(pl.multiple_of(span.start - half * (half_tiles * TILE), TILE), TILE)
            grad_block = jnp.where(
                half == ints[ROLE], gb_refs[0][inner, :].astype(f32), gb_refs[1][inner, :].astype(f32)
            )
        gain = vec_ref[LOCAL + expert : LOCAL + expert + 1, :]
        shift = vec_ref[2 * LOCAL + expert : 2 * LOCAL + expert + 1, :]
        scale = cols[:, SCALE + expert : SCALE + expert + 1]
        grad_exp = cols[:, COEF + expert : COEF + expert + 1] * grad_block
        scaled = grad_exp * norm
        dx = grad_exp * gain
        first_mean = jnp.mean(dx, axis=1, keepdims=True)
        second_mean = jnp.mean(dx * norm, axis=1, keepdims=True)
        grad_sum = scale * (dx - first_mean - norm * second_mean)
        grad_low = grad_sum.astype(bf16)
        pre_a = nn(x, wi_a[...]) + bi_ref[expert : expert + 1, :HALF]
        act_a, slope_a = gelu_parts(pre_a)
        low_a = (nn(grad_low, wo_a[...]) * slope_a).astype(bf16)
        pre_b = nn(x, wi_b[...]) + bi_ref[expert : expert + 1, HALF:]
        act_b, slope_b = gelu_parts(pre_b)
        low_b = (nn(grad_low, wo_b[...]) * slope_b).astype(bf16)
        add(out_a, tn(grad_low, act_a.astype(bf16)))
        add(in_a, tn(x, low_a))
        add(out_b, tn(grad_low, act_b.astype(bf16)))
        add(in_b, tn(x, low_b))
        back_ref[span, :] += nt(low_a, wi_a[...]) + nt(low_b, wi_b[...])
        dcoef = jnp.sum(grad_block * (norm * gain + shift), axis=1, keepdims=True)
        if expert < 2:
            cols_ref[span, :] = with_column(cols, DCOEF + expert, dcoef)
        else:
            mine = cols[:, DOMAIN : DOMAIN + 1] == ints[DOMAIN_OF + expert - 2].astype(f32)
            column = cols[:, DCOEF + 2 : DCOEF + 3] + jnp.where(mine, dcoef, 0.0)
            cols_ref[span, :] = with_column(cols, DCOEF + 2, column)
        dvec_ref[0, 0:1, :] += jnp.sum(grad_sum, axis=0, keepdims=True)
        dvec_ref[0, 1:2, :] += jnp.sum(scaled, axis=0, keepdims=True)
        dvec_ref[0, 2:3, :] += jnp.sum(grad_exp, axis=0, keepdims=True)
        dbi_ref[0, 0:1, :HALF] += jnp.sum(low_a.astype(f32), axis=0, keepdims=True)
        dbi_ref[0, 0:1, HALF:] += jnp.sum(low_b.astype(f32), axis=0, keepdims=True)

    for place, expert in enumerate(experts):

        @pl.when(step == place)
        def _(expert=expert):
            if expert >= 2:
                for ref in (in_a, in_b, out_a, out_b):
                    ref[...] = jnp.zeros_like(ref)
            each_span(expert, ints, first, rows, functools.partial(work, expert))

    keep_ref[0, 0] = in_a[...].astype(bf16)
    keep_ref[0, 1] = out_a[...].astype(bf16)
    give_ref[0, 0] = in_b[...].astype(bf16)
    give_ref[0, 1] = out_b[...].astype(bf16)


def tower_kernel(
    ints, mix_ref, other_ref, cols_ref, tw_ref, tv_ref, out_ref, gb_ref, low_ref, dw_ref, dv_ref, db_ref
):
    @pl.when(pl.program_id(0) == 0)
    def _():
        db_ref[...] = jnp.zeros_like(db_ref)
        dw_ref[...] = jnp.zeros_like(dw_ref)
        dv_ref[...] = jnp.zeros_like(dv_ref)

    bias = tv_ref[0:1, :]
    head = tv_ref[1:2, :]
    cols = cols_ref[...]
    block = (mix_ref[...] + other_ref[...].astype(f32)).astype(bf16)
    pre = nn(block, tw_ref[...]) + bias
    act, slope = gelu_parts(pre)
    group = lax.broadcasted_iota(jnp.int32, pre.shape, 1) // TW
    mine = group == cols[:, DOMAIN : DOMAIN + 1].astype(jnp.int32)
    act = jnp.where(mine, act, 0.0)
    logit = jnp.sum(act * head, axis=1, keepdims=True) + cols[:, BIAS : BIAS + 1]
    predicted = 1.0 / (1.0 + jnp.exp(-logit))
    grad_logit = cols[:, WEIGHT : WEIGHT + 1] * (predicted - cols[:, LABEL : LABEL + 1])
    lane = lax.broadcasted_iota(jnp.int32, cols.shape, 1)
    out_ref[...] = jnp.transpose(jnp.where(lane == 0, predicted, jnp.where(lane == 1, grad_logit, 0.0)))[:8]
    by_domain = jnp.where(lane.astype(f32) == cols[:, DOMAIN : DOMAIN + 1], grad_logit, 0.0)
    db_ref[0:1, :] += jnp.sum(by_domain, axis=0, keepdims=True)
    dv_ref[1:2, :] += jnp.sum(grad_logit * act, axis=0, keepdims=True)
    grad_pre = jnp.where(mine, grad_logit * head * slope, 0.0)
    dv_ref[0:1, :] += jnp.sum(grad_pre, axis=0, keepdims=True)
    grad_low = grad_pre.astype(bf16)
    grad_block = nt(grad_low, tw_ref[...])
    gb_ref[...] = grad_block
    low_ref[...] = grad_block.astype(bf16)
    dw_ref[...] += tn(block, grad_low)


def softmax_back(probability, grad_probs):
    return probability * (grad_probs - jnp.sum(probability * grad_probs, axis=0, keepdims=True))


def gate_kernel(own, ints, back_ref, cols_ref, prob_ref, x_ref, gates_ref, sum_ref, low_ref, gate_ref):
    index = pl.program_id(0)
    half = ints[ROLE] if own else 1 - ints[ROLE]
    first = ints[ROLE] == 0

    @pl.when(index == 0)
    def _():
        gate_ref[...] = jnp.zeros_like(gate_ref)

    mine = jnp.transpose(cols_ref[...])[DCOEF : DCOEF + 3]
    none = jnp.zeros_like(mine)
    one, two = jnp.where(first, mine, none), jnp.where(first, none, mine)
    d_shared = jnp.concatenate([one[0:2], two[0:2]], axis=0)
    d_domain = jnp.concatenate([one[2:3], two[2:3]], axis=0)
    top, shared, domain = prob_ref[0:2, :], prob_ref[2:6, :], prob_ref[6:8, :]
    d_top = jnp.concatenate(
        [
            jnp.sum(d_shared * shared, axis=0, keepdims=True),
            jnp.sum(d_domain * domain, axis=0, keepdims=True),
        ],
        axis=0,
    )
    grads = (
        softmax_back(top, d_top),
        softmax_back(shared, d_shared * top[0:1]),
        softmax_back(domain, d_domain * top[1:2]),
    )
    rows = top.shape[1]
    place = (half * pl.num_programs(0) + index) * rows + lax.broadcasted_iota(jnp.int32, (1, rows), 1)
    picks = [
        jnp.where((place >= ints[START + d]) & (place < ints[END + d]), 1.0, 0.0) for d in range(DOM)
    ]
    spread = jnp.concatenate(
        [picks[d] * grad for grad in grads for d in range(DOM)] + [jnp.zeros((96, rows), f32)],
        axis=0,
    )
    spread = jnp.transpose(spread).astype(bf16)
    gate_ref[...] += tn(x_ref[...], spread)
    added = back_ref[...] + nt(spread, gates_ref[...])
    sum_ref[...] = added
    low_ref[...] = added.astype(bf16)


def call_gate(own, ints, back, cols, probs, x, gates):
    rows = x.shape[0]
    half = rows // 2

    def index(ints):
        return ints[ROLE] if own else 1 - ints[ROLE]

    return pl.pallas_call(
        functools.partial(gate_kernel, own),
        grid_spec=pltpu.PrefetchScalarGridSpec(
            num_scalar_prefetch=1,
            grid=(1,),
            in_specs=[
                half_spec(own, (half, D)),
                half_spec(own, (half, 128)),
                pl.BlockSpec((8, half), lambda i, ints: (0, index(ints))),
                half_spec(own, (half, D)),
                fixed(gates.shape),
            ],
            out_specs=(fixed((half, D)), fixed((half, D)), fixed((D, 128))),
        ),
        out_shape=(
            jax.ShapeDtypeStruct((half, D), f32),
            jax.ShapeDtypeStruct((half, D), bf16),
            jax.ShapeDtypeStruct((D, 128), f32),
        ),
        compiler_params=params(),
        cost_estimate=pl.CostEstimate(
            flops=4 * half * D * 128, bytes_accessed=5_000_000, transcendentals=0
        ),
        name="gates",
    )(ints, back, cols, probs, x, gates)


def hidden_lines(ints, lane_ref, tv_ref, line_refs):
    first_set, first_core = ints[ROLE] == 0, ints[CORE] == 0
    mine = [r[k, 0:1, :] for r in line_refs for k in range(r.shape[0])]
    mine = jnp.concatenate(mine, axis=0)
    mine = jnp.where(first_core, mine, pltpu.roll(mine, HALF, 1))
    mine = jnp.where(first_set, mine, 0.0), jnp.where(first_set, 0.0, mine)
    found = {j: mine[r][i : i + 1] for r, row in enumerate(SETS) for i, j in enumerate(row)}
    mine = jnp.concatenate([found[j] for j in range(2 * LOCAL)], axis=0).astype(bf16)

    def lanes(values, row):
        lane = lax.broadcasted_iota(jnp.int32, (H, D), 0)
        chosen = jnp.where(lane == lane_ref[row : row + 1, :], 1.0, 0.0).astype(bf16)
        return nn(values, chosen)

    tower = tv_ref[...].astype(bf16)
    rows = [lanes(mine, 0), lanes(mine, 1)]
    head = lane_ref[6:7, :] == 1
    for d in range(DOM):
        both = lanes(tower, 2 + d)
        rows.append(jnp.where(head, both[1:2], both[0:1]))
    return rows


def finish_kernel(
    ints, gb_ref, gb_in_ref, own_ref, other_ref, own_in_ref, other_in_ref, ev_ref, proj_ref, tower_ref, gate_a, gate_b, *refs
):
    lane_ref, tv_ref, *vec_refs, ge_ref, small_ref, proj_sum, bias_sum = refs
    vec_refs, line_refs = vec_refs[: len(vec_refs) // 2], vec_refs[len(vec_refs) // 2 :]
    index = pl.program_id(0)
    last = pl.num_programs(0) - 1
    first = ints[ROLE] == 0
    at_home = jnp.where(ints[CORE] == ints[ROLE], 1.0, 0.0)
    mine_half = index == ints[ROLE]

    @pl.when(index == 0)
    def _():
        for ref in (proj_sum, bias_sum):
            ref[...] = jnp.zeros_like(ref)

    grad_mixed = at_home * jnp.where(
        mine_half,
        gb_ref[...] + own_ref[...] + other_in_ref[...].astype(f32),
        gb_in_ref[...].astype(f32) + other_ref[...] + own_in_ref[...].astype(f32),
    )
    bias_sum[0:1, :] += jnp.sum(grad_mixed, axis=0, keepdims=True)
    low = grad_mixed.astype(bf16)
    proj_sum[...] += tn(low, ev_ref[...])
    ge_ref[...] = nn(low, proj_ref[...]).astype(bf16)

    @pl.when(index == last)
    def _():
        e_in = proj_sum.shape[1]
        vectors = jnp.concatenate(
            [r[k, 0:3, :] for r in vec_refs for k in range(r.shape[0])], axis=0
        )
        rows = jnp.concatenate(
            [
                jnp.zeros((32, D), f32),
                jnp.where(first, vectors, 0.0),
                jnp.where(first, 0.0, vectors),
                bias_sum[0:1, :],
                *hidden_lines(ints, lane_ref, tv_ref, line_refs),
                jnp.zeros((31, D), f32),
            ],
            axis=0,
        )
        small_ref[:, :e_in] = proj_sum[...].astype(bf16)
        small_ref[:, e_in : e_in + DOM * TW] = tower_ref[...].astype(bf16)
        small_ref[:, e_in + DOM * TW :] = (gate_a[...] + gate_b[...] + jnp.transpose(rows)).astype(bf16)


def call_finish(
    ints, gb, gb_in, own, other, own_in, other_in, events, proj_t, tower, gate_a, gate_b, lanes, tower_vec, sums
):
    rows, e_in = events.shape
    half = rows // 2

    def tile(width):
        return pl.BlockSpec((half, width), lambda i, *_: (i, 0))

    halves = (gb, gb_in, own, other, own_in, other_in)
    wholes = (proj_t, tower, gate_a, gate_b, lanes, tower_vec)
    vecs = [v for v, _ in sums] + [b for _, b in sums]
    return pl.pallas_call(
        finish_kernel,
        grid_spec=pltpu.PrefetchScalarGridSpec(
            num_scalar_prefetch=1,
            grid=(2,),
            in_specs=[fixed(a.shape) for a in halves]
            + [tile(e_in)]
            + [fixed(a.shape) for a in (*wholes, *vecs)],
            out_specs=(tile(e_in), fixed((D, PACK))),
            scratch_shapes=[pltpu.VMEM((D, e_in), f32), pltpu.VMEM((8, D), f32)],
        ),
        out_shape=(jax.ShapeDtypeStruct((rows, e_in), bf16), jax.ShapeDtypeStruct((D, PACK), bf16)),
        compiler_params=params(),
        cost_estimate=pl.CostEstimate(flops=4 * rows * D * e_in, bytes_accessed=14_000_000, transcendentals=0),
        name="finish",
    )(ints, *halves, events, *wholes, *vecs)


VECTOR_ROW = {j: 32 + 18 * r + 3 * i for r, row in enumerate(SETS) for i, j in enumerate(row)}


def small_kernel(*refs):
    parts, vec_refs = refs[:-12], refs[-3:]
    proj_ref, tower_ref, top_ref, shared_ref, domain_ref, bias_ref, hidden_ref, tb_ref, to_ref = refs[-12:-3]
    added = functools.reduce(jnp.add, [p[...].astype(f32) for p in parts])
    width, e_in = proj_ref.shape
    proj_ref[...] = added[:, :e_in]
    for d in range(DOM):
        tower_ref[d] = added[:, e_in + d * TW : e_in + (d + 1) * TW]
    rows = jnp.concatenate([added[:, e_in + DOM * TW :], jnp.zeros((128 - width, 128), f32)], axis=0)
    rows = jnp.transpose(rows)[:, :width]
    for ref, low, size in ((top_ref, 0, 2), (shared_ref, 2 * DOM, S), (domain_ref, (2 + S) * DOM, K)):
        for d in range(DOM):
            ref[d] = rows[low + d * size : low + (d + 1) * size]
    bias_ref[...] = rows[68:69]
    hidden_ref[:, :width] = rows[69:81]
    hidden_ref[:, width:] = rows[81:93]
    tb_ref[...] = rows[93:97, : width // 2]
    to_ref[...] = rows[93:97, width // 2 :]
    for which, ref in enumerate(vec_refs):
        for j in range(2 * LOCAL):
            ref[j : j + 1, :] = rows[VECTOR_ROW[j] + which : VECTOR_ROW[j] + which + 1]


def call_small(parts):
    width = parts[0].shape[0]
    e_in = PACK - DOM * TW - 128
    shapes = [(width, e_in), (DOM, width, TW), (DOM, 2, width), (DOM, S, width), (DOM, K, width), (1, width)]
    shapes += [(2 * LOCAL, 2 * width), (DOM, width // 2), (DOM, width // 2)]
    shapes += [(2 * LOCAL, width)] * 3
    return pl.pallas_call(
        small_kernel,
        grid=(1,),
        in_specs=[fixed(p.shape) for p in parts],
        out_specs=tuple(fixed(shape) for shape in shapes),
        out_shape=tuple(jax.ShapeDtypeStruct(shape, f32) for shape in shapes),
        compiler_params=params(),
        name="small",
    )(*parts)


def place_kernel(ints, *refs):
    *parts, in_ref, out_ref = refs
    half = len(parts) // 2
    first = ints[ROLE] == 0
    for chunk, (own, other) in enumerate(zip(parts[:half], parts[half:])):
        for place, expert in enumerate(CHUNKS[chunk]):
            for which, ref in enumerate((in_ref, out_ref)):
                a, b = own[which, place].astype(f32), other[which, place].astype(f32)
                ref[SETS[0][expert]] = jnp.where(first, a, b)
                ref[SETS[1][expert]] = jnp.where(first, b, a)


def call_place(ints, own, other):
    rows, width = own[0].shape[2:]
    shape = (2 * LOCAL, rows, width)
    return pl.pallas_call(
        place_kernel,
        grid_spec=pltpu.PrefetchScalarGridSpec(
            num_scalar_prefetch=1,
            grid=(1,),
            in_specs=[fixed(a.shape) for a in (*own, *other)],
            out_specs=(fixed(shape), fixed(shape)),
        ),
        out_shape=(jax.ShapeDtypeStruct(shape, f32),) * 2,
        compiler_params=params(),
        name="place",
    )(ints, *own, *other)


def params():
    return pltpu.CompilerParams(vmem_limit_bytes=VMEM_LIMIT)


def fixed(shape):
    return pl.BlockSpec(shape, lambda i, *_: (0,) * len(shape))


def pack_kernel(proj_ref, tower_ref, *refs):
    *row_refs, in_bias_ref, tower_b_ref, tower_out_ref, out_ref = refs
    width, e_in = proj_ref.shape
    out_ref[:, :e_in] = proj_ref[...]
    for d in range(DOM):
        out_ref[:, e_in + d * TW : e_in + (d + 1) * TW] = tower_ref[d]
    rows = [r[...].astype(f32) for r in row_refs]
    bias = in_bias_ref[...].astype(f32)
    rows += [bias[:, :width], bias[:, width:]]
    rows.append(
        jnp.concatenate([tower_b_ref[...].astype(f32), tower_out_ref[...].astype(f32)], axis=1)
    )
    rows = jnp.concatenate(rows + [jnp.zeros((31, width), f32)], axis=0)
    rows = jnp.concatenate([rows, jnp.zeros((128, 128 - width), f32)], axis=1)
    out_ref[:, e_in + DOM * TW :] = jnp.transpose(rows)[:width].astype(bf16)


def call_pack(*arrays):
    width = arrays[0].shape[0]
    return pl.pallas_call(
        pack_kernel,
        grid=(1,),
        in_specs=[fixed(a.shape) for a in arrays],
        out_specs=fixed((width, PACK)),
        out_shape=jax.ShapeDtypeStruct((width, PACK), bf16),
        compiler_params=params(),
        name="pack",
    )(*arrays)


def choose_kernel(own_ids, other_ids, in_own, out_own, in_other, out_other, own_ref, other_ref):
    own_ref[0], own_ref[1] = in_own[...], out_own[...]
    other_ref[0], other_ref[1] = in_other[...], out_other[...]


def call_choose(own_ids, other_ids, w_in, w_out_t):
    block = (1,) + w_in.shape[1:]
    shape = jax.ShapeDtypeStruct((2, own_ids.shape[0]) + w_in.shape[1:], bf16)
    own = pl.BlockSpec(block, lambda i, a, b: (a[i], 0, 0))
    other = pl.BlockSpec(block, lambda i, a, b: (b[i], 0, 0))
    out = pl.BlockSpec((2,) + block, lambda i, a, b: (0, i, 0, 0))
    return pl.pallas_call(
        choose_kernel,
        grid_spec=pltpu.PrefetchScalarGridSpec(
            num_scalar_prefetch=2, grid=(own_ids.shape[0],), in_specs=[own, own, other, other], out_specs=(out, out)
        ),
        out_shape=(shape, shape),
        compiler_params=params(),
        cost_estimate=pl.CostEstimate(flops=0, bytes_accessed=2_000_000, transcendentals=0),
        name="choose",
    )(own_ids, other_ids, w_in, w_out_t, w_in, w_out_t)


def call_prepare(ints, floats, table, embeds, proj_t, gates, vec):
    rows = embeds.shape[0]
    tiles = rows // TILE
    e_in = embeds.shape[1]

    def tile(width):
        return pl.BlockSpec((TILE, width), lambda i, *_: (i, 0))

    return pl.pallas_call(
        prepare_kernel,
        grid_spec=pltpu.PrefetchScalarGridSpec(
            num_scalar_prefetch=2,
            grid=(tiles,),
            in_specs=[fixed(table.shape), fixed(embeds.shape), fixed(proj_t.shape), fixed(gates.shape), fixed(vec.shape)],
            out_specs=(
                tile(e_in),
                tile(D),
                tile(D),
                tile(128),
                pl.BlockSpec((8, TILE), lambda i, *_: (0, i)),
            ),
        ),
        out_shape=(
            jax.ShapeDtypeStruct((rows, e_in), bf16),
            jax.ShapeDtypeStruct((rows, D), bf16),
            jax.ShapeDtypeStruct((rows, D), f32),
            jax.ShapeDtypeStruct((rows, 128), f32),
            jax.ShapeDtypeStruct((8, rows), f32),
        ),
        compiler_params=params(),
        cost_estimate=pl.CostEstimate(
            flops=2 * rows * e_in * (rows + D), bytes_accessed=12_000_000, transcendentals=rows * 8
        ),
        name="prepare",
    )(ints, floats, table, embeds, proj_t, gates, vec)


def half_spec(own, shape):
    rest = (0,) * (len(shape) - 1)
    return pl.BlockSpec(shape, lambda i, ints: ((ints[ROLE] if own else 1 - ints[ROLE]),) + rest)


def piece_spec(array, place):
    a, b, _, rows, width = array.shape
    return pl.BlockSpec((a, b, 1, rows, width), lambda i, *_: (0, 0, place(i), 0, 0))


MATRICES = [pltpu.VMEM((D, HALF), bf16)] * 4


def call_forward(experts, own, ints, x, weights, bi, vec, cols, mix, norms):
    rows = x.shape[0]
    half = rows // 2
    arrays = sorted({e // 3 for e in experts})
    first = {a: min(k for k, e in enumerate(experts) if e // 3 == a) for a in arrays}
    number = {a: sum(1 for e in experts if e // 3 == a) for a in arrays}

    def place(a):
        return lambda i: jnp.clip(i - first[a], 0, number[a] - 1)

    weight_specs = [piece_spec(w, place(a)) for a in arrays for w in weights[a]]
    norm_specs = [
        pl.BlockSpec(
            (1, half, D),
            lambda i, ints, a=a: (place(a)(i), ints[ROLE] if own else 1 - ints[ROLE], 0),
        )
        for a in arrays
    ]
    kept = [norms[a] for a in arrays if a in norms]
    inputs = [x] + [w for a in arrays for w in weights[a]] + [bi, vec, cols, mix] + kept
    at = len(inputs) - len(kept)
    aliases = {at - 1: 0, at: 1}
    aliases.update({at + 1 + k: 2 + k for k in range(len(kept))})
    shared = sum(1 for e in experts if e < 2)
    out = pl.pallas_call(
        functools.partial(forward_kernel, experts, own, len(kept), len(weights[arrays[0]])),
        grid_spec=pltpu.PrefetchScalarGridSpec(
            num_scalar_prefetch=1,
            grid=(len(experts),),
            in_specs=[half_spec(own, (half, D))]
            + weight_specs
            + [fixed(bi.shape), fixed(vec.shape), half_spec(own, (half, 128)), half_spec(own, (half, D))]
            + [pl.BlockSpec(memory_space=pl.ANY)] * len(kept),
            out_specs=(half_spec(own, (half, 128)), half_spec(own, (half, D)), *norm_specs),
            scratch_shapes=MATRICES,
        ),
        out_shape=(
            jax.ShapeDtypeStruct((rows, 128), f32),
            jax.ShapeDtypeStruct((rows, D), f32),
            *[jax.ShapeDtypeStruct((3, rows, D), bf16)] * len(arrays),
        ),
        input_output_aliases=aliases,
        compiler_params=params(),
        cost_estimate=pl.CostEstimate(
            flops=4 * (shared + 1) * half * D * H, bytes_accessed=12_000_000, transcendentals=0
        ),
        name="experts_forward",
    )(ints, *inputs)
    return out[0], out[1], {**norms, **dict(zip(arrays, out[2:]))}


def call_backward(experts, halves, ints, x, gbs, norms, weights, bi, vec, cols, back, sums=None):
    rows, count = x.shape[0], len(experts)
    part = rows // 2 * len(halves)
    array, low = experts[0] // 3, experts[0] % 3
    split = any(e // 3 != array for e in experts)

    def span(width):
        if len(halves) == 2:
            return fixed((rows, width))
        return half_spec(halves[0] == "own", (part, width))

    def norm_index(i, ints):
        if len(halves) == 2:
            return (low + i, 0, 0)
        return (low + i, ints[ROLE] if halves[0] == "own" else 1 - ints[ROLE], 0)

    assert not split
    pairs = pl.BlockSpec((1, 2, D, HALF), lambda i, *_: (i, 0, 0, 0))
    vec_spec = pl.BlockSpec((1, 8, D), lambda i, *_: (i, 0, 0))
    bi_spec = pl.BlockSpec((1, 8, H), lambda i, *_: (i, 0, 0))
    mode, back_array = back if back is not None else ("fresh", jnp.zeros((8, 128), f32))
    inputs = [x, *gbs, norms[array], *weights[array], bi, vec, cols, back_array]
    in_specs = (
        [span(D)]
        + [fixed(g.shape) for g in gbs]
        + [pl.BlockSpec((1, part, D), norm_index)]
        + [piece_spec(w, lambda i: low + i) for w in weights[array]]
        + [fixed(bi.shape), fixed(vec.shape), span(128)]
        + [span(D) if mode == "add" else pl.BlockSpec(memory_space=pl.ANY)]
    )
    aliases = {len(inputs) - 1: 0}
    if back is not None:
        aliases[len(inputs)] = 1
    if sums is not None:
        inputs += list(sums)
        in_specs += [vec_spec, bi_spec]
    return pl.pallas_call(
        functools.partial(
            backward_kernel, experts, halves, mode == "add", sums is not None, len(weights[array])
        ),
        grid_spec=pltpu.PrefetchScalarGridSpec(
            num_scalar_prefetch=1,
            grid=(count,),
            in_specs=in_specs,
            out_specs=(span(128), span(D), pairs, pairs, vec_spec, bi_spec),
            scratch_shapes=[pltpu.VMEM((D, HALF), f32)] * 4 + MATRICES,
        ),
        out_shape=(
            jax.ShapeDtypeStruct((rows, 128), f32),
            jax.ShapeDtypeStruct((rows, D), f32),
            jax.ShapeDtypeStruct((count, 2, D, HALF), bf16),
            jax.ShapeDtypeStruct((count, 2, D, HALF), bf16),
            jax.ShapeDtypeStruct((count, 8, D), f32),
            jax.ShapeDtypeStruct((count, 8, H), f32),
        ),
        input_output_aliases=aliases,
        compiler_params=params(),
        cost_estimate=pl.CostEstimate(
            flops=10 * count * (rows // 2) * D * H, bytes_accessed=20_000_000, transcendentals=0
        ),
        name="experts_backward",
    )(ints, *inputs)


def call_tower(ints, mix, other, cols, tower, tower_vec):
    rows = other.shape[0]
    tiles = rows // TILE

    def kept(width):
        return pl.BlockSpec((TILE, width), lambda i, ints: (ints[ROLE] * tiles + i, 0))

    def tile(width):
        return pl.BlockSpec((TILE, width), lambda i, *_: (i, 0))

    return pl.pallas_call(
        tower_kernel,
        grid_spec=pltpu.PrefetchScalarGridSpec(
            num_scalar_prefetch=1,
            grid=(tiles,),
            in_specs=[kept(D), tile(D), kept(128), fixed(tower.shape), fixed(tower_vec.shape)],
            out_specs=(
                pl.BlockSpec((8, TILE), lambda i, *_: (0, i)),
                tile(D),
                tile(D),
                fixed((D, DOM * TW)),
                fixed((8, DOM * TW)),
                fixed((8, 128)),
            ),
        ),
        out_shape=(
            jax.ShapeDtypeStruct((8, rows), f32),
            jax.ShapeDtypeStruct((rows, D), f32),
            jax.ShapeDtypeStruct((rows, D), bf16),
            jax.ShapeDtypeStruct((D, DOM * TW), f32),
            jax.ShapeDtypeStruct((8, DOM * TW), f32),
            jax.ShapeDtypeStruct((8, 128), f32),
        ),
        compiler_params=params(),
        cost_estimate=pl.CostEstimate(
            flops=6 * rows * D * DOM * TW, bytes_accessed=10_000_000, transcendentals=rows * DOM * TW
        ),
        name="towers",
    )(ints, mix, other, cols, tower, tower_vec)


def per_device(
    box,
    embeds,
    domain,
    frozen,
    labels,
    proj_w,
    proj_b,
    w_in,
    in_bias,
    w_out,
    out_bias,
    ln_gain,
    ln_shift,
    gate_top,
    gate_shared,
    gate_domain,
    tower_w,
    tower_b,
    tower_out,
    tower_out_b,
):
    core = lax.axis_index("tensor")
    role = box.role(lax.axis_index("dp"))
    at_home = core == role
    places = box.count
    rows = embeds.shape[0]
    half_rows = rows // 2
    width = proj_w.shape[1]
    e_in = proj_w.shape[0]
    place_of = box.places()
    nz, ny, nx = box.dims[1:]
    sets = jnp.array(SETS, jnp.int32)
    set_own, set_other = sets[role], sets[1 - role]

    def half(values, which, axis=0):
        return lax.dynamic_slice_in_dim(values, which * half_rows, half_rows, axis)

    w_out_t = jnp.swapaxes(w_out, 1, 2)
    first = call_choose(set_own[:3], set_other[:3], w_in, w_out_t)
    second = call_choose(set_own[3:], set_other[3:], w_in, w_out_t)

    arrays = (
        proj_w.T,
        tower_w,
        jnp.swapaxes(gate_top, 1, 2).reshape(2 * DOM, width),
        jnp.swapaxes(gate_shared, 1, 2).reshape(S * DOM, width),
        jnp.swapaxes(gate_domain, 1, 2).reshape(K * DOM, width),
        out_bias,
        ln_gain,
        ln_shift,
        proj_b[None],
        in_bias,
        tower_b,
        tower_out,
    )
    first_z = box.line(first)
    pack = call_pack(*step(arrays, first_z[0])[0])
    pack_z = box.line((pack, pack))
    first, first_z, second = step(first, first_z, second)

    def along_z(shard, found):
        found = box.in_line(shard[0], found, role, 2)
        return jnp.stack([b[0] for b in found]), jnp.stack([b[1] for b in found])

    first_i, first_o = along_z(first, first_z)
    first_iy, first_ox = box.pieces(first_i, "y"), box.pieces(first_o, "x")
    second_z = box.line(second)
    pack = step(jnp.concatenate(box.in_line(pack, pack_z, role, 0)), second_z[0])[0]
    pack = jnp.concatenate(box.gather_plane(pack), axis=0).reshape(places, 1, width, PACK)
    event_rows = jnp.concatenate(
        [domain.astype(f32).T, labels.astype(f32)[None], jnp.zeros((6, rows), f32)]
    )
    event_rows = jnp.where(at_home, event_rows, box.to_partner(event_rows, True))
    ids = event_rows[0]
    onehot = (ids[None, :] == jnp.arange(DOM, dtype=f32)[:, None]).astype(f32)
    rank = jnp.cumsum(onehot, axis=1)
    counts = rank[:, -1]
    ends = jnp.cumsum(counts)
    starts = ends - counts
    position = jnp.sum(onehot * (rank + starts[:, None]), axis=0) - 1.0
    embeds_in = box.to_partner(step(embeds, event_rows)[0], True)
    first_i, first_o, first_iy, first_ox, second, second_z, starts, ends, position = step(
        first_i, first_o, first_iy, first_ox, second, second_z, starts, ends, position
    )

    small = in_order(core, pack, swap_cores(pack), 1).reshape(D, PACK)
    first_i = jnp.stack([first_i] + first_iy)
    first_o = jnp.stack([first_o] + first_ox)
    first_ix, first_oy = box.pieces(first_i, "x"), box.pieces(first_o, "y")
    second_i, second_o = along_z(second, second_z)
    second_iy, second_ox = box.pieces(second_i, "y"), box.pieces(second_o, "x")

    proj_t = small[:, :e_in]
    tower = small[:, e_in : e_in + DOM * TW]
    gates = small[:, e_in + DOM * TW :]
    picked = jnp.concatenate(
        [
            32 + set_own,
            44 + set_own,
            56 + set_own,
            jnp.array([68] + [128] * 5),
            69 + set_own,
            81 + set_own,
            93 + jnp.arange(4),
        ]
    )
    choose = (picked[:, None] == jnp.arange(128)[None, :]).astype(bf16)
    vec = nt(choose, gates)
    blocks = jnp.take(vec[24:].reshape(16, places, 2 * width), place_of, axis=1)
    bi = (
        blocks[:12]
        .reshape(2, LOCAL, places, 2, width)
        .transpose(1, 2, 3, 0, 4)
        .reshape(LOCAL, H)
    )
    bi = jnp.pad(bi, ((0, 2), (0, 0)))
    bi = jnp.where(core == 0, bi, jnp.concatenate([bi[:, HALF:], bi[:, :HALF]], axis=1))
    tower_vec = (
        blocks[12:]
        .reshape(DOM, places, 2, 2, width // 2)
        .transpose(3, 0, 1, 2, 4)
        .reshape(2, DOM * TW)
    )
    tower_vec = jnp.pad(tower_vec, ((0, 6), (0, 0)))

    table = jnp.concatenate([position[None], event_rows[1:]])
    start_i, end_i = starts.astype(jnp.int32), ends.astype(jnp.int32)
    empty = end_i == start_i
    low = jnp.where(empty, 0, start_i // TILE)
    high = jnp.where(empty, 0, (end_i + TILE - 1) // TILE)
    domains = jnp.arange(DOM, dtype=jnp.int32)
    device = (2 * box.ahead()[:, None, None] + jnp.arange(2)[None, :, None]).astype(jnp.int32)
    unit = jnp.arange(width, dtype=jnp.int32)[None, None, :]
    narrow = width // 2
    lanes = [device * 2 * width + unit, device * 2 * width + width + unit]
    lanes += [d * TW + device * narrow + unit % narrow for d in range(DOM)]
    lanes += [jnp.broadcast_to(unit // narrow, (places, 2, width))] * 2
    lanes = jnp.stack([jnp.broadcast_to(v, (places, 2, width)).reshape(D) for v in lanes])

    ints = jnp.concatenate(
        [
            jnp.where(role == 0, low[::-1], low),
            jnp.where(role == 0, high[::-1], high),
            role[None],
            jnp.where(role == 0, DOM - 1 - domains, domains),
            start_i,
            end_i,
            core[None],
            jnp.zeros((2,), jnp.int32),
        ]
    )
    loss_weight = 1.0 - (1.0 - FROZEN_SHARE) * frozen.astype(f32)
    floats = jnp.concatenate([loss_weight, tower_out_b.astype(f32)])
    embeds = jnp.where(at_home, embeds, embeds_in)
    events, x, mix, cols, probs = call_prepare(ints, floats, table, embeds, proj_t, gates, vec)
    (
        first_i, first_o, first_ix, first_oy, second_i, second_o, second_iy, second_ox,
        ints, events, x, mix, cols, probs, vec, bi, tower, tower_vec, lanes,
    ) = step(
        first_i, first_o, first_ix, first_oy, second_i, second_o, second_iy, second_ox,
        ints, events, x, mix, cols, probs, vec, bi, tower, tower_vec, lanes,
    )

    def pieces(i, ix, o, oy):
        own = [i] + ix + [o] + oy
        return own + [swap_cores(w) for w in own]

    second_i = jnp.stack([second_i] + second_iy)
    second_o = jnp.stack([second_o] + second_ox)
    second_ix, second_oy = box.pieces(second_i, "x"), box.pieces(second_o, "y")
    weights = {0: pieces(first_i, first_ix, first_o, first_oy)}
    cols, mix, norms = call_forward((0, 1, 2), False, ints, x, weights, bi, vec, cols, mix, {})
    second_ix, second_oy, cols, mix = step(second_ix, second_oy, cols, mix)
    weights[1] = pieces(second_i, second_ix, second_o, second_oy)
    cols, mix, norms = call_forward((3, 4), False, ints, x, weights, bi, vec, cols, mix, norms)
    give_mix = half(mix, 1 - role).astype(bf16)
    give_mix, mix = step(give_mix, mix)
    other_mix = box.send(give_mix, flip=1)
    cols, mix, norms = call_forward(
        tuple(range(LOCAL)), True, ints, x, weights, bi, vec, cols, mix, norms
    )
    row_out, grad_block, grad_low, d_tower, d_tower_vec, d_logit_bias = call_tower(
        ints, mix, other_mix, cols, tower, tower_vec
    )

    box_shape = (nx, ny, nz, 2, 2 * width, HALF)

    def both_cores(keeps, gives):
        def one(which):
            added = total(keeps[0][:, which], [a[:, which] for a in keeps[1:] + gives])
            return added.astype(bf16).reshape((-1,) + box_shape)

        return one(0), one(1)

    class Scatter:
        def __init__(self, *parts):
            i, o = [jnp.concatenate(p) for p in zip(*parts)]
            i, o = [i[:, k] for k in range(nx)], [o[:, :, k] for k in range(ny)]
            self.state = (i[0], o[0], box.hand_out(i, "x"), box.hand_out(o, "y"))

        def second(self):
            i, o, i_in, o_in = self.state
            i, o = total(i, i_in).astype(bf16), total(o, o_in).astype(bf16)
            i, o = [i[:, k] for k in range(ny)], [o[:, k] for k in range(nx)]
            self.state = (i[0], o[0], box.hand_out(i, "y"), box.hand_out(o, "x"))

        def third(self):
            i, o, i_in, o_in = self.state
            both = jnp.stack([total(i, i_in).astype(bf16), total(o, o_in).astype(bf16)])
            both = [both[:, :, k] for k in range(nz)]
            self.state = (both[0], box.hand_out(both, "z"))

        def fourth(self):
            both = total(*self.state)
            mine = lax.dynamic_index_in_dim(both, role, 2, keepdims=False)
            other = lax.dynamic_index_in_dim(both, 1 - role, 2, keepdims=False).astype(bf16)
            self.state = (mine, box.send(other, flip=1))

    def sync(scatters, *values):
        states, values = step([c.state for c in scatters], values)
        for c, state in zip(scatters, states):
            c.state = state
        return values

    common = (ints, x)
    shared = (norms, weights, bi, vec)
    grad_in = box.send(grad_low, flip=1)
    cols, back, keep_a, give_a, *sums = call_backward(
        (0, 1), ("own",), *common, [grad_low], *shared, cols, None
    )
    d_logit_bias = d_logit_bias + swap_cores(d_logit_bias)
    d_logit_bias = box.same_sum(box.same_sum(d_logit_bias, "y"), "x")
    grad_in, cols, back, keep_a, give_a, sums, d_logit_bias = step(
        grad_in, cols, back, keep_a, give_a, sums, d_logit_bias
    )
    give_a = swap_cores(give_a)
    cols, back, keep_b, give_b, *sums_0 = call_backward(
        (0, 1), ("other",), *common, [grad_in], *shared, cols, ("fresh", back), sums
    )
    d_logit_bias = box.same_sum(box.same_sum(d_logit_bias, "flip"), "z")
    cols, back, keep_a, give_a, keep_b, give_b, d_logit_bias = step(
        cols, back, keep_a, give_a, keep_b, give_b, d_logit_bias
    )
    give_b = swap_cores(give_b)
    grads = [grad_low, grad_in]
    cols, back, keep_c, give_c, *sums_1 = call_backward(
        (2,), ("own", "other"), *common, grads, *shared, cols, ("add", back)
    )
    cols, back, keep_b, give_b, keep_c, give_c, row_out, d_logit_bias = step(
        cols, back, keep_b, give_b, keep_c, give_c, row_out, d_logit_bias
    )
    give_c = swap_cores(give_c)
    ab = both_cores([keep_a, keep_b], [give_a, give_b])
    give_c, keep_c, ab, cols = step(give_c, keep_c, ab, cols)
    c0 = Scatter(ab, both_cores([keep_c], [give_c]))
    cols, back, keep_d, give_d, *sums_2 = call_backward(
        (3, 4), ("own", "other"), *common, grads, *shared, cols, ("add", back)
    )
    rows_in = box.to_partner(row_out, False)
    cols, back, keep_d, give_d, rows_in = sync([c0], cols, back, keep_d, give_d, rows_in)
    c0.second()
    give_d = swap_cores(give_d)
    cols, back, _ = step(cols, back, c0.state[:2])
    g_other, g_other_low, d_gate_a = call_gate(False, ints, back, cols, probs, x, gates)
    back_other = box.to_partner(g_other_low, False)
    cols, back, _ = step(cols, back, g_other_low)
    cols, back, keep_e, give_e, *sums_3 = call_backward(
        (5,), ("own",), *common, [grad_low], *shared, cols, ("add", back)
    )
    cd = both_cores([keep_d], [give_d])
    cols, back, back_other, cd, keep_e, give_e = sync(
        [c0], cols, back, back_other, cd, keep_e, give_e
    )
    give_e = swap_cores(give_e)
    c0.third()
    c1 = Scatter(cd, both_cores([keep_e], [give_e]))
    g_own, g_own_low, d_gate_b = call_gate(True, ints, back, cols, probs, x, gates)
    back_own = box.to_partner(g_own_low, False)
    back_own, g_own, d_gate_b = sync([c0, c1], back_own, g_own, d_gate_b)
    c0.fourth()
    c1.second()
    back_own, _ = step(back_own, c1.state[:2])
    grad_events, d_small = call_finish(
        ints, grad_block, grad_in, g_own, g_other, back_own, back_other, events, proj_t, d_tower,
        d_gate_a, d_gate_b, lanes, d_tower_vec, [sums_0, sums_1, sums_2, sums_3],
    )
    grad_events, d_small = sync([c0, c1], grad_events, d_small)
    c1.third()
    d_small, _ = step(d_small, c1.state[0])
    d_small = d_small.reshape(places, 2, width, PACK)
    d_other = swap_cores(lax.dynamic_index_in_dim(d_small, 1 - core, 1, keepdims=False))
    d_mine = total(lax.dynamic_index_in_dim(d_small, core, 1, keepdims=False), [d_other])
    d_mine = d_mine.astype(bf16).reshape(nx * ny, nz, 2, width, PACK)
    d_parts = [d_mine[k] for k in range(nx * ny)]
    d_in = box.hand_out_plane(d_parts)
    order = position[None, :] == jnp.arange(rows, dtype=f32)[:, None]
    grad_embeds = lax.dot_general(
        order.astype(bf16), grad_events, (((0,), (0,)), ((), ())), preferred_element_type=f32
    ).astype(bf16)
    predicted = in_order(role, row_out, rows_in, 1)
    predictions = jnp.sum(jnp.where(order, predicted[0][:, None], 0.0), axis=0)
    predictions = jnp.broadcast_to(predictions[None], (8, rows))
    d_mine, d_in, grad_embeds, predictions = sync(
        [c0, c1], d_parts[0], d_in, grad_embeds, predictions
    )
    c1.fourth()
    d_mine = total(d_mine, d_in).astype(bf16)
    same = [lax.dynamic_index_in_dim(d_mine[k], role, 0, keepdims=False) for k in range(nz)]
    flip = [lax.dynamic_index_in_dim(d_mine[k], 1 - role, 0, keepdims=False) for k in range(nz)]
    d_in = box.hand_out(same, "z") + box.hand_out_flip(flip)
    grad_embeds = jnp.where(at_home, grad_embeds, swap_cores(grad_embeds))
    predictions = jnp.where(at_home, predictions, swap_cores(predictions))[0]
    d_in, grad_embeds, predictions = sync([c1], d_in, grad_embeds, predictions)
    (
        proj_grad, tower_grad, top, shared_gate, domain_gate, proj_b_grad, in_bias_grad, tower_b_grad,
        tower_out_grad, *vectors,
    ) = call_small([same[0]] + d_in)
    grad_w_in, grad_w_out = call_place(
        ints, [c0.state[0], c1.state[0]], [c0.state[1], c1.state[1]]
    )
    return (
        predictions,
        grad_embeds,
        proj_grad.T,
        proj_b_grad[0],
        grad_w_in,
        in_bias_grad,
        jnp.swapaxes(grad_w_out, 1, 2),
        *vectors,
        jnp.swapaxes(top, 1, 2),
        jnp.swapaxes(shared_gate, 1, 2),
        jnp.swapaxes(domain_gate, 1, 2),
        tower_grad,
        tower_b_grad,
        tower_out_grad,
        d_logit_bias[0, :DOM],
    )


def solution(mesh):
    both = ("dp", "tensor")
    in_specs = (
        P("dp", None),
        P("dp", None),
        P(),
        P("dp"),
        P(None, both),
        P(both),
        P(None, "dp", "tensor"),
        P(None, both),
        P(None, "tensor", "dp"),
        P(None, both),
        P(None, both),
        P(None, both),
        P(None, both, None),
        P(None, both, None),
        P(None, both, None),
        P(None, both, None),
        P(None, both),
        P(None, both),
        P(),
    )
    out_specs = (
        P("dp"),
        P("dp", None),
        P(None, both),
        P(both),
        P(None, "dp", "tensor"),
        P(None, both),
        P(None, "tensor", "dp"),
        P(None, both),
        P(None, both),
        P(None, both),
        P(None, both, None),
        P(None, both, None),
        P(None, both, None),
        P(None, both, None),
        P(None, both),
        P(None, both),
        P(),
    )
    return jax.shard_map(
        functools.partial(per_device, Box(mesh.shape["dp"])),
        mesh=mesh,
        in_specs=in_specs,
        out_specs=out_specs,
        check_vma=False,
    )
```

time: 453 us -> 372 us (0.82)
  local copies, waits for them, and re-layouts: 67.7 us -> 20.3 us
  starting transfers between devices: 92.8 us -> 71.4 us
  other arithmetic: 48.5 us -> 36.4 us
  Pallas kernels: 148 us -> 156 us
  waiting for transfers between devices: 82 us -> 75.2 us
    unnamed x165 -> x167, local copies, waits for them, and re-layouts: 32.2 us -> 11.4 us
    ppermute x48 -> x44, starting transfers between devices: 72.9 us -> 55.4 us  [send(): return lax.ppermute(values, 'dp', pairs)]
    ppermute x5, starting transfers between devices: 17.7 us -> 10.1 us  [to_partner(): return lax.ppermute(values, ('dp', 'tensor'), pairs)]
    another operation x18 -> x12, other arithmetic: 14.3 us -> 6.76 us  [the longest x2 2.23 us: full(): wo = jnp.stack([o] + oy, axis=2).reshape(count, D, HALF)]
    ppermute x48 -> x44, waiting for transfers between devices: 73 us -> 66.1 us  [send(): return lax.ppermute(values, 'dp', pairs)]
    slice x16 -> x6, local copies, waits for them, and re-layouts: 6.72 us -> 0.34 us  [the longest x5 2.14 us: per_device(): columns[low:low + DOM * size].reshape(DOM, size, width)]
    pallas_call x13 -> x11, Pallas kernels: 115 us -> 121 us  [the longest x5 75.1 us: call_backward(): pl.pallas_call(functools.partial(backward_kernel, experts, halves, mode =...]
    another operation x12 -> x3, local copies, waits for them, and re-layouts: 5.09 us -> 0.13 us  [the longest x2 0.13 us: per_device(): jnp.stack([jnp.broadcast_to(v, (places, 2, width)).reshape(D) for v in la...]
  transfers between devices with their start and end apart: 68 -> 67, of which waited for: 21 -> 21; matrix products, arithmetic and copies ran while one was open for 18% -> 12% of each run, Pallas kernels for 28% -> 37%
where the time goes in v2:
time: 372 us; the launch traced here: 367 us
  Pallas kernels  156 us (42%)
  waiting for transfers between devices  75.2 us (20%)
  starting transfers between devices  71.4 us (19%)
  other arithmetic  36.4 us (10%)
  local copies, waits for them, and re-layouts  20.3 us (5%)
  matrix products  4.47 us (1%)
    pallas_call x5, Pallas kernels, call_backward(): pl.pallas_call(functools.partial(backward_kernel, experts, halves, mode =...  75.1 us
    ppermute x44, waiting for transfers between devices, send(): return lax.ppermute(values, 'dp', pairs)  66.1 us
    ppermute x44, starting transfers between devices, send(): return lax.ppermute(values, 'dp', pairs)  55.4 us
    pallas_call x3, Pallas kernels, call_forward(): pl.pallas_call(functools.partial(forward_kernel, experts, own, len(kept),...  39 us
    unnamed x167, local copies, waits for them, and re-layouts  11.4 us
    pallas_call x1, Pallas kernels, call_prepare(): pl.pallas_call(prepare_kernel, grid_spec=pltpu.PrefetchScalarGridSpec(num...  11.2 us
    pallas_call x1, Pallas kernels, call_finish(): pl.pallas_call(finish_kernel, grid_spec=pltpu.PrefetchScalarGridSpec(num_...  10.8 us
    ppermute x5, starting transfers between devices, to_partner(): return lax.ppermute(values, ('dp', 'tensor'), pairs)  10.1 us
  transfers between devices with their start and end apart: 67, of which 21 were waited for; matrix products, arithmetic and copies ran while one was open for 12% of the time, Pallas kernels for 37%

profile of v2, /device:TPU:0, one launch (start us, length us, event | category | flops | bytes accessed | tf_op | source)
XLA Modules:
  0.0 366.9 jit_solution(15010985044289917328)
XLA Ops:
  4.4 3.1 collective-permute-start.1
  11.6 3.7 %collective-permute-start.8 = (f32[8,1536]{1,0:T(8,128)S(1)}, f32[8,1536]{1,0:T(8,128)S(1)}, u32[]{:S(2)}, u32[]{:S(2)}) collective-permute-start(f32[8,1536]{1,0:T(8,128)S(1)} %maximum_maximum_fusion), channel_id=1, source_target_pairs={{0,8},{2,10},{4,12},{6,14},{9,1},{11,3},{13,5},{15,7},{16,24},{18,... | collective-permute-start | bytes 147464 | tf_op jit(solution)/shard_map/ppermute | solution.py:74
  22.8 4.5 %collective-permute-done = bf16[2,3,32,512]{3,2,1,0:T(8,128)(2,1)S(1)} collective-permute-done((bf16[2,3,32,512]{3,2,1,0:T(8,128)(2,1)S(1)}, bf16[2,3,32,512]{3,2,1,0:T(8,128)(2,1)S(1)}, u32[]{:S(2)}, u32[]{:S(2)}) %collective-permute-start) | collective-permute-done | bytes 196640 | tf_op jit(solution)/shard_map/ppermute | solution.py:66
  40.2 11.3 %collective-permute-done.5 = bf16[2,3,32,512]{3,2,1,0:T(8,128)(2,1)S(1)} collective-permute-done((bf16[2,3,32,512]{3,2,1,0:T(8,128)(2,1)S(1)}, bf16[2,3,32,512]{3,2,1,0:T(8,128)(2,1)S(1)}, u32[]{:S(2)}, u32[]{:S(2)}) %collective-permute-start.5) | collective-permute-done | bytes 196640 | tf_op jit(solution)/shard_map/ppermute | solution.py:66
  65.5 3.6 collective-permute-done.19
  81.3 3.0 broadcast_select_fusion.1.embeds_ref
  84.4 11.2 %prepare.1 = (bf16[1536,640]{1,0:T(8,128)(2,1)S(1)}, bf16[1536,512]{1,0:T(8,128)(2,1)S(1)}, f32[1536,512]{1,0:T(8,128)}, f32[1536,128]{1,0:T(8,128)S(1)}, f32[8,1536]{1,0:T(8,128)S(1)}) custom-call(s32[24]{0:T(128)S(1)} %concatenate.93.ints, f32[8]{0:T(128)S(1)} %pad_maximum_fusion.19.floats, f32[8,1536]{1,0:T(8,128)S(1)} %pad_maximum_fusion.16.rows_ref, ...), custom_call_target="tpu_custom_call" | custom-call | flops 4026531840 | bytes 12000000 | tf_op jit(solution)/shard_map/prepare/pallas_call | solution.py:773
  104.8 11.0 %experts_forward.3 = (f32[1536,128]{1,0:T(8,128)S(1)}, f32[1536,512]{1,0:T(8,128)}, bf16[3,1536,512]{2,1,0:T(8,128)(2,1)}) custom-call(s32[24]{0:T(128)S(1)} %concatenate.93.ints, bf16[1536,512]{1,0:T(8,128)(2,1)} %copy-done, bf16[2,2,3,64,512]{4,3,2,1,0:T(8,128)(2,1)} %pad_maximum_fusion.5.refs_0_.refs_2_.refs_3_, ...), custom_call_target="tpu_custom_call", output_to_operand_aliasing={{0}: (12, {}), {1}: (13, {})} | custom-call | flops 4831838208 | bytes 12000000 | tf_op jit(solution)/shard_map/experts_forward/pallas_call | solution.py:839
  115.8 4.0 %collective-permute-done.26.refs_3_.refs_11_.refs_6_.refs_5_ = bf16[2,2,3,64,512]{4,3,2,1,0:T(8,128)(2,1)S(1)} collective-permute-done((bf16[2,2,3,64,512]{4,3,2,1,0:T(8,128)(2,1)S(1)}, bf16[2,2,3,64,512]{4,3,2,1,0:T(8,128)(2,1)S(1)}, u32[]{:S(2)}, u32[]{:S(2)}) %collective-permute-start.26) | collective-permute-done | bytes 786464 | tf_op jit(solution)/shard_map/ppermute | solution.py:66
  121.8 3.2 collective-permute-done.28.refs_5_.refs_13_.refs_8_.refs_7_
  125.0 9.2 %experts_forward.4 = (f32[1536,128]{1,0:T(8,128)S(1)}, f32[1536,512]{1,0:T(8,128)}, bf16[3,1536,512]{2,1,0:T(8,128)(2,1)}) custom-call(s32[24]{0:T(128)S(1)} %concatenate.93.ints, bf16[1536,512]{1,0:T(8,128)(2,1)} %copy-done, ...), custom_call_target="tpu_custom_call", output_to_operand_aliasing={{0}: (12, {}), {1}: (13, {})} | custom-call | flops 1610612736 | bytes 12000000 | tf_op jit(solution)/shard_map/experts_forward/pallas_call | solution.py:839
  136.0 18.8 %experts_forward.5 = (f32[1536,128]{1,0:T(8,128)S(1)}, f32[1536,512]{1,0:T(8,128)}, bf16[3,1536,512]{2,1,0:T(8,128)(2,1)}, bf16[3,1536,512]{2,1,0:T(8,128)(2,1)}) custom-call(s32[24]{0:T(128)S(1)} %concatenate.93.ints, bf16[1536,512]{1,0:T(8,128)(2,1)} %copy-done, ...), custom_call_target="tpu_custom_call", output_to_operand_aliasing={{0}: (20, {}), {1}: (21, {}), {2}: (22, {}), {3}: (23, {})} | custom-call | flops 4831838208 | bytes 12000000 | tf_op jit(solution)/shard_map/experts_forward/pallas_call | solution.py:839
  155.5 9.5 %towers.1 = (f32[8,768]{1,0:T(8,128)S(1)}, f32[768,512]{1,0:T(8,128)S(1)}, bf16[768,512]{1,0:T(8,128)(2,1)S(1)}, f32[512,1024]{1,0:T(8,128)}, f32[8,1024]{1,0:T(8,128)S(1)}, /*index=5*/f32[8,128]{1,0:T(8,128)S(1)}) custom-call(s32[24]{0:T(128)S(1)} %concatenate.93.ints, f32[1536,512]{1,0:T(8,128)} %get-tuple-element.303.mix_ref, ...), custom_call_target="tpu_custom_call" | custom-call | flops 2415919104 | bytes 10000000 | tf_op jit(solution)/shard_map/towers/pallas_call | solution.py:940
  172.5 17.2 %experts_backward.5 = (f32[1536,128]{1,0:T(8,128)S(1)}, f32[1536,512]{1,0:T(8,128)}, bf16[2,2,512,512]{3,2,1,0:T(8,128)(2,1)}, bf16[2,2,512,512]{3,2,1,0:T(8,128...) custom-call(s32[24]{0:T(128)S(1)} %concatenate.93.ints, ...), custom_call_target="tpu_custom_call", output_to_operand_aliasing={{0}: (14, {})} | custom-call | flops 8053063680 | bytes 20000000 | tf_op jit(solution)/shard_map/experts_backward/pallas_call | solution.py:902
  193.9 17.6 %experts_backward.6 = (f32[1536,128]{1,0:T(8,128)S(1)}, f32[1536,512]{1,0:T(8,128)}, bf16[2,2,512,512]{3,2,1,0:T(8,128)(2,1)}, bf16[2,2,512,512]{3,2,1,0:T(8,128...) custom-call(s32[24]{0:T(128)S(1)} %concatenate.93.ints, ...), custom_call_target="tpu_custom_call", output_to_operand_aliasing={{0}: (14, {}), {1}: (15, {})} | custom-call | flops 8053063680 | bytes 20000000 | tf_op jit(solution)/shard_map/experts_backward/pallas_call | solution.py:902
  211.6 9.6 %experts_backward.7 = (f32[1536,128]{1,0:T(8,128)S(1)}, f32[1536,512]{1,0:T(8,128)}, bf16[1,2,512,512]{3,2,1,0:T(8,128)(2,1)}, bf16[1,2,512,512]{3,2,1,0:T(8,128...) custom-call(s32[24]{0:T(128)S(1)} %concatenate.93.ints, ...), custom_call_target="tpu_custom_call", output_to_operand_aliasing={{0}: (15, {}), {1}: (16, {})} | custom-call | flops 4026531840 | bytes 20000000 | tf_op jit(solution)/shard_map/experts_backward/pallas_call | solution.py:902
  226.1 3.7 %collective-permute-start.41 = (bf16[3,2,2,2,32,512]{5,4,0,3,2,1:T(8,128)(2,1)S(1)}, bf16[3,2,2,2,32,512]{5,4,0,3,2,1:T(8,128)(2,1)S(1)}, u32[]{:S(2)}, u32[]{:S(2)}) collective-permute-start(bf16[3,2,2,2,32,512]{5,4,0,3,2,1:T(8,128)(2,1)S(1)} %get-tuple-element.476), channel_id=1, source_target_pairs={{0,2},{2,0},{4,6},{6,4},{8,10},{10,8},{12,14},{14,12},{16,18},{18,... | collective-permute-start | bytes 2359304 | tf_op jit(solution)/shard_map/ppermute | solution.py:66
  231.1 18.6 %experts_backward.8 = (f32[1536,128]{1,0:T(8,128)S(1)}, f32[1536,512]{1,0:T(8,128)}, bf16[2,2,512,512]{3,2,1,0:T(8,128)(2,1)}, bf16[2,2,512,512]{3,2,1,0:T(8,128...) custom-call(s32[24]{0:T(128)S(1)} %concatenate.93.ints, ...), custom_call_target="tpu_custom_call", output_to_operand_aliasing={{0}: (15, {}), {1}: (16, {})} | custom-call | flops 8053063680 | bytes 20000000 | tf_op jit(solution)/shard_map/experts_backward/pallas_call | solution.py:902
  262.0 12.1 %experts_backward.9 = (f32[1536,128]{1,0:T(8,128)S(1)}, f32[1536,512]{1,0:T(8,128)}, bf16[1,2,512,512]{3,2,1,0:T(8,128)(2,1)}, bf16[1,2,512,512]{3,2,1,0:T(8,128...) custom-call(s32[24]{0:T(128)S(1)} %concatenate.93.ints, ...), custom_call_target="tpu_custom_call", output_to_operand_aliasing={{0}: (14, {}), {1}: (15, {})} | custom-call | flops 4026531840 | bytes 20000000 | tf_op jit(solution)/shard_map/experts_backward/pallas_call | solution.py:902
  276.7 3.7 %gates.3 = (f32[768,512]{1,0:T(8,128)S(1)}, bf16[768,512]{1,0:T(8,128)(2,1)}, f32[512,128]{1,0:T(8,128)S(1)}) custom-call(s32[24]{0:T(128)S(1)} %concatenate.93.ints, f32[1536,512]{1,0:T(8,128)} %get-tuple-element.384.back_ref, f32[1536,128]{1,0:T(8,128)S(1)} %get-tuple-element.385.cols_ref, f32[8,1536]{1,0:T(8,128)S(1)} %get-tuple-element.366.prob_ref, ...), custom_call_target="tpu_custom_call" | custom-call | flops 201326592 | bytes 5000000 | tf_op jit(solution)/shard_map/gates/pallas_call | solution.py:504
  291.6 17.7 %collective-permute-done.48 = bf16[2,3,2,32,512]{4,3,1,0,2:T(8,128)(2,1)} collective-permute-done((bf16[2,3,2,32,512]{4,3,1,0,2:T(8,128)(2,1)}, bf16[2,3,2,32,512]{4,3,1,0,2:T(8,128)(2,1)}, u32[]{:S(2)}, u32[]{:S(2)}) %collective-permute-start.48) | collective-permute-done | bytes 393248 | tf_op jit(solution)/shard_map/ppermute | solution.py:66
  314.6 10.8 %finish.1 = (bf16[1536,640]{1,0:T(8,128)(2,1)}, bf16[512,1792]{1,0:T(8,128)(2,1)}) custom-call(s32[24]{0:T(128)S(1)} %concatenate.93.ints, f32[768,512]{1,0:T(8,128)S(1)} %copy-done.21, bf16[768,512]{1,0:T(8,128)(2,1)S(1)} %collective-permute-done.32.refs_0_.refs_1_.gb_in_ref, f32[768,512]{1,0:T(8,128)} %copy-done.23, f32[768,512]{1,0:T(8,128)} %copy-done.22, ...), custom_call_target="tpu_custom_call" | custom-call | flops 2013265920 | bytes 14000000 | tf_op jit(solution)/shard_map/finish/pallas_call | solution.py:614
  337.2 4.3 %fusion.2 = bf16[1536,640]{1,0:T(8,128)(2,1)S(1)} fusion(bf16[1536,640]{1,0:T(8,128)(2,1)S(1)} %copy-done.79, f32[1536]{0:T(1024)S(1)} %copy-done.75), kind=kOutput, calls=%fused_computation.5 | convolution fusion | flops 3023241216 | bytes 3938304 | tf_op jit(solution)/shard_map/dot_general | solution.py:1268
  341.4 9.6 %collective-permute-done.56 = bf16[2,3,2,32,512]{4,3,1,0,2:T(8,128)(2,1)S(1)} collective-permute-done((bf16[2,3,2,32,512]{4,3,1,0,2:T(8,128)(2,1)}, bf16[2,3,2,32,512]{4,3,1,0,2:T(8,128)(2,1)S(1)}, u32[]{:S(2)}, u32[]{:S(2)}) %collective-permute-start.56) | collective-permute-done | bytes 393248 | tf_op jit(solution)/shard_map/ppermute | solution.py:66
  (442 shorter events, 143.1 us)
Async XLA Ops:
  4.4 26.7 %collective-permute-start.1 = (bf16[2,3,32,512]{3,2,1,0:T(8,128)(2,1)S(1)}, bf16[2,3,32,512]{3,2,1,0:T(8,128)(2,1)S(1)}, u32[]{:S(2)}, u32[]{:S(2)}) collective-permute-start(bf16[2,3,32,512]{3,2,1,0:T(8,128)(2,1)S(1)} %get-tuple-element.239), channel_id=1, source_target_pairs={{0,8},{2,10},{4,12},{6,14},{8,0},{10,2},{12,4},{14,6},{16,24},{18,... | collective-permute-start | bytes 589832 | tf_op jit(solution)/shard_map/ppermute | solution.py:66
  7.4 23.6 %collective-permute-start.2 = (bf16[2,3,32,512]{3,2,1,0:T(8,128)(2,1)S(1)}, bf16[2,3,32,512]{3,2,1,0:T(8,128)(2,1)S(1)}, u32[]{:S(2)}, u32[]{:S(2)}) collective-permute-start(bf16[2,3,32,512]{3,2,1,0:T(8,128)(2,1)S(1)} %get-tuple-element.239), channel_id=1, source_target_pairs={{0,24},{2,26},{4,28},{6,30},{8,16},{10,18},{12,20},{14,22},{16,8},... | collective-permute-start | bytes 589832 | tf_op jit(solution)/shard_map/ppermute | solution.py:66
  31.0 23.0 %collective-permute-start.6 = (bf16[2,3,32,512]{3,2,1,0:T(8,128)(2,1)S(1)}, bf16[2,3,32,512]{3,2,1,0:T(8,128)(2,1)}, u32[]{:S(2)}, u32[]{:S(2)}) collective-permute-start(bf16[2,3,32,512]{3,2,1,0:T(8,128)(2,1)S(1)} %get-tuple-element.247), channel_id=1, source_target_pairs={{0,8},{2,10},{4,12},{6,14},{8,0},{10,2},{12,4},{14,6},{16,24},{18,... | collective-permute-start | bytes 589832 | tf_op jit(solution)/shard_map/ppermute | solution.py:66
  32.3 23.3 %collective-permute-start.7 = (bf16[2,3,32,512]{3,2,1,0:T(8,128)(2,1)S(1)}, bf16[2,3,32,512]{3,2,1,0:T(8,128)(2,1)}, u32[]{:S(2)}, u32[]{:S(2)}) collective-permute-start(bf16[2,3,32,512]{3,2,1,0:T(8,128)(2,1)S(1)} %get-tuple-element.247), channel_id=1, source_target_pairs={{0,24},{2,26},{4,28},{6,30},{8,16},{10,18},{12,20},{14,22},{16,8},... | collective-permute-start | bytes 589832 | tf_op jit(solution)/shard_map/ppermute | solution.py:66
  37.1 20.0 %collective-permute-start.4 = (bf16[2,3,64,512]{3,2,1,0:T(8,128)(2,1)S(1)}, bf16[2,3,64,512]{3,2,1,0:T(8,128)(2,1)S(1)}, u32[]{:S(2)}, u32[]{:S(2)}) collective-permute-start(bf16[2,3,64,512]{3,2,1,0:T(8,128)(2,1)S(1)} %pad_maximum_fusion.12), channel_id=1, source_target_pairs={{0,2},{2,0},{4,6},{6,4},{8,10},{10,8},{12,14},{14,12},{16,18},{18,... | collective-permute-start | bytes 1179656 | tf_op jit(solution)/shard_map/ppermute | solution.py:66
  51.5 29.8 %collective-permute-start.13 = (bf16[1536,640]{1,0:T(8,128)(2,1)}, bf16[1536,640]{1,0:T(8,128)(2,1)}, u32[]{:S(2)}, u32[]{:S(2)}) collective-permute-start(bf16[1536,640]{1,0:T(8,128)(2,1)} %param.21), channel_id=1, source_target_pairs={{0,8},{2,10},{4,12},{6,14},{9,1},{11,3},{13,5},{15,7},{16,24},{18,... | collective-permute-start | bytes 5898248 | tf_op jit(solution)/shard_map/ppermute | solution.py:74
  60.3 37.7 %collective-permute-start.12 = (bf16[2,3,64,512]{3,2,1,0:T(8,128)(2,1)S(1)}, bf16[2,3,64,512]{3,2,1,0:T(8,128)(2,1)}, u32[]{:S(2)}, u32[]{:S(2)}) collective-permute-start(bf16[2,3,64,512]{3,2,1,0:T(8,128)(2,1)S(1)} %pad_maximum_fusion.14), channel_id=1, source_target_pairs={{0,2},{2,0},{4,6},{6,4},{8,10},{10,8},{12,14},{14,12},{16,18},{18,... | collective-permute-start | bytes 1179656 | tf_op jit(solution)/shard_map/ppermute | solution.py:66
  64.0 34.0 %collective-permute-start.11 = (bf16[2,3,64,512]{3,2,1,0:T(8,128)(2,1)S(1)}, bf16[2,3,64,512]{3,2,1,0:T(8,128)(2,1)}, u32[]{:S(2)}, u32[]{:S(2)}) collective-permute-start(bf16[2,3,64,512]{3,2,1,0:T(8,128)(2,1)S(1)} %pad_maximum_fusion.13), channel_id=1, source_target_pairs={{0,4},{2,6},{4,0},{6,2},{8,12},{10,14},{12,8},{14,10},{16,20},{18,... | collective-permute-start | bytes 1179656 | tf_op jit(solution)/shard_map/ppermute | solution.py:66
  71.4 26.6 %collective-permute-start.10 = (bf16[2,2,3,64,512]{4,3,2,1,0:T(8,128)(2,1)}, bf16[2,2,3,64,512]{4,3,2,1,0:T(8,128)(2,1)}, u32[]{:S(2)}, u32[]{:S(2)}) collective-permute-start(bf16[2,2,3,64,512]{4,3,2,1,0:T(8,128)(2,1)} %pad_maximum_fusion.6.refs_2_.refs_4_.refs_5_), channel_id=1, source_target_pairs={{0,4},{2,6},{4,0},{6,2},{8,12},{10,14},{12,8},{14,10},{16,20},{18,... | collective-permute-start | bytes 2359304 | tf_op jit(solution)/shard_map/ppermute | solution.py:66
  74.0 24.0 %collective-permute-start.9 = (bf16[2,2,3,64,512]{4,3,2,1,0:T(8,128)(2,1)}, bf16[2,2,3,64,512]{4,3,2,1,0:T(8,128)(2,1)}, u32[]{:S(2)}, u32[]{:S(2)}) collective-permute-start(bf16[2,2,3,64,512]{4,3,2,1,0:T(8,128)(2,1)} %pad_maximum_fusion.5.refs_0_.refs_2_.refs_3_), channel_id=1, source_target_pairs={{0,2},{2,0},{4,6},{6,4},{8,10},{10,8},{12,14},{14,12},{16,18},{18,... | collective-permute-start | bytes 2359304 | tf_op jit(solution)/shard_map/ppermute | solution.py:66
  100.2 19.6 %collective-permute-start.26 = (bf16[2,2,3,64,512]{4,3,2,1,0:T(8,128)(2,1)S(1)}, bf16[2,2,3,64,512]{4,3,2,1,0:T(8,128)(2,1)S(1)}, u32[]{:S(2)}, u32[]{:S(2)}) collective-permute-start(bf16[2,2,3,64,512]{4,3,2,1,0:T(8,128)(2,1)S(1)} %pad_maximum_fusion.8.refs_2_.refs_10_.refs_5_.refs_4_), channel_id=1, source_target_pairs={{0,4},{2,6},{4,0},{6,2},{8,12},{10,14},{12,8},{14,10},{16,20},{18,... | collective-permute-start | bytes 2359304 | tf_op jit(solution)/shard_map/ppermute | solution.py:66
  101.8 19.4 %collective-permute-start.25 = (bf16[2,2,3,64,512]{4,3,2,1,0:T(8,128)(2,1)S(1)}, bf16[2,2,3,64,512]{4,3,2,1,0:T(8,128)(2,1)}, u32[]{:S(2)}, u32[]{:S(2)}) collective-permute-start(bf16[2,2,3,64,512]{4,3,2,1,0:T(8,128)(2,1)S(1)} %pad_maximum_fusion.7.refs_0_.refs_8_.refs_3_.refs_2_), channel_id=1, source_target_pairs={{0,2},{2,0},{4,6},{6,4},{8,10},{10,8},{12,14},{14,12},{16,18},{18,... | collective-permute-start | bytes 2359304 | tf_op jit(solution)/shard_map/ppermute | solution.py:66
  135.8 19.6 %collective-permute-start.31 = (bf16[768,512]{1,0:T(8,128)(2,1)S(1)}, bf16[768,512]{1,0:T(8,128)(2,1)S(1)}, u32[]{:S(2)}, u32[]{:S(2)}) collective-permute-start(bf16[768,512]{1,0:T(8,128)(2,1)S(1)} %dynamic-slice_convert_fusion), channel_id=1, source_target_pairs={{0,8},{2,10},{4,12},{6,14},{8,0},{10,2},{12,4},{14,6},{16,24},{18,... | collective-permute-start | bytes 2359304 | tf_op jit(solution)/shard_map/ppermute | solution.py:66
  166.1 23.7 %collective-permute-start.32 = (bf16[768,512]{1,0:T(8,128)(2,1)S(1)}, bf16[768,512]{1,0:T(8,128)(2,1)S(1)}, u32[]{:S(2)}, u32[]{:S(2)}) collective-permute-start(bf16[768,512]{1,0:T(8,128)(2,1)S(1)} %get-tuple-element.308.refs_0_), channel_id=1, source_target_pairs={{0,8},{2,10},{4,12},{6,14},{8,0},{10,2},{12,4},{14,6},{16,24},{18,... | collective-permute-start | bytes 2359304 | tf_op jit(solution)/shard_map/ppermute | solution.py:66
  189.8 21.6 %collective-permute-start.36 = (bf16[2,2,512,512]{3,2,1,0:T(8,128)(2,1)}, bf16[2,2,512,512]{3,2,1,0:T(8,128)(2,1)S(1)}, u32[]{:S(2)}, u32[]{:S(2)}) collective-permute-start(bf16[2,2,512,512]{3,2,1,0:T(8,128)(2,1)} %get-tuple-element.325), channel_id=1, source_target_pairs={{0,1},{1,0},{2,3},{3,2},{4,5},{5,4},{6,7},{7,6},{8,9},{9,8},{10,11... | collective-permute-start | bytes 6291464 | tf_op jit(solution)/shard_map/ppermute | solution.py:138
  224.6 25.2 %collective-permute-start.42 = (bf16[3,2,2,2,32,512]{5,4,0,3,2,1:T(8,128)(2,1)S(1)}, bf16[3,2,2,2,32,512]{5,4,0,3,2,1:T(8,128)(2,1)S(1)}, u32[]{:S(2)}, u32[]{:S(2)}) collective-permute-start(bf16[3,2,2,2,32,512]{5,4,0,3,2,1:T(8,128)(2,1)S(1)} %bitcast.193), channel_id=1, source_target_pairs={{0,4},{2,6},{4,0},{6,2},{8,12},{10,14},{12,8},{14,10},{16,20},{18,... | collective-permute-start | bytes 2359304 | tf_op jit(solution)/shard_map/ppermute | solution.py:66
  226.1 23.8 %collective-permute-start.41 = (bf16[3,2,2,2,32,512]{5,4,0,3,2,1:T(8,128)(2,1)S(1)}, bf16[3,2,2,2,32,512]{5,4,0,3,2,1:T(8,128)(2,1)S(1)}, u32[]{:S(2)}, u32[]{:S(2)}) collective-permute-start(bf16[3,2,2,2,32,512]{5,4,0,3,2,1:T(8,128)(2,1)S(1)} %get-tuple-element.476), channel_id=1, source_target_pairs={{0,2},{2,0},{4,6},{6,4},{8,10},{10,8},{12,14},{14,12},{16,18},{18,... | collective-permute-start | bytes 2359304 | tf_op jit(solution)/shard_map/ppermute | solution.py:66
  229.8 20.1 %collective-permute-start.43 = (f32[8,768]{1,0:T(8,128)S(1)}, f32[8,768]{1,0:T(8,128)S(1)}, u32[]{:S(2)}, u32[]{:S(2)}) collective-permute-start(f32[8,768]{1,0:T(8,128)S(1)} %get-tuple-element.357), channel_id=1, source_target_pairs={{1,9},{3,11},{5,13},{7,15},{8,0},{10,2},{12,4},{14,6},{17,25},{19,... | collective-permute-start | bytes 73736 | tf_op jit(solution)/shard_map/ppermute | solution.py:74
  250.5 23.7 %collective-permute-start.47 = (bf16[2,2,512,512]{3,2,1,0:T(8,128)(2,1)}, bf16[2,2,512,512]{3,2,1,0:T(8,128)(2,1)}, u32[]{:S(2)}, u32[]{:S(2)}) collective-permute-start(bf16[2,2,512,512]{3,2,1,0:T(8,128)(2,1)} %get-tuple-element.373), channel_id=1, source_target_pairs={{0,1},{1,0},{2,3},{3,2},{4,5},{5,4},{6,7},{7,6},{8,9},{9,8},{10,11... | collective-permute-start | bytes 6291464 | tf_op jit(solution)/shard_map/ppermute | solution.py:138
  280.4 28.9 %collective-permute-start.52 = (bf16[768,512]{1,0:T(8,128)(2,1)}, bf16[768,512]{1,0:T(8,128)(2,1)S(1)}, u32[]{:S(2)}, u32[]{:S(2)}) collective-permute-start(bf16[768,512]{1,0:T(8,128)(2,1)} %get-tuple-element.386), channel_id=1, source_target_pairs={{1,9},{3,11},{5,13},{7,15},{8,0},{10,2},{12,4},{14,6},{17,25},{19,... | collective-permute-start | bytes 2359304 | tf_op jit(solution)/shard_map/ppermute | solution.py:74
  283.1 26.1 %collective-permute-start.51 = (bf16[3,2,2,2,32,512]{5,4,0,3,2,1:T(8,128)(2,1)}, bf16[3,2,2,2,32,512]{5,4,0,3,2,1:T(8,128)(2,1)}, u32[]{:S(2)}, u32[]{:S(2)}) collective-permute-start(bf16[3,2,2,2,32,512]{5,4,0,3,2,1:T(8,128)(2,1)} %bitcast.154), channel_id=1, source_target_pairs={{0,4},{2,6},{4,0},{6,2},{8,12},{10,14},{12,8},{14,10},{16,20},{18,... | collective-permute-start | bytes 2359304 | tf_op jit(solution)/shard_map/ppermute | solution.py:66
  285.9 23.4 %collective-permute-start.50 = (bf16[3,2,2,2,32,512]{5,4,0,3,2,1:T(8,128)(2,1)}, bf16[3,2,2,2,32,512]{5,4,0,3,2,1:T(8,128)(2,1)}, u32[]{:S(2)}, u32[]{:S(2)}) collective-permute-start(bf16[3,2,2,2,32,512]{5,4,0,3,2,1:T(8,128)(2,1)} %get-tuple-element.472), channel_id=1, source_target_pairs={{0,2},{2,0},{4,6},{6,4},{8,10},{10,8},{12,14},{14,12},{16,18},{18,... | collective-permute-start | bytes 2359304 | tf_op jit(solution)/shard_map/ppermute | solution.py:66
  288.6 20.7 %collective-permute-start.48 = (bf16[2,3,2,32,512]{4,3,1,0,2:T(8,128)(2,1)}, bf16[2,3,2,32,512]{4,3,1,0,2:T(8,128)(2,1)}, u32[]{:S(2)}, u32[]{:S(2)}) collective-permute-start(bf16[2,3,2,32,512]{4,3,1,0,2:T(8,128)(2,1)} %get-tuple-element.488), channel_id=1, source_target_pairs={{0,16},{2,18},{4,20},{6,22},{8,24},{10,26},{12,28},{14,30},{16,0},... | collective-permute-start | bytes 1179656 | tf_op jit(solution)/shard_map/ppermute | solution.py:66
  329.9 21.1 %collective-permute-start.56 = (bf16[2,3,2,32,512]{4,3,1,0,2:T(8,128)(2,1)}, bf16[2,3,2,32,512]{4,3,1,0,2:T(8,128)(2,1)S(1)}, u32[]{:S(2)}, u32[]{:S(2)}) collective-permute-start(bf16[2,3,2,32,512]{4,3,1,0,2:T(8,128)(2,1)} %get-tuple-element.482), channel_id=1, source_target_pairs={{0,16},{2,18},{4,20},{6,22},{8,24},{10,26},{12,28},{14,30},{16,0},... | collective-permute-start | bytes 1179656 | tf_op jit(solution)/shard_map/ppermute | solution.py:66
  (124 other events, 1174.1 us)

commit v3 on v2

--- a/solution.py
+++ b/solution.py
@@ -3,6 +3,7 @@
 
 import jax
 import jax.numpy as jnp
+import numpy as np
 from jax import lax
 from jax.experimental import pallas as pl
 from jax.experimental.pallas import tpu as pltpu
@@ -80,16 +81,13 @@
     def hand_out(self, parts, dim):
         return [self.send(part, **{dim: k}) for k, part in enumerate(parts) if k]
 
-    def line(self, shards):
-        same, other = shards
-        steps = range(self.dims[1])
-        return [self.send(same, z=-z) for z in steps if z], [
-            self.send(other, flip=1, z=-z) for z in steps
-        ]
-
-    def in_line(self, own, found, role, axis):
+    def line(self, same, other):
+        steps = range(1, self.dims[1])
+        return [self.send(same, z=-z) for z in steps], [self.send(other, flip=1, z=-z) for z in steps]
+
+    def in_line(self, own, flip, found, role, axis):
         same, other = found
-        return [in_order(role, s, o, axis) for s, o in zip([own] + same, other)]
+        return [in_order(role, s, o, axis) for s, o in zip([own] + same, [flip] + other)]
 
     def hand_out_flip(self, parts):
         return [self.send(part, flip=1, z=k) for k, part in enumerate(parts)]
@@ -104,10 +102,10 @@
     def hand_out_plane(self, parts):
         return [self.send(part, y=y, x=x) for part, (x, y) in zip(parts[1:], self.plane())]
 
-    def same_sum(self, values, dim):
+    def same_sum(self, values, found, dim):
         number = ("flip", "z", "y", "x").index(dim)
         size, stride = self.dims[number], self.strides[number]
-        found = jnp.stack([values] + self.pieces(values, dim))
+        found = jnp.stack([values] + found)
         if size > 2:
             mine = (lax.axis_index("dp") // stride) % size
             found = jnp.take(found, (jnp.arange(size) - mine) % size, axis=0)
@@ -277,7 +275,7 @@
     return pieces[:nx], pieces[nx:]
 
 
-def forward_kernel(experts, own, aliased, number, ints, x_ref, *refs):
+def forward_kernel(experts, own, aliased, number, gives, ints, x_ref, *refs):
     arrays = sorted({e // 3 for e in experts})
     weights = {a: refs[number * k : number * (k + 1)] for k, a in enumerate(arrays)}
     refs = refs[number * len(arrays) :]
@@ -285,6 +283,8 @@
     wi_a, wi_b, wo_a, wo_b = held
     bi_ref, vec_ref, cols_in, mix_in = refs[:4]
     cols_ref, mix_ref, *norm_refs = refs[4 + aliased :]
+    if gives:
+        *norm_refs, give_ref = norm_refs
     norm_refs = dict(zip(arrays, norm_refs))
     rows = x_ref.shape[0]
     half = ints[ROLE] if own else 1 - ints[ROLE]
@@ -320,6 +320,12 @@
             join(weights[expert // 3], held)
             each_span(expert, ints, half * (rows // TILE), rows, functools.partial(work, expert))
 
+    if gives:
+
+        @pl.when(step == len(experts) - 1)
+        def _():
+            give_ref[...] = mix_ref[...].astype(bf16)
+
 
 def backward_kernel(experts, halves, keeps_back, adds, number, ints, x_ref, *refs):
     gb_refs, refs = refs[: len(halves)], refs[len(halves) :]
@@ -349,8 +355,11 @@
     def work(expert, span):
         whole = isinstance(span, slice)
 
-        def add(ref, values):
-            ref[...] = values if whole else ref[...] + values
+        def add(ref, target, which, values):
+            if whole:
+                target[0, which] = values.astype(bf16)
+            else:
+                ref[...] += values
 
         x = x_ref[span, :]
         norm = norm_ref[0, span, :].astype(f32)
@@ -379,10 +388,10 @@
         pre_b = nn(x, wi_b[...]) + bi_ref[expert : expert + 1, HALF:]
         act_b, slope_b = gelu_parts(pre_b)
         low_b = (nn(grad_low, wo_b[...]) * slope_b).astype(bf16)
-        add(out_a, tn(grad_low, act_a.astype(bf16)))
-        add(in_a, tn(x, low_a))
-        add(out_b, tn(grad_low, act_b.astype(bf16)))
-        add(in_b, tn(x, low_b))
+        add(out_a, keep_ref, 1, tn(grad_low, act_a.astype(bf16)))
+        add(in_a, keep_ref, 0, tn(x, low_a))
+        add(out_b, give_ref, 1, tn(grad_low, act_b.astype(bf16)))
+        add(in_b, give_ref, 0, tn(x, low_b))
         back_ref[span, :] += nt(low_a, wi_a[...]) + nt(low_b, wi_b[...])
         dcoef = jnp.sum(grad_block * (norm * gain + shift), axis=1, keepdims=True)
         if expert < 2:
@@ -405,11 +414,11 @@
                 for ref in (in_a, in_b, out_a, out_b):
                     ref[...] = jnp.zeros_like(ref)
             each_span(expert, ints, first, rows, functools.partial(work, expert))
-
-    keep_ref[0, 0] = in_a[...].astype(bf16)
-    keep_ref[0, 1] = out_a[...].astype(bf16)
-    give_ref[0, 0] = in_b[...].astype(bf16)
-    give_ref[0, 1] = out_b[...].astype(bf16)
+            if expert >= 2:
+                keep_ref[0, 0] = in_a[...].astype(bf16)
+                keep_ref[0, 1] = out_a[...].astype(bf16)
+                give_ref[0, 0] = in_b[...].astype(bf16)
+                give_ref[0, 1] = out_b[...].astype(bf16)
 
 
 def tower_kernel(
@@ -425,7 +434,8 @@
     head = tv_ref[1:2, :]
     cols = cols_ref[...]
     block = (mix_ref[...] + other_ref[...].astype(f32)).astype(bf16)
-    pre = nn(block, tw_ref[...]) + bias
+    tower = slice(PACK - 128 - DOM * TW, PACK - 128)
+    pre = nn(block, tw_ref[:, tower]) + bias
     act, slope = gelu_parts(pre)
     group = lax.broadcasted_iota(jnp.int32, pre.shape, 1) // TW
     mine = group == cols[:, DOMAIN : DOMAIN + 1].astype(jnp.int32)
@@ -441,7 +451,7 @@
     grad_pre = jnp.where(mine, grad_logit * head * slope, 0.0)
     dv_ref[0:1, :] += jnp.sum(grad_pre, axis=0, keepdims=True)
     grad_low = grad_pre.astype(bf16)
-    grad_block = nt(grad_low, tw_ref[...])
+    grad_block = nt(grad_low, tw_ref[:, tower])
     gb_ref[...] = grad_block
     low_ref[...] = grad_block.astype(bf16)
     dw_ref[...] += tn(block, grad_low)
@@ -451,9 +461,8 @@
     return probability * (grad_probs - jnp.sum(probability * grad_probs, axis=0, keepdims=True))
 
 
-def gate_kernel(own, ints, back_ref, cols_ref, prob_ref, x_ref, gates_ref, sum_ref, low_ref, gate_ref):
+def gate_kernel(ints, back_ref, cols_ref, prob_ref, x_ref, gates_ref, sum_ref, low_ref, gate_ref):
     index = pl.program_id(0)
-    half = ints[ROLE] if own else 1 - ints[ROLE]
     first = ints[ROLE] == 0
 
     @pl.when(index == 0)
@@ -479,7 +488,7 @@
         softmax_back(domain, d_domain * top[1:2]),
     )
     rows = top.shape[1]
-    place = (half * pl.num_programs(0) + index) * rows + lax.broadcasted_iota(jnp.int32, (1, rows), 1)
+    place = index * rows + lax.broadcasted_iota(jnp.int32, (1, rows), 1)
     picks = [
         jnp.where((place >= ints[START + d]) & (place < ints[END + d]), 1.0, 0.0) for d in range(DOM)
     ]
@@ -494,38 +503,38 @@
     low_ref[...] = added.astype(bf16)
 
 
-def call_gate(own, ints, back, cols, probs, x, gates):
+def call_gate(ints, back, cols, probs, x, small):
     rows = x.shape[0]
     half = rows // 2
 
-    def index(ints):
-        return ints[ROLE] if own else 1 - ints[ROLE]
+    def tile(width):
+        return pl.BlockSpec((half, width), lambda i, *_: (i, 0))
 
     return pl.pallas_call(
-        functools.partial(gate_kernel, own),
+        gate_kernel,
         grid_spec=pltpu.PrefetchScalarGridSpec(
             num_scalar_prefetch=1,
-            grid=(1,),
+            grid=(2,),
             in_specs=[
-                half_spec(own, (half, D)),
-                half_spec(own, (half, 128)),
-                pl.BlockSpec((8, half), lambda i, ints: (0, index(ints))),
-                half_spec(own, (half, D)),
-                fixed(gates.shape),
+                tile(D),
+                tile(128),
+                pl.BlockSpec((8, half), lambda i, *_: (0, i)),
+                tile(D),
+                GATES_SPEC,
             ],
-            out_specs=(fixed((half, D)), fixed((half, D)), fixed((D, 128))),
+            out_specs=(tile(D), tile(D), fixed((D, 128))),
         ),
         out_shape=(
-            jax.ShapeDtypeStruct((half, D), f32),
-            jax.ShapeDtypeStruct((half, D), bf16),
+            jax.ShapeDtypeStruct((rows, D), f32),
+            jax.ShapeDtypeStruct((rows, D), bf16),
             jax.ShapeDtypeStruct((D, 128), f32),
         ),
         compiler_params=params(),
         cost_estimate=pl.CostEstimate(
-            flops=4 * half * D * 128, bytes_accessed=5_000_000, transcendentals=0
+            flops=4 * rows * D * 128, bytes_accessed=10_000_000, transcendentals=0
         ),
         name="gates",
-    )(ints, back, cols, probs, x, gates)
+    )(ints, back, cols, probs, x, small)
 
 
 def hidden_lines(ints, lane_ref, tv_ref, line_refs):
@@ -552,7 +561,7 @@
 
 
 def finish_kernel(
-    ints, gb_ref, gb_in_ref, own_ref, other_ref, own_in_ref, other_in_ref, ev_ref, proj_ref, tower_ref, gate_a, gate_b, *refs
+    ints, gb_ref, gb_in_ref, sum_ref, in_ref, ev_ref, proj_ref, tower_ref, gate_ref, *refs
 ):
     lane_ref, tv_ref, *vec_refs, ge_ref, small_ref, proj_sum, bias_sum = refs
     vec_refs, line_refs = vec_refs[: len(vec_refs) // 2], vec_refs[len(vec_refs) // 2 :]
@@ -567,11 +576,8 @@
         for ref in (proj_sum, bias_sum):
             ref[...] = jnp.zeros_like(ref)
 
-    grad_mixed = at_home * jnp.where(
-        mine_half,
-        gb_ref[...] + own_ref[...] + other_in_ref[...].astype(f32),
-        gb_in_ref[...].astype(f32) + other_ref[...] + own_in_ref[...].astype(f32),
-    )
+    grad_mixed = jnp.where(mine_half, gb_ref[...], gb_in_ref[...].astype(f32))
+    grad_mixed = at_home * (grad_mixed + sum_ref[...] + in_ref[...].astype(f32))
     bias_sum[0:1, :] += jnp.sum(grad_mixed, axis=0, keepdims=True)
     low = grad_mixed.astype(bf16)
     proj_sum[...] += tn(low, ev_ref[...])
@@ -596,20 +602,18 @@
         )
         small_ref[:, :e_in] = proj_sum[...].astype(bf16)
         small_ref[:, e_in : e_in + DOM * TW] = tower_ref[...].astype(bf16)
-        small_ref[:, e_in + DOM * TW :] = (gate_a[...] + gate_b[...] + jnp.transpose(rows)).astype(bf16)
-
-
-def call_finish(
-    ints, gb, gb_in, own, other, own_in, other_in, events, proj_t, tower, gate_a, gate_b, lanes, tower_vec, sums
-):
+        small_ref[:, e_in + DOM * TW :] = (gate_ref[...] + jnp.transpose(rows)).astype(bf16)
+
+
+def call_finish(ints, gb, gb_in, added, arrived, events, small, tower, gate, lanes, tower_vec, sums):
     rows, e_in = events.shape
     half = rows // 2
 
     def tile(width):
         return pl.BlockSpec((half, width), lambda i, *_: (i, 0))
 
-    halves = (gb, gb_in, own, other, own_in, other_in)
-    wholes = (proj_t, tower, gate_a, gate_b, lanes, tower_vec)
+    halves = (gb, gb_in)
+    wholes = (tower, gate, lanes, tower_vec)
     vecs = [v for v, _ in sums] + [b for _, b in sums]
     return pl.pallas_call(
         finish_kernel,
@@ -617,7 +621,7 @@
             num_scalar_prefetch=1,
             grid=(2,),
             in_specs=[fixed(a.shape) for a in halves]
-            + [tile(e_in)]
+            + [tile(D), tile(D), tile(e_in), proj_spec(e_in)]
             + [fixed(a.shape) for a in (*wholes, *vecs)],
             out_specs=(tile(e_in), fixed((D, PACK))),
             scratch_shapes=[pltpu.VMEM((D, e_in), f32), pltpu.VMEM((8, D), f32)],
@@ -626,7 +630,7 @@
         compiler_params=params(),
         cost_estimate=pl.CostEstimate(flops=4 * rows * D * e_in, bytes_accessed=14_000_000, transcendentals=0),
         name="finish",
-    )(ints, *halves, events, *wholes, *vecs)
+    )(ints, *halves, added, arrived, events, small, *wholes, *vecs)
 
 
 VECTOR_ROW = {j: 32 + 18 * r + 3 * i for r, row in enumerate(SETS) for i, j in enumerate(row)}
@@ -709,8 +713,14 @@
     return pl.BlockSpec(shape, lambda i, *_: (0,) * len(shape))
 
 
-def pack_kernel(proj_ref, tower_ref, *refs):
-    *row_refs, in_bias_ref, tower_b_ref, tower_out_ref, out_ref = refs
+def pack_kernel(count, *refs):
+    sources, out_ref, held, arrived = refs[:count], refs[count], refs[count + 1 : -1], refs[-1]
+    copies = [pltpu.make_async_copy(a, b, arrived.at[k]) for k, (a, b) in enumerate(zip(sources, held))]
+    for copy in copies:
+        copy.start()
+    for copy in copies:
+        copy.wait()
+    proj_ref, tower_ref, *row_refs, in_bias_ref, tower_b_ref, tower_out_ref = held
     width, e_in = proj_ref.shape
     out_ref[:, :e_in] = proj_ref[...]
     for d in range(DOM):
@@ -729,40 +739,117 @@
 def call_pack(*arrays):
     width = arrays[0].shape[0]
     return pl.pallas_call(
-        pack_kernel,
-        grid=(1,),
-        in_specs=[fixed(a.shape) for a in arrays],
-        out_specs=fixed((width, PACK)),
+        functools.partial(pack_kernel, len(arrays)),
+        in_specs=[pl.BlockSpec(memory_space=pltpu.HBM)] * len(arrays),
+        out_specs=pl.BlockSpec(memory_space=pltpu.VMEM),
         out_shape=jax.ShapeDtypeStruct((width, PACK), bf16),
+        scratch_shapes=[pltpu.VMEM(a.shape, a.dtype) for a in arrays]
+        + [pltpu.SemaphoreType.DMA((len(arrays),))],
         compiler_params=params(),
         name="pack",
     )(*arrays)
 
 
-def choose_kernel(own_ids, other_ids, in_own, out_own, in_other, out_other, own_ref, other_ref):
-    own_ref[0], own_ref[1] = in_own[...], out_own[...]
-    other_ref[0], other_ref[1] = in_other[...], out_other[...]
+PICKED = [
+    [32 + e for e in row] + [44 + e for e in row] + [56 + e for e in row] + [68] + [127] * 5
+    + [69 + e for e in row] + [81 + e for e in row] + [93 + d for d in range(DOM)]
+    for row in SETS
+]
+
+
+def unpack_kernel(ints, small_ref, choose_ref, lane_ref, vec_ref, bi_ref, tower_ref):
+    vec = nt(choose_ref[0], small_ref[...])
+    vec_ref[...] = vec
+
+    def lanes(values, row):
+        lane = lax.broadcasted_iota(jnp.int32, (H, D), 0)
+        chosen = jnp.where(lane == lane_ref[row : row + 1, :], 1.0, 0.0).astype(bf16)
+        return nt(values.astype(bf16), chosen)
+
+    bias = lanes(jnp.concatenate([vec[24:30], jnp.zeros((2, D), f32)], axis=0), 0)
+    bias += lanes(jnp.concatenate([vec[30:36], jnp.zeros((2, D), f32)], axis=0), 1)
+    bi_ref[...] = jnp.where(ints[1] == 0, bias, pltpu.roll(bias, HALF, 1))
+    head = lane_ref[6:7, :] == 1
+    tower = jnp.zeros((8, H), f32)
+    for d in range(DOM):
+        row = vec[36 + d : 37 + d]
+        rows = [jnp.where(head, 0.0, row), jnp.where(head, row, 0.0), jnp.zeros((6, D), f32)]
+        tower += lanes(jnp.concatenate(rows, axis=0), 2 + d)
+    tower_ref[...] = tower
+
+
+def call_unpack(ints, small, lanes):
+    choose = np.zeros((2, 40, 128), np.float32)
+    for r in range(2):
+        for row, column in enumerate(PICKED[r]):
+            choose[r, row, column] = 1.0
+    shapes = [(40, D), (8, H), (8, DOM * TW)]
+    return pl.pallas_call(
+        unpack_kernel,
+        grid_spec=pltpu.PrefetchScalarGridSpec(
+            num_scalar_prefetch=1,
+            grid=(1,),
+            in_specs=[
+                pl.BlockSpec((D, 128), lambda i, ints: (0, PACK // 128 - 1)),
+                pl.BlockSpec((1, 40, 128), lambda i, ints: (ints[0], 0, 0)),
+                fixed(lanes.shape),
+            ],
+            out_specs=tuple(fixed(shape) for shape in shapes),
+        ),
+        out_shape=tuple(jax.ShapeDtypeStruct(shape, f32) for shape in shapes),
+        compiler_params=params(),
+        name="unpack",
+    )(ints, small, jnp.asarray(choose, bf16), lanes)
+
+
+def choose_kernel(own_ids, other_ids, in_own, out_own, in_other, out_other, *refs):
+    own_refs, other_refs, all_ref = refs[:2], refs[2:4], refs[4]
+    step = pl.program_id(0)
+    for part in range(2):
+
+        @pl.when(step // 3 == part)
+        def _(part=part):
+            own_refs[part][0], own_refs[part][1] = in_own[...], out_own[...]
+            other_refs[part][0], other_refs[part][1] = in_other[...], out_other[...]
+
+    all_ref[0], all_ref[1] = in_other[...], out_other[...]
 
 
 def call_choose(own_ids, other_ids, w_in, w_out_t):
-    block = (1,) + w_in.shape[1:]
-    shape = jax.ShapeDtypeStruct((2, own_ids.shape[0]) + w_in.shape[1:], bf16)
+    tail = w_in.shape[1:]
+    block = (1,) + tail
+
+    def shape(count):
+        return jax.ShapeDtypeStruct((2, count) + tail, bf16)
+
     own = pl.BlockSpec(block, lambda i, a, b: (a[i], 0, 0))
     other = pl.BlockSpec(block, lambda i, a, b: (b[i], 0, 0))
-    out = pl.BlockSpec((2,) + block, lambda i, a, b: (0, i, 0, 0))
+    low = pl.BlockSpec((2,) + block, lambda i, a, b: (0, jnp.minimum(i, 2), 0, 0))
+    high = pl.BlockSpec((2,) + block, lambda i, a, b: (0, jnp.maximum(i - 3, 0), 0, 0))
+    every = pl.BlockSpec((2,) + block, lambda i, a, b: (0, i, 0, 0))
     return pl.pallas_call(
         choose_kernel,
         grid_spec=pltpu.PrefetchScalarGridSpec(
-            num_scalar_prefetch=2, grid=(own_ids.shape[0],), in_specs=[own, own, other, other], out_specs=(out, out)
-        ),
-        out_shape=(shape, shape),
+            num_scalar_prefetch=2,
+            grid=(LOCAL,),
+            in_specs=[own, own, other, other],
+            out_specs=(low, high, low, high, every),
+        ),
+        out_shape=(shape(3), shape(3), shape(3), shape(3), shape(6)),
         compiler_params=params(),
-        cost_estimate=pl.CostEstimate(flops=0, bytes_accessed=2_000_000, transcendentals=0),
+        cost_estimate=pl.CostEstimate(flops=0, bytes_accessed=3_000_000, transcendentals=0),
         name="choose",
     )(own_ids, other_ids, w_in, w_out_t, w_in, w_out_t)
 
 
-def call_prepare(ints, floats, table, embeds, proj_t, gates, vec):
+def proj_spec(e_in):
+    return pl.BlockSpec((D, e_in), lambda *_: (0, 0))
+
+
+GATES_SPEC = pl.BlockSpec((D, 128), lambda *_: (0, PACK // 128 - 1))
+
+
+def call_prepare(ints, floats, table, embeds, small, vec):
     rows = embeds.shape[0]
     tiles = rows // TILE
     e_in = embeds.shape[1]
@@ -775,7 +862,7 @@
         grid_spec=pltpu.PrefetchScalarGridSpec(
             num_scalar_prefetch=2,
             grid=(tiles,),
-            in_specs=[fixed(table.shape), fixed(embeds.shape), fixed(proj_t.shape), fixed(gates.shape), fixed(vec.shape)],
+            in_specs=[fixed(table.shape), fixed(embeds.shape), proj_spec(e_in), GATES_SPEC, fixed(vec.shape)],
             out_specs=(
                 tile(e_in),
                 tile(D),
@@ -796,7 +883,7 @@
             flops=2 * rows * e_in * (rows + D), bytes_accessed=12_000_000, transcendentals=rows * 8
         ),
         name="prepare",
-    )(ints, floats, table, embeds, proj_t, gates, vec)
+    )(ints, floats, table, embeds, small, small, vec)
 
 
 def half_spec(own, shape):
@@ -812,7 +899,7 @@
 MATRICES = [pltpu.VMEM((D, HALF), bf16)] * 4
 
 
-def call_forward(experts, own, ints, x, weights, bi, vec, cols, mix, norms):
+def call_forward(experts, own, ints, x, weights, bi, vec, cols, mix, norms, gives=False):
     rows = x.shape[0]
     half = rows // 2
     arrays = sorted({e // 3 for e in experts})
@@ -837,7 +924,9 @@
     aliases.update({at + 1 + k: 2 + k for k in range(len(kept))})
     shared = sum(1 for e in experts if e < 2)
     out = pl.pallas_call(
-        functools.partial(forward_kernel, experts, own, len(kept), len(weights[arrays[0]])),
+        functools.partial(
+            forward_kernel, experts, own, len(kept), len(weights[arrays[0]]), gives
+        ),
         grid_spec=pltpu.PrefetchScalarGridSpec(
             num_scalar_prefetch=1,
             grid=(len(experts),),
@@ -845,14 +934,16 @@
             + weight_specs
             + [fixed(bi.shape), fixed(vec.shape), half_spec(own, (half, 128)), half_spec(own, (half, D))]
             + [pl.BlockSpec(memory_space=pl.ANY)] * len(kept),
-            out_specs=(half_spec(own, (half, 128)), half_spec(own, (half, D)), *norm_specs),
+            out_specs=(half_spec(own, (half, 128)), half_spec(own, (half, D)), *norm_specs)
+            + ((fixed((half, D)),) if gives else ()),
             scratch_shapes=MATRICES,
         ),
         out_shape=(
             jax.ShapeDtypeStruct((rows, 128), f32),
             jax.ShapeDtypeStruct((rows, D), f32),
             *[jax.ShapeDtypeStruct((3, rows, D), bf16)] * len(arrays),
-        ),
+        )
+        + ((jax.ShapeDtypeStruct((half, D), bf16),) if gives else ()),
         input_output_aliases=aliases,
         compiler_params=params(),
         cost_estimate=pl.CostEstimate(
@@ -860,7 +951,8 @@
         ),
         name="experts_forward",
     )(ints, *inputs)
-    return out[0], out[1], {**norms, **dict(zip(arrays, out[2:]))}
+    found = out[0], out[1], {**norms, **dict(zip(arrays, out[2:]))}
+    return found + (out[-1],) if gives else found
 
 
 def call_backward(experts, halves, ints, x, gbs, norms, weights, bi, vec, cols, back, sums=None):
@@ -927,24 +1019,25 @@
     )(ints, *inputs)
 
 
-def call_tower(ints, mix, other, cols, tower, tower_vec):
+def call_tower(ints, mix, other, cols, small, tower_vec):
     rows = other.shape[0]
-    tiles = rows // TILE
+    tiles = 2
+    size = rows // tiles
 
     def kept(width):
-        return pl.BlockSpec((TILE, width), lambda i, ints: (ints[ROLE] * tiles + i, 0))
+        return pl.BlockSpec((size, width), lambda i, ints: (ints[ROLE] * tiles + i, 0))
 
     def tile(width):
-        return pl.BlockSpec((TILE, width), lambda i, *_: (i, 0))
+        return pl.BlockSpec((size, width), lambda i, *_: (i, 0))
 
     return pl.pallas_call(
         tower_kernel,
         grid_spec=pltpu.PrefetchScalarGridSpec(
             num_scalar_prefetch=1,
             grid=(tiles,),
-            in_specs=[kept(D), tile(D), kept(128), fixed(tower.shape), fixed(tower_vec.shape)],
+            in_specs=[kept(D), tile(D), kept(128), fixed(small.shape), fixed(tower_vec.shape)],
             out_specs=(
-                pl.BlockSpec((8, TILE), lambda i, *_: (0, i)),
+                pl.BlockSpec((8, size), lambda i, *_: (0, i)),
                 tile(D),
                 tile(D),
                 fixed((D, DOM * TW)),
@@ -965,7 +1058,7 @@
             flops=6 * rows * D * DOM * TW, bytes_accessed=10_000_000, transcendentals=rows * DOM * TW
         ),
         name="towers",
-    )(ints, mix, other, cols, tower, tower_vec)
+    )(ints, mix, other, cols, small, tower_vec)
 
 
 def per_device(
@@ -1007,8 +1100,7 @@
         return lax.dynamic_slice_in_dim(values, which * half_rows, half_rows, axis)
 
     w_out_t = jnp.swapaxes(w_out, 1, 2)
-    first = call_choose(set_own[:3], set_other[:3], w_in, w_out_t)
-    second = call_choose(set_own[3:], set_other[3:], w_in, w_out_t)
+    first, second, first_other, second_other, others = call_choose(set_own, set_other, w_in, w_out_t)
 
     arrays = (
         proj_w.T,
@@ -1024,20 +1116,23 @@
         tower_b,
         tower_out,
     )
-    first_z = box.line(first)
-    pack = call_pack(*step(arrays, first_z[0])[0])
-    pack_z = box.line((pack, pack))
-    first, first_z, second = step(first, first_z, second)
-
-    def along_z(shard, found):
-        found = box.in_line(shard[0], found, role, 2)
+    flips = box.send(others, flip=1)
+    first_z = box.line(first, first_other)
+    pack = call_pack(*step(arrays, flips)[0])
+    pack = in_order(role, pack, box.send(pack, flip=1), 0)
+    pack = jnp.concatenate([pack] + box.pieces(pack, "z"))
+    flips, first, first_z, second, second_other = step(flips, first, first_z, second, second_other)
+
+    def along_z(shard, flip, found):
+        found = box.in_line(shard, flip, found, role, 2)
         return jnp.stack([b[0] for b in found]), jnp.stack([b[1] for b in found])
 
-    first_i, first_o = along_z(first, first_z)
+    first_i, first_o = along_z(first, flips[:, :3], first_z)
     first_iy, first_ox = box.pieces(first_i, "y"), box.pieces(first_o, "x")
-    second_z = box.line(second)
-    pack = step(jnp.concatenate(box.in_line(pack, pack_z, role, 0)), second_z[0])[0]
-    pack = jnp.concatenate(box.gather_plane(pack), axis=0).reshape(places, 1, width, PACK)
+    second_z = box.line(second, second_other)
+    pack = jnp.concatenate([pack] + box.pieces(pack, "y"))
+    pack = jnp.concatenate([pack] + box.pieces(pack, "x")).reshape(places, 1, width, PACK)
+    domain, labels = step((domain, labels), first)[0]
     event_rows = jnp.concatenate(
         [domain.astype(f32).T, labels.astype(f32)[None], jnp.zeros((6, rows), f32)]
     )
@@ -1049,57 +1144,18 @@
     ends = jnp.cumsum(counts)
     starts = ends - counts
     position = jnp.sum(onehot * (rank + starts[:, None]), axis=0) - 1.0
-    embeds_in = box.to_partner(step(embeds, event_rows)[0], True)
-    first_i, first_o, first_iy, first_ox, second, second_z, starts, ends, position = step(
-        first_i, first_o, first_iy, first_ox, second, second_z, starts, ends, position
+    embeds_in = box.to_partner(step(embeds, second_z[0])[0], True)
+    first_i, first_o, first_iy, first_ox, second, second_z, flips, starts, ends, position = step(
+        first_i, first_o, first_iy, first_ox, second, second_z, flips, starts, ends, position
     )
 
     small = in_order(core, pack, swap_cores(pack), 1).reshape(D, PACK)
     first_i = jnp.stack([first_i] + first_iy)
     first_o = jnp.stack([first_o] + first_ox)
     first_ix, first_oy = box.pieces(first_i, "x"), box.pieces(first_o, "y")
-    second_i, second_o = along_z(second, second_z)
+    second_i, second_o = along_z(second, flips[:, 3:], second_z)
     second_iy, second_ox = box.pieces(second_i, "y"), box.pieces(second_o, "x")
 
-    proj_t = small[:, :e_in]
-    tower = small[:, e_in : e_in + DOM * TW]
-    gates = small[:, e_in + DOM * TW :]
-    picked = jnp.concatenate(
-        [
-            32 + set_own,
-            44 + set_own,
-            56 + set_own,
-            jnp.array([68] + [128] * 5),
-            69 + set_own,
-            81 + set_own,
-            93 + jnp.arange(4),
-        ]
-    )
-    choose = (picked[:, None] == jnp.arange(128)[None, :]).astype(bf16)
-    vec = nt(choose, gates)
-    blocks = jnp.take(vec[24:].reshape(16, places, 2 * width), place_of, axis=1)
-    bi = (
-        blocks[:12]
-        .reshape(2, LOCAL, places, 2, width)
-        .transpose(1, 2, 3, 0, 4)
-        .reshape(LOCAL, H)
-    )
-    bi = jnp.pad(bi, ((0, 2), (0, 0)))
-    bi = jnp.where(core == 0, bi, jnp.concatenate([bi[:, HALF:], bi[:, :HALF]], axis=1))
-    tower_vec = (
-        blocks[12:]
-        .reshape(DOM, places, 2, 2, width // 2)
-        .transpose(3, 0, 1, 2, 4)
-        .reshape(2, DOM * TW)
-    )
-    tower_vec = jnp.pad(tower_vec, ((0, 6), (0, 0)))
-
-    table = jnp.concatenate([position[None], event_rows[1:]])
-    start_i, end_i = starts.astype(jnp.int32), ends.astype(jnp.int32)
-    empty = end_i == start_i
-    low = jnp.where(empty, 0, start_i // TILE)
-    high = jnp.where(empty, 0, (end_i + TILE - 1) // TILE)
-    domains = jnp.arange(DOM, dtype=jnp.int32)
     device = (2 * box.ahead()[:, None, None] + jnp.arange(2)[None, :, None]).astype(jnp.int32)
     unit = jnp.arange(width, dtype=jnp.int32)[None, None, :]
     narrow = width // 2
@@ -1107,7 +1163,14 @@
     lanes += [d * TW + device * narrow + unit % narrow for d in range(DOM)]
     lanes += [jnp.broadcast_to(unit // narrow, (places, 2, width))] * 2
     lanes = jnp.stack([jnp.broadcast_to(v, (places, 2, width)).reshape(D) for v in lanes])
-
+    vec, bi, tower_vec = call_unpack(jnp.stack([role, core]), small, lanes)
+
+    table = jnp.concatenate([position[None], event_rows[1:]])
+    start_i, end_i = starts.astype(jnp.int32), ends.astype(jnp.int32)
+    empty = end_i == start_i
+    low = jnp.where(empty, 0, start_i // TILE)
+    high = jnp.where(empty, 0, (end_i + TILE - 1) // TILE)
+    domains = jnp.arange(DOM, dtype=jnp.int32)
     ints = jnp.concatenate(
         [
             jnp.where(role == 0, low[::-1], low),
@@ -1123,13 +1186,13 @@
     loss_weight = 1.0 - (1.0 - FROZEN_SHARE) * frozen.astype(f32)
     floats = jnp.concatenate([loss_weight, tower_out_b.astype(f32)])
     embeds = jnp.where(at_home, embeds, embeds_in)
-    events, x, mix, cols, probs = call_prepare(ints, floats, table, embeds, proj_t, gates, vec)
+    events, x, mix, cols, probs = call_prepare(ints, floats, table, embeds, small, vec)
     (
         first_i, first_o, first_ix, first_oy, second_i, second_o, second_iy, second_ox,
-        ints, events, x, mix, cols, probs, vec, bi, tower, tower_vec, lanes,
+        ints, events, x, mix, cols, probs, vec, bi, small, tower_vec, lanes,
     ) = step(
         first_i, first_o, first_ix, first_oy, second_i, second_o, second_iy, second_ox,
-        ints, events, x, mix, cols, probs, vec, bi, tower, tower_vec, lanes,
+        ints, events, x, mix, cols, probs, vec, bi, small, tower_vec, lanes,
     )
 
     def pieces(i, ix, o, oy):
@@ -1143,15 +1206,16 @@
     cols, mix, norms = call_forward((0, 1, 2), False, ints, x, weights, bi, vec, cols, mix, {})
     second_ix, second_oy, cols, mix = step(second_ix, second_oy, cols, mix)
     weights[1] = pieces(second_i, second_ix, second_o, second_oy)
-    cols, mix, norms = call_forward((3, 4), False, ints, x, weights, bi, vec, cols, mix, norms)
-    give_mix = half(mix, 1 - role).astype(bf16)
+    cols, mix, norms, give_mix = call_forward(
+        (3, 4), False, ints, x, weights, bi, vec, cols, mix, norms, True
+    )
     give_mix, mix = step(give_mix, mix)
     other_mix = box.send(give_mix, flip=1)
     cols, mix, norms = call_forward(
         tuple(range(LOCAL)), True, ints, x, weights, bi, vec, cols, mix, norms
     )
     row_out, grad_block, grad_low, d_tower, d_tower_vec, d_logit_bias = call_tower(
-        ints, mix, other_mix, cols, tower, tower_vec
+        ints, mix, other_mix, cols, small, tower_vec
     )
 
     box_shape = (nx, ny, nz, 2, 2 * width, HALF)
@@ -1200,62 +1264,59 @@
         (0, 1), ("own",), *common, [grad_low], *shared, cols, None
     )
     d_logit_bias = d_logit_bias + swap_cores(d_logit_bias)
-    d_logit_bias = box.same_sum(box.same_sum(d_logit_bias, "y"), "x")
-    grad_in, cols, back, keep_a, give_a, sums, d_logit_bias = step(
-        grad_in, cols, back, keep_a, give_a, sums, d_logit_bias
-    )
+    logit_in = box.pieces(d_logit_bias, "y")
+    grad_in, cols, back, keep_a, give_a, sums, logit_in = step(
+        grad_in, cols, back, keep_a, give_a, sums, logit_in
+    )
+    d_logit_bias = box.same_sum(d_logit_bias, logit_in, "y")
     give_a = swap_cores(give_a)
     cols, back, keep_b, give_b, *sums_0 = call_backward(
         (0, 1), ("other",), *common, [grad_in], *shared, cols, ("fresh", back), sums
     )
-    d_logit_bias = box.same_sum(box.same_sum(d_logit_bias, "flip"), "z")
-    cols, back, keep_a, give_a, keep_b, give_b, d_logit_bias = step(
-        cols, back, keep_a, give_a, keep_b, give_b, d_logit_bias
-    )
+    logit_in = box.pieces(d_logit_bias, "x")
+    cols, back, keep_a, give_a, keep_b, give_b, logit_in = step(
+        cols, back, keep_a, give_a, keep_b, give_b, logit_in
+    )
+    d_logit_bias = box.same_sum(d_logit_bias, logit_in, "x")
     give_b = swap_cores(give_b)
     grads = [grad_low, grad_in]
     cols, back, keep_c, give_c, *sums_1 = call_backward(
         (2,), ("own", "other"), *common, grads, *shared, cols, ("add", back)
     )
-    cols, back, keep_b, give_b, keep_c, give_c, row_out, d_logit_bias = step(
-        cols, back, keep_b, give_b, keep_c, give_c, row_out, d_logit_bias
-    )
+    logit_in = box.pieces(d_logit_bias, "flip")
+    cols, back, keep_b, give_b, keep_c, give_c, row_out, logit_in = step(
+        cols, back, keep_b, give_b, keep_c, give_c, row_out, logit_in
+    )
+    d_logit_bias = box.same_sum(d_logit_bias, logit_in, "flip")
     give_c = swap_cores(give_c)
     ab = both_cores([keep_a, keep_b], [give_a, give_b])
     give_c, keep_c, ab, cols = step(give_c, keep_c, ab, cols)
     c0 = Scatter(ab, both_cores([keep_c], [give_c]))
     cols, back, keep_d, give_d, *sums_2 = call_backward(
-        (3, 4), ("own", "other"), *common, grads, *shared, cols, ("add", back)
+        (3, 4, 5), ("own", "other"), *common, grads, *shared, cols, ("add", back)
     )
     rows_in = box.to_partner(row_out, False)
-    cols, back, keep_d, give_d, rows_in = sync([c0], cols, back, keep_d, give_d, rows_in)
+    logit_in = box.pieces(d_logit_bias, "z")
+    cols, back, keep_d, give_d, rows_in, logit_in = sync(
+        [c0], cols, back, keep_d, give_d, rows_in, logit_in
+    )
+    d_logit_bias = box.same_sum(d_logit_bias, logit_in, "z")
     c0.second()
     give_d = swap_cores(give_d)
-    cols, back, _ = step(cols, back, c0.state[:2])
-    g_other, g_other_low, d_gate_a = call_gate(False, ints, back, cols, probs, x, gates)
-    back_other = box.to_partner(g_other_low, False)
-    cols, back, _ = step(cols, back, g_other_low)
-    cols, back, keep_e, give_e, *sums_3 = call_backward(
-        (5,), ("own",), *common, [grad_low], *shared, cols, ("add", back)
-    )
-    cd = both_cores([keep_d], [give_d])
-    cols, back, back_other, cd, keep_e, give_e = sync(
-        [c0], cols, back, back_other, cd, keep_e, give_e
-    )
-    give_e = swap_cores(give_e)
+    c1 = Scatter(both_cores([keep_d], [give_d]))
+    cols, back, _ = step(cols, back, (c0.state[:2], c1.state[:2]))
+    g_sum, g_low, d_gate = call_gate(ints, back, cols, probs, x, small)
+    back_in = box.to_partner(g_low, False)
+    (back_in,) = sync([c0, c1], back_in)
     c0.third()
-    c1 = Scatter(cd, both_cores([keep_e], [give_e]))
-    g_own, g_own_low, d_gate_b = call_gate(True, ints, back, cols, probs, x, gates)
-    back_own = box.to_partner(g_own_low, False)
-    back_own, g_own, d_gate_b = sync([c0, c1], back_own, g_own, d_gate_b)
+    c1.second()
+    back_in, _ = step(back_in, c1.state[:2])
+    grad_events, d_small = call_finish(
+        ints, grad_block, grad_in, g_sum, back_in, events, small, d_tower, d_gate, lanes, d_tower_vec,
+        [sums_0, sums_1, sums_2],
+    )
+    grad_events, d_small = sync([c0, c1], grad_events, d_small)
     c0.fourth()
-    c1.second()
-    back_own, _ = step(back_own, c1.state[:2])
-    grad_events, d_small = call_finish(
-        ints, grad_block, grad_in, g_own, g_other, back_own, back_other, events, proj_t, d_tower,
-        d_gate_a, d_gate_b, lanes, d_tower_vec, [sums_0, sums_1, sums_2, sums_3],
-    )
-    grad_events, d_small = sync([c0, c1], grad_events, d_small)
     c1.third()
     d_small, _ = step(d_small, c1.state[0])
     d_small = d_small.reshape(places, 2, width, PACK)
@@ -1275,6 +1336,7 @@
         [c0, c1], d_parts[0], d_in, grad_embeds, predictions
     )
     c1.fourth()
+    d_mine, _ = step(d_mine, c1.state[0])
     d_mine = total(d_mine, d_in).astype(bf16)
     same = [lax.dynamic_index_in_dim(d_mine[k], role, 0, keepdims=False) for k in range(nz)]
     flip = [lax.dynamic_index_in_dim(d_mine[k], 1 - role, 0, keepdims=False) for k in range(nz)]

time: 372 us -> 365 us (0.981)
  waiting for transfers between devices: 75.2 us -> 90.1 us
  Pallas kernels: 156 us -> 147 us
  other arithmetic: 36.4 us -> 29.4 us
  local copies, waits for them, and re-layouts: 20.3 us -> 16.3 us
    ppermute x44 -> x41, waiting for transfers between devices: 66.1 us -> 81.2 us  [send(): return lax.ppermute(values, 'dp', pairs)]
    pallas_call x5 -> x4, Pallas kernels: 75.1 us -> 67.5 us  [call_backward(): pl.pallas_call(functools.partial(backward_kernel, experts, halves, mode =...]
    ppermute x44 -> x41, starting transfers between devices: 55.4 us -> 51.7 us  [send(): return lax.ppermute(values, 'dp', pairs)]
    ppermute x18 -> x17, waiting for transfers between devices: 7.16 us -> 8.88 us  [swap_cores(): return lax.ppermute(values, 'tensor', [(0, 1), (1, 0)])]
    ppermute x5 -> x4, starting transfers between devices: 10.1 us -> 9.34 us  [to_partner(): return lax.ppermute(values, ('dp', 'tensor'), pairs)]
    unnamed x167 -> x147, local copies, waits for them, and re-layouts: 11.4 us -> 10.9 us
  transfers between devices with their start and end apart: 67 -> 62, of which waited for: 21 -> 18; matrix products, arithmetic and copies ran while one was open for 12% -> 9% of each run, Pallas kernels for 37% -> 34%
where the time goes in v3:
time: 365 us; the launch traced here: 358 us
  Pallas kernels  147 us (40%)
  waiting for transfers between devices  90.1 us (25%)
  starting transfers between devices  67.9 us (19%)
  other arithmetic  29.4 us (8%)
  local copies, waits for them, and re-layouts  16.3 us (4%)
  matrix products  4.32 us (1%)
    ppermute x41, waiting for transfers between devices, send(): return lax.ppermute(values, 'dp', pairs)  81.2 us
    pallas_call x4, Pallas kernels, call_backward(): pl.pallas_call(functools.partial(backward_kernel, experts, halves, mode =...  67.5 us
    ppermute x41, starting transfers between devices, send(): return lax.ppermute(values, 'dp', pairs)  51.7 us
    pallas_call x3, Pallas kernels, call_forward(): pl.pallas_call(functools.partial(forward_kernel, experts, own, len(kept),...  38.3 us
    pallas_call x1, Pallas kernels, call_prepare(): pl.pallas_call(prepare_kernel, grid_spec=pltpu.PrefetchScalarGridSpec(num...  11.4 us
    unnamed x147, local copies, waits for them, and re-layouts  10.9 us
    pallas_call x1, Pallas kernels, call_finish(): pl.pallas_call(finish_kernel, grid_spec=pltpu.PrefetchScalarGridSpec(num_...  9.78 us
    ppermute x4, starting transfers between devices, to_partner(): return lax.ppermute(values, ('dp', 'tensor'), pairs)  9.34 us
  transfers between devices with their start and end apart: 62, of which 18 were waited for; matrix products, arithmetic and copies ran while one was open for 9% of the time, Pallas kernels for 34%

profile of v3, /device:TPU:0, one launch (start us, length us, event | category | flops | bytes accessed | tf_op | source)
XLA Modules:
  0.0 357.9 jit_solution(17477079412874768829)
XLA Ops:
  4.7 5.1 %collective-permute-start.2 = (bf16[2,3,32,512]{3,2,1,0:T(8,128)(2,1)S(1)}, bf16[2,3,32,512]{3,2,1,0:T(8,128)(2,1)S(1)}, u32[]{:S(2)}, u32[]{:S(2)}) collective-permute-start(bf16[2,3,32,512]{3,2,1,0:T(8,128)(2,1)S(1)} %get-tuple-element.226), channel_id=1, source_target_pairs={{0,24},{2,26},{4,28},{6,30},{8,16},{10,18},{12,20},{14,22},{16,8},... | collective-permute-start | bytes 589832 | tf_op jit(solution)/shard_map/ppermute | solution.py:67
  12.5 3.3 collective-permute-done.2
  15.7 10.9 %collective-permute-done.1 = bf16[2,3,32,512]{3,2,1,0:T(8,128)(2,1)S(1)} collective-permute-done((bf16[2,3,32,512]{3,2,1,0:T(8,128)(2,1)S(1)}, bf16[2,3,32,512]{3,2,1,0:T(8,128)(2,1)S(1)}, u32[]{:S(2)}, u32[]{:S(2)}) %collective-permute-start.1) | collective-permute-done | bytes 196640 | tf_op jit(solution)/shard_map/ppermute | solution.py:67
  27.6 3.6 %collective-permute-start.7 = (f32[8,1536]{1,0:T(8,128)S(1)}, f32[8,1536]{1,0:T(8,128)S(1)}, u32[]{:S(2)}, u32[]{:S(2)}) collective-permute-start(f32[8,1536]{1,0:T(8,128)S(1)} %maximum_maximum_fusion), channel_id=1, source_target_pairs={{0,8},{2,10},{4,12},{6,14},{9,1},{11,3},{13,5},{15,7},{16,24},{18,... | collective-permute-start | bytes 147464 | tf_op jit(solution)/shard_map/ppermute | solution.py:75
  32.2 3.9 %collective-permute-start.6 = (bf16[2,3,32,512]{3,2,1,0:T(8,128)(2,1)S(1)}, bf16[2,3,32,512]{3,2,1,0:T(8,128)(2,1)}, u32[]{:S(2)}, u32[]{:S(2)}) collective-permute-start(bf16[2,3,32,512]{3,2,1,0:T(8,128)(2,1)S(1)} %get-tuple-element.234), channel_id=1, source_target_pairs={{0,24},{2,26},{4,28},{6,30},{8,16},{10,18},{12,20},{14,22},{16,8},... | collective-permute-start | bytes 589832 | tf_op jit(solution)/shard_map/ppermute | solution.py:67
  44.6 11.8 %collective-permute-done.14 = bf16[32,1792]{1,0:T(8,128)(2,1)S(1)} collective-permute-done((bf16[32,1792]{1,0:T(8,128)(2,1)S(1)}, bf16[32,1792]{1,0:T(8,128)(2,1)S(1)}, u32[]{:S(2)}, u32[]{:S(2)}) %collective-permute-start.14) | collective-permute-done | bytes 114720 | tf_op jit(solution)/shard_map/ppermute | solution.py:67
  67.8 8.6 %collective-permute-done.16 = bf16[128,1792]{1,0:T(8,128)(2,1)S(1)} collective-permute-done((bf16[128,1792]{1,0:T(8,128)(2,1)S(1)}, bf16[128,1792]{1,0:T(8,128)(2,1)S(1)}, u32[]{:S(2)}, u32[]{:S(2)}) %collective-permute-start.16) | collective-permute-done | bytes 458784 | tf_op jit(solution)/shard_map/ppermute | solution.py:67
  87.8 11.4 %prepare.1 = (bf16[1536,640]{1,0:T(8,128)(2,1)}, bf16[1536,512]{1,0:T(8,128)(2,1)S(1)}, f32[1536,512]{1,0:T(8,128)}, f32[1536,128]{1,0:T(8,128)S(1)}, f32[8,1536]{1,0:T(8,128)S(1)}) custom-call(s32[24]{0:T(128)S(1)} %concatenate.80.ints, f32[8]{0:T(128)S(1)} %pad_maximum_fusion.18.floats, f32[8,1536]{1,0:T(8,128)S(1)} %pad_maximum_fusion.15.rows_ref, ...), custom_call_target="tpu_custom_call" | custom-call | flops 4026531840 | bytes 12000000 | tf_op jit(solution)/shard_map/prepare/pallas_call | solution.py:860
  107.7 11.9 %experts_forward.3 = (f32[1536,128]{1,0:T(8,128)S(1)}, f32[1536,512]{1,0:T(8,128)}, bf16[3,1536,512]{2,1,0:T(8,128)(2,1)}) custom-call(s32[24]{0:T(128)S(1)} %concatenate.80.ints, bf16[1536,512]{1,0:T(8,128)(2,1)} %copy-done.1, ...), custom_call_target="tpu_custom_call", output_to_operand_aliasing={{0}: (12, {}), {1}: (13, {})} | custom-call | flops 4831838208 | bytes 12000000 | tf_op jit(solution)/shard_map/experts_forward/pallas_call | solution.py:926
  128.7 8.0 %experts_forward.4 = (f32[1536,128]{1,0:T(8,128)S(1)}, f32[1536,512]{1,0:T(8,128)}, bf16[3,1536,512]{2,1,0:T(8,128)(2,1)}, bf16[768,512]{1,0:T(8,128)(2,1)S(1)}) custom-call(s32[24]{0:T(128)S(1)} %concatenate.80.ints, bf16[1536,512]{1,0:T(8,128)(2,1)} %copy-done.1, ...), custom_call_target="tpu_custom_call", output_to_operand_aliasing={{0}: (12, {}), {1}: (13, {})} | custom-call | flops 1610612736 | bytes 12000000 | tf_op jit(solution)/shard_map/experts_forward/pallas_call | solution.py:926
  136.8 18.4 %experts_forward.5 = (f32[1536,128]{1,0:T(8,128)S(1)}, f32[1536,512]{1,0:T(8,128)}, bf16[3,1536,512]{2,1,0:T(8,128)(2,1)}, bf16[3,1536,512]{2,1,0:T(8,128)(2,1)}) custom-call(s32[24]{0:T(128)S(1)} %concatenate.80.ints, bf16[1536,512]{1,0:T(8,128)(2,1)} %copy-done.1, ...), custom_call_target="tpu_custom_call", output_to_operand_aliasing={{0}: (20, {}), {1}: (21, {}), {2}: (22, {}), {3}: (23, {})} | custom-call | flops 4831838208 | bytes 12000000 | tf_op jit(solution)/shard_map/experts_forward/pallas_call | solution.py:926
  156.4 9.1 %towers.1 = (f32[8,768]{1,0:T(8,128)S(1)}, f32[768,512]{1,0:T(8,128)S(1)}, bf16[768,512]{1,0:T(8,128)(2,1)S(1)}, f32[512,1024]{1,0:T(8,128)}, f32[8,1024]{1,0:T(8,128)S(1)}, /*index=5*/f32[8,128]{1,0:T(8,128)S(1)}) custom-call(s32[24]{0:T(128)S(1)} %concatenate.80.ints, f32[1536,512]{1,0:T(8,128)} %get-tuple-element.295.mix_ref, ...), custom_call_target="tpu_custom_call" | custom-call | flops 2415919104 | bytes 10000000 | tf_op jit(solution)/shard_map/towers/pallas_call | solution.py:1033
  169.2 16.2 %experts_backward.4 = (f32[1536,128]{1,0:T(8,128)S(1)}, f32[1536,512]{1,0:T(8,128)}, bf16[2,2,512,512]{3,2,1,0:T(8,128)(2,1)}, bf16[2,2,512,512]{3,2,1,0:T(8,128...) custom-call(s32[24]{0:T(128)S(1)} %concatenate.80.ints, ...), custom_call_target="tpu_custom_call", output_to_operand_aliasing={{0}: (14, {})} | custom-call | flops 8053063680 | bytes 20000000 | tf_op jit(solution)/shard_map/experts_backward/pallas_call | solution.py:994
  187.3 16.3 %experts_backward.5 = (f32[1536,128]{1,0:T(8,128)S(1)}, f32[1536,512]{1,0:T(8,128)}, bf16[2,2,512,512]{3,2,1,0:T(8,128)(2,1)}, bf16[2,2,512,512]{3,2,1,0:T(8,128...) custom-call(s32[24]{0:T(128)S(1)} %concatenate.80.ints, ...), custom_call_target="tpu_custom_call", output_to_operand_aliasing={{0}: (14, {}), {1}: (15, {})} | custom-call | flops 8053063680 | bytes 20000000 | tf_op jit(solution)/shard_map/experts_backward/pallas_call | solution.py:994
  204.7 11.1 %experts_backward.6 = (f32[1536,128]{1,0:T(8,128)S(1)}, f32[1536,512]{1,0:T(8,128)}, bf16[1,2,512,512]{3,2,1,0:T(8,128)(2,1)}, bf16[1,2,512,512]{3,2,1,0:T(8,128...) custom-call(s32[24]{0:T(128)S(1)} %concatenate.80.ints, ...), custom_call_target="tpu_custom_call", output_to_operand_aliasing={{0}: (15, {}), {1}: (16, {})} | custom-call | flops 4026531840 | bytes 20000000 | tf_op jit(solution)/shard_map/experts_backward/pallas_call | solution.py:994
  218.4 3.3 add_convert_fusion.2
  224.1 23.9 %experts_backward.7 = (f32[1536,128]{1,0:T(8,128)S(1)}, f32[1536,512]{1,0:T(8,128)}, bf16[3,2,512,512]{3,2,1,0:T(8,128)(2,1)}, bf16[3,2,512,512]{3,2,1,0:T(8,128...) custom-call(s32[24]{0:T(128)S(1)} %copy-done.32, ...), custom_call_target="tpu_custom_call", output_to_operand_aliasing={{0}: (15, {}), {1}: (16, {})} | custom-call | flops 12079595520 | bytes 20000000 | tf_op jit(solution)/shard_map/experts_backward/pallas_call | solution.py:994
  248.2 3.4 collective-permute-start.43
  252.3 4.8 %collective-permute-done.43 = bf16[3,2,512,512]{3,2,1,0:T(8,128)(2,1)S(1)} collective-permute-done((bf16[3,2,512,512]{3,2,1,0:T(8,128)(2,1)}, bf16[3,2,512,512]{3,2,1,0:T(8,128)(2,1)S(1)}, u32[]{:S(2)}, u32[]{:S(2)}) %collective-permute-start.43) | collective-permute-done | bytes 3145760 | tf_op jit(solution)/shard_map/ppermute | solution.py:136
  259.9 4.9 %gates.1 = (f32[1536,512]{1,0:T(8,128)}, bf16[1536,512]{1,0:T(8,128)(2,1)S(1)}, f32[512,128]{1,0:T(8,128)S(1)}) custom-call(s32[24]{0:T(128)S(1)} %copy-done.32, f32[1536,512]{1,0:T(8,128)} %get-tuple-element.359.back_ref, f32[1536,128]{1,0:T(8,128)S(1)} %get-tuple-element.360.cols_ref, f32[8,1536]{1,0:T(8,128)S(1)} %get-tuple-element.361.prob_ref, ...), custom_call_target="tpu_custom_call" | custom-call | flops 402653184 | bytes 10000000 | tf_op jit(solution)/shard_map/gates/pallas_call | solution.py:513
  271.5 23.3 %collective-permute-done.41 = bf16[3,2,2,32,512]{4,3,0,2,1:T(8,128)(2,1)S(1)} collective-permute-done((bf16[3,2,2,32,512]{4,3,0,2,1:T(8,128)(2,1)S(1)}, bf16[3,2,2,32,512]{4,3,0,2,1:T(8,128)(2,1)S(1)}, u32[]{:S(2)}, u32[]{:S(2)}) %collective-permute-start.41) | collective-permute-done | bytes 393248 | tf_op jit(solution)/shard_map/ppermute | solution.py:67
  305.0 9.8 %finish.1 = (bf16[1536,640]{1,0:T(8,128)(2,1)}, bf16[512,1792]{1,0:T(8,128)(2,1)}) custom-call(s32[24]{0:T(128)S(1)} %copy-done.33, f32[768,512]{1,0:T(8,128)S(1)} %copy-done.19, bf16[768,512]{1,0:T(8,128)(2,1)S(1)} %collective-permute-done.29.refs_0_.refs_1_.gb_in_ref, f32[1536,512]{1,0:T(8,128)} %get-tuple-element.372.sum_ref, ...), custom_call_target="tpu_custom_call" | custom-call | flops 2013265920 | bytes 14000000 | tf_op jit(solution)/shard_map/finish/pallas_call | solution.py:618
  327.2 4.3 %fusion.2 = bf16[1536,640]{1,0:T(8,128)(2,1)S(1)} fusion(bf16[1536,640]{1,0:T(8,128)(2,1)S(1)} %copy-done.68, f32[1536]{0:T(1024)S(1)} %add_bitcast_fusion.1), kind=kOutput, calls=%fused_computation.4 | convolution fusion | flops 3023241216 | bytes 3938304 | tf_op jit(solution)/shard_map/dot_general | solution.py:1329
  333.0 8.6 %collective-permute-done.51 = bf16[2,3,2,32,512]{4,3,1,0,2:T(8,128)(2,1)S(1)} collective-permute-done((bf16[2,3,2,32,512]{4,3,1,0,2:T(8,128)(2,1)S(1)}, bf16[2,3,2,32,512]{4,3,1,0,2:T(8,128)(2,1)S(1)}, u32[]{:S(2)}, u32[]{:S(2)}) %collective-permute-start.51) | collective-permute-done | bytes 393248 | tf_op jit(solution)/shard_map/ppermute | solution.py:67
  (384 shorter events, 119.4 us)
Async XLA Ops:
  32.2 28.8 %collective-permute-start.6 = (bf16[2,3,32,512]{3,2,1,0:T(8,128)(2,1)S(1)}, bf16[2,3,32,512]{3,2,1,0:T(8,128)(2,1)}, u32[]{:S(2)}, u32[]{:S(2)}) collective-permute-start(bf16[2,3,32,512]{3,2,1,0:T(8,128)(2,1)S(1)} %get-tuple-element.234), channel_id=1, source_target_pairs={{0,24},{2,26},{4,28},{6,30},{8,16},{10,18},{12,20},{14,22},{16,8},... | collective-permute-start | bytes 589832 | tf_op jit(solution)/shard_map/ppermute | solution.py:67
  36.1 21.9 %collective-permute-start.5 = (bf16[2,3,32,512]{3,2,1,0:T(8,128)(2,1)S(1)}, bf16[2,3,32,512]{3,2,1,0:T(8,128)(2,1)}, u32[]{:S(2)}, u32[]{:S(2)}) collective-permute-start(bf16[2,3,32,512]{3,2,1,0:T(8,128)(2,1)S(1)} %get-tuple-element.241), channel_id=1, source_target_pairs={{0,16},{2,18},{4,20},{6,22},{8,24},{10,26},{12,28},{14,30},{16,0},... | collective-permute-start | bytes 589832 | tf_op jit(solution)/shard_map/ppermute | solution.py:67
  36.2 24.8 %collective-permute-start.3 = (bf16[2,3,64,512]{3,2,1,0:T(8,128)(2,1)S(1)}, bf16[2,3,64,512]{3,2,1,0:T(8,128)(2,1)S(1)}, u32[]{:S(2)}, u32[]{:S(2)}) collective-permute-start(bf16[2,3,64,512]{3,2,1,0:T(8,128)(2,1)S(1)} %pad_maximum_fusion.10), channel_id=1, source_target_pairs={{0,4},{2,6},{4,0},{6,2},{8,12},{10,14},{12,8},{14,10},{16,20},{18,... | collective-permute-start | bytes 1179656 | tf_op jit(solution)/shard_map/ppermute | solution.py:67
  37.8 23.2 %collective-permute-start.4 = (bf16[2,3,64,512]{3,2,1,0:T(8,128)(2,1)S(1)}, bf16[2,3,64,512]{3,2,1,0:T(8,128)(2,1)S(1)}, u32[]{:S(2)}, u32[]{:S(2)}) collective-permute-start(bf16[2,3,64,512]{3,2,1,0:T(8,128)(2,1)S(1)} %pad_maximum_fusion.11), channel_id=1, source_target_pairs={{0,2},{2,0},{4,6},{6,4},{8,10},{10,8},{12,14},{14,12},{16,18},{18,... | collective-permute-start | bytes 1179656 | tf_op jit(solution)/shard_map/ppermute | solution.py:67
  58.0 26.8 %collective-permute-start.12 = (bf16[1536,640]{1,0:T(8,128)(2,1)}, bf16[1536,640]{1,0:T(8,128)(2,1)}, u32[]{:S(2)}, u32[]{:S(2)}) collective-permute-start(bf16[1536,640]{1,0:T(8,128)(2,1)} %param.21), channel_id=1, source_target_pairs={{0,8},{2,10},{4,12},{6,14},{9,1},{11,3},{13,5},{15,7},{16,24},{18,... | collective-permute-start | bytes 5898248 | tf_op jit(solution)/shard_map/ppermute | solution.py:75
  65.7 34.6 %collective-permute-start.10 = (bf16[2,3,64,512]{3,2,1,0:T(8,128)(2,1)}, bf16[2,3,64,512]{3,2,1,0:T(8,128)(2,1)}, u32[]{:S(2)}, u32[]{:S(2)}) collective-permute-start(bf16[2,3,64,512]{3,2,1,0:T(8,128)(2,1)} %pad_maximum_fusion.12), channel_id=1, source_target_pairs={{0,4},{2,6},{4,0},{6,2},{8,12},{10,14},{12,8},{14,10},{16,20},{18,... | collective-permute-start | bytes 1179656 | tf_op jit(solution)/shard_map/ppermute | solution.py:67
  67.2 33.1 %collective-permute-start.11 = (bf16[2,3,64,512]{3,2,1,0:T(8,128)(2,1)}, bf16[2,3,64,512]{3,2,1,0:T(8,128)(2,1)}, u32[]{:S(2)}, u32[]{:S(2)}) collective-permute-start(bf16[2,3,64,512]{3,2,1,0:T(8,128)(2,1)} %pad_maximum_fusion.13), channel_id=1, source_target_pairs={{0,2},{2,0},{4,6},{6,4},{8,10},{10,8},{12,14},{14,12},{16,18},{18,... | collective-permute-start | bytes 1179656 | tf_op jit(solution)/shard_map/ppermute | solution.py:67
  76.6 23.7 %collective-permute-start.9 = (bf16[2,2,3,64,512]{4,3,2,1,0:T(8,128)(2,1)S(1)}, bf16[2,2,3,64,512]{4,3,2,1,0:T(8,128)(2,1)S(1)}, u32[]{:S(2)}, u32[]{:S(2)}) collective-permute-start(bf16[2,2,3,64,512]{4,3,2,1,0:T(8,128)(2,1)S(1)} %pad_maximum_fusion.4.refs_2_.refs_4_.refs_5_), channel_id=1, source_target_pairs={{0,4},{2,6},{4,0},{6,2},{8,12},{10,14},{12,8},{14,10},{16,20},{18,... | collective-permute-start | bytes 2359304 | tf_op jit(solution)/shard_map/ppermute | solution.py:67
  79.1 21.2 %collective-permute-start.8 = (bf16[2,2,3,64,512]{4,3,2,1,0:T(8,128)(2,1)S(1)}, bf16[2,2,3,64,512]{4,3,2,1,0:T(8,128)(2,1)S(1)}, u32[]{:S(2)}, u32[]{:S(2)}) collective-permute-start(bf16[2,2,3,64,512]{4,3,2,1,0:T(8,128)(2,1)S(1)} %pad_maximum_fusion.3.refs_0_.refs_2_.refs_3_), channel_id=1, source_target_pairs={{0,2},{2,0},{4,6},{6,4},{8,10},{10,8},{12,14},{14,12},{16,18},{18,... | collective-permute-start | bytes 2359304 | tf_op jit(solution)/shard_map/ppermute | solution.py:67
  102.6 19.6 %collective-permute-start.23 = (bf16[2,2,3,64,512]{4,3,2,1,0:T(8,128)(2,1)S(1)}, bf16[2,2,3,64,512]{4,3,2,1,0:T(8,128)(2,1)S(1)}, u32[]{:S(2)}, u32[]{:S(2)}) collective-permute-start(bf16[2,2,3,64,512]{4,3,2,1,0:T(8,128)(2,1)S(1)} %pad_maximum_fusion.6.refs_2_.refs_10_.refs_5_), channel_id=1, source_target_pairs={{0,4},{2,6},{4,0},{6,2},{8,12},{10,14},{12,8},{14,10},{16,20},{18,... | collective-permute-start | bytes 2359304 | tf_op jit(solution)/shard_map/ppermute | solution.py:67
  105.1 19.3 %collective-permute-start.22 = (bf16[2,2,3,64,512]{4,3,2,1,0:T(8,128)(2,1)S(1)}, bf16[2,2,3,64,512]{4,3,2,1,0:T(8,128)(2,1)S(1)}, u32[]{:S(2)}, u32[]{:S(2)}) collective-permute-start(bf16[2,2,3,64,512]{4,3,2,1,0:T(8,128)(2,1)S(1)} %pad_maximum_fusion.5.refs_0_.refs_8_.refs_3_), channel_id=1, source_target_pairs={{0,2},{2,0},{4,6},{6,4},{8,10},{10,8},{12,14},{14,12},{16,18},{18,... | collective-permute-start | bytes 2359304 | tf_op jit(solution)/shard_map/ppermute | solution.py:67
  105.7 19.2 %collective-permute-start.26 = (bf16[2,2,3,64,512]{4,3,2,1,0:T(8,128)(2,1)S(1)}, bf16[2,2,3,64,512]{4,3,2,1,0:T(8,128)(2,1)S(1)}, u32[]{:S(2)}, u32[]{:S(2)}) collective-permute-start(bf16[2,2,3,64,512]{4,3,2,1,0:T(8,128)(2,1)S(1)} %pad_maximum_fusion.6.refs_2_.refs_10_.refs_5_), channel_id=1, source_target_pairs={{0,1},{1,0},{2,3},{3,2},{4,5},{5,4},{6,7},{7,6},{8,9},{9,8},{10,11... | collective-permute-start | bytes 2359304 | tf_op jit(solution)/shard_map/ppermute | solution.py:136
  105.7 19.2 %collective-permute-start.24 = (bf16[2,2,3,64,512]{4,3,2,1,0:T(8,128)(2,1)S(1)}, bf16[2,2,3,64,512]{4,3,2,1,0:T(8,128)(2,1)S(1)}, u32[]{:S(2)}, u32[]{:S(2)}) collective-permute-start(bf16[2,2,3,64,512]{4,3,2,1,0:T(8,128)(2,1)S(1)} %pad_maximum_fusion.5.refs_0_.refs_8_.refs_3_), channel_id=1, source_target_pairs={{0,1},{1,0},{2,3},{3,2},{4,5},{5,4},{6,7},{7,6},{8,9},{9,8},{10,11... | collective-permute-start | bytes 2359304 | tf_op jit(solution)/shard_map/ppermute | solution.py:136
  136.7 19.6 %collective-permute-start.28 = (bf16[768,512]{1,0:T(8,128)(2,1)S(1)}, bf16[768,512]{1,0:T(8,128)(2,1)S(1)}, u32[]{:S(2)}, u32[]{:S(2)}) collective-permute-start(bf16[768,512]{1,0:T(8,128)(2,1)S(1)} %get-tuple-element.296), channel_id=1, source_target_pairs={{0,8},{2,10},{4,12},{6,14},{8,0},{10,2},{12,4},{14,6},{16,24},{18,... | collective-permute-start | bytes 2359304 | tf_op jit(solution)/shard_map/ppermute | solution.py:67
  216.0 32.1 %collective-permute-start.40 = (f32[8,128]{1,0:T(8,128)S(1)}, f32[8,128]{1,0:T(8,128)S(1)}, u32[]{:S(2)}, u32[]{:S(2)}) collective-permute-start(f32[8,128]{1,0:T(8,128)S(1)} %add.634), channel_id=1, source_target_pairs={{0,16},{2,18},{4,20},{6,22},{8,24},{10,26},{12,28},{14,30},{16,0},... | collective-permute-start | bytes 12296 | tf_op jit(solution)/shard_map/ppermute | solution.py:67
  217.1 31.1 %collective-permute-start.39 = (f32[8,768]{1,0:T(8,128)S(1)}, f32[8,768]{1,0:T(8,128)S(1)}, u32[]{:S(2)}, u32[]{:S(2)}) collective-permute-start(f32[8,768]{1,0:T(8,128)S(1)} %get-tuple-element.349), channel_id=1, source_target_pairs={{1,9},{3,11},{5,13},{7,15},{8,0},{10,2},{12,4},{14,6},{17,25},{19,... | collective-permute-start | bytes 73736 | tf_op jit(solution)/shard_map/ppermute | solution.py:75
  222.3 25.8 %collective-permute-start.38 = (bf16[3,2,2,2,32,512]{5,4,0,3,2,1:T(8,128)(2,1)S(1)}, bf16[3,2,2,2,32,512]{5,4,0,3,2,1:T(8,128)(2,1)S(1)}, u32[]{:S(2)}, u32[]{:S(2)}) collective-permute-start(bf16[3,2,2,2,32,512]{5,4,0,3,2,1:T(8,128)(2,1)S(1)} %bitcast.167), channel_id=1, source_target_pairs={{0,4},{2,6},{4,0},{6,2},{8,12},{10,14},{12,8},{14,10},{16,20},{18,... | collective-permute-start | bytes 2359304 | tf_op jit(solution)/shard_map/ppermute | solution.py:67
  223.1 25.1 %collective-permute-start.37 = (bf16[3,2,2,2,32,512]{5,4,0,3,2,1:T(8,128)(2,1)S(1)}, bf16[3,2,2,2,32,512]{5,4,0,3,2,1:T(8,128)(2,1)S(1)}, u32[]{:S(2)}, u32[]{:S(2)}) collective-permute-start(bf16[3,2,2,2,32,512]{5,4,0,3,2,1:T(8,128)(2,1)S(1)} %get-tuple-element.446), channel_id=1, source_target_pairs={{0,2},{2,0},{4,6},{6,4},{8,10},{10,8},{12,14},{14,12},{16,18},{18,... | collective-permute-start | bytes 2359304 | tf_op jit(solution)/shard_map/ppermute | solution.py:67
  264.8 31.4 %collective-permute-start.46 = (bf16[1536,512]{1,0:T(8,128)(2,1)S(1)}, bf16[1536,512]{1,0:T(8,128)(2,1)S(1)}, u32[]{:S(2)}, u32[]{:S(2)}) collective-permute-start(bf16[1536,512]{1,0:T(8,128)(2,1)S(1)} %get-tuple-element.362), channel_id=1, source_target_pairs={{1,9},{3,11},{5,13},{7,15},{8,0},{10,2},{12,4},{14,6},{17,25},{19,... | collective-permute-start | bytes 4718600 | tf_op jit(solution)/shard_map/ppermute | solution.py:75
  266.4 29.7 %collective-permute-start.45 = (bf16[3,2,2,2,32,512]{5,4,0,3,2,1:T(8,128)(2,1)S(1)}, bf16[3,2,2,2,32,512]{5,4,0,3,2,1:T(8,128)(2,1)S(1)}, u32[]{:S(2)}, u32[]{:S(2)}) collective-permute-start(bf16[3,2,2,2,32,512]{5,4,0,3,2,1:T(8,128)(2,1)S(1)} %bitcast.169), channel_id=1, source_target_pairs={{0,4},{2,6},{4,0},{6,2},{8,12},{10,14},{12,8},{14,10},{16,20},{18,... | collective-permute-start | bytes 2359304 | tf_op jit(solution)/shard_map/ppermute | solution.py:67
  267.3 28.9 %collective-permute-start.44 = (bf16[3,2,2,2,32,512]{5,4,0,3,2,1:T(8,128)(2,1)S(1)}, bf16[3,2,2,2,32,512]{5,4,0,3,2,1:T(8,128)(2,1)S(1)}, u32[]{:S(2)}, u32[]{:S(2)}) collective-permute-start(bf16[3,2,2,2,32,512]{5,4,0,3,2,1:T(8,128)(2,1)S(1)} %bitcast.168), channel_id=1, source_target_pairs={{0,2},{2,0},{4,6},{6,4},{8,10},{10,8},{12,14},{14,12},{16,18},{18,... | collective-permute-start | bytes 2359304 | tf_op jit(solution)/shard_map/ppermute | solution.py:67
  269.6 25.3 %collective-permute-start.41 = (bf16[3,2,2,32,512]{4,3,0,2,1:T(8,128)(2,1)S(1)}, bf16[3,2,2,32,512]{4,3,0,2,1:T(8,128)(2,1)S(1)}, u32[]{:S(2)}, u32[]{:S(2)}) collective-permute-start(bf16[3,2,2,32,512]{4,3,0,2,1:T(8,128)(2,1)S(1)} %get-tuple-element.462), channel_id=1, source_target_pairs={{0,4},{2,6},{4,0},{6,2},{8,12},{10,14},{12,8},{14,10},{16,20},{18,... | collective-permute-start | bytes 1179656 | tf_op jit(solution)/shard_map/ppermute | solution.py:67
  271.5 24.7 %collective-permute-start.42 = (bf16[3,2,2,32,512]{4,3,0,2,1:T(8,128)(2,1)S(1)}, bf16[3,2,2,32,512]{4,3,0,2,1:T(8,128)(2,1)S(1)}, u32[]{:S(2)}, u32[]{:S(2)}) collective-permute-start(bf16[3,2,2,32,512]{4,3,0,2,1:T(8,128)(2,1)S(1)} %get-tuple-element.460), channel_id=1, source_target_pairs={{0,2},{2,0},{4,6},{6,4},{8,10},{10,8},{12,14},{14,12},{16,18},{18,... | collective-permute-start | bytes 1179656 | tf_op jit(solution)/shard_map/ppermute | solution.py:67
  320.3 21.2 %collective-permute-start.51 = (bf16[2,3,2,32,512]{4,3,1,0,2:T(8,128)(2,1)S(1)}, bf16[2,3,2,32,512]{4,3,1,0,2:T(8,128)(2,1)S(1)}, u32[]{:S(2)}, u32[]{:S(2)}) collective-permute-start(bf16[2,3,2,32,512]{4,3,1,0,2:T(8,128)(2,1)S(1)} %get-tuple-element.452), channel_id=1, source_target_pairs={{0,16},{2,18},{4,20},{6,22},{8,24},{10,26},{12,28},{14,30},{16,0},... | collective-permute-start | bytes 1179656 | tf_op jit(solution)/shard_map/ppermute | solution.py:67
  (108 other events, 1636.6 us)

commit v4 on v3

--- a/solution.py
+++ b/solution.py
@@ -111,19 +111,8 @@
             found = jnp.take(found, (jnp.arange(size) - mine) % size, axis=0)
         return functools.reduce(jnp.add, [found[k] for k in range(size)])
 
-    def places(self):
+    def ahead(self, place):
         me = lax.axis_index("dp")
-        chip = jnp.arange(self.count)
-        place, weight = 0, 1
-        for dim, (size, stride) in enumerate(zip(self.dims, self.strides)):
-            mine = (me // stride) % size if dim else 0
-            place = place + (((chip // stride) % size - mine) % size) * weight
-            weight *= size
-        return place
-
-    def ahead(self):
-        me = lax.axis_index("dp")
-        place = jnp.arange(self.count)
         chip, weight = 0, 1
         for dim, (size, stride) in enumerate(zip(self.dims, self.strides)):
             mine = (me // stride) % size if dim else 0
@@ -179,11 +168,27 @@
     return e / jnp.sum(e, axis=0, keepdims=True)
 
 
-def prepare_kernel(ints, floats, rows_ref, embeds_ref, proj_ref, gates_ref, vec_ref, ev_ref, x_ref, mix_ref, cols_ref, prob_ref):
+def prepare_kernel(
+    ints, floats, rows_ref, own_ref, in_ref, proj_ref, gates_ref, vec_ref, ev_ref, x_ref, mix_ref, cols_ref, prob_ref, embeds_ref, arrived
+):
     tiles_of_half = pl.num_programs(0) // 2
     index = pl.program_id(0)
     role = ints[ROLE]
     count = rows_ref.shape[1]
+    at_home = ints[CORE] == role
+
+    @pl.when((index == 0) & at_home)
+    def _():
+        copy = pltpu.make_async_copy(own_ref, embeds_ref, arrived.at[0])
+        copy.start()
+        copy.wait()
+
+    @pl.when((index == 0) & jnp.logical_not(at_home))
+    def _():
+        copy = pltpu.make_async_copy(in_ref, embeds_ref, arrived.at[0])
+        copy.start()
+        copy.wait()
+
     slot = index * TILE + lax.broadcasted_iota(jnp.int32, (TILE, count), 0)
     here = rows_ref[0:1, :].astype(jnp.int32) == slot
     order = jnp.where(here, 1.0, 0.0).astype(bf16)
@@ -713,24 +718,17 @@
     return pl.BlockSpec(shape, lambda i, *_: (0,) * len(shape))
 
 
-def pack_kernel(count, *refs):
-    sources, out_ref, held, arrived = refs[:count], refs[count], refs[count + 1 : -1], refs[-1]
-    copies = [pltpu.make_async_copy(a, b, arrived.at[k]) for k, (a, b) in enumerate(zip(sources, held))]
-    for copy in copies:
-        copy.start()
-    for copy in copies:
-        copy.wait()
-    proj_ref, tower_ref, *row_refs, in_bias_ref, tower_b_ref, tower_out_ref = held
+def pack_kernel(proj_ref, tower_ref, gate_ref, rest_ref, out_ref):
     width, e_in = proj_ref.shape
     out_ref[:, :e_in] = proj_ref[...]
     for d in range(DOM):
         out_ref[:, e_in + d * TW : e_in + (d + 1) * TW] = tower_ref[d]
-    rows = [r[...].astype(f32) for r in row_refs]
-    bias = in_bias_ref[...].astype(f32)
-    rows += [bias[:, :width], bias[:, width:]]
-    rows.append(
-        jnp.concatenate([tower_b_ref[...].astype(f32), tower_out_ref[...].astype(f32)], axis=1)
-    )
+    gates, rest = gate_ref[...].astype(f32), rest_ref[...].astype(f32)
+    rows = []
+    for low, size in ((0, 2), (2, S), (2 + S, K)):
+        rows += [gates[d, low : low + size] for d in range(DOM)]
+    rows += [rest[:12, k * width : (k + 1) * width] for k in range(3)] + [rest[16:17, :width]]
+    rows += [rest[:12, k * width : (k + 1) * width] for k in (3, 4)] + [rest[12:16, :width]]
     rows = jnp.concatenate(rows + [jnp.zeros((31, width), f32)], axis=0)
     rows = jnp.concatenate([rows, jnp.zeros((128, 128 - width), f32)], axis=1)
     out_ref[:, e_in + DOM * TW :] = jnp.transpose(rows)[:width].astype(bf16)
@@ -739,12 +737,11 @@
 def call_pack(*arrays):
     width = arrays[0].shape[0]
     return pl.pallas_call(
-        functools.partial(pack_kernel, len(arrays)),
-        in_specs=[pl.BlockSpec(memory_space=pltpu.HBM)] * len(arrays),
-        out_specs=pl.BlockSpec(memory_space=pltpu.VMEM),
+        pack_kernel,
+        grid=(1,),
+        in_specs=[fixed(a.shape) for a in arrays],
+        out_specs=fixed((width, PACK)),
         out_shape=jax.ShapeDtypeStruct((width, PACK), bf16),
-        scratch_shapes=[pltpu.VMEM(a.shape, a.dtype) for a in arrays]
-        + [pltpu.SemaphoreType.DMA((len(arrays),))],
         compiler_params=params(),
         name="pack",
     )(*arrays)
@@ -849,7 +846,7 @@
 GATES_SPEC = pl.BlockSpec((D, 128), lambda *_: (0, PACK // 128 - 1))
 
 
-def call_prepare(ints, floats, table, embeds, small, vec):
+def call_prepare(ints, floats, table, embeds, embeds_in, small, vec):
     rows = embeds.shape[0]
     tiles = rows // TILE
     e_in = embeds.shape[1]
@@ -862,7 +859,10 @@
         grid_spec=pltpu.PrefetchScalarGridSpec(
             num_scalar_prefetch=2,
             grid=(tiles,),
-            in_specs=[fixed(table.shape), fixed(embeds.shape), proj_spec(e_in), GATES_SPEC, fixed(vec.shape)],
+            in_specs=[fixed(table.shape)]
+            + [pl.BlockSpec(memory_space=pl.ANY)] * 2
+            + [proj_spec(e_in), GATES_SPEC, fixed(vec.shape)],
+            scratch_shapes=[pltpu.VMEM(embeds.shape, bf16), pltpu.SemaphoreType.DMA((1,))],
             out_specs=(
                 tile(e_in),
                 tile(D),
@@ -883,7 +883,7 @@
             flops=2 * rows * e_in * (rows + D), bytes_accessed=12_000_000, transcendentals=rows * 8
         ),
         name="prepare",
-    )(ints, floats, table, embeds, small, small, vec)
+    )(ints, floats, table, embeds, embeds_in, small, small, vec)
 
 
 def half_spec(own, shape):
@@ -1091,7 +1091,6 @@
     half_rows = rows // 2
     width = proj_w.shape[1]
     e_in = proj_w.shape[0]
-    place_of = box.places()
     nz, ny, nx = box.dims[1:]
     sets = jnp.array(SETS, jnp.int32)
     set_own, set_other = sets[role], sets[1 - role]
@@ -1102,23 +1101,25 @@
     w_out_t = jnp.swapaxes(w_out, 1, 2)
     first, second, first_other, second_other, others = call_choose(set_own, set_other, w_in, w_out_t)
 
+    def wide(values):
+        return jnp.pad(values, ((0, 0), (0, 5 * width - values.shape[1])))
+
     arrays = (
         proj_w.T,
         tower_w,
-        jnp.swapaxes(gate_top, 1, 2).reshape(2 * DOM, width),
-        jnp.swapaxes(gate_shared, 1, 2).reshape(S * DOM, width),
-        jnp.swapaxes(gate_domain, 1, 2).reshape(K * DOM, width),
-        out_bias,
-        ln_gain,
-        ln_shift,
-        proj_b[None],
-        in_bias,
-        tower_b,
-        tower_out,
-    )
+        jnp.concatenate([jnp.swapaxes(g, 1, 2) for g in (gate_top, gate_shared, gate_domain)], axis=1),
+        jnp.concatenate(
+            [
+                jnp.concatenate([out_bias, ln_gain, ln_shift, in_bias], axis=1),
+                wide(jnp.concatenate([tower_b, tower_out], axis=1)),
+                wide(proj_b[None]),
+            ]
+        ),
+    )
+
     flips = box.send(others, flip=1)
     first_z = box.line(first, first_other)
-    pack = call_pack(*step(arrays, flips)[0])
+    pack = call_pack(*step(arrays, first)[0])
     pack = in_order(role, pack, box.send(pack, flip=1), 0)
     pack = jnp.concatenate([pack] + box.pieces(pack, "z"))
     flips, first, first_z, second, second_other = step(flips, first, first_z, second, second_other)
@@ -1156,13 +1157,13 @@
     second_i, second_o = along_z(second, flips[:, 3:], second_z)
     second_iy, second_ox = box.pieces(second_i, "y"), box.pieces(second_o, "x")
 
-    device = (2 * box.ahead()[:, None, None] + jnp.arange(2)[None, :, None]).astype(jnp.int32)
-    unit = jnp.arange(width, dtype=jnp.int32)[None, None, :]
-    narrow = width // 2
-    lanes = [device * 2 * width + unit, device * 2 * width + width + unit]
-    lanes += [d * TW + device * narrow + unit % narrow for d in range(DOM)]
-    lanes += [jnp.broadcast_to(unit // narrow, (places, 2, width))] * 2
-    lanes = jnp.stack([jnp.broadcast_to(v, (places, 2, width)).reshape(D) for v in lanes])
+    at = lax.broadcasted_iota(jnp.int32, (8, D), 1)
+    row = lax.broadcasted_iota(jnp.int32, (8, D), 0)
+    unit, narrow = at % width, width // 2
+    device = 2 * box.ahead(at // (2 * width)) + (at // width) % 2
+    hidden = device * (2 * width) + jnp.where(row == 1, width, 0) + unit
+    lanes = (row - 2) * TW + device * narrow + unit % narrow
+    lanes = jnp.where(row < 2, hidden, jnp.where(row < 2 + DOM, lanes, unit // narrow))
     vec, bi, tower_vec = call_unpack(jnp.stack([role, core]), small, lanes)
 
     table = jnp.concatenate([position[None], event_rows[1:]])
@@ -1185,8 +1186,7 @@
     )
     loss_weight = 1.0 - (1.0 - FROZEN_SHARE) * frozen.astype(f32)
     floats = jnp.concatenate([loss_weight, tower_out_b.astype(f32)])
-    embeds = jnp.where(at_home, embeds, embeds_in)
-    events, x, mix, cols, probs = call_prepare(ints, floats, table, embeds, small, vec)
+    events, x, mix, cols, probs = call_prepare(ints, floats, table, embeds, embeds_in, small, vec)
     (
         first_i, first_o, first_ix, first_oy, second_i, second_o, second_iy, second_ox,
         ints, events, x, mix, cols, probs, vec, bi, small, tower_vec, lanes,
@@ -1303,9 +1303,10 @@
     d_logit_bias = box.same_sum(d_logit_bias, logit_in, "z")
     c0.second()
     give_d = swap_cores(give_d)
-    c1 = Scatter(both_cores([keep_d], [give_d]))
-    cols, back, _ = step(cols, back, (c0.state[:2], c1.state[:2]))
     g_sum, g_low, d_gate = call_gate(ints, back, cols, probs, x, small)
+    cd = both_cores([keep_d], [give_d])
+    g_sum, g_low, d_gate, cd = sync([c0], g_sum, g_low, d_gate, cd)
+    c1 = Scatter(cd)
     back_in = box.to_partner(g_low, False)
     (back_in,) = sync([c0, c1], back_in)
     c0.third()
@@ -1316,8 +1317,8 @@
         [sums_0, sums_1, sums_2],
     )
     grad_events, d_small = sync([c0, c1], grad_events, d_small)
+    c1.third()
     c0.fourth()
-    c1.third()
     d_small, _ = step(d_small, c1.state[0])
     d_small = d_small.reshape(places, 2, width, PACK)
     d_other = swap_cores(lax.dynamic_index_in_dim(d_small, 1 - core, 1, keepdims=False))

time: 365 us -> 353 us (0.967)
  waiting for transfers between devices: 90.1 us -> 76.7 us
    ppermute x41, waiting for transfers between devices: 81.2 us -> 66.9 us  [send(): return lax.ppermute(values, 'dp', pairs)]
    ppermute x4, waiting for transfers between devices: 0.01 us -> 5.71 us  [to_partner(): return lax.ppermute(values, ('dp', 'tensor'), pairs)]
    ppermute x17, waiting for transfers between devices: 8.88 us -> 4.08 us  [swap_cores(): return lax.ppermute(values, 'tensor', [(0, 1), (1, 0)])]
    unnamed x147 -> x121, local copies, waits for them, and re-layouts: 10.9 us -> 11.5 us
  transfers between devices with their start and end apart: 62 -> 62, of which waited for: 18 -> 19; matrix products, arithmetic and copies ran while one was open for 9% -> 11% of each run, Pallas kernels for 34% -> 36%
where the time goes in v4:
time: 353 us; the launch traced here: 349 us
  Pallas kernels  147 us (42%)
  waiting for transfers between devices  76.7 us (22%)
  starting transfers between devices  68.7 us (19%)
  other arithmetic  30.3 us (9%)
  local copies, waits for them, and re-layouts  19.7 us (6%)
  matrix products  4.28 us (1%)
    pallas_call x4, Pallas kernels, call_backward(): pl.pallas_call(functools.partial(backward_kernel, experts, halves, mode =...  68 us
    ppermute x41, waiting for transfers between devices, send(): return lax.ppermute(values, 'dp', pairs)  66.9 us
    ppermute x41, starting transfers between devices, send(): return lax.ppermute(values, 'dp', pairs)  54.2 us
    pallas_call x3, Pallas kernels, call_forward(): pl.pallas_call(functools.partial(forward_kernel, experts, own, len(kept),...  36.9 us
    pallas_call x1, Pallas kernels, call_prepare(): pl.pallas_call(prepare_kernel, grid_spec=pltpu.PrefetchScalarGridSpec(num...  11.6 us
    unnamed x121, local copies, waits for them, and re-layouts  11.5 us
    pallas_call x1, Pallas kernels, call_finish(): pl.pallas_call(finish_kernel, grid_spec=pltpu.PrefetchScalarGridSpec(num_...  9.96 us
    pallas_call x1, Pallas kernels, call_tower(): pl.pallas_call(tower_kernel, grid_spec=pltpu.PrefetchScalarGridSpec(num_s...  9.09 us
  transfers between devices with their start and end apart: 62, of which 19 were waited for; matrix products, arithmetic and copies ran while one was open for 11% of the time, Pallas kernels for 36%

profile of v4, /device:TPU:0, one launch (start us, length us, event | category | flops | bytes accessed | tf_op | source)
XLA Modules:
  0.0 348.6 jit_solution(9297848779921938218)
XLA Ops:
  4.6 4.1 %collective-permute-start.1 = (bf16[2,3,32,512]{3,2,1,0:T(8,128)(2,1)S(1)}, bf16[2,3,32,512]{3,2,1,0:T(8,128)(2,1)S(1)}, u32[]{:S(2)}, u32[]{:S(2)}) collective-permute-start(bf16[2,3,32,512]{3,2,1,0:T(8,128)(2,1)S(1)} %get-tuple-element.228), channel_id=1, source_target_pairs={{0,16},{2,18},{4,20},{6,22},{8,24},{10,26},{12,28},{14,30},{16,0},... | collective-permute-start | bytes 589832 | tf_op jit(solution)/shard_map/ppermute | solution.py:67
  17.2 5.6 %collective-permute-done.13 = bf16[16,1792]{1,0:T(8,128)(2,1)S(1)} collective-permute-done((bf16[16,1792]{1,0:T(8,128)(2,1)S(1)}, bf16[16,1792]{1,0:T(8,128)(2,1)S(1)}, u32[]{:S(2)}, u32[]{:S(2)}) %collective-permute-start.13) | collective-permute-done | bytes 57376 | tf_op jit(solution)/shard_map/ppermute | solution.py:67
  25.1 5.2 %collective-permute-done.14 = bf16[32,1792]{1,0:T(8,128)(2,1)S(1)} collective-permute-done((bf16[32,1792]{1,0:T(8,128)(2,1)S(1)}, bf16[32,1792]{1,0:T(8,128)(2,1)S(1)}, u32[]{:S(2)}, u32[]{:S(2)}) %collective-permute-start.14) | collective-permute-done | bytes 114720 | tf_op jit(solution)/shard_map/ppermute | solution.py:67
  34.4 2.9 collective-permute-start.7
  47.4 11.1 %collective-permute-done.5 = bf16[2,3,32,512]{3,2,1,0:T(8,128)(2,1)} collective-permute-done((bf16[2,3,32,512]{3,2,1,0:T(8,128)(2,1)S(1)}, bf16[2,3,32,512]{3,2,1,0:T(8,128)(2,1)}, u32[]{:S(2)}, u32[]{:S(2)}) %collective-permute-start.5) | collective-permute-done | bytes 196640 | tf_op jit(solution)/shard_map/ppermute | solution.py:67
  78.1 4.1 %collective-permute-done.12.in_ref = bf16[1536,640]{1,0:T(8,128)(2,1)} collective-permute-done((bf16[1536,640]{1,0:T(8,128)(2,1)}, bf16[1536,640]{1,0:T(8,128)(2,1)}, u32[]{:S(2)}, u32[]{:S(2)}) %collective-permute-start.12) | collective-permute-done | bytes 1966112 | tf_op jit(solution)/shard_map/ppermute | solution.py:75
  82.2 11.6 %prepare.1 = (bf16[1536,640]{1,0:T(8,128)(2,1)}, bf16[1536,512]{1,0:T(8,128)(2,1)S(1)}, f32[1536,512]{1,0:T(8,128)}, f32[1536,128]{1,0:T(8,128)S(1)}, f32[8,1536]{1,0:T(8,128)S(1)}) custom-call(s32[24]{0:T(128)S(1)} %concatenate.92.ints, f32[8]{0:T(128)S(1)} %pad_maximum_fusion.19.floats, f32[8,1536]{1,0:T(8,128)S(1)} %pad_maximum_fusion.15.rows_ref, ...), custom_call_target="tpu_custom_call" | custom-call | flops 4026531840 | bytes 12000000 | tf_op jit(solution)/shard_map/prepare/pallas_call | solution.py:857
  94.9 3.5 collective-permute-done.11
  105.8 11.9 %experts_forward.3 = (f32[1536,128]{1,0:T(8,128)S(1)}, f32[1536,512]{1,0:T(8,128)}, bf16[3,1536,512]{2,1,0:T(8,128)(2,1)}) custom-call(s32[24]{0:T(128)S(1)} %concatenate.92.ints, bf16[1536,512]{1,0:T(8,128)(2,1)} %copy-done.1, ...), custom_call_target="tpu_custom_call", output_to_operand_aliasing={{0}: (12, {}), {1}: (13, {})} | custom-call | flops 4831838208 | bytes 12000000 | tf_op jit(solution)/shard_map/experts_forward/pallas_call | solution.py:926
  125.9 6.9 %experts_forward.4 = (f32[1536,128]{1,0:T(8,128)S(1)}, f32[1536,512]{1,0:T(8,128)}, bf16[3,1536,512]{2,1,0:T(8,128)(2,1)}, bf16[768,512]{1,0:T(8,128)(2,1)S(1)}) custom-call(s32[24]{0:T(128)S(1)} %concatenate.92.ints, bf16[1536,512]{1,0:T(8,128)(2,1)} %copy-done.1, ...), custom_call_target="tpu_custom_call", output_to_operand_aliasing={{0}: (12, {}), {1}: (13, {})} | custom-call | flops 1610612736 | bytes 12000000 | tf_op jit(solution)/shard_map/experts_forward/pallas_call | solution.py:926
  132.7 3.7 %collective-permute-start.28 = (bf16[768,512]{1,0:T(8,128)(2,1)S(1)}, bf16[768,512]{1,0:T(8,128)(2,1)S(1)}, u32[]{:S(2)}, u32[]{:S(2)}) collective-permute-start(bf16[768,512]{1,0:T(8,128)(2,1)S(1)} %get-tuple-element.287), channel_id=1, source_target_pairs={{0,8},{2,10},{4,12},{6,14},{8,0},{10,2},{12,4},{14,6},{16,24},{18,... | collective-permute-start | bytes 2359304 | tf_op jit(solution)/shard_map/ppermute | solution.py:67
  136.4 18.1 %experts_forward.5 = (f32[1536,128]{1,0:T(8,128)S(1)}, f32[1536,512]{1,0:T(8,128)}, bf16[3,1536,512]{2,1,0:T(8,128)(2,1)}, bf16[3,1536,512]{2,1,0:T(8,128)(2,1)}) custom-call(s32[24]{0:T(128)S(1)} %concatenate.92.ints, bf16[1536,512]{1,0:T(8,128)(2,1)} %copy-done.1, ...), custom_call_target="tpu_custom_call", output_to_operand_aliasing={{0}: (20, {}), {1}: (21, {}), {2}: (22, {}), {3}: (23, {})} | custom-call | flops 4831838208 | bytes 12000000 | tf_op jit(solution)/shard_map/experts_forward/pallas_call | solution.py:926
  154.6 9.1 %towers.1 = (f32[8,768]{1,0:T(8,128)S(1)}, f32[768,512]{1,0:T(8,128)S(1)}, bf16[768,512]{1,0:T(8,128)(2,1)S(1)}, f32[512,1024]{1,0:T(8,128)}, f32[8,1024]{1,0:T(8,128)S(1)}, /*index=5*/f32[8,128]{1,0:T(8,128)S(1)}) custom-call(s32[24]{0:T(128)S(1)} %concatenate.92.ints, f32[1536,512]{1,0:T(8,128)} %get-tuple-element.286.mix_ref, ...), custom_call_target="tpu_custom_call" | custom-call | flops 2415919104 | bytes 10000000 | tf_op jit(solution)/shard_map/towers/pallas_call | solution.py:1033
  167.6 16.3 %experts_backward.4 = (f32[1536,128]{1,0:T(8,128)S(1)}, f32[1536,512]{1,0:T(8,128)}, bf16[2,2,512,512]{3,2,1,0:T(8,128)(2,1)}, bf16[2,2,512,512]{3,2,1,0:T(8,128...) custom-call(s32[24]{0:T(128)S(1)} %concatenate.92.ints, ...), custom_call_target="tpu_custom_call", output_to_operand_aliasing={{0}: (14, {})} | custom-call | flops 8053063680 | bytes 20000000 | tf_op jit(solution)/shard_map/experts_backward/pallas_call | solution.py:994
  186.8 16.5 %experts_backward.5 = (f32[1536,128]{1,0:T(8,128)S(1)}, f32[1536,512]{1,0:T(8,128)}, bf16[2,2,512,512]{3,2,1,0:T(8,128)(2,1)}, bf16[2,2,512,512]{3,2,1,0:T(8,128...) custom-call(s32[24]{0:T(128)S(1)} %copy-done.26, ...), custom_call_target="tpu_custom_call", output_to_operand_aliasing={{0}: (14, {}), {1}: (15, {})} | custom-call | flops 8053063680 | bytes 20000000 | tf_op jit(solution)/shard_map/experts_backward/pallas_call | solution.py:994
  204.1 11.3 %experts_backward.6 = (f32[1536,128]{1,0:T(8,128)S(1)}, f32[1536,512]{1,0:T(8,128)}, bf16[1,2,512,512]{3,2,1,0:T(8,128)(2,1)}, bf16[1,2,512,512]{3,2,1,0:T(8,128...) custom-call(s32[24]{0:T(128)S(1)} %copy-done.26, ...), custom_call_target="tpu_custom_call", output_to_operand_aliasing={{0}: (15, {}), {1}: (16, {})} | custom-call | flops 4026531840 | bytes 20000000 | tf_op jit(solution)/shard_map/experts_backward/pallas_call | solution.py:994
  222.8 24.0 %experts_backward.7 = (f32[1536,128]{1,0:T(8,128)S(1)}, f32[1536,512]{1,0:T(8,128)}, bf16[3,2,512,512]{3,2,1,0:T(8,128)(2,1)}, bf16[3,2,512,512]{3,2,1,0:T(8,128...) custom-call(s32[24]{0:T(128)S(1)} %copy-done.26, ...), custom_call_target="tpu_custom_call", output_to_operand_aliasing={{0}: (15, {}), {1}: (16, {})} | custom-call | flops 12079595520 | bytes 20000000 | tf_op jit(solution)/shard_map/experts_backward/pallas_call | solution.py:994
  246.9 3.4 collective-permute-start.43
  252.0 4.9 %gates.1 = (f32[1536,512]{1,0:T(8,128)}, bf16[1536,512]{1,0:T(8,128)(2,1)S(1)}, f32[512,128]{1,0:T(8,128)S(1)}) custom-call(s32[24]{0:T(128)S(1)} %copy-done.26, f32[1536,512]{1,0:T(8,128)} %get-tuple-element.346.back_ref, f32[1536,128]{1,0:T(8,128)S(1)} %get-tuple-element.347.cols_ref, f32[8,1536]{1,0:T(8,128)S(1)} %get-tuple-element.348.prob_ref, ...), custom_call_target="tpu_custom_call" | custom-call | flops 402653184 | bytes 10000000 | tf_op jit(solution)/shard_map/gates/pallas_call | solution.py:518
  266.0 16.9 %collective-permute-done.44 = bf16[3,2,2,2,32,512]{5,4,0,3,2,1:T(8,128)(2,1)S(1)} collective-permute-done((bf16[3,2,2,2,32,512]{5,4,0,3,2,1:T(8,128)(2,1)S(1)}, bf16[3,2,2,2,32,512]{5,4,0,3,2,1:T(8,128)(2,1)S(1)}, u32[]{:S(2)}, u32[]{:S(2)}) %collective-permute-start.44) | collective-permute-done | bytes 786464 | tf_op jit(solution)/shard_map/ppermute | solution.py:67
  295.1 10.0 %finish.1 = (bf16[1536,640]{1,0:T(8,128)(2,1)}, bf16[512,1792]{1,0:T(8,128)(2,1)}) custom-call(s32[24]{0:T(128)S(1)} %copy-done.27, f32[768,512]{1,0:T(8,128)S(1)} %copy-done.19, bf16[768,512]{1,0:T(8,128)(2,1)S(1)} %copy-done.8, f32[1536,512]{1,0:T(8,128)} %get-tuple-element.370.sum_ref, bf16[1536,512]{1,0:T(8,128)(2,1)S(1)} %copy-done.21, ...), custom_call_target="tpu_custom_call" | custom-call | flops 2013265920 | bytes 14000000 | tf_op jit(solution)/shard_map/finish/pallas_call | solution.py:623
  312.1 3.4 collective-permute-start.51
  319.3 4.3 %fusion.2 = bf16[1536,640]{1,0:T(8,128)(2,1)S(1)} fusion(bf16[1536,640]{1,0:T(8,128)(2,1)S(1)} %copy-done.58, f32[1536]{0:T(1024)S(1)} %add_bitcast_fusion.1), kind=kOutput, calls=%fused_computation.4 | convolution fusion | flops 3023241216 | bytes 3938304 | tf_op jit(solution)/shard_map/dot_general | solution.py:1330
  323.7 9.7 %collective-permute-done.51 = bf16[2,3,2,32,512]{4,3,1,0,2:T(8,128)(2,1)S(1)} collective-permute-done((bf16[2,3,2,32,512]{4,3,1,0,2:T(8,128)(2,1)S(1)}, bf16[2,3,2,32,512]{4,3,1,0,2:T(8,128)(2,1)S(1)}, u32[]{:S(2)}, u32[]{:S(2)}) %collective-permute-start.51) | collective-permute-done | bytes 393248 | tf_op jit(solution)/shard_map/ppermute | solution.py:67
  (354 shorter events, 128.0 us)
Async XLA Ops:
  4.6 27.3 %collective-permute-start.1 = (bf16[2,3,32,512]{3,2,1,0:T(8,128)(2,1)S(1)}, bf16[2,3,32,512]{3,2,1,0:T(8,128)(2,1)S(1)}, u32[]{:S(2)}, u32[]{:S(2)}) collective-permute-start(bf16[2,3,32,512]{3,2,1,0:T(8,128)(2,1)S(1)} %get-tuple-element.228), channel_id=1, source_target_pairs={{0,16},{2,18},{4,20},{6,22},{8,24},{10,26},{12,28},{14,30},{16,0},... | collective-permute-start | bytes 589832 | tf_op jit(solution)/shard_map/ppermute | solution.py:67
  14.3 20.0 %collective-permute-start = (bf16[2,6,32,512]{3,2,1,0:T(8,128)(2,1)S(1)}, bf16[2,6,32,512]{3,2,1,0:T(8,128)(2,1)}, u32[]{:S(2)}, u32[]{:S(2)}) collective-permute-start(bf16[2,6,32,512]{3,2,1,0:T(8,128)(2,1)S(1)} %get-tuple-element.223), channel_id=1, source_target_pairs={{0,8},{2,10},{4,12},{6,14},{8,0},{10,2},{12,4},{14,6},{16,24},{18,... | collective-permute-start | bytes 1179656 | tf_op jit(solution)/shard_map/ppermute | solution.py:67
  38.6 22.4 %collective-permute-start.6 = (bf16[2,3,32,512]{3,2,1,0:T(8,128)(2,1)S(1)}, bf16[2,3,32,512]{3,2,1,0:T(8,128)(2,1)}, u32[]{:S(2)}, u32[]{:S(2)}) collective-permute-start(bf16[2,3,32,512]{3,2,1,0:T(8,128)(2,1)S(1)} %get-tuple-element.233), channel_id=1, source_target_pairs={{0,24},{2,26},{4,28},{6,30},{8,16},{10,18},{12,20},{14,22},{16,8},... | collective-permute-start | bytes 589832 | tf_op jit(solution)/shard_map/ppermute | solution.py:67
  41.3 19.7 %collective-permute-start.3 = (bf16[2,3,64,512]{3,2,1,0:T(8,128)(2,1)S(1)}, bf16[2,3,64,512]{3,2,1,0:T(8,128)(2,1)S(1)}, u32[]{:S(2)}, u32[]{:S(2)}) collective-permute-start(bf16[2,3,64,512]{3,2,1,0:T(8,128)(2,1)S(1)} %pad_maximum_fusion.10), channel_id=1, source_target_pairs={{0,4},{2,6},{4,0},{6,2},{8,12},{10,14},{12,8},{14,10},{16,20},{18,... | collective-permute-start | bytes 1179656 | tf_op jit(solution)/shard_map/ppermute | solution.py:67
  44.6 24.1 %collective-permute-start.16 = (bf16[128,1792]{1,0:T(8,128)(2,1)S(1)}, bf16[128,1792]{1,0:T(8,128)(2,1)}, u32[]{:S(2)}, u32[]{:S(2)}) collective-permute-start(bf16[128,1792]{1,0:T(8,128)(2,1)S(1)} %pad_maximum_fusion.7), channel_id=1, source_target_pairs={{0,2},{2,0},{4,6},{6,4},{8,10},{10,8},{12,14},{14,12},{16,18},{18,... | collective-permute-start | bytes 1376264 | tf_op jit(solution)/shard_map/ppermute | solution.py:67
  58.4 23.7 %collective-permute-start.12 = (bf16[1536,640]{1,0:T(8,128)(2,1)}, bf16[1536,640]{1,0:T(8,128)(2,1)}, u32[]{:S(2)}, u32[]{:S(2)}) collective-permute-start(bf16[1536,640]{1,0:T(8,128)(2,1)} %own_ref.1), channel_id=1, source_target_pairs={{0,8},{2,10},{4,12},{6,14},{9,1},{11,3},{13,5},{15,7},{16,24},{18,... | collective-permute-start | bytes 5898248 | tf_op jit(solution)/shard_map/ppermute | solution.py:75
  65.4 29.5 %collective-permute-start.10 = (bf16[2,3,64,512]{3,2,1,0:T(8,128)(2,1)S(1)}, bf16[2,3,64,512]{3,2,1,0:T(8,128)(2,1)}, u32[]{:S(2)}, u32[]{:S(2)}) collective-permute-start(bf16[2,3,64,512]{3,2,1,0:T(8,128)(2,1)S(1)} %pad_maximum_fusion.12), channel_id=1, source_target_pairs={{0,4},{2,6},{4,0},{6,2},{8,12},{10,14},{12,8},{14,10},{16,20},{18,... | collective-permute-start | bytes 1179656 | tf_op jit(solution)/shard_map/ppermute | solution.py:67
  68.2 30.2 %collective-permute-start.9 = (bf16[2,2,3,64,512]{4,3,2,1,0:T(8,128)(2,1)S(1)}, bf16[2,2,3,64,512]{4,3,2,1,0:T(8,128)(2,1)}, u32[]{:S(2)}, u32[]{:S(2)}) collective-permute-start(bf16[2,2,3,64,512]{4,3,2,1,0:T(8,128)(2,1)S(1)} %pad_maximum_fusion.4.refs_2_.refs_4_.refs_5_), channel_id=1, source_target_pairs={{0,4},{2,6},{4,0},{6,2},{8,12},{10,14},{12,8},{14,10},{16,20},{18,... | collective-permute-start | bytes 2359304 | tf_op jit(solution)/shard_map/ppermute | solution.py:67
  70.0 28.4 %collective-permute-start.8 = (bf16[2,2,3,64,512]{4,3,2,1,0:T(8,128)(2,1)S(1)}, bf16[2,2,3,64,512]{4,3,2,1,0:T(8,128)(2,1)}, u32[]{:S(2)}, u32[]{:S(2)}) collective-permute-start(bf16[2,2,3,64,512]{4,3,2,1,0:T(8,128)(2,1)S(1)} %pad_maximum_fusion.3.refs_0_.refs_2_.refs_3_), channel_id=1, source_target_pairs={{0,2},{2,0},{4,6},{6,4},{8,10},{10,8},{12,14},{14,12},{16,18},{18,... | collective-permute-start | bytes 2359304 | tf_op jit(solution)/shard_map/ppermute | solution.py:67
  72.8 25.5 %collective-permute-start.11 = (bf16[2,3,64,512]{3,2,1,0:T(8,128)(2,1)S(1)}, bf16[2,3,64,512]{3,2,1,0:T(8,128)(2,1)S(1)}, u32[]{:S(2)}, u32[]{:S(2)}) collective-permute-start(bf16[2,3,64,512]{3,2,1,0:T(8,128)(2,1)S(1)} %pad_maximum_fusion.13), channel_id=1, source_target_pairs={{0,2},{2,0},{4,6},{6,4},{8,10},{10,8},{12,14},{14,12},{16,18},{18,... | collective-permute-start | bytes 1179656 | tf_op jit(solution)/shard_map/ppermute | solution.py:67
  99.5 19.6 %collective-permute-start.23 = (bf16[2,2,3,64,512]{4,3,2,1,0:T(8,128)(2,1)S(1)}, bf16[2,2,3,64,512]{4,3,2,1,0:T(8,128)(2,1)S(1)}, u32[]{:S(2)}, u32[]{:S(2)}) collective-permute-start(bf16[2,2,3,64,512]{4,3,2,1,0:T(8,128)(2,1)S(1)} %pad_maximum_fusion.6.refs_2_.refs_10_.refs_5_), channel_id=1, source_target_pairs={{0,4},{2,6},{4,0},{6,2},{8,12},{10,14},{12,8},{14,10},{16,20},{18,... | collective-permute-start | bytes 2359304 | tf_op jit(solution)/shard_map/ppermute | solution.py:67
  102.2 19.3 %collective-permute-start.22 = (bf16[2,2,3,64,512]{4,3,2,1,0:T(8,128)(2,1)S(1)}, bf16[2,2,3,64,512]{4,3,2,1,0:T(8,128)(2,1)S(1)}, u32[]{:S(2)}, u32[]{:S(2)}) collective-permute-start(bf16[2,2,3,64,512]{4,3,2,1,0:T(8,128)(2,1)S(1)} %pad_maximum_fusion.5.refs_0_.refs_8_.refs_3_), channel_id=1, source_target_pairs={{0,2},{2,0},{4,6},{6,4},{8,10},{10,8},{12,14},{14,12},{16,18},{18,... | collective-permute-start | bytes 2359304 | tf_op jit(solution)/shard_map/ppermute | solution.py:67
  132.7 21.8 %collective-permute-start.28 = (bf16[768,512]{1,0:T(8,128)(2,1)S(1)}, bf16[768,512]{1,0:T(8,128)(2,1)S(1)}, u32[]{:S(2)}, u32[]{:S(2)}) collective-permute-start(bf16[768,512]{1,0:T(8,128)(2,1)S(1)} %get-tuple-element.287), channel_id=1, source_target_pairs={{0,8},{2,10},{4,12},{6,14},{8,0},{10,2},{12,4},{14,6},{16,24},{18,... | collective-permute-start | bytes 2359304 | tf_op jit(solution)/shard_map/ppermute | solution.py:67
  164.9 18.9 %collective-permute-start.29 = (bf16[768,512]{1,0:T(8,128)(2,1)S(1)}, bf16[768,512]{1,0:T(8,128)(2,1)S(1)}, u32[]{:S(2)}, u32[]{:S(2)}) collective-permute-start(bf16[768,512]{1,0:T(8,128)(2,1)S(1)} %get-tuple-element.291.refs_0_), channel_id=1, source_target_pairs={{0,8},{2,10},{4,12},{6,14},{8,0},{10,2},{12,4},{14,6},{16,24},{18,... | collective-permute-start | bytes 2359304 | tf_op jit(solution)/shard_map/ppermute | solution.py:67
  183.8 19.5 %collective-permute-start.32 = (bf16[2,2,512,512]{3,2,1,0:T(8,128)(2,1)}, bf16[2,2,512,512]{3,2,1,0:T(8,128)(2,1)S(1)}, u32[]{:S(2)}, u32[]{:S(2)}) collective-permute-start(bf16[2,2,512,512]{3,2,1,0:T(8,128)(2,1)} %get-tuple-element.308), channel_id=1, source_target_pairs={{0,1},{1,0},{2,3},{3,2},{4,5},{5,4},{6,7},{7,6},{8,9},{9,8},{10,11... | collective-permute-start | bytes 6291464 | tf_op jit(solution)/shard_map/ppermute | solution.py:125
  183.9 19.4 %collective-permute-start.33 = (f32[8,128]{1,0:T(8,128)S(1)}, f32[8,128]{1,0:T(8,128)S(1)}, u32[]{:S(2)}, u32[]{:S(2)}) collective-permute-start(f32[8,128]{1,0:T(8,128)S(1)} %add.330), channel_id=1, source_target_pairs={{0,2},{2,0},{4,6},{6,4},{8,10},{10,8},{12,14},{14,12},{16,18},{18,... | collective-permute-start | bytes 12296 | tf_op jit(solution)/shard_map/ppermute | solution.py:67
  215.5 31.3 %collective-permute-start.40 = (f32[8,128]{1,0:T(8,128)S(1)}, f32[8,128]{1,0:T(8,128)S(1)}, u32[]{:S(2)}, u32[]{:S(2)}) collective-permute-start(f32[8,128]{1,0:T(8,128)S(1)} %add.342), channel_id=1, source_target_pairs={{0,16},{2,18},{4,20},{6,22},{8,24},{10,26},{12,28},{14,30},{16,0},... | collective-permute-start | bytes 12296 | tf_op jit(solution)/shard_map/ppermute | solution.py:67
  215.9 30.9 %collective-permute-start.39 = (f32[8,768]{1,0:T(8,128)S(1)}, f32[8,768]{1,0:T(8,128)S(1)}, u32[]{:S(2)}, u32[]{:S(2)}) collective-permute-start(f32[8,768]{1,0:T(8,128)S(1)} %get-tuple-element.340), channel_id=1, source_target_pairs={{1,9},{3,11},{5,13},{7,15},{8,0},{10,2},{12,4},{14,6},{17,25},{19,... | collective-permute-start | bytes 73736 | tf_op jit(solution)/shard_map/ppermute | solution.py:75
  220.5 26.3 %collective-permute-start.38 = (bf16[3,2,2,2,32,512]{5,4,0,3,2,1:T(8,128)(2,1)S(1)}, bf16[3,2,2,2,32,512]{5,4,0,3,2,1:T(8,128)(2,1)S(1)}, u32[]{:S(2)}, u32[]{:S(2)}) collective-permute-start(bf16[3,2,2,2,32,512]{5,4,0,3,2,1:T(8,128)(2,1)S(1)} %bitcast.153), channel_id=1, source_target_pairs={{0,4},{2,6},{4,0},{6,2},{8,12},{10,14},{12,8},{14,10},{16,20},{18,... | collective-permute-start | bytes 2359304 | tf_op jit(solution)/shard_map/ppermute | solution.py:67
  222.2 24.6 %collective-permute-start.37 = (bf16[3,2,2,2,32,512]{5,4,0,3,2,1:T(8,128)(2,1)S(1)}, bf16[3,2,2,2,32,512]{5,4,0,3,2,1:T(8,128)(2,1)S(1)}, u32[]{:S(2)}, u32[]{:S(2)}) collective-permute-start(bf16[3,2,2,2,32,512]{5,4,0,3,2,1:T(8,128)(2,1)S(1)} %get-tuple-element.444), channel_id=1, source_target_pairs={{0,2},{2,0},{4,6},{6,4},{8,10},{10,8},{12,14},{14,12},{16,18},{18,... | collective-permute-start | bytes 2359304 | tf_op jit(solution)/shard_map/ppermute | solution.py:67
  262.2 22.3 %collective-permute-start.46 = (bf16[1536,512]{1,0:T(8,128)(2,1)S(1)}, bf16[1536,512]{1,0:T(8,128)(2,1)S(1)}, u32[]{:S(2)}, u32[]{:S(2)}) collective-permute-start(bf16[1536,512]{1,0:T(8,128)(2,1)S(1)} %get-tuple-element.360), channel_id=1, source_target_pairs={{1,9},{3,11},{5,13},{7,15},{8,0},{10,2},{12,4},{14,6},{17,25},{19,... | collective-permute-start | bytes 4718600 | tf_op jit(solution)/shard_map/ppermute | solution.py:75
  263.6 19.2 %collective-permute-start.44 = (bf16[3,2,2,2,32,512]{5,4,0,3,2,1:T(8,128)(2,1)S(1)}, bf16[3,2,2,2,32,512]{5,4,0,3,2,1:T(8,128)(2,1)S(1)}, u32[]{:S(2)}, u32[]{:S(2)}) collective-permute-start(bf16[3,2,2,2,32,512]{5,4,0,3,2,1:T(8,128)(2,1)S(1)} %get-tuple-element.440), channel_id=1, source_target_pairs={{0,2},{2,0},{4,6},{6,4},{8,10},{10,8},{12,14},{14,12},{16,18},{18,... | collective-permute-start | bytes 2359304 | tf_op jit(solution)/shard_map/ppermute | solution.py:67
  285.7 20.8 %collective-permute-start.47 = (bf16[2,3,2,32,512]{4,3,1,0,2:T(8,128)(2,1)}, bf16[2,3,2,32,512]{4,3,1,0,2:T(8,128)(2,1)}, u32[]{:S(2)}, u32[]{:S(2)}) collective-permute-start(bf16[2,3,2,32,512]{4,3,1,0,2:T(8,128)(2,1)} %get-tuple-element.456), channel_id=1, source_target_pairs={{0,16},{2,18},{4,20},{6,22},{8,24},{10,26},{12,28},{14,30},{16,0},... | collective-permute-start | bytes 1179656 | tf_op jit(solution)/shard_map/ppermute | solution.py:67
  312.1 21.3 %collective-permute-start.51 = (bf16[2,3,2,32,512]{4,3,1,0,2:T(8,128)(2,1)S(1)}, bf16[2,3,2,32,512]{4,3,1,0,2:T(8,128)(2,1)S(1)}, u32[]{:S(2)}, u32[]{:S(2)}) collective-permute-start(bf16[2,3,2,32,512]{4,3,1,0,2:T(8,128)(2,1)S(1)} %get-tuple-element.450), channel_id=1, source_target_pairs={{0,16},{2,18},{4,20},{6,22},{8,24},{10,26},{12,28},{14,30},{16,0},... | collective-permute-start | bytes 1179656 | tf_op jit(solution)/shard_map/ppermute | solution.py:67
  (97 other events, 1239.6 us)

commit v5 on v4

--- a/solution.py
+++ b/solution.py
@@ -341,8 +341,8 @@
     join(pieces, held)
     back_in, refs = refs[0], refs[1:]
     if adds:
-        dvec_in, dbi_in = refs[:2]
-        refs = refs[2:]
+        dvec_in, dbi_in, keep_in, give_in = refs[:4]
+        refs = refs[4:]
     cols_ref, back_ref, keep_ref, give_ref, dvec_ref, dbi_ref, in_a, in_b, out_a, out_b = refs
     rows = x_ref.shape[0]
     half_tiles = rows // TILE // len(halves)
@@ -361,7 +361,10 @@
         whole = isinstance(span, slice)
 
         def add(ref, target, which, values):
-            if whole:
+            if whole and adds:
+                before = keep_in if target is keep_ref else give_in
+                target[0, which] = (values + before[0, which].astype(f32)).astype(bf16)
+            elif whole:
                 target[0, which] = values.astype(bf16)
             else:
                 ref[...] += values
@@ -872,8 +875,8 @@
             ),
         ),
         out_shape=(
-            jax.ShapeDtypeStruct((rows, e_in), bf16),
-            jax.ShapeDtypeStruct((rows, D), bf16),
+            pltpu.HBM((rows, e_in), bf16),
+            pltpu.HBM((rows, D), bf16),
             jax.ShapeDtypeStruct((rows, D), f32),
             jax.ShapeDtypeStruct((rows, 128), f32),
             jax.ShapeDtypeStruct((8, rows), f32),
@@ -990,7 +993,7 @@
         aliases[len(inputs)] = 1
     if sums is not None:
         inputs += list(sums)
-        in_specs += [vec_spec, bi_spec]
+        in_specs += [vec_spec, bi_spec, pairs, pairs]
     return pl.pallas_call(
         functools.partial(
             backward_kernel, experts, halves, mode == "add", sums is not None, len(weights[array])
@@ -1047,7 +1050,7 @@
         ),
         out_shape=(
             jax.ShapeDtypeStruct((8, rows), f32),
-            jax.ShapeDtypeStruct((rows, D), f32),
+            pltpu.HBM((rows, D), f32),
             jax.ShapeDtypeStruct((rows, D), bf16),
             jax.ShapeDtypeStruct((D, DOM * TW), f32),
             jax.ShapeDtypeStruct((8, DOM * TW), f32),
@@ -1154,6 +1157,7 @@
     first_i = jnp.stack([first_i] + first_iy)
     first_o = jnp.stack([first_o] + first_ox)
     first_ix, first_oy = box.pieces(first_i, "x"), box.pieces(first_o, "y")
+    second, flips, second_z, _ = step(second, flips, second_z, (first_i, first_o))
     second_i, second_o = along_z(second, flips[:, 3:], second_z)
     second_iy, second_ox = box.pieces(second_i, "y"), box.pieces(second_o, "x")
 
@@ -1263,49 +1267,47 @@
     cols, back, keep_a, give_a, *sums = call_backward(
         (0, 1), ("own",), *common, [grad_low], *shared, cols, None
     )
-    d_logit_bias = d_logit_bias + swap_cores(d_logit_bias)
-    logit_in = box.pieces(d_logit_bias, "y")
+    logit_in = swap_cores(d_logit_bias)
     grad_in, cols, back, keep_a, give_a, sums, logit_in = step(
         grad_in, cols, back, keep_a, give_a, sums, logit_in
     )
+    d_logit_bias = d_logit_bias + logit_in
+    cols, back, keep_b, give_b, *sums_0 = call_backward(
+        (0, 1), ("other",), *common, [grad_in], *shared, cols, ("fresh", back), sums + [keep_a, give_a]
+    )
+    logit_in = box.pieces(d_logit_bias, "y")
+    cols, back, keep_b, give_b, logit_in = step(cols, back, keep_b, give_b, logit_in)
     d_logit_bias = box.same_sum(d_logit_bias, logit_in, "y")
-    give_a = swap_cores(give_a)
-    cols, back, keep_b, give_b, *sums_0 = call_backward(
-        (0, 1), ("other",), *common, [grad_in], *shared, cols, ("fresh", back), sums
-    )
-    logit_in = box.pieces(d_logit_bias, "x")
-    cols, back, keep_a, give_a, keep_b, give_b, logit_in = step(
-        cols, back, keep_a, give_a, keep_b, give_b, logit_in
-    )
-    d_logit_bias = box.same_sum(d_logit_bias, logit_in, "x")
     give_b = swap_cores(give_b)
     grads = [grad_low, grad_in]
     cols, back, keep_c, give_c, *sums_1 = call_backward(
         (2,), ("own", "other"), *common, grads, *shared, cols, ("add", back)
     )
-    logit_in = box.pieces(d_logit_bias, "flip")
+    logit_in = box.pieces(d_logit_bias, "x")
     cols, back, keep_b, give_b, keep_c, give_c, row_out, logit_in = step(
         cols, back, keep_b, give_b, keep_c, give_c, row_out, logit_in
     )
-    d_logit_bias = box.same_sum(d_logit_bias, logit_in, "flip")
+    d_logit_bias = box.same_sum(d_logit_bias, logit_in, "x")
     give_c = swap_cores(give_c)
-    ab = both_cores([keep_a, keep_b], [give_a, give_b])
+    ab = both_cores([keep_b], [give_b])
     give_c, keep_c, ab, cols = step(give_c, keep_c, ab, cols)
     c0 = Scatter(ab, both_cores([keep_c], [give_c]))
     cols, back, keep_d, give_d, *sums_2 = call_backward(
         (3, 4, 5), ("own", "other"), *common, grads, *shared, cols, ("add", back)
     )
     rows_in = box.to_partner(row_out, False)
-    logit_in = box.pieces(d_logit_bias, "z")
+    logit_in = box.pieces(d_logit_bias, "flip")
     cols, back, keep_d, give_d, rows_in, logit_in = sync(
         [c0], cols, back, keep_d, give_d, rows_in, logit_in
     )
-    d_logit_bias = box.same_sum(d_logit_bias, logit_in, "z")
+    d_logit_bias = box.same_sum(d_logit_bias, logit_in, "flip")
     c0.second()
     give_d = swap_cores(give_d)
     g_sum, g_low, d_gate = call_gate(ints, back, cols, probs, x, small)
     cd = both_cores([keep_d], [give_d])
-    g_sum, g_low, d_gate, cd = sync([c0], g_sum, g_low, d_gate, cd)
+    logit_in = box.pieces(d_logit_bias, "z")
+    g_sum, g_low, d_gate, cd, logit_in = sync([c0], g_sum, g_low, d_gate, cd, logit_in)
+    d_logit_bias = box.same_sum(d_logit_bias, logit_in, "z")
     c1 = Scatter(cd)
     back_in = box.to_partner(g_low, False)
     (back_in,) = sync([c0, c1], back_in)

time: 353 us -> 348 us (0.986)
  local copies, waits for them, and re-layouts: 19.7 us -> 14.4 us
    unnamed x121 -> x101, local copies, waits for them, and re-layouts: 11.5 us -> 9.01 us
  transfers between devices with their start and end apart: 62 -> 61, of which waited for: 19 -> 22; matrix products, arithmetic and copies ran while one was open for 11% -> 10% of each run, Pallas kernels for 36% -> 37%
where the time goes in v5:
time: 348 us; the launch traced here: 341 us
  Pallas kernels  149 us (43%)
  waiting for transfers between devices  75.6 us (22%)
  starting transfers between devices  65.4 us (19%)
  other arithmetic  30.2 us (9%)
  local copies, waits for them, and re-layouts  14.4 us (4%)
  matrix products  4.28 us (1%)
    pallas_call x4, Pallas kernels, call_backward(): pl.pallas_call(functools.partial(backward_kernel, experts, halves, mode =...  69.1 us
    ppermute x41, waiting for transfers between devices, send(): return lax.ppermute(values, 'dp', pairs)  67 us
    ppermute x41, starting transfers between devices, send(): return lax.ppermute(values, 'dp', pairs)  51.8 us
    pallas_call x3, Pallas kernels, call_forward(): pl.pallas_call(functools.partial(forward_kernel, experts, own, len(kept),...  38.3 us
    pallas_call x1, Pallas kernels, call_prepare(): pl.pallas_call(prepare_kernel, grid_spec=pltpu.PrefetchScalarGridSpec(num...  11.8 us
    pallas_call x1, Pallas kernels, call_finish(): pl.pallas_call(finish_kernel, grid_spec=pltpu.PrefetchScalarGridSpec(num_...  9.79 us
    unnamed x101, local copies, waits for them, and re-layouts  9.01 us
    pallas_call x1, Pallas kernels, call_tower(): pl.pallas_call(tower_kernel, grid_spec=pltpu.PrefetchScalarGridSpec(num_s...  8.78 us
  transfers between devices with their start and end apart: 61, of which 22 were waited for; matrix products, arithmetic and copies ran while one was open for 10% of the time, Pallas kernels for 37%

profile of v5, /device:TPU:0, one launch (start us, length us, event | category | flops | bytes accessed | tf_op | source)
XLA Modules:
  0.0 340.9 jit_solution(15740820449208059259)
XLA Ops:
  4.6 4.1 %collective-permute-start.1 = (bf16[2,3,32,512]{3,2,1,0:T(8,128)(2,1)S(1)}, bf16[2,3,32,512]{3,2,1,0:T(8,128)(2,1)S(1)}, u32[]{:S(2)}, u32[]{:S(2)}) collective-permute-start(bf16[2,3,32,512]{3,2,1,0:T(8,128)(2,1)S(1)} %get-tuple-element.231), channel_id=1, source_target_pairs={{0,16},{2,18},{4,20},{6,22},{8,24},{10,26},{12,28},{14,30},{16,0},... | collective-permute-start | bytes 589832 | tf_op jit(solution)/shard_map/ppermute | solution.py:67
  16.7 6.1 %collective-permute-done.13 = bf16[16,1792]{1,0:T(8,128)(2,1)S(1)} collective-permute-done((bf16[16,1792]{1,0:T(8,128)(2,1)S(1)}, bf16[16,1792]{1,0:T(8,128)(2,1)S(1)}, u32[]{:S(2)}, u32[]{:S(2)}) %collective-permute-start.13) | collective-permute-done | bytes 57376 | tf_op jit(solution)/shard_map/ppermute | solution.py:67
  25.1 5.2 %collective-permute-done.14 = bf16[32,1792]{1,0:T(8,128)(2,1)S(1)} collective-permute-done((bf16[32,1792]{1,0:T(8,128)(2,1)S(1)}, bf16[32,1792]{1,0:T(8,128)(2,1)S(1)}, u32[]{:S(2)}, u32[]{:S(2)}) %collective-permute-start.14) | collective-permute-done | bytes 114720 | tf_op jit(solution)/shard_map/ppermute | solution.py:67
  34.3 3.0 collective-permute-start.7
  48.0 10.4 %collective-permute-done.5 = bf16[2,3,32,512]{3,2,1,0:T(8,128)(2,1)} collective-permute-done((bf16[2,3,32,512]{3,2,1,0:T(8,128)(2,1)S(1)}, bf16[2,3,32,512]{3,2,1,0:T(8,128)(2,1)}, u32[]{:S(2)}, u32[]{:S(2)}) %collective-permute-start.5) | collective-permute-done | bytes 196640 | tf_op jit(solution)/shard_map/ppermute | solution.py:67
  77.7 4.4 %collective-permute-done.12.in_ref = bf16[1536,640]{1,0:T(8,128)(2,1)} collective-permute-done((bf16[1536,640]{1,0:T(8,128)(2,1)}, bf16[1536,640]{1,0:T(8,128)(2,1)}, u32[]{:S(2)}, u32[]{:S(2)}) %collective-permute-start.12) | collective-permute-done | bytes 1966112 | tf_op jit(solution)/shard_map/ppermute | solution.py:75
  82.1 11.8 %prepare.1 = (bf16[1536,640]{1,0:T(8,128)(2,1)}, bf16[1536,512]{1,0:T(8,128)(2,1)}, f32[1536,512]{1,0:T(8,128)}, f32[1536,128]{1,0:T(8,128)S(1)}, f32[8,1536]{1,0:T(8,128)S(1)}) custom-call(s32[24]{0:T(128)S(1)} %concatenate.92.ints, f32[8]{0:T(128)S(1)} %pad_maximum_fusion.19.floats, f32[8,1536]{1,0:T(8,128)S(1)} %pad_maximum_fusion.15.rows_ref, ...), custom_call_target="tpu_custom_call" | custom-call | flops 4026531840 | bytes 12000000 | tf_op jit(solution)/shard_map/prepare/pallas_call | solution.py:860
  103.2 10.7 %experts_forward.3 = (f32[1536,128]{1,0:T(8,128)S(1)}, f32[1536,512]{1,0:T(8,128)}, bf16[3,1536,512]{2,1,0:T(8,128)(2,1)}) custom-call(s32[24]{0:T(128)S(1)} %concatenate.92.ints, bf16[1536,512]{1,0:T(8,128)(2,1)} %get-tuple-element.268.x_ref, ...), custom_call_target="tpu_custom_call", output_to_operand_aliasing={{0}: (12, {}), {1}: (13, {})} | custom-call | flops 4831838208 | bytes 12000000 | tf_op jit(solution)/shard_map/experts_forward/pallas_call | solution.py:929
  114.0 2.9 collective-permute-done.23.refs_3_.refs_11_.refs_6_
  123.7 9.2 %experts_forward.4 = (f32[1536,128]{1,0:T(8,128)S(1)}, f32[1536,512]{1,0:T(8,128)}, bf16[3,1536,512]{2,1,0:T(8,128)(2,1)}, bf16[768,512]{1,0:T(8,128)(2,1)S(1)}) custom-call(s32[24]{0:T(128)S(1)} %concatenate.92.ints, bf16[1536,512]{1,0:T(8,128)(2,1)} %get-tuple-element.268.x_ref, ...), custom_call_target="tpu_custom_call", output_to_operand_aliasing={{0}: (12, {}), {1}: (13, {})} | custom-call | flops 1610612736 | bytes 12000000 | tf_op jit(solution)/shard_map/experts_forward/pallas_call | solution.py:929
  133.0 18.4 %experts_forward.5 = (f32[1536,128]{1,0:T(8,128)S(1)}, f32[1536,512]{1,0:T(8,128)}, bf16[3,1536,512]{2,1,0:T(8,128)(2,1)}, bf16[3,1536,512]{2,1,0:T(8,128)(2,1)}) custom-call(s32[24]{0:T(128)S(1)} %concatenate.92.ints, bf16[1536,512]{1,0:T(8,128)(2,1)} %get-tuple-element.268.x_ref, ...), custom_call_target="tpu_custom_call", output_to_operand_aliasing={{0}: (20, {}), {1}: (21, {}), {2}: (22, {}), {3}: (23, {})} | custom-call | flops 4831838208 | bytes 12000000 | tf_op jit(solution)/shard_map/experts_forward/pallas_call | solution.py:929
  152.5 8.8 %towers.1 = (f32[8,768]{1,0:T(8,128)S(1)}, f32[768,512]{1,0:T(8,128)}, bf16[768,512]{1,0:T(8,128)(2,1)S(1)}, f32[512,1024]{1,0:T(8,128)}, f32[8,1024]{1,0:T(8,128)S(1)}, /*index=5*/f32[8,128]{1,0:T(8,128)S(1)}) custom-call(s32[24]{0:T(128)S(1)} %concatenate.92.ints, f32[1536,512]{1,0:T(8,128)} %get-tuple-element.293.mix_ref, ...), custom_call_target="tpu_custom_call" | custom-call | flops 2415919104 | bytes 10000000 | tf_op jit(solution)/shard_map/towers/pallas_call | solution.py:1036
  161.9 16.8 %experts_backward.4 = (f32[1536,128]{1,0:T(8,128)S(1)}, f32[1536,512]{1,0:T(8,128)}, bf16[2,2,512,512]{3,2,1,0:T(8,128)(2,1)}, bf16[2,2,512,512]{3,2,1,0:T(8,128...) custom-call(s32[24]{0:T(128)S(1)} %concatenate.92.ints, ...), custom_call_target="tpu_custom_call", output_to_operand_aliasing={{0}: (14, {})} | custom-call | flops 8053063680 | bytes 20000000 | tf_op jit(solution)/shard_map/experts_backward/pallas_call | solution.py:997
  180.8 17.1 %experts_backward.5 = (f32[1536,128]{1,0:T(8,128)S(1)}, f32[1536,512]{1,0:T(8,128)}, bf16[2,2,512,512]{3,2,1,0:T(8,128)(2,1)}, bf16[2,2,512,512]{3,2,1,0:T(8,128...) custom-call(s32[24]{0:T(128)S(1)} %copy-done.24, ...), custom_call_target="tpu_custom_call", output_to_operand_aliasing={{0}: (14, {}), {1}: (15, {})} | custom-call | flops 8053063680 | bytes 20000000 | tf_op jit(solution)/shard_map/experts_backward/pallas_call | solution.py:997
  200.1 9.0 %experts_backward.6 = (f32[1536,128]{1,0:T(8,128)S(1)}, f32[1536,512]{1,0:T(8,128)}, bf16[1,2,512,512]{3,2,1,0:T(8,128)(2,1)}, bf16[1,2,512,512]{3,2,1,0:T(8,128...) custom-call(s32[24]{0:T(128)S(1)} %copy-done.24, ...), custom_call_target="tpu_custom_call", output_to_operand_aliasing={{0}: (15, {}), {1}: (16, {})} | custom-call | flops 4026531840 | bytes 20000000 | tf_op jit(solution)/shard_map/experts_backward/pallas_call | solution.py:997
  209.3 3.4 collective-permute-start.38
  217.6 26.2 %experts_backward.7 = (f32[1536,128]{1,0:T(8,128)S(1)}, f32[1536,512]{1,0:T(8,128)}, bf16[3,2,512,512]{3,2,1,0:T(8,128)(2,1)}, bf16[3,2,512,512]{3,2,1,0:T(8,128...) custom-call(s32[24]{0:T(128)S(1)} %copy-done.24, ...), custom_call_target="tpu_custom_call", output_to_operand_aliasing={{0}: (15, {}), {1}: (16, {})} | custom-call | flops 12079595520 | bytes 20000000 | tf_op jit(solution)/shard_map/experts_backward/pallas_call | solution.py:997
  247.4 4.9 %gates.1 = (f32[1536,512]{1,0:T(8,128)}, bf16[1536,512]{1,0:T(8,128)(2,1)S(1)}, f32[512,128]{1,0:T(8,128)S(1)}) custom-call(s32[24]{0:T(128)S(1)} %copy-done.25, f32[1536,512]{1,0:T(8,128)} %get-tuple-element.351.back_ref, f32[1536,128]{1,0:T(8,128)S(1)} %get-tuple-element.352.cols_ref, f32[8,1536]{1,0:T(8,128)S(1)} %get-tuple-element.353.prob_ref, ...), custom_call_target="tpu_custom_call" | custom-call | flops 402653184 | bytes 10000000 | tf_op jit(solution)/shard_map/gates/pallas_call | solution.py:521
  252.3 2.8 add_convert_fusion
  261.4 16.5 %collective-permute-done.43 = bf16[3,2,2,2,32,512]{5,4,0,3,2,1:T(8,128)(2,1)S(1)} collective-permute-done((bf16[3,2,2,2,32,512]{5,4,0,3,2,1:T(8,128)(2,1)S(1)}, bf16[3,2,2,2,32,512]{5,4,0,3,2,1:T(8,128)(2,1)S(1)}, u32[]{:S(2)}, u32[]{:S(2)}) %collective-permute-start.43) | collective-permute-done | bytes 786464 | tf_op jit(solution)/shard_map/ppermute | solution.py:67
  289.1 9.8 %finish.1 = (bf16[1536,640]{1,0:T(8,128)(2,1)}, bf16[512,1792]{1,0:T(8,128)(2,1)}) custom-call(s32[24]{0:T(128)S(1)} %copy-done.25, f32[768,512]{1,0:T(8,128)S(1)} %copy-done.17, bf16[768,512]{1,0:T(8,128)(2,1)S(1)} %copy-done.7, f32[1536,512]{1,0:T(8,128)} %get-tuple-element.376.sum_ref, bf16[1536,512]{1,0:T(8,128)(2,1)S(1)} %copy-done.19, ...), custom_call_target="tpu_custom_call" | custom-call | flops 2013265920 | bytes 14000000 | tf_op jit(solution)/shard_map/finish/pallas_call | solution.py:626
  304.7 2.7 collective-permute-start.50
  311.3 4.3 %fusion.2 = bf16[1536,640]{1,0:T(8,128)(2,1)S(1)} fusion(bf16[1536,640]{1,0:T(8,128)(2,1)S(1)} %copy-done.48, f32[1536]{0:T(1024)S(1)} %add_bitcast_fusion.1), kind=kOutput, calls=%fused_computation.4 | convolution fusion | flops 3023241216 | bytes 3938304 | tf_op jit(solution)/shard_map/dot_general | solution.py:1332
  315.7 10.0 %collective-permute-done.50 = bf16[2,3,2,32,512]{4,3,1,0,2:T(8,128)(2,1)S(1)} collective-permute-done((bf16[2,3,2,32,512]{4,3,1,0,2:T(8,128)(2,1)S(1)}, bf16[2,3,2,32,512]{4,3,1,0,2:T(8,128)(2,1)S(1)}, u32[]{:S(2)}, u32[]{:S(2)}) %collective-permute-start.50) | collective-permute-done | bytes 393248 | tf_op jit(solution)/shard_map/ppermute | solution.py:67
  (333 shorter events, 120.3 us)
Async XLA Ops:
  4.6 27.3 %collective-permute-start.1 = (bf16[2,3,32,512]{3,2,1,0:T(8,128)(2,1)S(1)}, bf16[2,3,32,512]{3,2,1,0:T(8,128)(2,1)S(1)}, u32[]{:S(2)}, u32[]{:S(2)}) collective-permute-start(bf16[2,3,32,512]{3,2,1,0:T(8,128)(2,1)S(1)} %get-tuple-element.231), channel_id=1, source_target_pairs={{0,16},{2,18},{4,20},{6,22},{8,24},{10,26},{12,28},{14,30},{16,0},... | collective-permute-start | bytes 589832 | tf_op jit(solution)/shard_map/ppermute | solution.py:67
  14.3 19.9 %collective-permute-start = (bf16[2,6,32,512]{3,2,1,0:T(8,128)(2,1)S(1)}, bf16[2,6,32,512]{3,2,1,0:T(8,128)(2,1)S(1)}, u32[]{:S(2)}, u32[]{:S(2)}) collective-permute-start(bf16[2,6,32,512]{3,2,1,0:T(8,128)(2,1)S(1)} %get-tuple-element.226), channel_id=1, source_target_pairs={{0,8},{2,10},{4,12},{6,14},{8,0},{10,2},{12,4},{14,6},{16,24},{18,... | collective-permute-start | bytes 1179656 | tf_op jit(solution)/shard_map/ppermute | solution.py:67
  38.7 22.2 %collective-permute-start.6 = (bf16[2,3,32,512]{3,2,1,0:T(8,128)(2,1)S(1)}, bf16[2,3,32,512]{3,2,1,0:T(8,128)(2,1)S(1)}, u32[]{:S(2)}, u32[]{:S(2)}) collective-permute-start(bf16[2,3,32,512]{3,2,1,0:T(8,128)(2,1)S(1)} %get-tuple-element.236), channel_id=1, source_target_pairs={{0,24},{2,26},{4,28},{6,30},{8,16},{10,18},{12,20},{14,22},{16,8},... | collective-permute-start | bytes 589832 | tf_op jit(solution)/shard_map/ppermute | solution.py:67
  41.3 19.7 %collective-permute-start.3 = (bf16[2,3,64,512]{3,2,1,0:T(8,128)(2,1)S(1)}, bf16[2,3,64,512]{3,2,1,0:T(8,128)(2,1)}, u32[]{:S(2)}, u32[]{:S(2)}) collective-permute-start(bf16[2,3,64,512]{3,2,1,0:T(8,128)(2,1)S(1)} %pad_maximum_fusion.10), channel_id=1, source_target_pairs={{0,4},{2,6},{4,0},{6,2},{8,12},{10,14},{12,8},{14,10},{16,20},{18,... | collective-permute-start | bytes 1179656 | tf_op jit(solution)/shard_map/ppermute | solution.py:67
  45.3 24.1 %collective-permute-start.16 = (bf16[128,1792]{1,0:T(8,128)(2,1)}, bf16[128,1792]{1,0:T(8,128)(2,1)}, u32[]{:S(2)}, u32[]{:S(2)}) collective-permute-start(bf16[128,1792]{1,0:T(8,128)(2,1)} %pad_maximum_fusion.7), channel_id=1, source_target_pairs={{0,2},{2,0},{4,6},{6,4},{8,10},{10,8},{12,14},{14,12},{16,18},{18,... | collective-permute-start | bytes 1376264 | tf_op jit(solution)/shard_map/ppermute | solution.py:67
  58.4 23.7 %collective-permute-start.12 = (bf16[1536,640]{1,0:T(8,128)(2,1)}, bf16[1536,640]{1,0:T(8,128)(2,1)}, u32[]{:S(2)}, u32[]{:S(2)}) collective-permute-start(bf16[1536,640]{1,0:T(8,128)(2,1)} %own_ref.1), channel_id=1, source_target_pairs={{0,8},{2,10},{4,12},{6,14},{9,1},{11,3},{13,5},{15,7},{16,24},{18,... | collective-permute-start | bytes 5898248 | tf_op jit(solution)/shard_map/ppermute | solution.py:75
  62.8 31.2 %collective-permute-start.9 = (bf16[2,2,3,64,512]{4,3,2,1,0:T(8,128)(2,1)S(1)}, bf16[2,2,3,64,512]{4,3,2,1,0:T(8,128)(2,1)}, u32[]{:S(2)}, u32[]{:S(2)}) collective-permute-start(bf16[2,2,3,64,512]{4,3,2,1,0:T(8,128)(2,1)S(1)} %pad_maximum_fusion.4.refs_2_.refs_4_.refs_5_), channel_id=1, source_target_pairs={{0,4},{2,6},{4,0},{6,2},{8,12},{10,14},{12,8},{14,10},{16,20},{18,... | collective-permute-start | bytes 2359304 | tf_op jit(solution)/shard_map/ppermute | solution.py:67
  65.5 28.4 %collective-permute-start.8 = (bf16[2,2,3,64,512]{4,3,2,1,0:T(8,128)(2,1)S(1)}, bf16[2,2,3,64,512]{4,3,2,1,0:T(8,128)(2,1)}, u32[]{:S(2)}, u32[]{:S(2)}) collective-permute-start(bf16[2,2,3,64,512]{4,3,2,1,0:T(8,128)(2,1)S(1)} %pad_maximum_fusion.3.refs_0_.refs_2_.refs_3_), channel_id=1, source_target_pairs={{0,2},{2,0},{4,6},{6,4},{8,10},{10,8},{12,14},{14,12},{16,18},{18,... | collective-permute-start | bytes 2359304 | tf_op jit(solution)/shard_map/ppermute | solution.py:67
  70.6 23.3 %collective-permute-start.10 = (bf16[2,3,64,512]{3,2,1,0:T(8,128)(2,1)S(1)}, bf16[2,3,64,512]{3,2,1,0:T(8,128)(2,1)}, u32[]{:S(2)}, u32[]{:S(2)}) collective-permute-start(bf16[2,3,64,512]{3,2,1,0:T(8,128)(2,1)S(1)} %pad_maximum_fusion.12), channel_id=1, source_target_pairs={{0,4},{2,6},{4,0},{6,2},{8,12},{10,14},{12,8},{14,10},{16,20},{18,... | collective-permute-start | bytes 1179656 | tf_op jit(solution)/shard_map/ppermute | solution.py:67
  73.1 20.8 %collective-permute-start.11 = (bf16[2,3,64,512]{3,2,1,0:T(8,128)(2,1)S(1)}, bf16[2,3,64,512]{3,2,1,0:T(8,128)(2,1)S(1)}, u32[]{:S(2)}, u32[]{:S(2)}) collective-permute-start(bf16[2,3,64,512]{3,2,1,0:T(8,128)(2,1)S(1)} %pad_maximum_fusion.13), channel_id=1, source_target_pairs={{0,2},{2,0},{4,6},{6,4},{8,10},{10,8},{12,14},{14,12},{16,18},{18,... | collective-permute-start | bytes 1179656 | tf_op jit(solution)/shard_map/ppermute | solution.py:67
  96.9 20.0 %collective-permute-start.23 = (bf16[2,2,3,64,512]{4,3,2,1,0:T(8,128)(2,1)S(1)}, bf16[2,2,3,64,512]{4,3,2,1,0:T(8,128)(2,1)S(1)}, u32[]{:S(2)}, u32[]{:S(2)}) collective-permute-start(bf16[2,2,3,64,512]{4,3,2,1,0:T(8,128)(2,1)S(1)} %pad_maximum_fusion.6.refs_2_.refs_10_.refs_5_), channel_id=1, source_target_pairs={{0,4},{2,6},{4,0},{6,2},{8,12},{10,14},{12,8},{14,10},{16,20},{18,... | collective-permute-start | bytes 2359304 | tf_op jit(solution)/shard_map/ppermute | solution.py:67
  99.7 19.7 %collective-permute-start.22 = (bf16[2,2,3,64,512]{4,3,2,1,0:T(8,128)(2,1)S(1)}, bf16[2,2,3,64,512]{4,3,2,1,0:T(8,128)(2,1)S(1)}, u32[]{:S(2)}, u32[]{:S(2)}) collective-permute-start(bf16[2,2,3,64,512]{4,3,2,1,0:T(8,128)(2,1)S(1)} %pad_maximum_fusion.5.refs_0_.refs_8_.refs_3_), channel_id=1, source_target_pairs={{0,2},{2,0},{4,6},{6,4},{8,10},{10,8},{12,14},{14,12},{16,18},{18,... | collective-permute-start | bytes 2359304 | tf_op jit(solution)/shard_map/ppermute | solution.py:67
  101.2 18.6 %collective-permute-start.26 = (bf16[2,2,3,64,512]{4,3,2,1,0:T(8,128)(2,1)S(1)}, bf16[2,2,3,64,512]{4,3,2,1,0:T(8,128)(2,1)S(1)}, u32[]{:S(2)}, u32[]{:S(2)}) collective-permute-start(bf16[2,2,3,64,512]{4,3,2,1,0:T(8,128)(2,1)S(1)} %pad_maximum_fusion.6.refs_2_.refs_10_.refs_5_), channel_id=1, source_target_pairs={{0,1},{1,0},{2,3},{3,2},{4,5},{5,4},{6,7},{7,6},{8,9},{9,8},{10,11... | collective-permute-start | bytes 2359304 | tf_op jit(solution)/shard_map/ppermute | solution.py:125
  101.3 18.6 %collective-permute-start.24 = (bf16[2,2,3,64,512]{4,3,2,1,0:T(8,128)(2,1)S(1)}, bf16[2,2,3,64,512]{4,3,2,1,0:T(8,128)(2,1)S(1)}, u32[]{:S(2)}, u32[]{:S(2)}) collective-permute-start(bf16[2,2,3,64,512]{4,3,2,1,0:T(8,128)(2,1)S(1)} %pad_maximum_fusion.5.refs_0_.refs_8_.refs_3_), channel_id=1, source_target_pairs={{0,1},{1,0},{2,3},{3,2},{4,5},{5,4},{6,7},{7,6},{8,9},{9,8},{10,11... | collective-permute-start | bytes 2359304 | tf_op jit(solution)/shard_map/ppermute | solution.py:125
  132.9 19.6 %collective-permute-start.28 = (bf16[768,512]{1,0:T(8,128)(2,1)S(1)}, bf16[768,512]{1,0:T(8,128)(2,1)S(1)}, u32[]{:S(2)}, u32[]{:S(2)}) collective-permute-start(bf16[768,512]{1,0:T(8,128)(2,1)S(1)} %get-tuple-element.294), channel_id=1, source_target_pairs={{0,8},{2,10},{4,12},{6,14},{8,0},{10,2},{12,4},{14,6},{16,24},{18,... | collective-permute-start | bytes 2359304 | tf_op jit(solution)/shard_map/ppermute | solution.py:67
  161.3 18.8 %collective-permute-start.29 = (bf16[768,512]{1,0:T(8,128)(2,1)S(1)}, bf16[768,512]{1,0:T(8,128)(2,1)S(1)}, u32[]{:S(2)}, u32[]{:S(2)}) collective-permute-start(bf16[768,512]{1,0:T(8,128)(2,1)S(1)} %get-tuple-element.298.refs_0_), channel_id=1, source_target_pairs={{0,8},{2,10},{4,12},{6,14},{8,0},{10,2},{12,4},{14,6},{16,24},{18,... | collective-permute-start | bytes 2359304 | tf_op jit(solution)/shard_map/ppermute | solution.py:67
  209.3 34.5 %collective-permute-start.38 = (f32[8,128]{1,0:T(8,128)S(1)}, f32[8,128]{1,0:T(8,128)S(1)}, u32[]{:S(2)}, u32[]{:S(2)}) collective-permute-start(f32[8,128]{1,0:T(8,128)S(1)} %add.311), channel_id=1, source_target_pairs={{0,8},{2,10},{4,12},{6,14},{8,0},{10,2},{12,4},{14,6},{16,24},{18,... | collective-permute-start | bytes 12296 | tf_op jit(solution)/shard_map/ppermute | solution.py:67
  212.7 31.1 %collective-permute-start.37 = (f32[8,768]{1,0:T(8,128)S(1)}, f32[8,768]{1,0:T(8,128)S(1)}, u32[]{:S(2)}, u32[]{:S(2)}) collective-permute-start(f32[8,768]{1,0:T(8,128)S(1)} %get-tuple-element.345), channel_id=1, source_target_pairs={{1,9},{3,11},{5,13},{7,15},{8,0},{10,2},{12,4},{14,6},{17,25},{19,... | collective-permute-start | bytes 73736 | tf_op jit(solution)/shard_map/ppermute | solution.py:75
  215.3 28.6 %collective-permute-start.36 = (bf16[3,2,2,2,32,512]{5,4,0,3,2,1:T(8,128)(2,1)S(1)}, bf16[3,2,2,2,32,512]{5,4,0,3,2,1:T(8,128)(2,1)S(1)}, u32[]{:S(2)}, u32[]{:S(2)}) collective-permute-start(bf16[3,2,2,2,32,512]{5,4,0,3,2,1:T(8,128)(2,1)S(1)} %bitcast.153), channel_id=1, source_target_pairs={{0,4},{2,6},{4,0},{6,2},{8,12},{10,14},{12,8},{14,10},{16,20},{18,... | collective-permute-start | bytes 2359304 | tf_op jit(solution)/shard_map/ppermute | solution.py:67
  216.0 27.9 %collective-permute-start.35 = (bf16[3,2,2,2,32,512]{5,4,0,3,2,1:T(8,128)(2,1)S(1)}, bf16[3,2,2,2,32,512]{5,4,0,3,2,1:T(8,128)(2,1)S(1)}, u32[]{:S(2)}, u32[]{:S(2)}) collective-permute-start(bf16[3,2,2,2,32,512]{5,4,0,3,2,1:T(8,128)(2,1)S(1)} %get-tuple-element.450), channel_id=1, source_target_pairs={{0,2},{2,0},{4,6},{6,4},{8,10},{10,8},{12,14},{14,12},{16,18},{18,... | collective-permute-start | bytes 2359304 | tf_op jit(solution)/shard_map/ppermute | solution.py:67
  257.3 22.3 %collective-permute-start.45 = (bf16[1536,512]{1,0:T(8,128)(2,1)S(1)}, bf16[1536,512]{1,0:T(8,128)(2,1)S(1)}, u32[]{:S(2)}, u32[]{:S(2)}) collective-permute-start(bf16[1536,512]{1,0:T(8,128)(2,1)S(1)} %get-tuple-element.366), channel_id=1, source_target_pairs={{1,9},{3,11},{5,13},{7,15},{8,0},{10,2},{12,4},{14,6},{17,25},{19,... | collective-permute-start | bytes 4718600 | tf_op jit(solution)/shard_map/ppermute | solution.py:75
  259.0 19.0 %collective-permute-start.43 = (bf16[3,2,2,2,32,512]{5,4,0,3,2,1:T(8,128)(2,1)S(1)}, bf16[3,2,2,2,32,512]{5,4,0,3,2,1:T(8,128)(2,1)S(1)}, u32[]{:S(2)}, u32[]{:S(2)}) collective-permute-start(bf16[3,2,2,2,32,512]{5,4,0,3,2,1:T(8,128)(2,1)S(1)} %get-tuple-element.446), channel_id=1, source_target_pairs={{0,2},{2,0},{4,6},{6,4},{8,10},{10,8},{12,14},{14,12},{16,18},{18,... | collective-permute-start | bytes 2359304 | tf_op jit(solution)/shard_map/ppermute | solution.py:67
  260.0 19.1 %collective-permute-start.44 = (bf16[3,2,2,2,32,512]{5,4,0,3,2,1:T(8,128)(2,1)S(1)}, bf16[3,2,2,2,32,512]{5,4,0,3,2,1:T(8,128)(2,1)S(1)}, u32[]{:S(2)}, u32[]{:S(2)}) collective-permute-start(bf16[3,2,2,2,32,512]{5,4,0,3,2,1:T(8,128)(2,1)S(1)} %get-tuple-element.444), channel_id=1, source_target_pairs={{0,4},{2,6},{4,0},{6,2},{8,12},{10,14},{12,8},{14,10},{16,20},{18,... | collective-permute-start | bytes 2359304 | tf_op jit(solution)/shard_map/ppermute | solution.py:67
  304.7 21.0 %collective-permute-start.50 = (bf16[2,3,2,32,512]{4,3,1,0,2:T(8,128)(2,1)S(1)}, bf16[2,3,2,32,512]{4,3,1,0,2:T(8,128)(2,1)S(1)}, u32[]{:S(2)}, u32[]{:S(2)}) collective-permute-start(bf16[2,3,2,32,512]{4,3,1,0,2:T(8,128)(2,1)S(1)} %get-tuple-element.456), channel_id=1, source_target_pairs={{0,16},{2,18},{4,20},{6,22},{8,24},{10,26},{12,28},{14,30},{16,0},... | collective-permute-start | bytes 1179656 | tf_op jit(solution)/shard_map/ppermute | solution.py:67
  (87 other events, 1155.2 us)

commit v6 on v5

--- a/solution.py
+++ b/solution.py
@@ -449,7 +449,8 @@
     mine = group == cols[:, DOMAIN : DOMAIN + 1].astype(jnp.int32)
     act = jnp.where(mine, act, 0.0)
     logit = jnp.sum(act * head, axis=1, keepdims=True) + cols[:, BIAS : BIAS + 1]
-    predicted = 1.0 / (1.0 + jnp.exp(-logit))
+    small = jnp.exp(-jnp.abs(logit))
+    predicted = jnp.where(logit >= 0.0, 1.0, small) / (1.0 + small)
     grad_logit = cols[:, WEIGHT : WEIGHT + 1] * (predicted - cols[:, LABEL : LABEL + 1])
     lane = lax.broadcasted_iota(jnp.int32, cols.shape, 1)
     out_ref[...] = jnp.transpose(jnp.where(lane == 0, predicted, jnp.where(lane == 1, grad_logit, 0.0)))[:8]

time: 348 us -> 349 us (level)
  no operation moved by 1% of the time
where the time goes in v6:
time: 349 us; the launch traced here: 344 us
  Pallas kernels  149 us (43%)
  waiting for transfers between devices  76.4 us (22%)
  starting transfers between devices  67.3 us (19%)
  other arithmetic  30.2 us (9%)
  local copies, waits for them, and re-layouts  14.4 us (4%)
  matrix products  4.28 us (1%)
    pallas_call x4, Pallas kernels, call_backward(): pl.pallas_call(functools.partial(backward_kernel, experts, halves, mode =...  69.2 us
    ppermute x41, waiting for transfers between devices, send(): return lax.ppermute(values, 'dp', pairs)  66.7 us
    ppermute x41, starting transfers between devices, send(): return lax.ppermute(values, 'dp', pairs)  53.7 us
    pallas_call x3, Pallas kernels, call_forward(): pl.pallas_call(functools.partial(forward_kernel, experts, own, len(kept),...  38.3 us
    pallas_call x1, Pallas kernels, call_prepare(): pl.pallas_call(prepare_kernel, grid_spec=pltpu.PrefetchScalarGridSpec(num...  11.8 us
    pallas_call x1, Pallas kernels, call_finish(): pl.pallas_call(finish_kernel, grid_spec=pltpu.PrefetchScalarGridSpec(num_...  9.79 us
    unnamed x101, local copies, waits for them, and re-layouts  8.97 us
    pallas_call x1, Pallas kernels, call_tower(): pl.pallas_call(tower_kernel, grid_spec=pltpu.PrefetchScalarGridSpec(num_s...  8.87 us
  transfers between devices with their start and end apart: 61, of which 22 were waited for; matrix products, arithmetic and copies ran while one was open for 10% of the time, Pallas kernels for 37%

profile of v6, /device:TPU:0, one launch (start us, length us, event | category | flops | bytes accessed | tf_op | source)
XLA Modules:
  0.0 343.7 jit_solution(13842722346611286895)
XLA Ops:
  4.6 4.1 %collective-permute-start.1 = (bf16[2,3,32,512]{3,2,1,0:T(8,128)(2,1)S(1)}, bf16[2,3,32,512]{3,2,1,0:T(8,128)(2,1)S(1)}, u32[]{:S(2)}, u32[]{:S(2)}) collective-permute-start(bf16[2,3,32,512]{3,2,1,0:T(8,128)(2,1)S(1)} %get-tuple-element.231), channel_id=1, source_target_pairs={{0,16},{2,18},{4,20},{6,22},{8,24},{10,26},{12,28},{14,30},{16,0},... | collective-permute-start | bytes 589832 | tf_op jit(solution)/shard_map/ppermute | solution.py:67
  16.7 6.1 %collective-permute-done.13 = bf16[16,1792]{1,0:T(8,128)(2,1)S(1)} collective-permute-done((bf16[16,1792]{1,0:T(8,128)(2,1)S(1)}, bf16[16,1792]{1,0:T(8,128)(2,1)S(1)}, u32[]{:S(2)}, u32[]{:S(2)}) %collective-permute-start.13) | collective-permute-done | bytes 57376 | tf_op jit(solution)/shard_map/ppermute | solution.py:67
  25.1 5.2 %collective-permute-done.14 = bf16[32,1792]{1,0:T(8,128)(2,1)S(1)} collective-permute-done((bf16[32,1792]{1,0:T(8,128)(2,1)S(1)}, bf16[32,1792]{1,0:T(8,128)(2,1)S(1)}, u32[]{:S(2)}, u32[]{:S(2)}) %collective-permute-start.14) | collective-permute-done | bytes 114720 | tf_op jit(solution)/shard_map/ppermute | solution.py:67
  34.3 3.0 collective-permute-start.7
  48.0 10.4 %collective-permute-done.5 = bf16[2,3,32,512]{3,2,1,0:T(8,128)(2,1)} collective-permute-done((bf16[2,3,32,512]{3,2,1,0:T(8,128)(2,1)S(1)}, bf16[2,3,32,512]{3,2,1,0:T(8,128)(2,1)}, u32[]{:S(2)}, u32[]{:S(2)}) %collective-permute-start.5) | collective-permute-done | bytes 196640 | tf_op jit(solution)/shard_map/ppermute | solution.py:67
  77.7 4.4 %collective-permute-done.12.in_ref = bf16[1536,640]{1,0:T(8,128)(2,1)} collective-permute-done((bf16[1536,640]{1,0:T(8,128)(2,1)}, bf16[1536,640]{1,0:T(8,128)(2,1)}, u32[]{:S(2)}, u32[]{:S(2)}) %collective-permute-start.12) | collective-permute-done | bytes 1966112 | tf_op jit(solution)/shard_map/ppermute | solution.py:75
  82.1 11.8 %prepare.1 = (bf16[1536,640]{1,0:T(8,128)(2,1)}, bf16[1536,512]{1,0:T(8,128)(2,1)}, f32[1536,512]{1,0:T(8,128)}, f32[1536,128]{1,0:T(8,128)S(1)}, f32[8,1536]{1,0:T(8,128)S(1)}) custom-call(s32[24]{0:T(128)S(1)} %concatenate.92.ints, f32[8]{0:T(128)S(1)} %pad_maximum_fusion.19.floats, f32[8,1536]{1,0:T(8,128)S(1)} %pad_maximum_fusion.15.rows_ref, ...), custom_call_target="tpu_custom_call" | custom-call | flops 4026531840 | bytes 12000000 | tf_op jit(solution)/shard_map/prepare/pallas_call | solution.py:861
  103.2 10.7 %experts_forward.3 = (f32[1536,128]{1,0:T(8,128)S(1)}, f32[1536,512]{1,0:T(8,128)}, bf16[3,1536,512]{2,1,0:T(8,128)(2,1)}) custom-call(s32[24]{0:T(128)S(1)} %concatenate.92.ints, bf16[1536,512]{1,0:T(8,128)(2,1)} %get-tuple-element.268.x_ref, ...), custom_call_target="tpu_custom_call", output_to_operand_aliasing={{0}: (12, {}), {1}: (13, {})} | custom-call | flops 4831838208 | bytes 12000000 | tf_op jit(solution)/shard_map/experts_forward/pallas_call | solution.py:930
  114.0 2.9 collective-permute-done.23.refs_3_.refs_11_.refs_6_
  123.7 9.2 %experts_forward.4 = (f32[1536,128]{1,0:T(8,128)S(1)}, f32[1536,512]{1,0:T(8,128)}, bf16[3,1536,512]{2,1,0:T(8,128)(2,1)}, bf16[768,512]{1,0:T(8,128)(2,1)S(1)}) custom-call(s32[24]{0:T(128)S(1)} %concatenate.92.ints, bf16[1536,512]{1,0:T(8,128)(2,1)} %get-tuple-element.268.x_ref, ...), custom_call_target="tpu_custom_call", output_to_operand_aliasing={{0}: (12, {}), {1}: (13, {})} | custom-call | flops 1610612736 | bytes 12000000 | tf_op jit(solution)/shard_map/experts_forward/pallas_call | solution.py:930
  133.0 18.4 %experts_forward.5 = (f32[1536,128]{1,0:T(8,128)S(1)}, f32[1536,512]{1,0:T(8,128)}, bf16[3,1536,512]{2,1,0:T(8,128)(2,1)}, bf16[3,1536,512]{2,1,0:T(8,128)(2,1)}) custom-call(s32[24]{0:T(128)S(1)} %concatenate.92.ints, bf16[1536,512]{1,0:T(8,128)(2,1)} %get-tuple-element.268.x_ref, ...), custom_call_target="tpu_custom_call", output_to_operand_aliasing={{0}: (20, {}), {1}: (21, {}), {2}: (22, {}), {3}: (23, {})} | custom-call | flops 4831838208 | bytes 12000000 | tf_op jit(solution)/shard_map/experts_forward/pallas_call | solution.py:930
  152.5 8.9 %towers.1 = (f32[8,768]{1,0:T(8,128)S(1)}, f32[768,512]{1,0:T(8,128)}, bf16[768,512]{1,0:T(8,128)(2,1)S(1)}, f32[512,1024]{1,0:T(8,128)}, f32[8,1024]{1,0:T(8,128)S(1)}, /*index=5*/f32[8,128]{1,0:T(8,128)S(1)}) custom-call(s32[24]{0:T(128)S(1)} %concatenate.92.ints, f32[1536,512]{1,0:T(8,128)} %get-tuple-element.293.mix_ref, ...), custom_call_target="tpu_custom_call" | custom-call | flops 2415919104 | bytes 10000000 | tf_op jit(solution)/shard_map/towers/pallas_call | solution.py:1037
  162.0 16.8 %experts_backward.4 = (f32[1536,128]{1,0:T(8,128)S(1)}, f32[1536,512]{1,0:T(8,128)}, bf16[2,2,512,512]{3,2,1,0:T(8,128)(2,1)}, bf16[2,2,512,512]{3,2,1,0:T(8,128...) custom-call(s32[24]{0:T(128)S(1)} %concatenate.92.ints, ...), custom_call_target="tpu_custom_call", output_to_operand_aliasing={{0}: (14, {})} | custom-call | flops 8053063680 | bytes 20000000 | tf_op jit(solution)/shard_map/experts_backward/pallas_call | solution.py:998
  181.4 17.1 %experts_backward.5 = (f32[1536,128]{1,0:T(8,128)S(1)}, f32[1536,512]{1,0:T(8,128)}, bf16[2,2,512,512]{3,2,1,0:T(8,128)(2,1)}, bf16[2,2,512,512]{3,2,1,0:T(8,128...) custom-call(s32[24]{0:T(128)S(1)} %copy-done.24, ...), custom_call_target="tpu_custom_call", output_to_operand_aliasing={{0}: (14, {}), {1}: (15, {})} | custom-call | flops 8053063680 | bytes 20000000 | tf_op jit(solution)/shard_map/experts_backward/pallas_call | solution.py:998
  200.2 9.0 %experts_backward.6 = (f32[1536,128]{1,0:T(8,128)S(1)}, f32[1536,512]{1,0:T(8,128)}, bf16[1,2,512,512]{3,2,1,0:T(8,128)(2,1)}, bf16[1,2,512,512]{3,2,1,0:T(8,128...) custom-call(s32[24]{0:T(128)S(1)} %copy-done.24, ...), custom_call_target="tpu_custom_call", output_to_operand_aliasing={{0}: (15, {}), {1}: (16, {})} | custom-call | flops 4026531840 | bytes 20000000 | tf_op jit(solution)/shard_map/experts_backward/pallas_call | solution.py:998
  209.4 5.5 %collective-permute-start.38 = (f32[8,128]{1,0:T(8,128)S(1)}, f32[8,128]{1,0:T(8,128)S(1)}, u32[]{:S(2)}, u32[]{:S(2)}) collective-permute-start(f32[8,128]{1,0:T(8,128)S(1)} %add.311), channel_id=1, source_target_pairs={{0,8},{2,10},{4,12},{6,14},{8,0},{10,2},{12,4},{14,6},{16,24},{18,... | collective-permute-start | bytes 12296 | tf_op jit(solution)/shard_map/ppermute | solution.py:67
  219.8 26.2 %experts_backward.7 = (f32[1536,128]{1,0:T(8,128)S(1)}, f32[1536,512]{1,0:T(8,128)}, bf16[3,2,512,512]{3,2,1,0:T(8,128)(2,1)}, bf16[3,2,512,512]{3,2,1,0:T(8,128...) custom-call(s32[24]{0:T(128)S(1)} %copy-done.24, ...), custom_call_target="tpu_custom_call", output_to_operand_aliasing={{0}: (15, {}), {1}: (16, {})} | custom-call | flops 12079595520 | bytes 20000000 | tf_op jit(solution)/shard_map/experts_backward/pallas_call | solution.py:998
  249.6 4.9 %gates.1 = (f32[1536,512]{1,0:T(8,128)}, bf16[1536,512]{1,0:T(8,128)(2,1)S(1)}, f32[512,128]{1,0:T(8,128)S(1)}) custom-call(s32[24]{0:T(128)S(1)} %copy-done.25, f32[1536,512]{1,0:T(8,128)} %get-tuple-element.351.back_ref, f32[1536,128]{1,0:T(8,128)S(1)} %get-tuple-element.352.cols_ref, f32[8,1536]{1,0:T(8,128)S(1)} %get-tuple-element.353.prob_ref, ...), custom_call_target="tpu_custom_call" | custom-call | flops 402653184 | bytes 10000000 | tf_op jit(solution)/shard_map/gates/pallas_call | solution.py:522
  254.6 2.8 add_convert_fusion
  263.8 15.9 %collective-permute-done.43 = bf16[3,2,2,2,32,512]{5,4,0,3,2,1:T(8,128)(2,1)S(1)} collective-permute-done((bf16[3,2,2,2,32,512]{5,4,0,3,2,1:T(8,128)(2,1)S(1)}, bf16[3,2,2,2,32,512]{5,4,0,3,2,1:T(8,128)(2,1)S(1)}, u32[]{:S(2)}, u32[]{:S(2)}) %collective-permute-start.43) | collective-permute-done | bytes 786464 | tf_op jit(solution)/shard_map/ppermute | solution.py:67
  283.2 3.0 collective-permute-start.46
  292.2 9.8 %finish.1 = (bf16[1536,640]{1,0:T(8,128)(2,1)}, bf16[512,1792]{1,0:T(8,128)(2,1)}) custom-call(s32[24]{0:T(128)S(1)} %copy-done.25, f32[768,512]{1,0:T(8,128)S(1)} %copy-done.17, bf16[768,512]{1,0:T(8,128)(2,1)S(1)} %copy-done.7, f32[1536,512]{1,0:T(8,128)} %get-tuple-element.376.sum_ref, bf16[1536,512]{1,0:T(8,128)(2,1)S(1)} %copy-done.19, ...), custom_call_target="tpu_custom_call" | custom-call | flops 2013265920 | bytes 14000000 | tf_op jit(solution)/shard_map/finish/pallas_call | solution.py:627
  313.1 4.3 %fusion.2 = bf16[1536,640]{1,0:T(8,128)(2,1)S(1)} fusion(bf16[1536,640]{1,0:T(8,128)(2,1)S(1)} %copy-done.48, f32[1536]{0:T(1024)S(1)} %add_bitcast_fusion.1), kind=kOutput, calls=%fused_computation.4 | convolution fusion | flops 3023241216 | bytes 3938304 | tf_op jit(solution)/shard_map/dot_general | solution.py:1333
  317.7 10.8 %collective-permute-done.50 = bf16[2,3,2,32,512]{4,3,1,0,2:T(8,128)(2,1)S(1)} collective-permute-done((bf16[2,3,2,32,512]{4,3,1,0,2:T(8,128)(2,1)S(1)}, bf16[2,3,2,32,512]{4,3,1,0,2:T(8,128)(2,1)S(1)}, u32[]{:S(2)}, u32[]{:S(2)}) %collective-permute-start.50) | collective-permute-done | bytes 393248 | tf_op jit(solution)/shard_map/ppermute | solution.py:67
  (333 shorter events, 120.4 us)
Async XLA Ops:
  4.6 27.3 %collective-permute-start.1 = (bf16[2,3,32,512]{3,2,1,0:T(8,128)(2,1)S(1)}, bf16[2,3,32,512]{3,2,1,0:T(8,128)(2,1)S(1)}, u32[]{:S(2)}, u32[]{:S(2)}) collective-permute-start(bf16[2,3,32,512]{3,2,1,0:T(8,128)(2,1)S(1)} %get-tuple-element.231), channel_id=1, source_target_pairs={{0,16},{2,18},{4,20},{6,22},{8,24},{10,26},{12,28},{14,30},{16,0},... | collective-permute-start | bytes 589832 | tf_op jit(solution)/shard_map/ppermute | solution.py:67
  14.3 19.9 %collective-permute-start = (bf16[2,6,32,512]{3,2,1,0:T(8,128)(2,1)S(1)}, bf16[2,6,32,512]{3,2,1,0:T(8,128)(2,1)S(1)}, u32[]{:S(2)}, u32[]{:S(2)}) collective-permute-start(bf16[2,6,32,512]{3,2,1,0:T(8,128)(2,1)S(1)} %get-tuple-element.226), channel_id=1, source_target_pairs={{0,8},{2,10},{4,12},{6,14},{8,0},{10,2},{12,4},{14,6},{16,24},{18,... | collective-permute-start | bytes 1179656 | tf_op jit(solution)/shard_map/ppermute | solution.py:67
  38.7 22.2 %collective-permute-start.6 = (bf16[2,3,32,512]{3,2,1,0:T(8,128)(2,1)S(1)}, bf16[2,3,32,512]{3,2,1,0:T(8,128)(2,1)S(1)}, u32[]{:S(2)}, u32[]{:S(2)}) collective-permute-start(bf16[2,3,32,512]{3,2,1,0:T(8,128)(2,1)S(1)} %get-tuple-element.236), channel_id=1, source_target_pairs={{0,24},{2,26},{4,28},{6,30},{8,16},{10,18},{12,20},{14,22},{16,8},... | collective-permute-start | bytes 589832 | tf_op jit(solution)/shard_map/ppermute | solution.py:67
  41.3 19.7 %collective-permute-start.3 = (bf16[2,3,64,512]{3,2,1,0:T(8,128)(2,1)S(1)}, bf16[2,3,64,512]{3,2,1,0:T(8,128)(2,1)}, u32[]{:S(2)}, u32[]{:S(2)}) collective-permute-start(bf16[2,3,64,512]{3,2,1,0:T(8,128)(2,1)S(1)} %pad_maximum_fusion.10), channel_id=1, source_target_pairs={{0,4},{2,6},{4,0},{6,2},{8,12},{10,14},{12,8},{14,10},{16,20},{18,... | collective-permute-start | bytes 1179656 | tf_op jit(solution)/shard_map/ppermute | solution.py:67
  45.3 24.1 %collective-permute-start.16 = (bf16[128,1792]{1,0:T(8,128)(2,1)}, bf16[128,1792]{1,0:T(8,128)(2,1)}, u32[]{:S(2)}, u32[]{:S(2)}) collective-permute-start(bf16[128,1792]{1,0:T(8,128)(2,1)} %pad_maximum_fusion.7), channel_id=1, source_target_pairs={{0,2},{2,0},{4,6},{6,4},{8,10},{10,8},{12,14},{14,12},{16,18},{18,... | collective-permute-start | bytes 1376264 | tf_op jit(solution)/shard_map/ppermute | solution.py:67
  58.4 23.7 %collective-permute-start.12 = (bf16[1536,640]{1,0:T(8,128)(2,1)}, bf16[1536,640]{1,0:T(8,128)(2,1)}, u32[]{:S(2)}, u32[]{:S(2)}) collective-permute-start(bf16[1536,640]{1,0:T(8,128)(2,1)} %own_ref.1), channel_id=1, source_target_pairs={{0,8},{2,10},{4,12},{6,14},{9,1},{11,3},{13,5},{15,7},{16,24},{18,... | collective-permute-start | bytes 5898248 | tf_op jit(solution)/shard_map/ppermute | solution.py:75
  62.8 31.2 %collective-permute-start.9 = (bf16[2,2,3,64,512]{4,3,2,1,0:T(8,128)(2,1)S(1)}, bf16[2,2,3,64,512]{4,3,2,1,0:T(8,128)(2,1)}, u32[]{:S(2)}, u32[]{:S(2)}) collective-permute-start(bf16[2,2,3,64,512]{4,3,2,1,0:T(8,128)(2,1)S(1)} %pad_maximum_fusion.4.refs_2_.refs_4_.refs_5_), channel_id=1, source_target_pairs={{0,4},{2,6},{4,0},{6,2},{8,12},{10,14},{12,8},{14,10},{16,20},{18,... | collective-permute-start | bytes 2359304 | tf_op jit(solution)/shard_map/ppermute | solution.py:67
  65.5 28.4 %collective-permute-start.8 = (bf16[2,2,3,64,512]{4,3,2,1,0:T(8,128)(2,1)S(1)}, bf16[2,2,3,64,512]{4,3,2,1,0:T(8,128)(2,1)}, u32[]{:S(2)}, u32[]{:S(2)}) collective-permute-start(bf16[2,2,3,64,512]{4,3,2,1,0:T(8,128)(2,1)S(1)} %pad_maximum_fusion.3.refs_0_.refs_2_.refs_3_), channel_id=1, source_target_pairs={{0,2},{2,0},{4,6},{6,4},{8,10},{10,8},{12,14},{14,12},{16,18},{18,... | collective-permute-start | bytes 2359304 | tf_op jit(solution)/shard_map/ppermute | solution.py:67
  70.6 23.3 %collective-permute-start.10 = (bf16[2,3,64,512]{3,2,1,0:T(8,128)(2,1)S(1)}, bf16[2,3,64,512]{3,2,1,0:T(8,128)(2,1)}, u32[]{:S(2)}, u32[]{:S(2)}) collective-permute-start(bf16[2,3,64,512]{3,2,1,0:T(8,128)(2,1)S(1)} %pad_maximum_fusion.12), channel_id=1, source_target_pairs={{0,4},{2,6},{4,0},{6,2},{8,12},{10,14},{12,8},{14,10},{16,20},{18,... | collective-permute-start | bytes 1179656 | tf_op jit(solution)/shard_map/ppermute | solution.py:67
  73.1 20.8 %collective-permute-start.11 = (bf16[2,3,64,512]{3,2,1,0:T(8,128)(2,1)S(1)}, bf16[2,3,64,512]{3,2,1,0:T(8,128)(2,1)S(1)}, u32[]{:S(2)}, u32[]{:S(2)}) collective-permute-start(bf16[2,3,64,512]{3,2,1,0:T(8,128)(2,1)S(1)} %pad_maximum_fusion.13), channel_id=1, source_target_pairs={{0,2},{2,0},{4,6},{6,4},{8,10},{10,8},{12,14},{14,12},{16,18},{18,... | collective-permute-start | bytes 1179656 | tf_op jit(solution)/shard_map/ppermute | solution.py:67
  96.9 20.0 %collective-permute-start.23 = (bf16[2,2,3,64,512]{4,3,2,1,0:T(8,128)(2,1)S(1)}, bf16[2,2,3,64,512]{4,3,2,1,0:T(8,128)(2,1)S(1)}, u32[]{:S(2)}, u32[]{:S(2)}) collective-permute-start(bf16[2,2,3,64,512]{4,3,2,1,0:T(8,128)(2,1)S(1)} %pad_maximum_fusion.6.refs_2_.refs_10_.refs_5_), channel_id=1, source_target_pairs={{0,4},{2,6},{4,0},{6,2},{8,12},{10,14},{12,8},{14,10},{16,20},{18,... | collective-permute-start | bytes 2359304 | tf_op jit(solution)/shard_map/ppermute | solution.py:67
  99.7 19.7 %collective-permute-start.22 = (bf16[2,2,3,64,512]{4,3,2,1,0:T(8,128)(2,1)S(1)}, bf16[2,2,3,64,512]{4,3,2,1,0:T(8,128)(2,1)S(1)}, u32[]{:S(2)}, u32[]{:S(2)}) collective-permute-start(bf16[2,2,3,64,512]{4,3,2,1,0:T(8,128)(2,1)S(1)} %pad_maximum_fusion.5.refs_0_.refs_8_.refs_3_), channel_id=1, source_target_pairs={{0,2},{2,0},{4,6},{6,4},{8,10},{10,8},{12,14},{14,12},{16,18},{18,... | collective-permute-start | bytes 2359304 | tf_op jit(solution)/shard_map/ppermute | solution.py:67
  101.2 18.6 %collective-permute-start.26 = (bf16[2,2,3,64,512]{4,3,2,1,0:T(8,128)(2,1)S(1)}, bf16[2,2,3,64,512]{4,3,2,1,0:T(8,128)(2,1)S(1)}, u32[]{:S(2)}, u32[]{:S(2)}) collective-permute-start(bf16[2,2,3,64,512]{4,3,2,1,0:T(8,128)(2,1)S(1)} %pad_maximum_fusion.6.refs_2_.refs_10_.refs_5_), channel_id=1, source_target_pairs={{0,1},{1,0},{2,3},{3,2},{4,5},{5,4},{6,7},{7,6},{8,9},{9,8},{10,11... | collective-permute-start | bytes 2359304 | tf_op jit(solution)/shard_map/ppermute | solution.py:125
  101.3 18.6 %collective-permute-start.24 = (bf16[2,2,3,64,512]{4,3,2,1,0:T(8,128)(2,1)S(1)}, bf16[2,2,3,64,512]{4,3,2,1,0:T(8,128)(2,1)S(1)}, u32[]{:S(2)}, u32[]{:S(2)}) collective-permute-start(bf16[2,2,3,64,512]{4,3,2,1,0:T(8,128)(2,1)S(1)} %pad_maximum_fusion.5.refs_0_.refs_8_.refs_3_), channel_id=1, source_target_pairs={{0,1},{1,0},{2,3},{3,2},{4,5},{5,4},{6,7},{7,6},{8,9},{9,8},{10,11... | collective-permute-start | bytes 2359304 | tf_op jit(solution)/shard_map/ppermute | solution.py:125
  132.9 19.6 %collective-permute-start.28 = (bf16[768,512]{1,0:T(8,128)(2,1)S(1)}, bf16[768,512]{1,0:T(8,128)(2,1)S(1)}, u32[]{:S(2)}, u32[]{:S(2)}) collective-permute-start(bf16[768,512]{1,0:T(8,128)(2,1)S(1)} %get-tuple-element.294), channel_id=1, source_target_pairs={{0,8},{2,10},{4,12},{6,14},{8,0},{10,2},{12,4},{14,6},{16,24},{18,... | collective-permute-start | bytes 2359304 | tf_op jit(solution)/shard_map/ppermute | solution.py:67
  161.4 18.8 %collective-permute-start.29 = (bf16[768,512]{1,0:T(8,128)(2,1)S(1)}, bf16[768,512]{1,0:T(8,128)(2,1)S(1)}, u32[]{:S(2)}, u32[]{:S(2)}) collective-permute-start(bf16[768,512]{1,0:T(8,128)(2,1)S(1)} %get-tuple-element.298.refs_0_), channel_id=1, source_target_pairs={{0,8},{2,10},{4,12},{6,14},{8,0},{10,2},{12,4},{14,6},{16,24},{18,... | collective-permute-start | bytes 2359304 | tf_op jit(solution)/shard_map/ppermute | solution.py:67
  209.4 36.6 %collective-permute-start.38 = (f32[8,128]{1,0:T(8,128)S(1)}, f32[8,128]{1,0:T(8,128)S(1)}, u32[]{:S(2)}, u32[]{:S(2)}) collective-permute-start(f32[8,128]{1,0:T(8,128)S(1)} %add.311), channel_id=1, source_target_pairs={{0,8},{2,10},{4,12},{6,14},{8,0},{10,2},{12,4},{14,6},{16,24},{18,... | collective-permute-start | bytes 12296 | tf_op jit(solution)/shard_map/ppermute | solution.py:67
  215.0 31.1 %collective-permute-start.37 = (f32[8,768]{1,0:T(8,128)S(1)}, f32[8,768]{1,0:T(8,128)S(1)}, u32[]{:S(2)}, u32[]{:S(2)}) collective-permute-start(f32[8,768]{1,0:T(8,128)S(1)} %get-tuple-element.345), channel_id=1, source_target_pairs={{1,9},{3,11},{5,13},{7,15},{8,0},{10,2},{12,4},{14,6},{17,25},{19,... | collective-permute-start | bytes 73736 | tf_op jit(solution)/shard_map/ppermute | solution.py:75
  217.5 28.6 %collective-permute-start.36 = (bf16[3,2,2,2,32,512]{5,4,0,3,2,1:T(8,128)(2,1)S(1)}, bf16[3,2,2,2,32,512]{5,4,0,3,2,1:T(8,128)(2,1)S(1)}, u32[]{:S(2)}, u32[]{:S(2)}) collective-permute-start(bf16[3,2,2,2,32,512]{5,4,0,3,2,1:T(8,128)(2,1)S(1)} %bitcast.153), channel_id=1, source_target_pairs={{0,4},{2,6},{4,0},{6,2},{8,12},{10,14},{12,8},{14,10},{16,20},{18,... | collective-permute-start | bytes 2359304 | tf_op jit(solution)/shard_map/ppermute | solution.py:67
  219.2 26.9 %collective-permute-start.35 = (bf16[3,2,2,2,32,512]{5,4,0,3,2,1:T(8,128)(2,1)S(1)}, bf16[3,2,2,2,32,512]{5,4,0,3,2,1:T(8,128)(2,1)S(1)}, u32[]{:S(2)}, u32[]{:S(2)}) collective-permute-start(bf16[3,2,2,2,32,512]{5,4,0,3,2,1:T(8,128)(2,1)S(1)} %get-tuple-element.450), channel_id=1, source_target_pairs={{0,2},{2,0},{4,6},{6,4},{8,10},{10,8},{12,14},{14,12},{16,18},{18,... | collective-permute-start | bytes 2359304 | tf_op jit(solution)/shard_map/ppermute | solution.py:67
  259.7 22.3 %collective-permute-start.45 = (bf16[1536,512]{1,0:T(8,128)(2,1)S(1)}, bf16[1536,512]{1,0:T(8,128)(2,1)S(1)}, u32[]{:S(2)}, u32[]{:S(2)}) collective-permute-start(bf16[1536,512]{1,0:T(8,128)(2,1)S(1)} %get-tuple-element.366), channel_id=1, source_target_pairs={{1,9},{3,11},{5,13},{7,15},{8,0},{10,2},{12,4},{14,6},{17,25},{19,... | collective-permute-start | bytes 4718600 | tf_op jit(solution)/shard_map/ppermute | solution.py:75
  283.2 18.7 %collective-permute-start.46 = (bf16[2,3,2,32,512]{4,3,1,0,2:T(8,128)(2,1)}, bf16[2,3,2,32,512]{4,3,1,0,2:T(8,128)(2,1)}, u32[]{:S(2)}, u32[]{:S(2)}) collective-permute-start(bf16[2,3,2,32,512]{4,3,1,0,2:T(8,128)(2,1)} %get-tuple-element.462), channel_id=1, source_target_pairs={{0,16},{2,18},{4,20},{6,22},{8,24},{10,26},{12,28},{14,30},{16,0},... | collective-permute-start | bytes 1179656 | tf_op jit(solution)/shard_map/ppermute | solution.py:67
  307.6 21.0 %collective-permute-start.50 = (bf16[2,3,2,32,512]{4,3,1,0,2:T(8,128)(2,1)S(1)}, bf16[2,3,2,32,512]{4,3,1,0,2:T(8,128)(2,1)S(1)}, u32[]{:S(2)}, u32[]{:S(2)}) collective-permute-start(bf16[2,3,2,32,512]{4,3,1,0,2:T(8,128)(2,1)S(1)} %get-tuple-element.456), channel_id=1, source_target_pairs={{0,16},{2,18},{4,20},{6,22},{8,24},{10,26},{12,28},{14,30},{16,0},... | collective-permute-start | bytes 1179656 | tf_op jit(solution)/shard_map/ppermute | solution.py:67
  309.5 19.0 %collective-permute-start.53 = (bf16[2,2,16,1792]{3,2,1,0:T(8,128)(2,1)S(1)}, bf16[2,2,16,1792]{3,2,1,0:T(8,128)(2,1)S(1)}, u32[]{:S(2)}, u32[]{:S(2)}) collective-permute-start(bf16[2,2,16,1792]{3,2,1,0:T(8,128)(2,1)S(1)} %bitcast.158), channel_id=1, source_target_pairs={{0,2},{2,0},{4,6},{6,4},{8,10},{10,8},{12,14},{14,12},{16,18},{18,... | collective-permute-start | bytes 688136 | tf_op jit(solution)/shard_map/ppermute | solution.py:67
  (87 other events, 1173.4 us)

commit v7 on v6

--- a/solution.py
+++ b/solution.py
@@ -539,9 +539,7 @@
             jax.ShapeDtypeStruct((D, 128), f32),
         ),
         compiler_params=params(),
-        cost_estimate=pl.CostEstimate(
-            flops=4 * rows * D * 128, bytes_accessed=10_000_000, transcendentals=0
-        ),
+        cost_estimate=cost(5),
         name="gates",
     )(ints, back, cols, probs, x, small)
 
@@ -637,7 +635,7 @@
         ),
         out_shape=(jax.ShapeDtypeStruct((rows, e_in), bf16), jax.ShapeDtypeStruct((D, PACK), bf16)),
         compiler_params=params(),
-        cost_estimate=pl.CostEstimate(flops=4 * rows * D * e_in, bytes_accessed=14_000_000, transcendentals=0),
+        cost_estimate=cost(10),
         name="finish",
     )(ints, *halves, added, arrived, events, small, *wholes, *vecs)
 
@@ -714,6 +712,10 @@
     )(ints, *own, *other)
 
 
+def cost(microseconds):
+    return pl.CostEstimate(flops=int(microseconds * 1.15e9), bytes_accessed=0, transcendentals=0)
+
+
 def params():
     return pltpu.CompilerParams(vmem_limit_bytes=VMEM_LIMIT)
 
@@ -838,7 +840,7 @@
         ),
         out_shape=(shape(3), shape(3), shape(3), shape(3), shape(6)),
         compiler_params=params(),
-        cost_estimate=pl.CostEstimate(flops=0, bytes_accessed=3_000_000, transcendentals=0),
+        cost_estimate=cost(1),
         name="choose",
     )(own_ids, other_ids, w_in, w_out_t, w_in, w_out_t)
 
@@ -883,9 +885,7 @@
             jax.ShapeDtypeStruct((8, rows), f32),
         ),
         compiler_params=params(),
-        cost_estimate=pl.CostEstimate(
-            flops=2 * rows * e_in * (rows + D), bytes_accessed=12_000_000, transcendentals=rows * 8
-        ),
+        cost_estimate=cost(11),
         name="prepare",
     )(ints, floats, table, embeds, embeds_in, small, small, vec)
 
@@ -950,9 +950,7 @@
         + ((jax.ShapeDtypeStruct((half, D), bf16),) if gives else ()),
         input_output_aliases=aliases,
         compiler_params=params(),
-        cost_estimate=pl.CostEstimate(
-            flops=4 * (shared + 1) * half * D * H, bytes_accessed=12_000_000, transcendentals=0
-        ),
+        cost_estimate=cost(5 * len(experts) - 5 * (len(experts) > 3)),
         name="experts_forward",
     )(ints, *inputs)
     found = out[0], out[1], {**norms, **dict(zip(arrays, out[2:]))}
@@ -1016,9 +1014,7 @@
         ),
         input_output_aliases=aliases,
         compiler_params=params(),
-        cost_estimate=pl.CostEstimate(
-            flops=10 * count * (rows // 2) * D * H, bytes_accessed=20_000_000, transcendentals=0
-        ),
+        cost_estimate=cost(8 * count),
         name="experts_backward",
     )(ints, *inputs)
 
@@ -1058,9 +1054,7 @@
             jax.ShapeDtypeStruct((8, 128), f32),
         ),
         compiler_params=params(),
-        cost_estimate=pl.CostEstimate(
-            flops=6 * rows * D * DOM * TW, bytes_accessed=10_000_000, transcendentals=rows * DOM * TW
-        ),
+        cost_estimate=cost(8.5),
         name="towers",
     )(ints, mix, other, cols, small, tower_vec)
 

time: 349 us -> 344 us (0.986)
  waiting for transfers between devices: 76.4 us -> 83.3 us
  other arithmetic: 30.2 us -> 23.4 us
    ppermute x41, waiting for transfers between devices: 66.7 us -> 73.1 us  [send(): return lax.ppermute(values, 'dp', pairs)]
    unnamed x101 -> x131, local copies, waits for them, and re-layouts: 8.97 us -> 7.3 us
  transfers between devices with their start and end apart: 61 -> 61, of which waited for: 22 -> 22; matrix products, arithmetic and copies ran while one was open for 10% -> 9% of each run, Pallas kernels for 37% -> 37%
where the time goes in v7:
time: 344 us; the launch traced here: 339 us
  Pallas kernels  146 us (42%)
  waiting for transfers between devices  83.3 us (24%)
  starting transfers between devices  65.4 us (19%)
  other arithmetic  23.4 us (7%)
  local copies, waits for them, and re-layouts  14.6 us (4%)
  matrix products  4.28 us (1%)
    ppermute x41, waiting for transfers between devices, send(): return lax.ppermute(values, 'dp', pairs)  73.1 us
    pallas_call x4, Pallas kernels, call_backward(): pl.pallas_call(functools.partial(backward_kernel, experts, halves, mode =...  66.9 us
    ppermute x41, starting transfers between devices, send(): return lax.ppermute(values, 'dp', pairs)  51.3 us
    pallas_call x3, Pallas kernels, call_forward(): pl.pallas_call(functools.partial(forward_kernel, experts, own, len(kept),...  37.7 us
    pallas_call x1, Pallas kernels, call_prepare(): pl.pallas_call(prepare_kernel, grid_spec=pltpu.PrefetchScalarGridSpec(num...  11.7 us
    pallas_call x1, Pallas kernels, call_finish(): pl.pallas_call(finish_kernel, grid_spec=pltpu.PrefetchScalarGridSpec(num_...  9.81 us
    pallas_call x1, Pallas kernels, call_tower(): pl.pallas_call(tower_kernel, grid_spec=pltpu.PrefetchScalarGridSpec(num_s...  8.8 us
    ppermute x4, starting transfers between devices, to_partner(): return lax.ppermute(values, ('dp', 'tensor'), pairs)  7.81 us
  transfers between devices with their start and end apart: 61, of which 22 were waited for; matrix products, arithmetic and copies ran while one was open for 9% of the time, Pallas kernels for 37%

profile of v7, /device:TPU:0, one launch (start us, length us, event | category | flops | bytes accessed | tf_op | source)
XLA Modules:
  0.0 339.5 jit_solution(11627231639400407807)
XLA Ops:
  4.8 4.1 %collective-permute-start.1 = (bf16[2,3,32,512]{3,2,1,0:T(8,128)(2,1)S(1)}, bf16[2,3,32,512]{3,2,1,0:T(8,128)(2,1)S(1)}, u32[]{:S(2)}, u32[]{:S(2)}) collective-permute-start(bf16[2,3,32,512]{3,2,1,0:T(8,128)(2,1)S(1)} %get-tuple-element.231), channel_id=1, source_target_pairs={{0,16},{2,18},{4,20},{6,22},{8,24},{10,26},{12,28},{14,30},{16,0},... | collective-permute-start | bytes 589832 | tf_op jit(solution)/shard_map/ppermute | solution.py:67
  12.0 3.4 %collective-permute-done.13 = bf16[16,1792]{1,0:T(8,128)(2,1)S(1)} collective-permute-done((bf16[16,1792]{1,0:T(8,128)(2,1)S(1)}, bf16[16,1792]{1,0:T(8,128)(2,1)S(1)}, u32[]{:S(2)}, u32[]{:S(2)}) %collective-permute-start.13) | collective-permute-done | bytes 57376 | tf_op jit(solution)/shard_map/ppermute | solution.py:67
  18.1 13.4 %collective-permute-done.14 = bf16[32,1792]{1,0:T(8,128)(2,1)S(1)} collective-permute-done((bf16[32,1792]{1,0:T(8,128)(2,1)S(1)}, bf16[32,1792]{1,0:T(8,128)(2,1)S(1)}, u32[]{:S(2)}, u32[]{:S(2)}) %collective-permute-start.14) | collective-permute-done | bytes 114720 | tf_op jit(solution)/shard_map/ppermute | solution.py:67
  45.5 8.8 %collective-permute-done.5 = bf16[2,3,32,512]{3,2,1,0:T(8,128)(2,1)} collective-permute-done((bf16[2,3,32,512]{3,2,1,0:T(8,128)(2,1)S(1)}, bf16[2,3,32,512]{3,2,1,0:T(8,128)(2,1)}, u32[]{:S(2)}, u32[]{:S(2)}) %collective-permute-start.5) | collective-permute-done | bytes 196640 | tf_op jit(solution)/shard_map/ppermute | solution.py:67
  72.2 5.9 %collective-permute-done.12.in_ref = bf16[1536,640]{1,0:T(8,128)(2,1)} collective-permute-done((bf16[1536,640]{1,0:T(8,128)(2,1)}, bf16[1536,640]{1,0:T(8,128)(2,1)}, u32[]{:S(2)}, u32[]{:S(2)}) %collective-permute-start.12) | collective-permute-done | bytes 1966112 | tf_op jit(solution)/shard_map/ppermute | solution.py:75
  78.1 11.7 %prepare.1 = (bf16[1536,640]{1,0:T(8,128)(2,1)}, bf16[1536,512]{1,0:T(8,128)(2,1)}, f32[1536,512]{1,0:T(8,128)}, f32[1536,128]{1,0:T(8,128)S(1)}, f32[8,1536]{1,0:T(8,128)S(1)}) custom-call(s32[24]{0:T(128)S(1)} %concatenate.92.ints, f32[8]{0:T(128)S(1)} %pad_maximum_fusion.19.floats, f32[8,1536]{1,0:T(8,128)S(1)} %pad_maximum_fusion.15.rows_ref, ...), custom_call_target="tpu_custom_call" | custom-call | flops 12650000384 | tf_op jit(solution)/shard_map/prepare/pallas_call | solution.py:863
  97.8 11.9 %experts_forward.3 = (f32[1536,128]{1,0:T(8,128)S(1)}, f32[1536,512]{1,0:T(8,128)}, bf16[3,1536,512]{2,1,0:T(8,128)(2,1)}) custom-call(s32[24]{0:T(128)S(1)} %concatenate.92.ints, bf16[1536,512]{1,0:T(8,128)(2,1)} %get-tuple-element.268.x_ref, ...), custom_call_target="tpu_custom_call", output_to_operand_aliasing={{0}: (12, {}), {1}: (13, {})} | custom-call | flops 17250000896 | tf_op jit(solution)/shard_map/experts_forward/pallas_call | solution.py:930
  109.7 2.7 collective-permute-done.23.refs_3_.refs_11_.refs_6_
  119.0 8.0 %experts_forward.4 = (f32[1536,128]{1,0:T(8,128)S(1)}, f32[1536,512]{1,0:T(8,128)}, bf16[3,1536,512]{2,1,0:T(8,128)(2,1)}, bf16[768,512]{1,0:T(8,128)(2,1)S(1)}) custom-call(s32[24]{0:T(128)S(1)} %concatenate.92.ints, bf16[1536,512]{1,0:T(8,128)(2,1)} %get-tuple-element.268.x_ref, ...), custom_call_target="tpu_custom_call", output_to_operand_aliasing={{0}: (12, {}), {1}: (13, {})} | custom-call | flops 11500000256 | tf_op jit(solution)/shard_map/experts_forward/pallas_call | solution.py:930
  127.1 17.8 %experts_forward.5 = (f32[1536,128]{1,0:T(8,128)S(1)}, f32[1536,512]{1,0:T(8,128)}, bf16[3,1536,512]{2,1,0:T(8,128)(2,1)}, bf16[3,1536,512]{2,1,0:T(8,128)(2,1)}) custom-call(s32[24]{0:T(128)S(1)} %concatenate.92.ints, bf16[1536,512]{1,0:T(8,128)(2,1)} %get-tuple-element.268.x_ref, ...), custom_call_target="tpu_custom_call", output_to_operand_aliasing={{0}: (20, {}), {1}: (21, {}), {2}: (22, {}), {3}: (23, {})} | custom-call | flops 28750000128 | tf_op jit(solution)/shard_map/experts_forward/pallas_call | solution.py:930
  146.6 8.8 %towers.1 = (f32[8,768]{1,0:T(8,128)S(1)}, f32[768,512]{1,0:T(8,128)}, bf16[768,512]{1,0:T(8,128)(2,1)S(1)}, f32[512,1024]{1,0:T(8,128)}, f32[8,1024]{1,0:T(8,128)S(1)}, /*index=5*/f32[8,128]{1,0:T(8,128)S(1)}) custom-call(s32[24]{0:T(128)S(1)} %concatenate.92.ints, f32[1536,512]{1,0:T(8,128)} %get-tuple-element.293.mix_ref, ...), custom_call_target="tpu_custom_call" | custom-call | flops 9774999552 | tf_op jit(solution)/shard_map/towers/pallas_call | solution.py:1033
  156.1 16.7 %experts_backward.4 = (f32[1536,128]{1,0:T(8,128)S(1)}, f32[1536,512]{1,0:T(8,128)}, bf16[2,2,512,512]{3,2,1,0:T(8,128)(2,1)}, bf16[2,2,512,512]{3,2,1,0:T(8,128...) custom-call(s32[24]{0:T(128)S(1)} %concatenate.92.ints, ...), custom_call_target="tpu_custom_call", output_to_operand_aliasing={{0}: (14, {})} | custom-call | flops 18400000000 | tf_op jit(solution)/shard_map/experts_backward/pallas_call | solution.py:996
  176.8 17.2 %experts_backward.5 = (f32[1536,128]{1,0:T(8,128)S(1)}, f32[1536,512]{1,0:T(8,128)}, bf16[2,2,512,512]{3,2,1,0:T(8,128)(2,1)}, bf16[2,2,512,512]{3,2,1,0:T(8,128...) custom-call(s32[24]{0:T(128)S(1)} %concatenate.92.ints, ...), custom_call_target="tpu_custom_call", output_to_operand_aliasing={{0}: (14, {}), {1}: (15, {})} | custom-call | flops 18400000000 | tf_op jit(solution)/shard_map/experts_backward/pallas_call | solution.py:996
  196.2 11.2 %experts_backward.6 = (f32[1536,128]{1,0:T(8,128)S(1)}, f32[1536,512]{1,0:T(8,128)}, bf16[1,2,512,512]{3,2,1,0:T(8,128)(2,1)}, bf16[1,2,512,512]{3,2,1,0:T(8,128...) custom-call(s32[24]{0:T(128)S(1)} %concatenate.92.ints, ...), custom_call_target="tpu_custom_call", output_to_operand_aliasing={{0}: (15, {}), {1}: (16, {})} | custom-call | flops 9200000000 | tf_op jit(solution)/shard_map/experts_backward/pallas_call | solution.py:996
  207.7 2.9 collective-permute-start.38
  214.9 21.8 %experts_backward.7 = (f32[1536,128]{1,0:T(8,128)S(1)}, f32[1536,512]{1,0:T(8,128)}, bf16[3,2,512,512]{3,2,1,0:T(8,128)(2,1)}, bf16[3,2,512,512]{3,2,1,0:T(8,128...) custom-call(s32[24]{0:T(128)S(1)} %concatenate.92.ints, ...), custom_call_target="tpu_custom_call", output_to_operand_aliasing={{0}: (15, {}), {1}: (16, {})} | custom-call | flops 27599998976 | tf_op jit(solution)/shard_map/experts_backward/pallas_call | solution.py:996
  236.8 3.1 collective-permute-start.41
  246.4 5.2 %gates.1 = (f32[1536,512]{1,0:T(8,128)}, bf16[1536,512]{1,0:T(8,128)(2,1)S(1)}, f32[512,128]{1,0:T(8,128)S(1)}) custom-call(s32[24]{0:T(128)S(1)} %concatenate.92.ints, f32[1536,512]{1,0:T(8,128)} %get-tuple-element.351.back_ref, f32[1536,128]{1,0:T(8,128)S(1)} %get-tuple-element.352.cols_ref, f32[8,1536]{1,0:T(8,128)S(1)} %get-tuple-element.353.prob_ref, ...), custom_call_target="tpu_custom_call" | custom-call | flops 5750000128 | tf_op jit(solution)/shard_map/gates/pallas_call | solution.py:522
  262.4 15.9 %collective-permute-done.43 = bf16[3,2,2,2,32,512]{5,4,0,3,2,1:T(8,128)(2,1)} collective-permute-done((bf16[3,2,2,2,32,512]{5,4,0,3,2,1:T(8,128)(2,1)}, bf16[3,2,2,2,32,512]{5,4,0,3,2,1:T(8,128)(2,1)}, u32[]{:S(2)}, u32[]{:S(2)}) %collective-permute-start.43) | collective-permute-done | bytes 786464 | tf_op jit(solution)/shard_map/ppermute | solution.py:67
  288.9 9.8 %finish.1 = (bf16[1536,640]{1,0:T(8,128)(2,1)}, bf16[512,1792]{1,0:T(8,128)(2,1)}) custom-call(s32[24]{0:T(128)S(1)} %concatenate.92.ints, f32[768,512]{1,0:T(8,128)S(1)} %copy-done.20, bf16[768,512]{1,0:T(8,128)(2,1)S(1)} %copy-done.9, f32[1536,512]{1,0:T(8,128)} %get-tuple-element.376.sum_ref, bf16[1536,512]{1,0:T(8,128)(2,1)S(1)} %collective-permute-done.45.in_ref, ...), custom_call_target="tpu_custom_call" | custom-call | flops 11500000256 | tf_op jit(solution)/shard_map/finish/pallas_call | solution.py:625
  308.7 4.3 %fusion.2 = bf16[1536,640]{1,0:T(8,128)(2,1)S(1)} fusion(bf16[1536,640]{1,0:T(8,128)(2,1)S(1)} %copy-done.63, f32[1536]{0:T(1024)S(1)} %copy-done.43), kind=kOutput, calls=%fused_computation.4 | convolution fusion | flops 3023241216 | bytes 3938304 | tf_op jit(solution)/shard_map/dot_general | solution.py:1327
  314.8 9.1 %collective-permute-done.50 = bf16[2,3,2,32,512]{4,3,1,0,2:T(8,128)(2,1)S(1)} collective-permute-done((bf16[2,3,2,32,512]{4,3,1,0,2:T(8,128)(2,1)S(1)}, bf16[2,3,2,32,512]{4,3,1,0,2:T(8,128)(2,1)S(1)}, u32[]{:S(2)}, u32[]{:S(2)}) %collective-permute-start.50) | collective-permute-done | bytes 393248 | tf_op jit(solution)/shard_map/ppermute | solution.py:67
  325.1 2.9 collective-permute-start.58
  334.1 2.7 collective-permute-done.55.refs_3_
  (362 shorter events, 118.1 us)
Async XLA Ops:
  4.8 28.4 %collective-permute-start.1 = (bf16[2,3,32,512]{3,2,1,0:T(8,128)(2,1)S(1)}, bf16[2,3,32,512]{3,2,1,0:T(8,128)(2,1)S(1)}, u32[]{:S(2)}, u32[]{:S(2)}) collective-permute-start(bf16[2,3,32,512]{3,2,1,0:T(8,128)(2,1)S(1)} %get-tuple-element.231), channel_id=1, source_target_pairs={{0,16},{2,18},{4,20},{6,22},{8,24},{10,26},{12,28},{14,30},{16,0},... | collective-permute-start | bytes 589832 | tf_op jit(solution)/shard_map/ppermute | solution.py:67
  10.8 22.3 %collective-permute-start.2 = (bf16[2,3,32,512]{3,2,1,0:T(8,128)(2,1)S(1)}, bf16[2,3,32,512]{3,2,1,0:T(8,128)(2,1)S(1)}, u32[]{:S(2)}, u32[]{:S(2)}) collective-permute-start(bf16[2,3,32,512]{3,2,1,0:T(8,128)(2,1)S(1)} %get-tuple-element.228), channel_id=1, source_target_pairs={{0,24},{2,26},{4,28},{6,30},{8,16},{10,18},{12,20},{14,22},{16,8},... | collective-permute-start | bytes 589832 | tf_op jit(solution)/shard_map/ppermute | solution.py:67
  10.8 22.3 %collective-permute-start = (bf16[2,6,32,512]{3,2,1,0:T(8,128)(2,1)S(1)}, bf16[2,6,32,512]{3,2,1,0:T(8,128)(2,1)S(1)}, u32[]{:S(2)}, u32[]{:S(2)}) collective-permute-start(bf16[2,6,32,512]{3,2,1,0:T(8,128)(2,1)S(1)} %get-tuple-element.226), channel_id=1, source_target_pairs={{0,8},{2,10},{4,12},{6,14},{8,0},{10,2},{12,4},{14,6},{16,24},{18,... | collective-permute-start | bytes 1179656 | tf_op jit(solution)/shard_map/ppermute | solution.py:67
  36.2 20.7 %collective-permute-start.6 = (bf16[2,3,32,512]{3,2,1,0:T(8,128)(2,1)S(1)}, bf16[2,3,32,512]{3,2,1,0:T(8,128)(2,1)}, u32[]{:S(2)}, u32[]{:S(2)}) collective-permute-start(bf16[2,3,32,512]{3,2,1,0:T(8,128)(2,1)S(1)} %get-tuple-element.236), channel_id=1, source_target_pairs={{0,24},{2,26},{4,28},{6,30},{8,16},{10,18},{12,20},{14,22},{16,8},... | collective-permute-start | bytes 589832 | tf_op jit(solution)/shard_map/ppermute | solution.py:67
  42.8 21.0 %collective-permute-start.16 = (bf16[128,1792]{1,0:T(8,128)(2,1)}, bf16[128,1792]{1,0:T(8,128)(2,1)}, u32[]{:S(2)}, u32[]{:S(2)}) collective-permute-start(bf16[128,1792]{1,0:T(8,128)(2,1)} %pad_maximum_fusion.7), channel_id=1, source_target_pairs={{0,2},{2,0},{4,6},{6,4},{8,10},{10,8},{12,14},{14,12},{16,18},{18,... | collective-permute-start | bytes 1376264 | tf_op jit(solution)/shard_map/ppermute | solution.py:67
  54.3 23.8 %collective-permute-start.12 = (bf16[1536,640]{1,0:T(8,128)(2,1)}, bf16[1536,640]{1,0:T(8,128)(2,1)}, u32[]{:S(2)}, u32[]{:S(2)}) collective-permute-start(bf16[1536,640]{1,0:T(8,128)(2,1)} %own_ref.1), channel_id=1, source_target_pairs={{0,8},{2,10},{4,12},{6,14},{9,1},{11,3},{13,5},{15,7},{16,24},{18,... | collective-permute-start | bytes 5898248 | tf_op jit(solution)/shard_map/ppermute | solution.py:75
  58.7 31.1 %collective-permute-start.9 = (bf16[2,2,3,64,512]{4,3,2,1,0:T(8,128)(2,1)S(1)}, bf16[2,2,3,64,512]{4,3,2,1,0:T(8,128)(2,1)}, u32[]{:S(2)}, u32[]{:S(2)}) collective-permute-start(bf16[2,2,3,64,512]{4,3,2,1,0:T(8,128)(2,1)S(1)} %pad_maximum_fusion.4.refs_2_.refs_4_.refs_5_), channel_id=1, source_target_pairs={{0,4},{2,6},{4,0},{6,2},{8,12},{10,14},{12,8},{14,10},{16,20},{18,... | collective-permute-start | bytes 2359304 | tf_op jit(solution)/shard_map/ppermute | solution.py:67
  59.8 30.1 %collective-permute-start.8 = (bf16[2,2,3,64,512]{4,3,2,1,0:T(8,128)(2,1)S(1)}, bf16[2,2,3,64,512]{4,3,2,1,0:T(8,128)(2,1)}, u32[]{:S(2)}, u32[]{:S(2)}) collective-permute-start(bf16[2,2,3,64,512]{4,3,2,1,0:T(8,128)(2,1)S(1)} %pad_maximum_fusion.3.refs_0_.refs_2_.refs_3_), channel_id=1, source_target_pairs={{0,2},{2,0},{4,6},{6,4},{8,10},{10,8},{12,14},{14,12},{16,18},{18,... | collective-permute-start | bytes 2359304 | tf_op jit(solution)/shard_map/ppermute | solution.py:67
  65.0 24.8 %collective-permute-start.10 = (bf16[2,3,64,512]{3,2,1,0:T(8,128)(2,1)S(1)}, bf16[2,3,64,512]{3,2,1,0:T(8,128)(2,1)}, u32[]{:S(2)}, u32[]{:S(2)}) collective-permute-start(bf16[2,3,64,512]{3,2,1,0:T(8,128)(2,1)S(1)} %pad_maximum_fusion.12), channel_id=1, source_target_pairs={{0,4},{2,6},{4,0},{6,2},{8,12},{10,14},{12,8},{14,10},{16,20},{18,... | collective-permute-start | bytes 1179656 | tf_op jit(solution)/shard_map/ppermute | solution.py:67
  67.6 22.2 %collective-permute-start.11 = (bf16[2,3,64,512]{3,2,1,0:T(8,128)(2,1)S(1)}, bf16[2,3,64,512]{3,2,1,0:T(8,128)(2,1)S(1)}, u32[]{:S(2)}, u32[]{:S(2)}) collective-permute-start(bf16[2,3,64,512]{3,2,1,0:T(8,128)(2,1)S(1)} %pad_maximum_fusion.13), channel_id=1, source_target_pairs={{0,2},{2,0},{4,6},{6,4},{8,10},{10,8},{12,14},{14,12},{16,18},{18,... | collective-permute-start | bytes 1179656 | tf_op jit(solution)/shard_map/ppermute | solution.py:67
  91.0 24.2 %collective-permute-start.26 = (bf16[2,2,3,64,512]{4,3,2,1,0:T(8,128)(2,1)S(1)}, bf16[2,2,3,64,512]{4,3,2,1,0:T(8,128)(2,1)S(1)}, u32[]{:S(2)}, u32[]{:S(2)}) collective-permute-start(bf16[2,2,3,64,512]{4,3,2,1,0:T(8,128)(2,1)S(1)} %pad_maximum_fusion.6.refs_2_.refs_10_.refs_5_), channel_id=1, source_target_pairs={{0,1},{1,0},{2,3},{3,2},{4,5},{5,4},{6,7},{7,6},{8,9},{9,8},{10,11... | collective-permute-start | bytes 2359304 | tf_op jit(solution)/shard_map/ppermute | solution.py:125
  92.6 19.8 %collective-permute-start.23 = (bf16[2,2,3,64,512]{4,3,2,1,0:T(8,128)(2,1)S(1)}, bf16[2,2,3,64,512]{4,3,2,1,0:T(8,128)(2,1)S(1)}, u32[]{:S(2)}, u32[]{:S(2)}) collective-permute-start(bf16[2,2,3,64,512]{4,3,2,1,0:T(8,128)(2,1)S(1)} %pad_maximum_fusion.6.refs_2_.refs_10_.refs_5_), channel_id=1, source_target_pairs={{0,4},{2,6},{4,0},{6,2},{8,12},{10,14},{12,8},{14,10},{16,20},{18,... | collective-permute-start | bytes 2359304 | tf_op jit(solution)/shard_map/ppermute | solution.py:67
  94.7 20.5 %collective-permute-start.24 = (bf16[2,2,3,64,512]{4,3,2,1,0:T(8,128)(2,1)S(1)}, bf16[2,2,3,64,512]{4,3,2,1,0:T(8,128)(2,1)S(1)}, u32[]{:S(2)}, u32[]{:S(2)}) collective-permute-start(bf16[2,2,3,64,512]{4,3,2,1,0:T(8,128)(2,1)S(1)} %pad_maximum_fusion.5.refs_0_.refs_8_.refs_3_), channel_id=1, source_target_pairs={{0,1},{1,0},{2,3},{3,2},{4,5},{5,4},{6,7},{7,6},{8,9},{9,8},{10,11... | collective-permute-start | bytes 2359304 | tf_op jit(solution)/shard_map/ppermute | solution.py:125
  94.9 19.8 %collective-permute-start.22 = (bf16[2,2,3,64,512]{4,3,2,1,0:T(8,128)(2,1)S(1)}, bf16[2,2,3,64,512]{4,3,2,1,0:T(8,128)(2,1)S(1)}, u32[]{:S(2)}, u32[]{:S(2)}) collective-permute-start(bf16[2,2,3,64,512]{4,3,2,1,0:T(8,128)(2,1)S(1)} %pad_maximum_fusion.5.refs_0_.refs_8_.refs_3_), channel_id=1, source_target_pairs={{0,2},{2,0},{4,6},{6,4},{8,10},{10,8},{12,14},{14,12},{16,18},{18,... | collective-permute-start | bytes 2359304 | tf_op jit(solution)/shard_map/ppermute | solution.py:67
  127.0 19.6 %collective-permute-start.28 = (bf16[768,512]{1,0:T(8,128)(2,1)S(1)}, bf16[768,512]{1,0:T(8,128)(2,1)S(1)}, u32[]{:S(2)}, u32[]{:S(2)}) collective-permute-start(bf16[768,512]{1,0:T(8,128)(2,1)S(1)} %get-tuple-element.294), channel_id=1, source_target_pairs={{0,8},{2,10},{4,12},{6,14},{8,0},{10,2},{12,4},{14,6},{16,24},{18,... | collective-permute-start | bytes 2359304 | tf_op jit(solution)/shard_map/ppermute | solution.py:67
  155.4 19.9 %collective-permute-start.29 = (bf16[768,512]{1,0:T(8,128)(2,1)S(1)}, bf16[768,512]{1,0:T(8,128)(2,1)S(1)}, u32[]{:S(2)}, u32[]{:S(2)}) collective-permute-start(bf16[768,512]{1,0:T(8,128)(2,1)S(1)} %get-tuple-element.298.refs_0_), channel_id=1, source_target_pairs={{0,8},{2,10},{4,12},{6,14},{8,0},{10,2},{12,4},{14,6},{16,24},{18,... | collective-permute-start | bytes 2359304 | tf_op jit(solution)/shard_map/ppermute | solution.py:67
  207.7 29.1 %collective-permute-start.38 = (f32[8,128]{1,0:T(8,128)S(1)}, f32[8,128]{1,0:T(8,128)S(1)}, u32[]{:S(2)}, u32[]{:S(2)}) collective-permute-start(f32[8,128]{1,0:T(8,128)S(1)} %add.311), channel_id=1, source_target_pairs={{0,8},{2,10},{4,12},{6,14},{8,0},{10,2},{12,4},{14,6},{16,24},{18,... | collective-permute-start | bytes 12296 | tf_op jit(solution)/shard_map/ppermute | solution.py:67
  210.6 26.2 %collective-permute-start.37 = (f32[8,768]{1,0:T(8,128)S(1)}, f32[8,768]{1,0:T(8,128)S(1)}, u32[]{:S(2)}, u32[]{:S(2)}) collective-permute-start(f32[8,768]{1,0:T(8,128)S(1)} %get-tuple-element.345), channel_id=1, source_target_pairs={{1,9},{3,11},{5,13},{7,15},{8,0},{10,2},{12,4},{14,6},{17,25},{19,... | collective-permute-start | bytes 73736 | tf_op jit(solution)/shard_map/ppermute | solution.py:75
  213.1 23.7 %collective-permute-start.36 = (bf16[3,2,2,2,32,512]{5,4,0,3,2,1:T(8,128)(2,1)S(1)}, bf16[3,2,2,2,32,512]{5,4,0,3,2,1:T(8,128)(2,1)S(1)}, u32[]{:S(2)}, u32[]{:S(2)}) collective-permute-start(bf16[3,2,2,2,32,512]{5,4,0,3,2,1:T(8,128)(2,1)S(1)} %bitcast.153), channel_id=1, source_target_pairs={{0,4},{2,6},{4,0},{6,2},{8,12},{10,14},{12,8},{14,10},{16,20},{18,... | collective-permute-start | bytes 2359304 | tf_op jit(solution)/shard_map/ppermute | solution.py:67
  213.6 23.2 %collective-permute-start.35 = (bf16[3,2,2,2,32,512]{5,4,0,3,2,1:T(8,128)(2,1)S(1)}, bf16[3,2,2,2,32,512]{5,4,0,3,2,1:T(8,128)(2,1)S(1)}, u32[]{:S(2)}, u32[]{:S(2)}) collective-permute-start(bf16[3,2,2,2,32,512]{5,4,0,3,2,1:T(8,128)(2,1)S(1)} %get-tuple-element.450), channel_id=1, source_target_pairs={{0,2},{2,0},{4,6},{6,4},{8,10},{10,8},{12,14},{14,12},{16,18},{18,... | collective-permute-start | bytes 2359304 | tf_op jit(solution)/shard_map/ppermute | solution.py:67
  256.2 24.0 %collective-permute-start.45 = (bf16[1536,512]{1,0:T(8,128)(2,1)S(1)}, bf16[1536,512]{1,0:T(8,128)(2,1)S(1)}, u32[]{:S(2)}, u32[]{:S(2)}) collective-permute-start(bf16[1536,512]{1,0:T(8,128)(2,1)S(1)} %get-tuple-element.366), channel_id=1, source_target_pairs={{1,9},{3,11},{5,13},{7,15},{8,0},{10,2},{12,4},{14,6},{17,25},{19,... | collective-permute-start | bytes 4718600 | tf_op jit(solution)/shard_map/ppermute | solution.py:75
  259.0 19.3 %collective-permute-start.43 = (bf16[3,2,2,2,32,512]{5,4,0,3,2,1:T(8,128)(2,1)}, bf16[3,2,2,2,32,512]{5,4,0,3,2,1:T(8,128)(2,1)}, u32[]{:S(2)}, u32[]{:S(2)}) collective-permute-start(bf16[3,2,2,2,32,512]{5,4,0,3,2,1:T(8,128)(2,1)} %get-tuple-element.446), channel_id=1, source_target_pairs={{0,2},{2,0},{4,6},{6,4},{8,10},{10,8},{12,14},{14,12},{16,18},{18,... | collective-permute-start | bytes 2359304 | tf_op jit(solution)/shard_map/ppermute | solution.py:67
  261.0 19.3 %collective-permute-start.44 = (bf16[3,2,2,2,32,512]{5,4,0,3,2,1:T(8,128)(2,1)}, bf16[3,2,2,2,32,512]{5,4,0,3,2,1:T(8,128)(2,1)}, u32[]{:S(2)}, u32[]{:S(2)}) collective-permute-start(bf16[3,2,2,2,32,512]{5,4,0,3,2,1:T(8,128)(2,1)} %get-tuple-element.444), channel_id=1, source_target_pairs={{0,4},{2,6},{4,0},{6,2},{8,12},{10,14},{12,8},{14,10},{16,20},{18,... | collective-permute-start | bytes 2359304 | tf_op jit(solution)/shard_map/ppermute | solution.py:67
  303.0 20.9 %collective-permute-start.50 = (bf16[2,3,2,32,512]{4,3,1,0,2:T(8,128)(2,1)S(1)}, bf16[2,3,2,32,512]{4,3,1,0,2:T(8,128)(2,1)S(1)}, u32[]{:S(2)}, u32[]{:S(2)}) collective-permute-start(bf16[2,3,2,32,512]{4,3,1,0,2:T(8,128)(2,1)S(1)} %get-tuple-element.456), channel_id=1, source_target_pairs={{0,16},{2,18},{4,20},{6,22},{8,24},{10,26},{12,28},{14,30},{16,0},... | collective-permute-start | bytes 1179656 | tf_op jit(solution)/shard_map/ppermute | solution.py:67
  (101 other events, 1110.3 us)
